TPU v7x, 512 devices: a whole 4x4x16 slice. The times are simulated.
512 devices in a mesh: blk: 8 (over y, x_lo), dp: 64 (over z, x_hi, core).
Axes of the slice: x: 4 (x_hi: 2, x_lo: 2; x = x_hi * 2 + x_lo), y: 4, z: 16, core: 2. Of those that a mesh axis runs over, the one named last changes fastest.
Arguments:
- image_features: bfloat16 [65536, 1536], P(('dp', 'blk')), may hold values from -11 to 11
- final_norm_gain: float32 [1536], replicated, may hold values from 0.25 to 1.75
- final_norm_bias: float32 [1536], replicated, may hold values from -3 to 3
- head_weight: bfloat16 [1536, 1536], P('blk'), may hold values from -0.15625 to 0.15625
- text_embed: bfloat16 [65536, 1536], P(('dp', 'blk')), may hold values from -6 to 6
- log_scale: float32 [1], replicated, may hold values from 1.6 to 2.6
- logit_bias: float32 [1], replicated, may hold values from -6 to -2
Outputs:
- grad_image_features: float32 [65536, 1536], P(('dp', 'blk'))
- grad_text: float32 [65536, 1536], P(('dp', 'blk'))
- grad_gain: float32 [1536], replicated
- grad_bias: float32 [1536], replicated
- grad_head: float32 [1536, 1536], P('blk')
All inputs are finite; a program needn't handle non-finite values.
Results may differ from a plain program's by a relative error of at most 0.005.
Values may be sent and summed in bfloat16 or wider, within the bound.
No kernel may reach another device: no remote copies, remote signals or barrier semaphores. Data moves between devices by JAX's collectives and lax.ppermute only.
A program may use at most 64 MiB of HBM per device.

v0:
```python
import jax
import jax.numpy as jnp
from jax import lax
from jax.sharding import PartitionSpec as P

epsilon = 1e-06
loss_scale = 64.0


def shifted(value, axis, steps):
    count = lax.axis_size(axis)
    pairs = [(source, (source + steps) % count) for source in range(count)]
    return lax.ppermute(value, axis, pairs)


def local(
    image_features, final_norm_gain, final_norm_bias, head_weight, text_embed, log_scale, logit_bias
):
    values = image_features.astype(jnp.float32)
    own_rows = values.shape[0]
    full_width = values.shape[1]
    scale = jnp.exp(log_scale[0])
    offset = logit_bias[0]
    full_weight = lax.all_gather(head_weight, "blk", axis=0, tiled=True)
    centre = jnp.mean(values, axis=1, keepdims=True)
    centered_input = values - centre
    spread = jnp.mean(centered_input * centered_input, axis=1, keepdims=True)
    inverse_deviation = lax.rsqrt(spread + epsilon)
    standardized_rows = centered_input * inverse_deviation
    normalized_output = (standardized_rows * final_norm_gain + final_norm_bias).astype(jnp.bfloat16)
    text_values = text_embed.astype(jnp.float32)
    inv_text = lax.rsqrt(jnp.sum(text_values * text_values, axis=1, keepdims=True) + epsilon)
    text_unit = (text_values * inv_text).astype(jnp.bfloat16)
    projected = jnp.dot(normalized_output, full_weight, preferred_element_type=jnp.float32)
    inv_proj = lax.rsqrt(jnp.sum(projected * projected, axis=1, keepdims=True) + epsilon)
    image_unit = (projected * inv_proj).astype(jnp.bfloat16)

    def logit_weights(image_rows, text_rows, diagonal):
        logits = (
            scale
            * lax.dot_general(
                image_rows, text_rows, (((1,), (1,)), ((), ())), preferred_element_type=jnp.float32
            )
            + offset
        )
        return (loss_scale * (jax.nn.sigmoid(logits) - diagonal)).astype(jnp.bfloat16)

    def transposed_product(weights, rows_data):
        return lax.dot_general(
            weights, rows_data, (((0,), (0,)), ((), ())), preferred_element_type=jnp.float32
        )

    empty_rows = jnp.zeros((own_rows, full_width), jnp.float32)
    eye_block = jnp.eye(own_rows, dtype=jnp.float32)

    def pass_grad(carried):
        return shifted(carried, "blk", 1)

    def accumulate(step, text_block, carried_grad, grad_image):
        diagonal = eye_block * jnp.asarray(step == 0).astype(jnp.float32)
        weights = logit_weights(image_unit, text_block, diagonal)
        grad_image = grad_image + scale * jnp.dot(
            weights, text_block, preferred_element_type=jnp.float32
        )
        carried_grad = carried_grad + scale * transposed_product(weights, image_unit)
        return (pass_grad(carried_grad), grad_image)

    def turn(step, loop_state):
        text_block, carried_grad, grad_image = loop_state
        carried_grad, grad_image = accumulate(step, text_block, carried_grad, grad_image)
        text_block = shifted(text_block, "blk", 1)
        return (text_block, carried_grad, grad_image)

    steps_total = lax.axis_size("blk")
    moved = lax.fori_loop(0, steps_total - 1, turn, (text_unit, empty_rows, empty_rows))
    grad_unit_text, grad_image = accumulate(steps_total - 1, moved[0], moved[1], moved[2])
    text_dot = jnp.sum(text_values * grad_unit_text, axis=1, keepdims=True)
    grad_text = inv_text * grad_unit_text - inv_text * inv_text * inv_text * text_dot * text_values
    proj_dot = jnp.sum(projected * grad_image, axis=1, keepdims=True)
    grad_proj = (
        inv_proj * grad_image - inv_proj * inv_proj * inv_proj * proj_dot * projected
    ).astype(jnp.bfloat16)
    normalized_gradient = lax.dot_general(
        grad_proj, full_weight, (((1,), (1,)), ((), ())), preferred_element_type=jnp.float32
    )
    scaled_output = normalized_gradient * final_norm_gain
    first_mean_term = jnp.mean(scaled_output, axis=1, keepdims=True)
    second_mean_term = jnp.mean(scaled_output * standardized_rows, axis=1, keepdims=True)
    feature_gradient = inverse_deviation * (
        scaled_output - first_mean_term - standardized_rows * second_mean_term
    )
    normed_columns = lax.all_to_all(
        normalized_output.T, "blk", split_axis=0, concat_axis=1, tiled=True
    )
    head_grad = jnp.dot(
        normed_columns,
        lax.all_gather(grad_proj, "blk", axis=0, tiled=True),
        preferred_element_type=jnp.float32,
    )
    gain_portion = jnp.sum(normalized_gradient * standardized_rows, axis=0)
    bias_part = jnp.sum(normalized_gradient, axis=0)
    head_total = lax.psum(head_grad, "dp")
    gain_total, bias_total = lax.psum((gain_portion, bias_part), ("blk", "dp"))
    group_count = lax.axis_size("dp")
    return (
        feature_gradient,
        grad_text,
        gain_total / group_count,
        bias_total / group_count,
        head_total / group_count,
    )


def solution(mesh):
    placed = (P(("dp", "blk"), None), P(), P(), P("blk", None), P(("dp", "blk"), None), P(), P())
    return jax.shard_map(
        local,
        mesh=mesh,
        in_specs=placed,
        out_specs=(P(("dp", "blk"), None), P(("dp", "blk"), None), P(), P(), P("blk", None)),
        check_vma=False,
    )
```

profile of v0, /device:TPU:1, one launch (start us, length us, event | category | flops | bytes accessed | tf_op | source)
XLA Modules:
  0.0 1006.7 jit_solution(5728597922265606092)
XLA Ops:
  13.0 110.3 %all-gather.3.cloned.1.call-done = bf16[1536,1536]{1,0:T(8,128)(2,1)} async-done(((bf16[192,1536]{1,0:T(8,128)(2,1)}), bf16[1536,1536]{1,0:T(8,128)(2,1)}) %all-gather.3.cloned.1.call-update) | async-done | bytes 4718608 | tf_op jit(solution)/shard_map/all_gather | solution.py:24
  123.2 3.4 multiply_reduce_fusion.1
  127.6 205.5 %while.18 = (s32[]{:T(128)}, bf16[128,1536]{1,0:T(8,128)(2,1)S(1)}, f32[128,1536]{1,0:T(8,128)S(1)}, f32[128,1536]{1,0:T(8,128)S(1)}, f32[]{:T(128)}, /*index=5*...) while((s32[]{:T(128)}, bf16[128,1536]{1,0:T(8,128)(2,1)S(1)}, ...), condition=%wide.region_5.0_spmd.clone, body=%wide.region_4.0_spmd.clone.sunk | while | flops 152141824 | bytes 10453228 | solution.py:75
  129.2 2.5 collective-permute-start.1
  131.7 3.1 collective-permute-start
  135.9 23.8 %collective-permute-done = bf16[128,1536]{1,0:T(8,128)(2,1)S(1)} collective-permute-done((bf16[128,1536]{1,0:T(8,128)(2,1)S(1)}, bf16[128,1536]{1,0:T(8,128)(2,1)S(1)}, u32[]{:S(2)}, u32[]{:S(2)}) %collective-permute-start) | collective-permute-done | bytes 393248 | tf_op jit(solution)/shard_map/while/body/eval_jaxpr/ppermute | solution.py:13
  163.3 2.8 collective-permute-start
  167.1 23.8 %collective-permute-done = bf16[128,1536]{1,0:T(8,128)(2,1)S(1)} collective-permute-done((bf16[128,1536]{1,0:T(8,128)(2,1)S(1)}, bf16[128,1536]{1,0:T(8,128)(2,1)S(1)}, u32[]{:S(2)}, u32[]{:S(2)}) %collective-permute-start) | collective-permute-done | bytes 393248 | tf_op jit(solution)/shard_map/while/body/eval_jaxpr/ppermute | solution.py:13
  194.5 1.9 collective-permute-start
  197.5 23.7 %collective-permute-done = bf16[128,1536]{1,0:T(8,128)(2,1)S(1)} collective-permute-done((bf16[128,1536]{1,0:T(8,128)(2,1)S(1)}, bf16[128,1536]{1,0:T(8,128)(2,1)S(1)}, u32[]{:S(2)}, u32[]{:S(2)}) %collective-permute-start) | collective-permute-done | bytes 393248 | tf_op jit(solution)/shard_map/while/body/eval_jaxpr/ppermute | solution.py:13
  224.8 1.9 collective-permute-start
  227.8 22.8 %collective-permute-done = bf16[128,1536]{1,0:T(8,128)(2,1)S(1)} collective-permute-done((bf16[128,1536]{1,0:T(8,128)(2,1)S(1)}, bf16[128,1536]{1,0:T(8,128)(2,1)S(1)}, u32[]{:S(2)}, u32[]{:S(2)}) %collective-permute-start) | collective-permute-done | bytes 393248 | tf_op jit(solution)/shard_map/while/body/eval_jaxpr/ppermute | solution.py:13
  254.1 1.9 collective-permute-start
  257.1 21.9 %collective-permute-done = bf16[128,1536]{1,0:T(8,128)(2,1)S(1)} collective-permute-done((bf16[128,1536]{1,0:T(8,128)(2,1)S(1)}, bf16[128,1536]{1,0:T(8,128)(2,1)S(1)}, u32[]{:S(2)}, u32[]{:S(2)}) %collective-permute-start) | collective-permute-done | bytes 393248 | tf_op jit(solution)/shard_map/while/body/eval_jaxpr/ppermute | solution.py:13
  282.5 1.9 collective-permute-start
  285.6 21.0 %collective-permute-done = bf16[128,1536]{1,0:T(8,128)(2,1)S(1)} collective-permute-done((bf16[128,1536]{1,0:T(8,128)(2,1)S(1)}, bf16[128,1536]{1,0:T(8,128)(2,1)S(1)}, u32[]{:S(2)}, u32[]{:S(2)}) %collective-permute-start) | collective-permute-done | bytes 393248 | tf_op jit(solution)/shard_map/while/body/eval_jaxpr/ppermute | solution.py:13
  313.1 20.0 %collective-permute-done = bf16[128,1536]{1,0:T(8,128)(2,1)S(1)} collective-permute-done((bf16[128,1536]{1,0:T(8,128)(2,1)S(1)}, bf16[128,1536]{1,0:T(8,128)(2,1)S(1)}, u32[]{:S(2)}, u32[]{:S(2)}) %collective-permute-start) | collective-permute-done | bytes 393248 | tf_op jit(solution)/shard_map/while/body/eval_jaxpr/ppermute | solution.py:13
  335.9 4.1 fusion.46
  342.0 3.5 all-to-all-start
  346.6 3.2 collective-permute-start.2
  349.8 135.8 %all-reduce = (f32[1536]{0:T(1024)}, f32[1536]{0:T(1024)}) all-reduce(f32[1536]{0:T(1024)S(1)} %get-tuple-element.175, f32[1536]{0:T(1024)} %get-tuple-element.178), channel_id=1, replica_groups=mesh['blk'=8,'dp'=64] {'blk','dp'}, use_global_device_ids=true, to_apply=%region_11.0 | all-reduce | flops 3072 | bytes 24576 | tf_op jit(solution)/shard_map/psum | solution.py:103
  488.7 3.7 fusion.38
  495.0 502.8 %all-reduce.3.cloned.1.call-done = f32[192,1536]{1,0:T(8,128)} async-done(((f32[192,1536]{1,0:T(8,128)}), f32[192,1536]{1,0:T(8,128)}) %all-reduce.3.cloned.1.call-update) | async-done | bytes 1179664 | tf_op jit(solution)/shard_map/psum | solution.py:102
  997.8 2.4 broadcast_multiply_fusion
  (126 shorter events, 48.6 us)
Async XLA Ops:
  7.2 116.1 %all-gather.3.cloned.1.call-start = ((), (), s32[]{:S(2)}) async-start(), calls=%async_computation.1 | async-start | bytes 5308416 | tf_op jit(solution)/shard_map/all_gather | solution.py:24
  7.9 480.8 %all-gather.5.cloned.1.call-start = ((), (), s32[]{:S(2)}) async-start(), calls=%async_computation.2 | async-start | bytes 3538944 | tf_op jit(solution)/shard_map/all_gather | solution.py:97
  11.6 115.1 %copy-start.17 = (f32[128]{0:T(128)}, f32[128]{0:T(128)S(1)}, u32[]{:S(2)}) copy-start(f32[128]{0:T(128)S(1)} %fusion.34) | copy-start | bytes 1540
  11.6 115.1 %copy-start.9 = (f32[128]{0:T(128)}, f32[128]{0:T(128)S(1)}, u32[]{:S(2)}) copy-start(f32[128]{0:T(128)S(1)} %broadcast_multiply_fusion.5) | copy-start | bytes 1540
  11.6 115.1 %copy-start.3 = (bf16[128,1536]{1,0:T(8,128)(2,1)S(1)}, bf16[128,1536]{1,0:T(8,128)(2,1)}, u32[]{:S(2)}) copy-start(bf16[128,1536]{1,0:T(8,128)(2,1)} %param.13) | copy-start | bytes 1179652
  12.9 113.8 %copy-start.13 = (f32[128]{0:T(128)}, f32[128]{0:T(128)S(1)}, u32[]{:S(2)}) copy-start(f32[128]{0:T(128)S(1)} %add_rsqrt_fusion.2) | copy-start | bytes 1540
  12.9 113.9 %copy-start.15 = (f32[128]{0:T(128)}, f32[128]{0:T(128)S(1)}, u32[]{:S(2)}) copy-start(f32[128]{0:T(128)S(1)} %add_rsqrt_fusion) | copy-start | bytes 1540
  129.2 30.5 %collective-permute-start.1 = (f32[128,1536]{1,0:T(8,128)S(1)}, f32[128,1536]{1,0:T(8,128)S(1)}, u32[]{:S(2)}, u32[]{:S(2)}) collective-permute-start(f32[128,1536]{1,0:T(8,128)S(1)} %fusion.80), channel_id=1, source_target_pairs={{0,64},{64,128},{128,192},{192,256},{256,320},{320,384},{384,448},... | collective-permute-start | bytes 2359304 | tf_op jit(solution)/shard_map/while/body/eval_jaxpr/ppermute | solution.py:13
  131.7 28.0 %collective-permute-start = (bf16[128,1536]{1,0:T(8,128)(2,1)S(1)}, bf16[128,1536]{1,0:T(8,128)(2,1)S(1)}, u32[]{:S(2)}, u32[]{:S(2)}) collective-permute-start(bf16[128,1536]{1,0:T(8,128)(2,1)S(1)} %copy.24), channel_id=1, source_target_pairs={{0,64},{64,128},{128,192},{192,256},{256,320},{320,384},{384,448},... | collective-permute-start | bytes 1179656 | tf_op jit(solution)/shard_map/while/body/eval_jaxpr/ppermute | solution.py:13
  161.3 29.6 %collective-permute-start.1 = (f32[128,1536]{1,0:T(8,128)S(1)}, f32[128,1536]{1,0:T(8,128)S(1)}, u32[]{:S(2)}, u32[]{:S(2)}) collective-permute-start(f32[128,1536]{1,0:T(8,128)S(1)} %fusion.80), channel_id=1, source_target_pairs={{0,64},{64,128},{128,192},{192,256},{256,320},{320,384},{384,448},... | collective-permute-start | bytes 2359304 | tf_op jit(solution)/shard_map/while/body/eval_jaxpr/ppermute | solution.py:13
  163.3 27.7 %collective-permute-start = (bf16[128,1536]{1,0:T(8,128)(2,1)S(1)}, bf16[128,1536]{1,0:T(8,128)(2,1)S(1)}, u32[]{:S(2)}, u32[]{:S(2)}) collective-permute-start(bf16[128,1536]{1,0:T(8,128)(2,1)S(1)} %copy.24), channel_id=1, source_target_pairs={{0,64},{64,128},{128,192},{192,256},{256,320},{320,384},{384,448},... | collective-permute-start | bytes 1179656 | tf_op jit(solution)/shard_map/while/body/eval_jaxpr/ppermute | solution.py:13
  192.6 28.7 %collective-permute-start.1 = (f32[128,1536]{1,0:T(8,128)S(1)}, f32[128,1536]{1,0:T(8,128)S(1)}, u32[]{:S(2)}, u32[]{:S(2)}) collective-permute-start(f32[128,1536]{1,0:T(8,128)S(1)} %fusion.80), channel_id=1, source_target_pairs={{0,64},{64,128},{128,192},{192,256},{256,320},{320,384},{384,448},... | collective-permute-start | bytes 2359304 | tf_op jit(solution)/shard_map/while/body/eval_jaxpr/ppermute | solution.py:13
  194.5 26.8 %collective-permute-start = (bf16[128,1536]{1,0:T(8,128)(2,1)S(1)}, bf16[128,1536]{1,0:T(8,128)(2,1)S(1)}, u32[]{:S(2)}, u32[]{:S(2)}) collective-permute-start(bf16[128,1536]{1,0:T(8,128)(2,1)S(1)} %copy.24), channel_id=1, source_target_pairs={{0,64},{64,128},{128,192},{192,256},{256,320},{320,384},{384,448},... | collective-permute-start | bytes 1179656 | tf_op jit(solution)/shard_map/while/body/eval_jaxpr/ppermute | solution.py:13
  222.8 27.8 %collective-permute-start.1 = (f32[128,1536]{1,0:T(8,128)S(1)}, f32[128,1536]{1,0:T(8,128)S(1)}, u32[]{:S(2)}, u32[]{:S(2)}) collective-permute-start(f32[128,1536]{1,0:T(8,128)S(1)} %fusion.80), channel_id=1, source_target_pairs={{0,64},{64,128},{128,192},{192,256},{256,320},{320,384},{384,448},... | collective-permute-start | bytes 2359304 | tf_op jit(solution)/shard_map/while/body/eval_jaxpr/ppermute | solution.py:13
  224.8 25.8 %collective-permute-start = (bf16[128,1536]{1,0:T(8,128)(2,1)S(1)}, bf16[128,1536]{1,0:T(8,128)(2,1)S(1)}, u32[]{:S(2)}, u32[]{:S(2)}) collective-permute-start(bf16[128,1536]{1,0:T(8,128)(2,1)S(1)} %copy.24), channel_id=1, source_target_pairs={{0,64},{64,128},{128,192},{192,256},{256,320},{320,384},{384,448},... | collective-permute-start | bytes 1179656 | tf_op jit(solution)/shard_map/while/body/eval_jaxpr/ppermute | solution.py:13
  252.2 26.8 %collective-permute-start.1 = (f32[128,1536]{1,0:T(8,128)S(1)}, f32[128,1536]{1,0:T(8,128)S(1)}, u32[]{:S(2)}, u32[]{:S(2)}) collective-permute-start(f32[128,1536]{1,0:T(8,128)S(1)} %fusion.80), channel_id=1, source_target_pairs={{0,64},{64,128},{128,192},{192,256},{256,320},{320,384},{384,448},... | collective-permute-start | bytes 2359304 | tf_op jit(solution)/shard_map/while/body/eval_jaxpr/ppermute | solution.py:13
  254.1 24.9 %collective-permute-start = (bf16[128,1536]{1,0:T(8,128)(2,1)S(1)}, bf16[128,1536]{1,0:T(8,128)(2,1)S(1)}, u32[]{:S(2)}, u32[]{:S(2)}) collective-permute-start(bf16[128,1536]{1,0:T(8,128)(2,1)S(1)} %copy.24), channel_id=1, source_target_pairs={{0,64},{64,128},{128,192},{192,256},{256,320},{320,384},{384,448},... | collective-permute-start | bytes 1179656 | tf_op jit(solution)/shard_map/while/body/eval_jaxpr/ppermute | solution.py:13
  280.6 25.9 %collective-permute-start.1 = (f32[128,1536]{1,0:T(8,128)S(1)}, f32[128,1536]{1,0:T(8,128)S(1)}, u32[]{:S(2)}, u32[]{:S(2)}) collective-permute-start(f32[128,1536]{1,0:T(8,128)S(1)} %fusion.80), channel_id=1, source_target_pairs={{0,64},{64,128},{128,192},{192,256},{256,320},{320,384},{384,448},... | collective-permute-start | bytes 2359304 | tf_op jit(solution)/shard_map/while/body/eval_jaxpr/ppermute | solution.py:13
  282.5 24.0 %collective-permute-start = (bf16[128,1536]{1,0:T(8,128)(2,1)S(1)}, bf16[128,1536]{1,0:T(8,128)(2,1)S(1)}, u32[]{:S(2)}, u32[]{:S(2)}) collective-permute-start(bf16[128,1536]{1,0:T(8,128)(2,1)S(1)} %copy.24), channel_id=1, source_target_pairs={{0,64},{64,128},{128,192},{192,256},{256,320},{320,384},{384,448},... | collective-permute-start | bytes 1179656 | tf_op jit(solution)/shard_map/while/body/eval_jaxpr/ppermute | solution.py:13
  308.1 25.0 %collective-permute-start.1 = (f32[128,1536]{1,0:T(8,128)S(1)}, f32[128,1536]{1,0:T(8,128)S(1)}, u32[]{:S(2)}, u32[]{:S(2)}) collective-permute-start(f32[128,1536]{1,0:T(8,128)S(1)} %fusion.80), channel_id=1, source_target_pairs={{0,64},{64,128},{128,192},{192,256},{256,320},{320,384},{384,448},... | collective-permute-start | bytes 2359304 | tf_op jit(solution)/shard_map/while/body/eval_jaxpr/ppermute | solution.py:13
  310.0 23.1 %collective-permute-start = (bf16[128,1536]{1,0:T(8,128)(2,1)S(1)}, bf16[128,1536]{1,0:T(8,128)(2,1)S(1)}, u32[]{:S(2)}, u32[]{:S(2)}) collective-permute-start(bf16[128,1536]{1,0:T(8,128)(2,1)S(1)} %copy.24), channel_id=1, source_target_pairs={{0,64},{64,128},{128,192},{192,256},{256,320},{320,384},{384,448},... | collective-permute-start | bytes 1179656 | tf_op jit(solution)/shard_map/while/body/eval_jaxpr/ppermute | solution.py:13
  342.0 146.7 %all-to-all-start = ((bf16[8,192,128]{2,1,0:T(8,128)(2,1)}), bf16[8,192,128]{2,1,0:T(8,128)(2,1)S(1)}, u32[]{:S(2)}, u32[]{:S(2)}) async-start(bf16[8,192,128]{2,1,0:T(8,128)(2,1)} %bitcast.3), calls=%async_computation | async-start | bytes 786432 | tf_op jit(solution)/shard_map/all_to_all | solution.py:92
  345.5 652.3 %all-reduce.3.cloned.1.call-start = ((), (), s32[]{:S(2)}) async-start(), calls=%async_computation.3 | async-start | bytes 2359296 | tf_op jit(solution)/shard_map/psum | solution.py:102
  346.6 147.2 %collective-permute-start.2 = (f32[128,1536]{1,0:T(8,128)S(1)}, f32[128,1536]{1,0:T(8,128)S(1)}, u32[]{:S(2)}, u32[]{:S(2)}) collective-permute-start(f32[128,1536]{1,0:T(8,128)S(1)} %fusion.12), channel_id=1, source_target_pairs={{0,64},{64,128},{128,192},{192,256},{256,320},{320,384},{384,448},... | collective-permute-start | bytes 2359304 | tf_op jit(solution)/shard_map/ppermute | solution.py:13
  (20 other events, 53.2 us)
Sparse Core Ops, SparseCore 0:
  10.1 113.1 all-gather.2
  336.0 95.3 all-gather.4
  492.6 505.1 all-reduce.2
where the time goes:
time: 1010 us
  waiting for transfers between devices  771 us (76%)
  blocking collectives  136 us (13%)
  starting transfers between devices  36.2 us (4%)
  matrix products  30.2 us (3%)
  between operations  15.4 us (2%)
  other arithmetic  13.7 us (1%)
    psum x1, waiting for transfers between devices, local(): head_total = lax.psum(head_grad, 'dp')  503 us
    ppermute x15, waiting for transfers between devices, shifted(): return lax.ppermute(value, axis, pairs)  157 us
    psum x1, blocking collectives, local(): gain_total, bias_total = lax.psum((gain_portion, bias_part), ('blk', 'dp'))  136 us
    all_gather x1, waiting for transfers between devices, local(): full_weight = lax.all_gather(head_weight, 'blk', axis=0, tiled=True)  110 us
    ppermute x15, starting transfers between devices, shifted(): return lax.ppermute(value, axis, pairs)  32.6 us
  transfers between devices with their start and end apart: 19, of which 9 were waited for; matrix products, arithmetic and copies ran while one was open for 3% of the time, Pallas kernels for 0%

commit v1 on v0

v1 whole, which is shorter than its diff:
```python
import jax
import jax.numpy as jnp
from jax import lax
from jax.sharding import Mesh, PartitionSpec as P

epsilon = 1e-06
loss_scale = 64.0
AXES = ("y", "xl", "z", "xh", "core")
SIZES = (4, 2, 16, 2, 2)
ROWS = ("z", "xh", "core", "y", "xl")
bf16 = jnp.bfloat16
f32 = jnp.float32


def shift(value, axis, steps):
    count = lax.axis_size(axis)
    return lax.ppermute(value, axis, [(i, (i + steps) % count) for i in range(count)])


def shift_x(value, steps):
    def index(place):
        place = place % 4
        return (place % 2) * 2 + place // 2

    return lax.ppermute(value, ("xl", "xh"), [(index(i), index(i + steps)) for i in range(4)])


def swap(value):
    return lax.ppermute(value, ("xl", "core"), [(0, 0), (1, 2), (2, 1), (3, 3)])


def around(value):
    return value, shift(value, "y", -1), shift(value, "y", 1), shift(value, "y", 2)


def halves(flag, first, second, axis):
    return jnp.where(
        flag == 0,
        jnp.concatenate([first, second], axis),
        jnp.concatenate([second, first], axis),
    )


def dot(a, b, da, db):
    return lax.dot_general(a, b, (((da,), (db,)), ((), ())), preferred_element_type=f32)


def split16(value):
    high = value.astype(bf16)
    return high, (value - high.astype(f32)).astype(bf16)


def spread_to(value, axes):
    count = lax.axis_size(axes)
    many = jnp.broadcast_to(value[None], (count,) + value.shape)
    return lax.all_to_all(many, axes, split_axis=0, concat_axis=0, tiled=True)


def gather_weight(head_weight, y, xl, core):
    rows, width = head_weight.shape
    half = width // 2
    part = lax.dynamic_slice(head_weight, (0, core * half), (rows, half))
    blocks = around(part)
    column = jnp.zeros((4, rows, half), bf16)
    for step, block in zip((0, 1, 3, 2), blocks):
        column = lax.dynamic_update_slice(column, block[None], ((y + step) % 4, 0, 0))
    other = jnp.concatenate(
        [shift_x(column[:2], 1), shift_x(column[2:], -1)], 0
    )
    own_half = halves(xl, column, other, 1).reshape(8 * rows, half)
    return halves(core, own_half, shift(own_half, "core", 1), 1)


def local(
    image_features, final_norm_gain, final_norm_bias, head_weight, text_embed, log_scale, logit_bias
):
    y, xl, xh, core = (lax.axis_index(a) for a in ("y", "xl", "xh", "core"))
    scale = jnp.exp(log_scale[0])
    offset = logit_bias[0]
    weight = gather_weight(head_weight, y, xl, core)

    text_values = swap(text_embed).astype(f32)
    values = swap(image_features).astype(f32)
    own, width = values.shape
    inv_text = lax.rsqrt(jnp.sum(text_values * text_values, axis=1, keepdims=True) + epsilon)
    text_unit = (text_values * inv_text).astype(bf16)
    centre = jnp.mean(values, axis=1, keepdims=True)
    centered = values - centre
    spread = jnp.mean(centered * centered, axis=1, keepdims=True)
    inverse_deviation = lax.rsqrt(spread + epsilon)
    xhat = centered * inverse_deviation
    normed_own = (xhat * final_norm_gain + final_norm_bias).astype(bf16)

    text_same = jnp.concatenate(around(text_unit), 0)
    text_other = shift(text_same, "core", 1)
    normed = jnp.concatenate(around(normed_own), 0)
    rows = normed.shape[0]

    projected = dot(normed, weight, 1, 0)
    inv_proj = lax.rsqrt(jnp.sum(projected * projected, axis=1, keepdims=True) + epsilon)
    image_unit = (projected * inv_proj).astype(bf16)

    def weights_of(text_rows, diagonal):
        logits = scale * dot(image_unit, text_rows, 1, 1) + offset
        return (loss_scale * (jax.nn.sigmoid(logits) - diagonal)).astype(bf16)

    weights_same = weights_of(text_same, jnp.eye(rows, dtype=f32))
    weights_other = weights_of(text_other, 0.0)
    grad_image = scale * (dot(weights_same, text_same, 1, 0) + dot(weights_other, text_other, 1, 0))
    proj_dot = jnp.sum(projected * grad_image, axis=1, keepdims=True)
    grad_proj = (
        inv_proj * grad_image - inv_proj * inv_proj * inv_proj * proj_dot * projected
    ).astype(bf16)

    half = width // 2
    block = width // 4
    normed_block = lax.dynamic_slice(normed, (0, y * block), (rows, block))
    mine = lax.dynamic_slice(grad_proj, (0, core * half), (rows, half))
    theirs = lax.dynamic_slice(grad_proj, (0, (1 - core) * half), (rows, half))
    head = dot(normed_block, mine, 0, 0) + shift(
        dot(normed_block, theirs, 0, 0).astype(bf16), "core", 1
    ).astype(f32)
    part = block // 4
    head = head.reshape(4, part, half)
    x_place = xh * 2 + xl

    def for_x(place):
        place = place % 4
        return lax.dynamic_index_in_dim(head, (place % 2) * 2 + place // 2, 0, keepdims=False)

    head_part = for_x(x_place)
    for step in (1, -1, 2):
        head_part = head_part + shift_x(for_x(x_place + step).astype(bf16), step).astype(f32)

    grad_normed = dot(grad_proj[:own], weight, 1, 1)
    scaled = grad_normed * final_norm_gain
    first_mean = jnp.mean(scaled, axis=1, keepdims=True)
    second_mean = jnp.mean(scaled * xhat, axis=1, keepdims=True)
    grad_features = inverse_deviation * (scaled - first_mean - xhat * second_mean)
    vectors = jnp.stack([jnp.sum(grad_normed * xhat, axis=0), jnp.sum(grad_normed, axis=0)], 0)
    vectors = jnp.sum(spread_to(vectors, ("y", "xl", "xh", "core")), axis=0)

    planes = lax.axis_size("z")
    vector_part = 2 * width // planes

    def payload(head_rows, vector):
        high, low = split16(vector)
        rest = jnp.zeros(high.shape[:-1] + (half - 2 * vector_part,), bf16)
        line = jnp.concatenate([high, low, rest], -1)[..., None, :]
        return jnp.concatenate([head_rows.astype(bf16), line], -2)

    def unpack(received):
        line = received[..., -1, :]
        return received[..., :-1, :], line[..., :vector_part] + line[..., vector_part : 2 * vector_part]

    sent = payload(head_part.reshape(planes, part // planes, half), vectors.reshape(planes, vector_part))
    received = lax.all_to_all(sent, "z", split_axis=0, concat_axis=0, tiled=True).astype(f32)
    head_sum, vector_sum = unpack(jnp.sum(received, axis=0))
    head_all, vector_all = unpack(spread_to(payload(head_sum, vector_sum), "z").astype(f32))
    vector_all = vector_all.reshape(2, width) / 64.0

    head_all = head_all.reshape(part, half).astype(bf16)
    head_all = halves(xh, head_all, shift(head_all, "xh", 1), 0)
    head_all = halves(core, head_all, shift(head_all, "core", 1), 1).astype(f32) / 64.0

    grad_unit_text = dot(weights_same[:, :own], image_unit, 0, 0) + shift(
        dot(weights_other[:, :own], image_unit, 0, 0), "core", 1
    )
    grad_unit_text = scale * grad_unit_text
    text_dot = jnp.sum(text_values * grad_unit_text, axis=1, keepdims=True)
    grad_text = inv_text * grad_unit_text - inv_text * inv_text * inv_text * text_dot * text_values

    return (swap(grad_features), swap(grad_text), vector_all[0], vector_all[1], head_all)


def solution(mesh):
    fine = Mesh(mesh.devices.reshape(SIZES), AXES)
    placed = (P(ROWS, None), P(), P(), P(("y", "xl"), None), P(ROWS, None), P(), P())
    return jax.shard_map(
        local,
        mesh=fine,
        in_specs=placed,
        out_specs=(P(ROWS, None), P(ROWS, None), P(), P(), P(("y", "xl"), None)),
        check_vma=False,
    )
```

time: 1010 us -> 226 us (0.22)
  waiting for transfers between devices: 771 us -> 73.5 us
  blocking collectives: 136 us -> 0 us
  starting transfers between devices: 36.2 us -> 103 us
  between operations: 15.4 us -> 2.92 us
    psum x1 -> x0, waiting for transfers between devices: 503 us -> none  [local(): head_total = lax.psum(head_grad, 'dp')]
    psum x1 -> x0, blocking collectives: 136 us -> none  [local(): gain_total, bias_total = lax.psum((gain_portion, bias_part), ('blk', 'dp'))]
    all_gather x2 -> x0, waiting for transfers between devices: 110 us -> none  [the longest x1 110 us: local(): full_weight = lax.all_gather(head_weight, 'blk', axis=0, tiled=True)]
    ppermute x15 -> x24, waiting for transfers between devices: 157 us -> 50.6 us  [the longest x15 31.5 us: shift(): lax.ppermute(value, axis, [(i, (i + steps) % count) for i in range(count)])]
    ppermute x15 -> x24, starting transfers between devices: 32.6 us -> 78.7 us  [the longest x15 47.4 us: shift(): lax.ppermute(value, axis, [(i, (i + steps) % count) for i in range(count)])]
    all_to_all x1 -> x3, waiting for transfers between devices: 0.01 us -> 22.9 us  [the longest x2 12.8 us: spread_to(): return lax.all_to_all(many, axes, split_axis=0, concat_axis=0, tiled=True)]
    all_to_all x1 -> x3, starting transfers between devices: 3.45 us -> 24.5 us  [the longest x1 14.5 us: local(): lax.all_to_all(sent, 'z', split_axis=0, concat_axis=0, tiled=True)]
    dot_general x27 -> x10, matrix products: 30.2 us -> 25.5 us  [dot(): lax.dot_general(a, b, (((da,), (db,)), ((), ())), preferred_element_type=...]
  transfers between devices with their start and end apart: 19 -> 27, of which waited for: 9 -> 13; matrix products, arithmetic and copies ran while one was open for 3% -> 16% of each run, Pallas kernels for 0% -> 0%
where the time goes in v1:
time: 226 us; the launch traced here: 225 us
  starting transfers between devices  103 us (46%)
  waiting for transfers between devices  73.5 us (33%)
  matrix products  25.5 us (11%)
  other arithmetic  11.3 us (5%)
  local copies, waits for them, and re-layouts  8.13 us (4%)
  between operations  2.92 us (1%)
    ppermute x15, starting transfers between devices, shift(): lax.ppermute(value, axis, [(i, (i + steps) % count) for i in range(count)])  47.4 us
    ppermute x15, waiting for transfers between devices, shift(): lax.ppermute(value, axis, [(i, (i + steps) % count) for i in range(count)])  31.5 us
    dot_general x10, matrix products, dot(): lax.dot_general(a, b, (((da,), (db,)), ((), ())), preferred_element_type=...  25.5 us
    ppermute x5, starting transfers between devices, shift_x(): lax.ppermute(value, ('xl', 'xh'), [(index(i), index(i + steps)) for i in...  16.5 us
    ppermute x4, starting transfers between devices, swap(): return lax.ppermute(value, ('xl', 'core'), [(0, 0), (1, 2), (2, 1), (3, 3)])  14.8 us
    all_to_all x1, starting transfers between devices, local(): lax.all_to_all(sent, 'z', split_axis=0, concat_axis=0, tiled=True)  14.5 us
    all_to_all x2, waiting for transfers between devices, spread_to(): return lax.all_to_all(many, axes, split_axis=0, concat_axis=0, tiled=True)  12.8 us
    ppermute x5, waiting for transfers between devices, shift_x(): lax.ppermute(value, ('xl', 'xh'), [(index(i), index(i + steps)) for i in...  11.6 us
  transfers between devices with their start and end apart: 27, of which 13 were waited for; matrix products, arithmetic and copies ran while one was open for 16% of the time, Pallas kernels for 0%

profile of v1, /device:TPU:1, one launch (start us, length us, event | category | flops | bytes accessed | tf_op | source)
XLA Modules:
  0.0 224.5 jit_solution(5722240855716822658)
XLA Ops:
  1.8 5.5 %collective-permute-start.4 = (bf16[192,768]{1,0:T(8,128)(2,1)S(1)}, bf16[192,768]{1,0:T(8,128)(2,1)S(1)}, u32[]{:S(2)}, u32[]{:S(2)}) collective-permute-start(bf16[192,768]{1,0:T(8,128)(2,1)S(1)} %get-tuple-element.14), channel_id=1, source_target_pairs={{0,384},{128,0},{256,128},{384,256},{1,385},{129,1},{257,129},{385... | collective-permute-start | bytes 884744 | tf_op jit(solution)/shard_map/ppermute | solution.py:17
  9.2 3.5 %collective-permute-start.6 = (bf16[192,768]{1,0:T(8,128)(2,1)S(1)}, bf16[192,768]{1,0:T(8,128)(2,1)S(1)}, u32[]{:S(2)}, u32[]{:S(2)}) collective-permute-start(bf16[192,768]{1,0:T(8,128)(2,1)S(1)} %get-tuple-element.14), channel_id=1, source_target_pairs={{0,256},{128,384},{256,0},{384,128},{1,257},{129,385},{257,1},{385... | collective-permute-start | bytes 884744 | tf_op jit(solution)/shard_map/ppermute | solution.py:17
  16.0 6.0 %collective-permute-done.6 = bf16[192,768]{1,0:T(8,128)(2,1)S(1)} collective-permute-done((bf16[192,768]{1,0:T(8,128)(2,1)S(1)}, bf16[192,768]{1,0:T(8,128)(2,1)S(1)}, u32[]{:S(2)}, u32[]{:S(2)}) %collective-permute-start.6) | collective-permute-done | bytes 294944 | tf_op jit(solution)/shard_map/ppermute | solution.py:17
  23.1 4.4 %collective-permute-start.7 = (bf16[2,192,768]{2,1,0:T(8,128)(2,1)}, bf16[2,192,768]{2,1,0:T(8,128)(2,1)S(1)}, u32[]{:S(2)}, u32[]{:S(2)}) collective-permute-start(bf16[2,192,768]{2,1,0:T(8,128)(2,1)} %get-tuple-element.19), channel_id=1, source_target_pairs={{0,64},{64,2},{2,66},{66,0},{1,65},{65,3},{3,67},{67,1},{4,68},{68... | collective-permute-start | bytes 1769480 | tf_op jit(solution)/shard_map/ppermute | solution.py:25
  27.5 6.2 %collective-permute-start.10 = (bf16[128,1536]{1,0:T(8,128)(2,1)S(1)}, bf16[128,1536]{1,0:T(8,128)(2,1)S(1)}, u32[]{:S(2)}, u32[]{:S(2)}) collective-permute-start(bf16[128,1536]{1,0:T(8,128)(2,1)S(1)} %copy-done.14), channel_id=1, source_target_pairs={{0,0},{1,64},{64,1},{65,65},{2,2},{3,66},{66,3},{67,67},{4,4},{5,6... | collective-permute-start | bytes 1179656 | tf_op jit(solution)/shard_map/ppermute | solution.py:29
  37.6 7.5 %collective-permute-done.10 = bf16[128,1536]{1,0:T(8,128)(2,1)S(1)} collective-permute-done((bf16[128,1536]{1,0:T(8,128)(2,1)S(1)}, bf16[128,1536]{1,0:T(8,128)(2,1)S(1)}, u32[]{:S(2)}, u32[]{:S(2)}) %collective-permute-start.10) | collective-permute-done | bytes 393248 | tf_op jit(solution)/shard_map/ppermute | solution.py:29
  45.3 5.9 %collective-permute-done.8 = bf16[2,192,768]{2,1,0:T(8,128)(2,1)S(1)} collective-permute-done((bf16[2,192,768]{2,1,0:T(8,128)(2,1)}, bf16[2,192,768]{2,1,0:T(8,128)(2,1)S(1)}, u32[]{:S(2)}, u32[]{:S(2)}) %collective-permute-start.8) | collective-permute-done | bytes 589856 | tf_op jit(solution)/shard_map/ppermute | solution.py:25
  60.5 4.6 %collective-permute-start.11 = (bf16[128,1536]{1,0:T(8,128)(2,1)S(1)}, bf16[128,1536]{1,0:T(8,128)(2,1)S(1)}, u32[]{:S(2)}, u32[]{:S(2)}) collective-permute-start(bf16[128,1536]{1,0:T(8,128)(2,1)S(1)} %fusion.33), channel_id=1, source_target_pairs={{0,384},{128,0},{256,128},{384,256},{1,385},{129,1},{257,129},{385... | collective-permute-start | bytes 1179656 | tf_op jit(solution)/shard_map/ppermute | solution.py:17
  65.8 3.4 %collective-permute-start.3 = (bf16[128,1536]{1,0:T(8,128)(2,1)S(1)}, bf16[128,1536]{1,0:T(8,128)(2,1)S(1)}, u32[]{:S(2)}, u32[]{:S(2)}) collective-permute-start(bf16[128,1536]{1,0:T(8,128)(2,1)S(1)} %fusion.26), channel_id=1, source_target_pairs={{0,256},{128,384},{256,0},{384,128},{1,257},{129,385},{257,1},{385... | collective-permute-start | bytes 1179656 | tf_op jit(solution)/shard_map/ppermute | solution.py:17
  72.5 7.1 %collective-permute-done.12 = bf16[128,1536]{1,0:T(8,128)(2,1)S(1)} collective-permute-done((bf16[128,1536]{1,0:T(8,128)(2,1)S(1)}, bf16[128,1536]{1,0:T(8,128)(2,1)S(1)}, u32[]{:S(2)}, u32[]{:S(2)}) %collective-permute-start.12) | collective-permute-done | bytes 393248 | tf_op jit(solution)/shard_map/ppermute | solution.py:17
  87.5 8.7 %collective-permute-done.2 = bf16[128,1536]{1,0:T(8,128)(2,1)S(1)} collective-permute-done((bf16[128,1536]{1,0:T(8,128)(2,1)S(1)}, bf16[128,1536]{1,0:T(8,128)(2,1)S(1)}, u32[]{:S(2)}, u32[]{:S(2)}) %collective-permute-start.2) | collective-permute-done | bytes 393248 | tf_op jit(solution)/shard_map/ppermute | solution.py:17
  98.4 6.6 %multiply_reduce_fusion.1 = (f32[512]{0:T(512)S(1)}, f32[512,1536]{1,0:T(8,128)S(1)}) fusion(bf16[1536,768]{1,0:T(8,128)(2,1)} %collective-permute-done.9, bf16[1536,768]{1,0:T(8,128)(2,1)} %bitcast.4, pred[]{:T(512)S(6)} %eq.26, bf16[128,1536]{1,0:T(8,128)(2,1)S(1)} %collective-permute-done.3, bf16[128,1536]{1,0:T(8,128)(2,1)S(1)} %collective-permute-done.2, ...), kind=kOutput, calls=%fused_computation.6 | convolution fusion | flops 2445016576 | bytes 9439233 | tf_op jit(solution)/shard_map/dot_general | solution.py:45
  114.6 6.6 %fusion.30 = (f32[1536]{0:T(1024)S(1)}, f32[128]{0:T(128)}, f32[128]{0:T(128)}, f32[1536]{0:T(1024)S(1)}, f32[128,1536]{1,0:T(8,128)S(1)}) fusion(bf16[128,1536]{1,0:T(8,128)(2,1)S(1)} %collective-permute-done, f32[128]{0:T(128)S(1)} %copy-done.9, f32[128]{0:T(128)S(1)} %broadcast_multiply_fusion.2, f32[1536]{0:T(1024)S(1)} %copy-done.4, ...), kind=kOutput, calls=%fused_computation.52 | convolution fusion | flops 627176192 | bytes 6313985 | tf_op jit(solution)/shard_map/dot_general | solution.py:45
  122.1 4.0 %all-to-all-start = ((f32[32,2,1536]{2,1,0:T(2,128)}), f32[32,2,1536]{2,1,0:T(2,128)S(1)}, u32[]{:S(2)}, u32[]{:S(2)}) async-start(f32[32,2,1536]{2,1,0:T(2,128)} %broadcast_in_dim.27), calls=%async_computation | async-start | bytes 786432 | tf_op jit(solution)/shard_map/all_to_all | solution.py:56
  133.6 3.4 %collective-permute-start.15 = (f32[128,1536]{1,0:T(8,128)}, f32[128,1536]{1,0:T(8,128)S(1)}, u32[]{:S(2)}, u32[]{:S(2)}) collective-permute-start(f32[128,1536]{1,0:T(8,128)} %fusion.29), channel_id=1, source_target_pairs={{0,0},{1,64},{64,1},{65,65},{2,2},{3,66},{66,3},{67,67},{4,4},{5,6... | collective-permute-start | bytes 2359304 | tf_op jit(solution)/shard_map/ppermute | solution.py:29
  141.2 4.3 %collective-permute-start.21 = (bf16[96,768]{1,0:T(8,128)(2,1)S(1)}, bf16[96,768]{1,0:T(8,128)(2,1)S(1)}, u32[]{:S(2)}, u32[]{:S(2)}) collective-permute-start(bf16[96,768]{1,0:T(8,128)(2,1)S(1)} %get-tuple-element.16), channel_id=1, source_target_pairs={{0,2},{64,66},{2,0},{66,64},{1,3},{65,67},{3,1},{67,65},{4,6},{68,... | collective-permute-start | bytes 442376 | tf_op jit(solution)/shard_map/ppermute | solution.py:25
  145.5 4.0 %collective-permute-start.20 = (bf16[96,768]{1,0:T(8,128)(2,1)S(1)}, bf16[96,768]{1,0:T(8,128)(2,1)S(1)}, u32[]{:S(2)}, u32[]{:S(2)}) collective-permute-start(bf16[96,768]{1,0:T(8,128)(2,1)S(1)} %get-tuple-element.17), channel_id=1, source_target_pairs={{0,66},{64,0},{2,64},{66,2},{1,67},{65,1},{3,65},{67,3},{4,70},{68... | collective-permute-start | bytes 442376 | tf_op jit(solution)/shard_map/ppermute | solution.py:25
  150.9 4.4 %collective-permute-done.21 = bf16[96,768]{1,0:T(8,128)(2,1)S(1)} collective-permute-done((bf16[96,768]{1,0:T(8,128)(2,1)S(1)}, bf16[96,768]{1,0:T(8,128)(2,1)S(1)}, u32[]{:S(2)}, u32[]{:S(2)}) %collective-permute-start.21) | collective-permute-done | bytes 147488 | tf_op jit(solution)/shard_map/ppermute | solution.py:25
  156.2 14.5 %all-to-all-start.1 = ((bf16[16,7,768]{2,1,0:T(8,128)(2,1)}), bf16[16,7,768]{2,1,0:T(8,128)(2,1)S(1)}, u32[]{:S(2)}, u32[]{:S(2)}) async-start(bf16[16,7,768]{2,1,0:T(8,128)(2,1)} %pad_maximum_fusion.2), calls=%async_computation.1 | async-start | bytes 393216 | tf_op jit(solution)/shard_map/all_to_all | solution.py:157
  176.0 10.1 %all-to-all-done.1 = bf16[16,7,768]{2,1,0:T(8,128)(2,1)S(1)} async-done(((bf16[16,7,768]{2,1,0:T(8,128)(2,1)}), bf16[16,7,768]{2,1,0:T(8,128)(2,1)S(1)}, u32[]{:S(2)}, u32[]{:S(2)}) %all-to-all-start.1) | async-done | bytes 172064 | tf_op jit(solution)/shard_map/all_to_all | solution.py:157
  187.0 6.0 %all-to-all-start.2 = ((bf16[16,7,768]{2,1,0:T(8,128)(2,1)}), bf16[16,7,768]{2,1,0:T(8,128)(2,1)S(1)}, u32[]{:S(2)}, u32[]{:S(2)}) async-start(bf16[16,7,768]{2,1,0:T(8,128)(2,1)} %broadcast_in_dim.60), calls=%async_computation.2 | async-start | bytes 393216 | tf_op jit(solution)/shard_map/all_to_all | solution.py:56
  193.0 12.8 %all-to-all-done.2 = bf16[16,7,768]{2,1,0:T(8,128)(2,1)S(1)} async-done(((bf16[16,7,768]{2,1,0:T(8,128)(2,1)}), bf16[16,7,768]{2,1,0:T(8,128)(2,1)S(1)}, u32[]{:S(2)}, u32[]{:S(2)}) %all-to-all-start.2) | async-done | bytes 172064 | tf_op jit(solution)/shard_map/all_to_all | solution.py:56
  208.7 4.6 %collective-permute-done.22 = bf16[96,768]{1,0:T(8,128)(2,1)S(1)} collective-permute-done((bf16[96,768]{1,0:T(8,128)(2,1)S(1)}, bf16[96,768]{1,0:T(8,128)(2,1)S(1)}, u32[]{:S(2)}, u32[]{:S(2)}) %collective-permute-start.22) | collective-permute-done | bytes 147488 | tf_op jit(solution)/shard_map/ppermute | solution.py:17
  213.4 6.8 %collective-permute-start.23 = (bf16[192,768]{1,0:T(8,128)(2,1)S(1)}, bf16[192,768]{1,0:T(8,128)(2,1)S(1)}, u32[]{:S(2)}, u32[]{:S(2)}) collective-permute-start(bf16[192,768]{1,0:T(8,128)(2,1)S(1)} %maximum_select_fusion.5), channel_id=1, source_target_pairs={{0,1},{1,0},{2,3},{3,2},{4,5},{5,4},{6,7},{7,6},{8,9},{9,8},{10,11... | collective-permute-start | bytes 884744 | tf_op jit(solution)/shard_map/ppermute | solution.py:17
  (131 shorter events, 70.7 us)
Async XLA Ops:
  1.8 11.0 %collective-permute-start.4 = (bf16[192,768]{1,0:T(8,128)(2,1)S(1)}, bf16[192,768]{1,0:T(8,128)(2,1)S(1)}, u32[]{:S(2)}, u32[]{:S(2)}) collective-permute-start(bf16[192,768]{1,0:T(8,128)(2,1)S(1)} %get-tuple-element.14), channel_id=1, source_target_pairs={{0,384},{128,0},{256,128},{384,256},{1,385},{129,1},{257,129},{385... | collective-permute-start | bytes 884744 | tf_op jit(solution)/shard_map/ppermute | solution.py:17
  7.3 8.7 %collective-permute-start.5 = (bf16[192,768]{1,0:T(8,128)(2,1)S(1)}, bf16[192,768]{1,0:T(8,128)(2,1)S(1)}, u32[]{:S(2)}, u32[]{:S(2)}) collective-permute-start(bf16[192,768]{1,0:T(8,128)(2,1)S(1)} %get-tuple-element.14), channel_id=1, source_target_pairs={{0,128},{128,256},{256,384},{384,0},{1,129},{129,257},{257,385},{3... | collective-permute-start | bytes 884744 | tf_op jit(solution)/shard_map/ppermute | solution.py:17
  9.2 12.8 %collective-permute-start.6 = (bf16[192,768]{1,0:T(8,128)(2,1)S(1)}, bf16[192,768]{1,0:T(8,128)(2,1)S(1)}, u32[]{:S(2)}, u32[]{:S(2)}) collective-permute-start(bf16[192,768]{1,0:T(8,128)(2,1)S(1)} %get-tuple-element.14), channel_id=1, source_target_pairs={{0,256},{128,384},{256,0},{384,128},{1,257},{129,385},{257,1},{385... | collective-permute-start | bytes 884744 | tf_op jit(solution)/shard_map/ppermute | solution.py:17
  23.1 22.1 %collective-permute-start.7 = (bf16[2,192,768]{2,1,0:T(8,128)(2,1)}, bf16[2,192,768]{2,1,0:T(8,128)(2,1)S(1)}, u32[]{:S(2)}, u32[]{:S(2)}) collective-permute-start(bf16[2,192,768]{2,1,0:T(8,128)(2,1)} %get-tuple-element.19), channel_id=1, source_target_pairs={{0,64},{64,2},{2,66},{66,0},{1,65},{65,3},{3,67},{67,1},{4,68},{68... | collective-permute-start | bytes 1769480 | tf_op jit(solution)/shard_map/ppermute | solution.py:25
  27.5 17.5 %collective-permute-start.10 = (bf16[128,1536]{1,0:T(8,128)(2,1)S(1)}, bf16[128,1536]{1,0:T(8,128)(2,1)S(1)}, u32[]{:S(2)}, u32[]{:S(2)}) collective-permute-start(bf16[128,1536]{1,0:T(8,128)(2,1)S(1)} %copy-done.14), channel_id=1, source_target_pairs={{0,0},{1,64},{64,1},{65,65},{2,2},{3,66},{66,3},{67,67},{4,4},{5,6... | collective-permute-start | bytes 1179656 | tf_op jit(solution)/shard_map/ppermute | solution.py:29
  33.7 17.5 %collective-permute-start.8 = (bf16[2,192,768]{2,1,0:T(8,128)(2,1)}, bf16[2,192,768]{2,1,0:T(8,128)(2,1)S(1)}, u32[]{:S(2)}, u32[]{:S(2)}) collective-permute-start(bf16[2,192,768]{2,1,0:T(8,128)(2,1)} %get-tuple-element.18), channel_id=1, source_target_pairs={{0,66},{64,0},{2,64},{66,2},{1,67},{65,1},{3,65},{67,3},{4,70},{68... | collective-permute-start | bytes 1769480 | tf_op jit(solution)/shard_map/ppermute | solution.py:25
  35.6 29.4 %collective-permute-start = (bf16[128,1536]{1,0:T(8,128)(2,1)}, bf16[128,1536]{1,0:T(8,128)(2,1)S(1)}, u32[]{:S(2)}, u32[]{:S(2)}) collective-permute-start(bf16[128,1536]{1,0:T(8,128)(2,1)} %param.7), channel_id=1, source_target_pairs={{0,0},{1,64},{64,1},{65,65},{2,2},{3,66},{66,3},{67,67},{4,4},{5,6... | collective-permute-start | bytes 1179656 | tf_op jit(solution)/shard_map/ppermute | solution.py:29
  53.0 45.4 %collective-permute-start.9 = (bf16[1536,768]{1,0:T(8,128)(2,1)}, bf16[1536,768]{1,0:T(8,128)(2,1)}, u32[]{:S(2)}, u32[]{:S(2)}) collective-permute-start(bf16[1536,768]{1,0:T(8,128)(2,1)} %bitcast.4), channel_id=1, source_target_pairs={{0,1},{1,0},{2,3},{3,2},{4,5},{5,4},{6,7},{7,6},{8,9},{9,8},{10,11... | collective-permute-start | bytes 7077896 | tf_op jit(solution)/shard_map/ppermute | solution.py:17
  56.4 14.2 %collective-permute-start.13 = (bf16[128,1536]{1,0:T(8,128)(2,1)S(1)}, bf16[128,1536]{1,0:T(8,128)(2,1)S(1)}, u32[]{:S(2)}, u32[]{:S(2)}) collective-permute-start(bf16[128,1536]{1,0:T(8,128)(2,1)S(1)} %fusion.33), channel_id=1, source_target_pairs={{0,256},{128,384},{256,0},{384,128},{1,257},{129,385},{257,1},{385... | collective-permute-start | bytes 1179656 | tf_op jit(solution)/shard_map/ppermute | solution.py:17
  58.6 21.0 %collective-permute-start.12 = (bf16[128,1536]{1,0:T(8,128)(2,1)S(1)}, bf16[128,1536]{1,0:T(8,128)(2,1)S(1)}, u32[]{:S(2)}, u32[]{:S(2)}) collective-permute-start(bf16[128,1536]{1,0:T(8,128)(2,1)S(1)} %fusion.33), channel_id=1, source_target_pairs={{0,128},{128,256},{256,384},{384,0},{1,129},{129,257},{257,385},{3... | collective-permute-start | bytes 1179656 | tf_op jit(solution)/shard_map/ppermute | solution.py:17
  60.5 23.1 %collective-permute-start.11 = (bf16[128,1536]{1,0:T(8,128)(2,1)S(1)}, bf16[128,1536]{1,0:T(8,128)(2,1)S(1)}, u32[]{:S(2)}, u32[]{:S(2)}) collective-permute-start(bf16[128,1536]{1,0:T(8,128)(2,1)S(1)} %fusion.33), channel_id=1, source_target_pairs={{0,384},{128,0},{256,128},{384,256},{1,385},{129,1},{257,129},{385... | collective-permute-start | bytes 1179656 | tf_op jit(solution)/shard_map/ppermute | solution.py:17
  65.8 21.6 %collective-permute-start.3 = (bf16[128,1536]{1,0:T(8,128)(2,1)S(1)}, bf16[128,1536]{1,0:T(8,128)(2,1)S(1)}, u32[]{:S(2)}, u32[]{:S(2)}) collective-permute-start(bf16[128,1536]{1,0:T(8,128)(2,1)S(1)} %fusion.26), channel_id=1, source_target_pairs={{0,256},{128,384},{256,0},{384,128},{1,257},{129,385},{257,1},{385... | collective-permute-start | bytes 1179656 | tf_op jit(solution)/shard_map/ppermute | solution.py:17
  70.6 25.6 %collective-permute-start.2 = (bf16[128,1536]{1,0:T(8,128)(2,1)S(1)}, bf16[128,1536]{1,0:T(8,128)(2,1)S(1)}, u32[]{:S(2)}, u32[]{:S(2)}) collective-permute-start(bf16[128,1536]{1,0:T(8,128)(2,1)S(1)} %fusion.26), channel_id=1, source_target_pairs={{0,128},{128,256},{256,384},{384,0},{1,129},{129,257},{257,385},{3... | collective-permute-start | bytes 1179656 | tf_op jit(solution)/shard_map/ppermute | solution.py:17
  79.6 16.6 %collective-permute-start.1 = (bf16[128,1536]{1,0:T(8,128)(2,1)S(1)}, bf16[128,1536]{1,0:T(8,128)(2,1)}, u32[]{:S(2)}, u32[]{:S(2)}) collective-permute-start(bf16[128,1536]{1,0:T(8,128)(2,1)S(1)} %fusion.26), channel_id=1, source_target_pairs={{0,384},{128,0},{256,128},{384,256},{1,385},{129,1},{257,129},{385... | collective-permute-start | bytes 1179656 | tf_op jit(solution)/shard_map/ppermute | solution.py:17
  83.7 21.6 %collective-permute-start.14 = (bf16[512,1536]{1,0:T(8,128)(2,1)S(1)}, bf16[512,1536]{1,0:T(8,128)(2,1)S(1)}, u32[]{:S(2)}, u32[]{:S(2)}) collective-permute-start(bf16[512,1536]{1,0:T(8,128)(2,1)S(1)} %pad_maximum_fusion.1), channel_id=1, source_target_pairs={{0,1},{1,0},{2,3},{3,2},{4,5},{5,4},{6,7},{7,6},{8,9},{9,8},{10,11... | collective-permute-start | bytes 4718600 | tf_op jit(solution)/shard_map/ppermute | solution.py:17
  107.8 63.0 %collective-permute-start.16 = (f32[128,1536]{1,0:T(8,128)}, f32[128,1536]{1,0:T(8,128)}, u32[]{:S(2)}, u32[]{:S(2)}) collective-permute-start(f32[128,1536]{1,0:T(8,128)} %fusion.47), channel_id=1, source_target_pairs={{0,1},{1,0},{2,3},{3,2},{4,5},{5,4},{6,7},{7,6},{8,9},{9,8},{10,11... | collective-permute-start | bytes 2359304 | tf_op jit(solution)/shard_map/ppermute | solution.py:17
  122.1 14.9 %all-to-all-start = ((f32[32,2,1536]{2,1,0:T(2,128)}), f32[32,2,1536]{2,1,0:T(2,128)S(1)}, u32[]{:S(2)}, u32[]{:S(2)}) async-start(f32[32,2,1536]{2,1,0:T(2,128)} %broadcast_in_dim.27), calls=%async_computation | async-start | bytes 786432 | tf_op jit(solution)/shard_map/all_to_all | solution.py:56
  133.6 59.5 %collective-permute-start.15 = (f32[128,1536]{1,0:T(8,128)}, f32[128,1536]{1,0:T(8,128)S(1)}, u32[]{:S(2)}, u32[]{:S(2)}) collective-permute-start(f32[128,1536]{1,0:T(8,128)} %fusion.29), channel_id=1, source_target_pairs={{0,0},{1,64},{64,1},{65,65},{2,2},{3,66},{66,3},{67,67},{4,4},{5,6... | collective-permute-start | bytes 2359304 | tf_op jit(solution)/shard_map/ppermute | solution.py:29
  139.2 11.6 %collective-permute-start.19 = (bf16[96,768]{1,0:T(8,128)(2,1)S(1)}, bf16[96,768]{1,0:T(8,128)(2,1)S(1)}, u32[]{:S(2)}, u32[]{:S(2)}) collective-permute-start(bf16[96,768]{1,0:T(8,128)(2,1)S(1)} %get-tuple-element.15), channel_id=1, source_target_pairs={{0,64},{64,2},{2,66},{66,0},{1,65},{65,3},{3,67},{67,1},{4,68},{68... | collective-permute-start | bytes 442376 | tf_op jit(solution)/shard_map/ppermute | solution.py:25
  141.2 14.1 %collective-permute-start.21 = (bf16[96,768]{1,0:T(8,128)(2,1)S(1)}, bf16[96,768]{1,0:T(8,128)(2,1)S(1)}, u32[]{:S(2)}, u32[]{:S(2)}) collective-permute-start(bf16[96,768]{1,0:T(8,128)(2,1)S(1)} %get-tuple-element.16), channel_id=1, source_target_pairs={{0,2},{64,66},{2,0},{66,64},{1,3},{65,67},{3,1},{67,65},{4,6},{68,... | collective-permute-start | bytes 442376 | tf_op jit(solution)/shard_map/ppermute | solution.py:25
  145.5 9.8 %collective-permute-start.20 = (bf16[96,768]{1,0:T(8,128)(2,1)S(1)}, bf16[96,768]{1,0:T(8,128)(2,1)S(1)}, u32[]{:S(2)}, u32[]{:S(2)}) collective-permute-start(bf16[96,768]{1,0:T(8,128)(2,1)S(1)} %get-tuple-element.17), channel_id=1, source_target_pairs={{0,66},{64,0},{2,64},{66,2},{1,67},{65,1},{3,65},{67,3},{4,70},{68... | collective-permute-start | bytes 442376 | tf_op jit(solution)/shard_map/ppermute | solution.py:25
  156.2 29.9 %all-to-all-start.1 = ((bf16[16,7,768]{2,1,0:T(8,128)(2,1)}), bf16[16,7,768]{2,1,0:T(8,128)(2,1)S(1)}, u32[]{:S(2)}, u32[]{:S(2)}) async-start(bf16[16,7,768]{2,1,0:T(8,128)(2,1)} %pad_maximum_fusion.2), calls=%async_computation.1 | async-start | bytes 393216 | tf_op jit(solution)/shard_map/all_to_all | solution.py:157
  172.7 20.3 %collective-permute-start.17 = (f32[128,1536]{1,0:T(8,128)S(1)}, f32[128,1536]{1,0:T(8,128)S(1)}, u32[]{:S(2)}, u32[]{:S(2)}) collective-permute-start(f32[128,1536]{1,0:T(8,128)S(1)} %fusion.35), channel_id=1, source_target_pairs={{0,0},{1,64},{64,1},{65,65},{2,2},{3,66},{66,3},{67,67},{4,4},{5,6... | collective-permute-start | bytes 2359304 | tf_op jit(solution)/shard_map/ppermute | solution.py:29
  187.0 18.9 %all-to-all-start.2 = ((bf16[16,7,768]{2,1,0:T(8,128)(2,1)}), bf16[16,7,768]{2,1,0:T(8,128)(2,1)S(1)}, u32[]{:S(2)}, u32[]{:S(2)}) async-start(bf16[16,7,768]{2,1,0:T(8,128)(2,1)} %broadcast_in_dim.60), calls=%async_computation.2 | async-start | bytes 393216 | tf_op jit(solution)/shard_map/all_to_all | solution.py:56
  (18 other events, 187.6 us)

commit v2 on v1

v2 whole, which is shorter than its diff:
```python
import jax
import jax.numpy as jnp
from jax import lax
from jax.sharding import Mesh, PartitionSpec as P

epsilon = 1e-06
loss_scale = 64.0
AXES = ("y", "xl", "zh", "zl", "xh", "core")
SIZES = (4, 2, 4, 4, 2, 2)
ROWS = ("zh", "zl", "xh", "core", "y", "xl")
bf16 = jnp.bfloat16
f32 = jnp.float32


def shift(value, axis, steps):
    count = lax.axis_size(axis)
    return lax.ppermute(value, axis, [(i, (i + steps) % count) for i in range(count)])


def shift_x(value, steps):
    def index(place):
        place = place % 4
        return (place % 2) * 2 + place // 2

    return lax.ppermute(value, ("xl", "xh"), [(index(i), index(i + steps)) for i in range(4)])


def swap(value):
    return lax.ppermute(value, ("xl", "core"), [(0, 0), (1, 2), (2, 1), (3, 3)])


def halves(flag, first, second, axis):
    return jnp.where(
        flag == 0,
        jnp.concatenate([first, second], axis),
        jnp.concatenate([second, first], axis),
    )


def dot(a, b, da, db):
    return lax.dot_general(a, b, (((da,), (db,)), ((), ())), preferred_element_type=f32)


def split16(value):
    high = value.astype(bf16)
    return high, (value - high.astype(f32)).astype(bf16)


def spread_to(value, axes):
    count = lax.axis_size(axes)
    many = jnp.broadcast_to(value[None], (count,) + value.shape)
    return lax.all_to_all(many, axes, split_axis=0, concat_axis=0, tiled=True)


def gather_weight(blocks, xl, core):
    other = jnp.concatenate([shift_x(blocks[:2], 1), shift_x(blocks[2:], -1)], 0)
    rows, half = blocks.shape[1:]
    own_half = halves(xl, blocks, other, 1).reshape(8 * rows, half)
    own_half = lax.optimization_barrier(own_half)
    return lax.optimization_barrier(halves(core, own_half, shift(own_half, "core", 1), 1))


def local(
    image_features, final_norm_gain, final_norm_bias, head_weight, text_embed, log_scale, logit_bias
):
    y, xl, xh, core = (lax.axis_index(a) for a in ("y", "xl", "xh", "core"))
    scale = jnp.exp(log_scale[0])
    offset = logit_bias[0]
    own, width = image_features.shape
    half = width // 2
    block = width // 4

    text_rows = swap(text_embed)
    feature_rows = swap(image_features)
    weight_part = lax.dynamic_slice(head_weight, (0, core * half), (head_weight.shape[0], half))
    weight_blocks = spread_to(weight_part, "y")

    text_values = text_rows.astype(f32)
    inv_text = lax.rsqrt(jnp.sum(text_values * text_values, axis=1, keepdims=True) + epsilon)
    text_unit = (text_values * inv_text).astype(bf16)
    text_same = spread_to(text_unit, "y").reshape(4 * own, width)

    values = feature_rows.astype(f32)
    centre = jnp.mean(values, axis=1, keepdims=True)
    centered = values - centre
    spread = jnp.mean(centered * centered, axis=1, keepdims=True)
    inverse_deviation = lax.rsqrt(spread + epsilon)
    xhat = centered * inverse_deviation
    normed_own = (xhat * final_norm_gain + final_norm_bias).astype(bf16)
    weight_blocks, normed_own = lax.optimization_barrier((weight_blocks, normed_own))
    normed = spread_to(normed_own, "y").reshape(4 * own, width)
    rows = normed.shape[0]

    weight = gather_weight(weight_blocks, xl, core)
    text_other = shift(text_same, "core", 1)

    projected = dot(normed, weight, 1, 0)
    inv_proj = lax.rsqrt(jnp.sum(projected * projected, axis=1, keepdims=True) + epsilon)
    image_unit = (projected * inv_proj).astype(bf16)

    def weights_of(text_rows, diagonal):
        logits = scale * dot(image_unit, text_rows, 1, 1) + offset
        return (loss_scale * (jax.nn.sigmoid(logits) - diagonal)).astype(bf16)

    weights_same = weights_of(text_same, jnp.eye(rows, dtype=f32))
    weights_other = weights_of(text_other, 0.0)
    grad_image = scale * (dot(weights_same, text_same, 1, 0) + dot(weights_other, text_other, 1, 0))
    proj_dot = jnp.sum(projected * grad_image, axis=1, keepdims=True)
    grad_proj = (
        inv_proj * grad_image - inv_proj * inv_proj * inv_proj * proj_dot * projected
    ).astype(bf16)

    normed_block = lax.dynamic_slice(normed, (0, y * block), (rows, block))
    mine = lax.dynamic_slice(grad_proj, (0, core * half), (rows, half))
    theirs = lax.dynamic_slice(grad_proj, (0, (1 - core) * half), (rows, half))
    sent = dot(normed_block, theirs, 0, 0).astype(bf16)
    mine, sent = lax.optimization_barrier((mine, sent))
    head = dot(normed_block, mine, 0, 0) + shift(sent, "core", 1).astype(f32)
    part = block // 4
    head = head.astype(bf16).reshape(4, part, half)
    head = lax.all_to_all(head, ("xl", "xh"), split_axis=0, concat_axis=0, tiled=True)
    head = jnp.sum(head.astype(f32), axis=0)

    grad_own = lax.dynamic_slice(grad_proj, (y * own, 0), (own, width))
    weights_text, weights_text_other = (
        lax.dynamic_slice(w, (0, y * own), (rows, own)) for w in (weights_same, weights_other)
    )
    grad_own, weights_text, weights_text_other, image_unit, sent = lax.optimization_barrier(
        (grad_own, weights_text, weights_text_other, image_unit, sent)
    )
    grad_normed = dot(grad_own, weight, 1, 1)
    scaled = grad_normed * final_norm_gain
    first_mean = jnp.mean(scaled, axis=1, keepdims=True)
    second_mean = jnp.mean(scaled * xhat, axis=1, keepdims=True)
    grad_features = inverse_deviation * (scaled - first_mean - xhat * second_mean)
    vectors = jnp.stack([jnp.sum(grad_normed * xhat, axis=0), jnp.sum(grad_normed, axis=0)], 0)
    vectors = jnp.sum(spread_to(vectors, ("y", "xl", "xh", "core")), axis=0)

    lanes = 128
    lines = part // 4

    def payload(head_rows, vector):
        lead = vector.shape[:-1]
        high, low = (t.reshape(lead + (-1, lanes)) for t in split16(vector))
        rest = jnp.zeros(lead + (lines - 2 * high.shape[-2], lanes), bf16)
        side = jnp.concatenate([high, low, rest], -2)
        return jnp.concatenate([head_rows.astype(bf16), side], -1)

    def unpack(received):
        side = received[..., half:]
        count = 2 * width // 4 // lanes
        vector = side[..., :count, :] + side[..., count : 2 * count, :]
        return received[..., :half], vector.reshape(vector.shape[:-2] + (-1,))

    sent = payload(head.reshape(4, lines, half), vectors.reshape(4, 2 * width // 4))
    received = lax.all_to_all(sent, "zl", split_axis=0, concat_axis=0, tiled=True).astype(f32)
    received = spread_to(payload(*unpack(jnp.sum(received, axis=0))), "zh").astype(f32)
    sent = payload(*unpack(jnp.sum(received, axis=0)))
    received = spread_to(sent, ("zl", "xh")).reshape(4, 2, lines, half + lanes)
    vector_all = unpack(received[:, 0].astype(f32))[1].reshape(2, width) / 64.0
    head_all = received[..., :half].transpose(1, 0, 2, 3).reshape(2 * part, half)
    head_all = halves(core, head_all, shift(head_all, "core", 1), 1).astype(f32) / 64.0

    grad_unit_text = dot(weights_text, image_unit, 0, 0) + shift(
        dot(weights_text_other, image_unit, 0, 0), "core", 1
    )
    grad_unit_text = scale * grad_unit_text
    text_dot = jnp.sum(text_values * grad_unit_text, axis=1, keepdims=True)
    grad_text = inv_text * grad_unit_text - inv_text * inv_text * inv_text * text_dot * text_values

    return (
        swap(grad_features.astype(bf16)).astype(f32),
        swap(grad_text.astype(bf16)).astype(f32),
        vector_all[0],
        vector_all[1],
        head_all,
    )


def solution(mesh):
    fine = Mesh(mesh.devices.reshape(SIZES), AXES)
    placed = (P(ROWS, None), P(), P(), P(("y", "xl"), None), P(ROWS, None), P(), P())
    return jax.shard_map(
        local,
        mesh=fine,
        in_specs=placed,
        out_specs=(P(ROWS, None), P(ROWS, None), P(), P(), P(("y", "xl"), None)),
        check_vma=False,
    )
```

time: 226 us -> 227 us (level)
  blocking collectives: 0 us -> 23.8 us
  starting transfers between devices: 103 us -> 80 us
  waiting for transfers between devices: 73.5 us -> 55.9 us
  other arithmetic: 11.3 us -> 22.6 us
  local copies, waits for them, and re-layouts: 8.13 us -> 12.7 us
    ppermute x15 -> x5, starting transfers between devices: 47.4 us -> 14.9 us  [shift(): lax.ppermute(value, axis, [(i, (i + steps) % count) for i in range(count)])]
    ppermute x15 -> x5, waiting for transfers between devices: 31.5 us -> 0.33 us  [shift(): lax.ppermute(value, axis, [(i, (i + steps) % count) for i in range(count)])]
    all_to_all x0 -> x1, blocking collectives: none -> 23.8 us  [spread_to(): return lax.all_to_all(many, axes, split_axis=0, concat_axis=0, tiled=True)]
    all_to_all x2 -> x5, waiting for transfers between devices: 12.8 us -> 34.6 us  [spread_to(): return lax.all_to_all(many, axes, split_axis=0, concat_axis=0, tiled=True)]
    all_to_all x2 -> x5, starting transfers between devices: 9.96 us -> 30.1 us  [spread_to(): return lax.all_to_all(many, axes, split_axis=0, concat_axis=0, tiled=True)]
    ppermute x5 -> x2, starting transfers between devices: 16.5 us -> 6.48 us  [shift_x(): lax.ppermute(value, ('xl', 'xh'), [(index(i), index(i + steps)) for i in...]
    select_n x2, other arithmetic: 1.81 us -> 9.38 us  [halves(): jnp.where(flag == 0, jnp.concatenate([first, second], axis), jnp.concaten...]
    convert_element_type x1 -> x5, other arithmetic: 0.07 us -> 5.33 us  [the longest x1 2.21 us: local(): grad_features.astype(bf16)]
  transfers between devices with their start and end apart: 27 -> 18, of which waited for: 13 -> 10; matrix products, arithmetic and copies ran while one was open for 16% -> 21% of each run, Pallas kernels for 0% -> 0%
where the time goes in v2:
time: 227 us; the launch traced here: 225 us
  starting transfers between devices  80 us (35%)
  waiting for transfers between devices  55.9 us (25%)
  matrix products  27.3 us (12%)
  blocking collectives  23.8 us (10%)
  other arithmetic  22.6 us (10%)
  local copies, waits for them, and re-layouts  12.7 us (6%)
  between operations  2.61 us (1%)
    all_to_all x5, waiting for transfers between devices, spread_to(): return lax.all_to_all(many, axes, split_axis=0, concat_axis=0, tiled=True)  34.6 us
    all_to_all x5, starting transfers between devices, spread_to(): return lax.all_to_all(many, axes, split_axis=0, concat_axis=0, tiled=True)  30.1 us
    dot_general x10, matrix products, dot(): lax.dot_general(a, b, (((da,), (db,)), ((), ())), preferred_element_type=...  27.3 us
    all_to_all x1, blocking collectives, spread_to(): return lax.all_to_all(many, axes, split_axis=0, concat_axis=0, tiled=True)  23.8 us
    ppermute x4, starting transfers between devices, swap(): return lax.ppermute(value, ('xl', 'core'), [(0, 0), (1, 2), (2, 1), (3, 3)])  18.4 us
    ppermute x5, starting transfers between devices, shift(): lax.ppermute(value, axis, [(i, (i + steps) % count) for i in range(count)])  14.9 us
    ppermute x2, waiting for transfers between devices, shift_x(): lax.ppermute(value, ('xl', 'xh'), [(index(i), index(i + steps)) for i in...  9.65 us
    select_n x2, other arithmetic, halves(): jnp.where(flag == 0, jnp.concatenate([first, second], axis), jnp.concaten...  9.38 us
  transfers between devices with their start and end apart: 18, of which 10 were waited for; matrix products, arithmetic and copies ran while one was open for 21% of the time, Pallas kernels for 0%

profile of v2, /device:TPU:1, one launch (start us, length us, event | category | flops | bytes accessed | tf_op | source)
XLA Modules:
  0.0 224.9 jit_solution(6461244016014205748)
XLA Ops:
  0.6 4.6 %collective-permute-start = (bf16[128,1536]{1,0:T(8,128)(2,1)}, bf16[128,1536]{1,0:T(8,128)(2,1)S(1)}, u32[]{:S(2)}, u32[]{:S(2)}) collective-permute-start(bf16[128,1536]{1,0:T(8,128)(2,1)} %param.7), channel_id=1, source_target_pairs={{0,0},{1,64},{64,1},{65,65},{2,2},{3,66},{66,3},{67,67},{4,4},{5,6... | collective-permute-start | bytes 1179656 | tf_op jit(solution)/shard_map/ppermute | solution.py:29
  6.4 4.3 %all-to-all-start = ((bf16[4,192,768]{2,1,0:T(8,128)(2,1)}), bf16[4,192,768]{2,1,0:T(8,128)(2,1)S(1)}, u32[]{:S(2)}, u32[]{:S(2)}) async-start(bf16[4,192,768]{2,1,0:T(8,128)(2,1)} %broadcast_in_dim.14), calls=%async_computation | async-start | bytes 2359296 | tf_op jit(solution)/shard_map/all_to_all | solution.py:52
  11.7 12.0 %all-to-all-done = bf16[4,192,768]{2,1,0:T(8,128)(2,1)S(1)} async-done(((bf16[4,192,768]{2,1,0:T(8,128)(2,1)}), bf16[4,192,768]{2,1,0:T(8,128)(2,1)S(1)}, u32[]{:S(2)}, u32[]{:S(2)}) %all-to-all-start) | async-done | bytes 1179680 | tf_op jit(solution)/shard_map/all_to_all | solution.py:52
  24.8 3.4 %collective-permute-start.1 = (bf16[2,192,768]{2,1,0:T(8,128)(2,1)}, bf16[2,192,768]{2,1,0:T(8,128)(2,1)}, u32[]{:S(2)}, u32[]{:S(2)}) collective-permute-start(bf16[2,192,768]{2,1,0:T(8,128)(2,1)} %get-tuple-element.32), channel_id=1, source_target_pairs={{0,64},{64,2},{2,66},{66,0},{1,65},{65,3},{3,67},{67,1},{4,68},{68... | collective-permute-start | bytes 1769480 | tf_op jit(solution)/shard_map/ppermute | solution.py:25
  31.3 5.5 %collective-permute-start.4 = (bf16[128,1536]{1,0:T(8,128)(2,1)}, bf16[128,1536]{1,0:T(8,128)(2,1)S(1)}, u32[]{:S(2)}, u32[]{:S(2)}) collective-permute-start(bf16[128,1536]{1,0:T(8,128)(2,1)} %param.11), channel_id=1, source_target_pairs={{0,0},{1,64},{64,1},{65,65},{2,2},{3,66},{66,3},{67,67},{4,4},{5,6... | collective-permute-start | bytes 1179656 | tf_op jit(solution)/shard_map/ppermute | solution.py:29
  39.6 7.9 %collective-permute-done.2 = bf16[2,192,768]{2,1,0:T(8,128)(2,1)S(1)} collective-permute-done((bf16[2,192,768]{2,1,0:T(8,128)(2,1)}, bf16[2,192,768]{2,1,0:T(8,128)(2,1)S(1)}, u32[]{:S(2)}, u32[]{:S(2)}) %collective-permute-start.2) | collective-permute-done | bytes 589856 | tf_op jit(solution)/shard_map/ppermute | solution.py:25
  52.9 23.8 %all_to_all.40 = bf16[4,128,1536]{2,1,0:T(8,128)(2,1)} all-to-all(bf16[4,128,1536]{2,1,0:T(8,128)(2,1)S(1)} %broadcast_in_dim.16), channel_id=1, replica_groups=mesh['y'=4,'xl'=2,'zh'=4,'zl'=4,'xh'=2,'core'=2] {'y'}, dimensions={0} | all-to-all | bytes 3145728 | tf_op jit(solution)/shard_map/all_to_all | solution.py:52
  78.0 3.6 %all-to-all-start.1 = ((bf16[4,128,1536]{2,1,0:T(8,128)(2,1)}), bf16[4,128,1536]{2,1,0:T(8,128)(2,1)S(1)}, u32[]{:S(2)}, u32[]{:S(2)}) async-start(bf16[4,128,1536]{2,1,0:T(8,128)(2,1)} %broadcast_in_dim.15), calls=%async_computation.1 | async-start | bytes 3145728 | tf_op jit(solution)/shard_map/all_to_all | solution.py:52
  85.9 7.6 %maximum_select_fusion = bf16[1536,1536]{1,0:T(8,128)(2,1)} fusion(bf16[1536,768]{1,0:T(8,128)(2,1)} %collective-permute-done.3, bf16[1536,768]{1,0:T(8,128)(2,1)} %bitcast.1, pred[]{:T(512)S(6)} %eq.10), kind=kLoop, calls=%fused_computation | loop fusion | flops 21233664 | bytes 9437185 | tf_op jit(solution)/shard_map/jit(_where)/select_n | solution.py:33
  93.5 7.7 %all-to-all-done.1 = bf16[4,128,1536]{2,1,0:T(8,128)(2,1)S(1)} async-done(((bf16[4,128,1536]{2,1,0:T(8,128)(2,1)}), bf16[4,128,1536]{2,1,0:T(8,128)(2,1)S(1)}, u32[]{:S(2)}, u32[]{:S(2)}) %all-to-all-start.1) | async-done | bytes 1572896 | tf_op jit(solution)/shard_map/all_to_all | solution.py:52
  101.2 5.2 %multiply_reduce_fusion.1 = (f32[512]{0:T(512)S(1)}, f32[512,1536]{1,0:T(8,128)S(1)}) fusion(bf16[512,1536]{1,0:T(8,128)(2,1)S(1)} %bitcast.39, bf16[1536,1536]{1,0:T(8,128)(2,1)} %maximum_select_fusion), kind=kOutput, calls=%fused_computation.6 | convolution fusion | flops 2417491456 | bytes 9439232 | tf_op jit(solution)/shard_map/dot_general | solution.py:41
  121.9 3.9 %collective-permute-start.9 = (bf16[384,768]{1,0:T(8,128)(2,1)}, bf16[384,768]{1,0:T(8,128)(2,1)}, u32[]{:S(2)}, u32[]{:S(2)}) collective-permute-start(bf16[384,768]{1,0:T(8,128)(2,1)} %convolution_convert_fusion), channel_id=1, source_target_pairs={{0,1},{1,0},{2,3},{3,2},{4,5},{5,4},{6,7},{7,6},{8,9},{9,8},{10,11... | collective-permute-start | bytes 1769480 | tf_op jit(solution)/shard_map/ppermute | solution.py:17
  125.9 3.2 %fusion.29 = (f32[1536]{0:T(1024)S(1)}, f32[128]{0:T(128)}, f32[128]{0:T(128)}, f32[1536]{0:T(1024)S(1)}, f32[128,1536]{1,0:T(8,128)}) fusion(bf16[128,1536]{1,0:T(8,128)(2,1)S(1)} %collective-permute-done, f32[128]{0:T(128)S(1)} %add_rsqrt_fusion.2, f32[128]{0:T(128)S(1)} %broadcast_multiply_fusion.2, f32[1536]{0:T(1024)S(1)} %copy-done.4, ...), kind=kOutput, calls=%fused_computation.49 | convolution fusion | flops 605942528 | bytes 6311936 | tf_op jit(solution)/shard_map/dot_general | solution.py:41
  129.9 4.2 %all-to-all-start.4 = ((f32[32,2,1536]{2,1,0:T(2,128)}), f32[32,2,1536]{2,1,0:T(2,128)S(1)}, u32[]{:S(2)}, u32[]{:S(2)}) async-start(f32[32,2,1536]{2,1,0:T(2,128)} %broadcast_in_dim.17), calls=%async_computation.4 | async-start | bytes 786432 | tf_op jit(solution)/shard_map/all_to_all | solution.py:52
  136.9 7.2 %all-to-all-done.4 = f32[32,2,1536]{2,1,0:T(2,128)S(1)} async-done(((f32[32,2,1536]{2,1,0:T(2,128)}), f32[32,2,1536]{2,1,0:T(2,128)S(1)}, u32[]{:S(2)}, u32[]{:S(2)}) %all-to-all-start.4) | async-done | bytes 393248 | tf_op jit(solution)/shard_map/all_to_all | solution.py:52
  144.8 3.5 %all-to-all-start.3 = ((bf16[4,96,768]{2,1,0:T(8,128)(2,1)}), bf16[4,96,768]{2,1,0:T(8,128)(2,1)S(1)}, u32[]{:S(2)}, u32[]{:S(2)}) async-start(bf16[4,96,768]{2,1,0:T(8,128)(2,1)} %bitcast.44), calls=%async_computation.3 | async-start | bytes 1179648 | tf_op jit(solution)/shard_map/all_to_all | solution.py:121
  152.1 6.3 %all-to-all-done.3 = bf16[4,96,768]{2,1,0:T(8,128)(2,1)S(1)} async-done(((bf16[4,96,768]{2,1,0:T(8,128)(2,1)}), bf16[4,96,768]{2,1,0:T(8,128)(2,1)S(1)}, u32[]{:S(2)}, u32[]{:S(2)}) %all-to-all-start.3) | async-done | bytes 589856 | tf_op jit(solution)/shard_map/all_to_all | solution.py:121
  160.7 6.7 %all-to-all-start.5 = ((bf16[4,24,896]{2,1,0:T(8,128)(2,1)}), bf16[4,24,896]{2,1,0:T(8,128)(2,1)S(1)}, u32[]{:S(2)}, u32[]{:S(2)}) async-start(bf16[4,24,896]{2,1,0:T(8,128)(2,1)} %maximum_maximum_fusion), calls=%async_computation.5 | async-start | bytes 344064 | tf_op jit(solution)/shard_map/all_to_all | solution.py:156
  173.4 12.4 %all-to-all-start.6 = ((bf16[4,24,896]{2,1,0:T(8,128)(2,1)}), bf16[4,24,896]{2,1,0:T(8,128)(2,1)S(1)}, u32[]{:S(2)}, u32[]{:S(2)}) async-start(bf16[4,24,896]{2,1,0:T(8,128)(2,1)} %broadcast_in_dim.19), calls=%async_computation.6 | async-start | bytes 344064 | tf_op jit(solution)/shard_map/all_to_all | solution.py:52
  188.0 4.7 %collective-permute-start.6 = (bf16[128,1536]{1,0:T(8,128)(2,1)}, bf16[128,1536]{1,0:T(8,128)(2,1)}, u32[]{:S(2)}, u32[]{:S(2)}) collective-permute-start(bf16[128,1536]{1,0:T(8,128)(2,1)} %fusion.28), channel_id=1, source_target_pairs={{0,0},{1,64},{64,1},{65,65},{2,2},{3,66},{66,3},{67,67},{4,4},{5,6... | collective-permute-start | bytes 1179656 | tf_op jit(solution)/shard_map/ppermute | solution.py:29
  192.7 7.8 %all-to-all-done.6 = bf16[4,24,896]{2,1,0:T(8,128)(2,1)S(1)} async-done(((bf16[4,24,896]{2,1,0:T(8,128)(2,1)}), bf16[4,24,896]{2,1,0:T(8,128)(2,1)S(1)}, u32[]{:S(2)}, u32[]{:S(2)}) %all-to-all-start.6) | async-done | bytes 172064 | tf_op jit(solution)/shard_map/all_to_all | solution.py:52
  201.4 5.6 %all-to-all-start.7 = ((bf16[8,24,896]{2,1,0:T(8,128)(2,1)}), bf16[8,24,896]{2,1,0:T(8,128)(2,1)S(1)}, u32[]{:S(2)}, u32[]{:S(2)}) async-start(bf16[8,24,896]{2,1,0:T(8,128)(2,1)} %broadcast_in_dim.20), calls=%async_computation.7 | async-start | bytes 688128 | tf_op jit(solution)/shard_map/all_to_all | solution.py:52
  208.9 3.5 %collective-permute-start.8 = (bf16[128,1536]{1,0:T(8,128)(2,1)S(1)}, bf16[128,1536]{1,0:T(8,128)(2,1)S(1)}, u32[]{:S(2)}, u32[]{:S(2)}) collective-permute-start(bf16[128,1536]{1,0:T(8,128)(2,1)S(1)} %fusion.35), channel_id=1, source_target_pairs={{0,0},{1,64},{64,1},{65,65},{2,2},{3,66},{66,3},{67,67},{4,4},{5,6... | collective-permute-start | bytes 1179656 | tf_op jit(solution)/shard_map/ppermute | solution.py:29
  214.4 4.8 %collective-permute-done.8 = bf16[128,1536]{1,0:T(8,128)(2,1)S(1)} collective-permute-done((bf16[128,1536]{1,0:T(8,128)(2,1)S(1)}, bf16[128,1536]{1,0:T(8,128)(2,1)S(1)}, u32[]{:S(2)}, u32[]{:S(2)}) %collective-permute-start.8) | collective-permute-done | bytes 393248 | tf_op jit(solution)/shard_map/ppermute | solution.py:29
  (122 shorter events, 63.1 us)
Async XLA Ops:
  0.6 10.3 %collective-permute-start = (bf16[128,1536]{1,0:T(8,128)(2,1)}, bf16[128,1536]{1,0:T(8,128)(2,1)S(1)}, u32[]{:S(2)}, u32[]{:S(2)}) collective-permute-start(bf16[128,1536]{1,0:T(8,128)(2,1)} %param.7), channel_id=1, source_target_pairs={{0,0},{1,64},{64,1},{65,65},{2,2},{3,66},{66,3},{67,67},{4,4},{5,6... | collective-permute-start | bytes 1179656 | tf_op jit(solution)/shard_map/ppermute | solution.py:29
  6.4 17.2 %all-to-all-start = ((bf16[4,192,768]{2,1,0:T(8,128)(2,1)}), bf16[4,192,768]{2,1,0:T(8,128)(2,1)S(1)}, u32[]{:S(2)}, u32[]{:S(2)}) async-start(bf16[4,192,768]{2,1,0:T(8,128)(2,1)} %broadcast_in_dim.14), calls=%async_computation | async-start | bytes 2359296 | tf_op jit(solution)/shard_map/all_to_all | solution.py:52
  11.1 114.7 %copy-start.7 = (f32[128]{0:T(128)}, f32[128]{0:T(128)S(1)}, u32[]{:S(2)}) copy-start(f32[128]{0:T(128)S(1)} %broadcast_multiply_fusion.2) | copy-start | bytes 1540
  11.4 114.4 %copy-start.9 = (f32[128]{0:T(128)}, f32[128]{0:T(128)S(1)}, u32[]{:S(2)}) copy-start(f32[128]{0:T(128)S(1)} %add_rsqrt_fusion.2) | copy-start | bytes 1540
  24.8 13.7 %collective-permute-start.1 = (bf16[2,192,768]{2,1,0:T(8,128)(2,1)}, bf16[2,192,768]{2,1,0:T(8,128)(2,1)}, u32[]{:S(2)}, u32[]{:S(2)}) collective-permute-start(bf16[2,192,768]{2,1,0:T(8,128)(2,1)} %get-tuple-element.32), channel_id=1, source_target_pairs={{0,64},{64,2},{2,66},{66,0},{1,65},{65,3},{3,67},{67,1},{4,68},{68... | collective-permute-start | bytes 1769480 | tf_op jit(solution)/shard_map/ppermute | solution.py:25
  28.2 19.3 %collective-permute-start.2 = (bf16[2,192,768]{2,1,0:T(8,128)(2,1)}, bf16[2,192,768]{2,1,0:T(8,128)(2,1)S(1)}, u32[]{:S(2)}, u32[]{:S(2)}) collective-permute-start(bf16[2,192,768]{2,1,0:T(8,128)(2,1)} %get-tuple-element.31), channel_id=1, source_target_pairs={{0,66},{64,0},{2,64},{66,2},{1,67},{65,1},{3,65},{67,3},{4,70},{68... | collective-permute-start | bytes 1769480 | tf_op jit(solution)/shard_map/ppermute | solution.py:25
  31.3 21.2 %collective-permute-start.4 = (bf16[128,1536]{1,0:T(8,128)(2,1)}, bf16[128,1536]{1,0:T(8,128)(2,1)S(1)}, u32[]{:S(2)}, u32[]{:S(2)}) collective-permute-start(bf16[128,1536]{1,0:T(8,128)(2,1)} %param.11), channel_id=1, source_target_pairs={{0,0},{1,64},{64,1},{65,65},{2,2},{3,66},{66,3},{67,67},{4,4},{5,6... | collective-permute-start | bytes 1179656 | tf_op jit(solution)/shard_map/ppermute | solution.py:29
  49.3 36.6 %collective-permute-start.3 = (bf16[1536,768]{1,0:T(8,128)(2,1)}, bf16[1536,768]{1,0:T(8,128)(2,1)}, u32[]{:S(2)}, u32[]{:S(2)}) collective-permute-start(bf16[1536,768]{1,0:T(8,128)(2,1)} %bitcast.1), channel_id=1, source_target_pairs={{0,1},{1,0},{2,3},{3,2},{4,5},{5,4},{6,7},{7,6},{8,9},{9,8},{10,11... | collective-permute-start | bytes 7077896 | tf_op jit(solution)/shard_map/ppermute | solution.py:17
  52.6 24.1 %copy-start.13 = (f32[128]{0:T(128)}, f32[128]{0:T(128)S(1)}, u32[]{:S(2)}) copy-start(f32[128]{0:T(128)S(1)} %fusion.31) | copy-start | bytes 1540
  52.6 24.1 %copy-start.11 = (f32[128]{0:T(128)}, f32[128]{0:T(128)S(1)}, u32[]{:S(2)}) copy-start(f32[128]{0:T(128)S(1)} %add_rsqrt_fusion.1) | copy-start | bytes 1540
  78.0 23.2 %all-to-all-start.1 = ((bf16[4,128,1536]{2,1,0:T(8,128)(2,1)}), bf16[4,128,1536]{2,1,0:T(8,128)(2,1)S(1)}, u32[]{:S(2)}, u32[]{:S(2)}) async-start(bf16[4,128,1536]{2,1,0:T(8,128)(2,1)} %broadcast_in_dim.15), calls=%async_computation.1 | async-start | bytes 3145728 | tf_op jit(solution)/shard_map/all_to_all | solution.py:52
  82.9 28.7 %collective-permute-start.5 = (bf16[512,1536]{1,0:T(8,128)(2,1)}, bf16[512,1536]{1,0:T(8,128)(2,1)}, u32[]{:S(2)}, u32[]{:S(2)}) collective-permute-start(bf16[512,1536]{1,0:T(8,128)(2,1)} %bitcast.3), channel_id=1, source_target_pairs={{0,1},{1,0},{2,3},{3,2},{4,5},{5,4},{6,7},{7,6},{8,9},{9,8},{10,11... | collective-permute-start | bytes 4718600 | tf_op jit(solution)/shard_map/ppermute | solution.py:17
  121.9 12.2 %collective-permute-start.9 = (bf16[384,768]{1,0:T(8,128)(2,1)}, bf16[384,768]{1,0:T(8,128)(2,1)}, u32[]{:S(2)}, u32[]{:S(2)}) collective-permute-start(bf16[384,768]{1,0:T(8,128)(2,1)} %convolution_convert_fusion), channel_id=1, source_target_pairs={{0,1},{1,0},{2,3},{3,2},{4,5},{5,4},{6,7},{7,6},{8,9},{9,8},{10,11... | collective-permute-start | bytes 1769480 | tf_op jit(solution)/shard_map/ppermute | solution.py:17
  129.9 14.2 %all-to-all-start.4 = ((f32[32,2,1536]{2,1,0:T(2,128)}), f32[32,2,1536]{2,1,0:T(2,128)S(1)}, u32[]{:S(2)}, u32[]{:S(2)}) async-start(f32[32,2,1536]{2,1,0:T(2,128)} %broadcast_in_dim.17), calls=%async_computation.4 | async-start | bytes 786432 | tf_op jit(solution)/shard_map/all_to_all | solution.py:52
  144.8 13.5 %all-to-all-start.3 = ((bf16[4,96,768]{2,1,0:T(8,128)(2,1)}), bf16[4,96,768]{2,1,0:T(8,128)(2,1)S(1)}, u32[]{:S(2)}, u32[]{:S(2)}) async-start(bf16[4,96,768]{2,1,0:T(8,128)(2,1)} %bitcast.44), calls=%async_computation.3 | async-start | bytes 1179648 | tf_op jit(solution)/shard_map/all_to_all | solution.py:121
  160.7 11.9 %all-to-all-start.5 = ((bf16[4,24,896]{2,1,0:T(8,128)(2,1)}), bf16[4,24,896]{2,1,0:T(8,128)(2,1)S(1)}, u32[]{:S(2)}, u32[]{:S(2)}) async-start(bf16[4,24,896]{2,1,0:T(8,128)(2,1)} %maximum_maximum_fusion), calls=%async_computation.5 | async-start | bytes 344064 | tf_op jit(solution)/shard_map/all_to_all | solution.py:156
  167.4 18.3 %copy-start.8 = (f32[128]{0:T(128)S(1)}, f32[128]{0:T(128)}, u32[]{:S(2)}) copy-start(f32[128]{0:T(128)} %copy-done.7) | copy-start | bytes 1540
  169.6 37.4 %collective-permute-start.7 = (f32[128,1536]{1,0:T(8,128)}, f32[128,1536]{1,0:T(8,128)}, u32[]{:S(2)}, u32[]{:S(2)}) collective-permute-start(f32[128,1536]{1,0:T(8,128)} %fusion.55), channel_id=1, source_target_pairs={{0,1},{1,0},{2,3},{3,2},{4,5},{5,4},{6,7},{7,6},{8,9},{9,8},{10,11... | collective-permute-start | bytes 2359304 | tf_op jit(solution)/shard_map/ppermute | solution.py:17
  173.4 27.2 %all-to-all-start.6 = ((bf16[4,24,896]{2,1,0:T(8,128)(2,1)}), bf16[4,24,896]{2,1,0:T(8,128)(2,1)S(1)}, u32[]{:S(2)}, u32[]{:S(2)}) async-start(bf16[4,24,896]{2,1,0:T(8,128)(2,1)} %broadcast_in_dim.19), calls=%async_computation.6 | async-start | bytes 344064 | tf_op jit(solution)/shard_map/all_to_all | solution.py:52
  185.7 21.3 %copy-start.3 = (bf16[512,128]{1,0:T(8,128)(2,1)S(1)}, bf16[512,128]{1,0:T(8,128)(2,1)}, u32[]{:S(2)}) copy-start(bf16[512,128]{1,0:T(8,128)(2,1)} %constant_dynamic-slice_fusion.2) | copy-start | bytes 393220
  188.0 24.5 %collective-permute-start.6 = (bf16[128,1536]{1,0:T(8,128)(2,1)}, bf16[128,1536]{1,0:T(8,128)(2,1)}, u32[]{:S(2)}, u32[]{:S(2)}) collective-permute-start(bf16[128,1536]{1,0:T(8,128)(2,1)} %fusion.28), channel_id=1, source_target_pairs={{0,0},{1,64},{64,1},{65,65},{2,2},{3,66},{66,3},{67,67},{4,4},{5,6... | collective-permute-start | bytes 1179656 | tf_op jit(solution)/shard_map/ppermute | solution.py:29
  201.4 18.8 %all-to-all-start.7 = ((bf16[8,24,896]{2,1,0:T(8,128)(2,1)}), bf16[8,24,896]{2,1,0:T(8,128)(2,1)S(1)}, u32[]{:S(2)}, u32[]{:S(2)}) async-start(bf16[8,24,896]{2,1,0:T(8,128)(2,1)} %broadcast_in_dim.20), calls=%async_computation.7 | async-start | bytes 688128 | tf_op jit(solution)/shard_map/all_to_all | solution.py:52
  208.9 10.3 %collective-permute-start.8 = (bf16[128,1536]{1,0:T(8,128)(2,1)S(1)}, bf16[128,1536]{1,0:T(8,128)(2,1)S(1)}, u32[]{:S(2)}, u32[]{:S(2)}) collective-permute-start(bf16[128,1536]{1,0:T(8,128)(2,1)S(1)} %fusion.35), channel_id=1, source_target_pairs={{0,0},{1,64},{64,1},{65,65},{2,2},{3,66},{66,3},{67,67},{4,4},{5,6... | collective-permute-start | bytes 1179656 | tf_op jit(solution)/shard_map/ppermute | solution.py:29
  220.3 3.5 %collective-permute-start.10 = (bf16[192,768]{1,0:T(8,128)(2,1)S(1)}, bf16[192,768]{1,0:T(8,128)(2,1)S(1)}, u32[]{:S(2)}, u32[]{:S(2)}) collective-permute-start(bf16[192,768]{1,0:T(8,128)(2,1)S(1)} %bitcast.42), channel_id=1, source_target_pairs={{0,1},{1,0},{2,3},{3,2},{4,5},{5,4},{6,7},{7,6},{8,9},{9,8},{10,11... | collective-permute-start | bytes 884744 | tf_op jit(solution)/shard_map/ppermute | solution.py:17
  (13 other events, 115.2 us)

commit v3 on v2

v3 whole, which is shorter than its diff:
```python
import jax
import jax.numpy as jnp
from jax import lax
from jax.sharding import Mesh, PartitionSpec as P

epsilon = 1e-06
loss_scale = 64.0
AXES = ("y", "xl", "zh", "zl", "xh", "core")
SIZES = (4, 2, 4, 4, 2, 2)
ROWS = ("zh", "zl", "xh", "core", "y", "xl")
bf16 = jnp.bfloat16
f32 = jnp.float32


def shift(value, axis, steps):
    count = lax.axis_size(axis)
    return lax.ppermute(value, axis, [(i, (i + steps) % count) for i in range(count)])


def shift_x(value, steps):
    def index(place):
        place = place % 4
        return (place % 2) * 2 + place // 2

    return lax.ppermute(value, ("xl", "xh"), [(index(i), index(i + steps)) for i in range(4)])


def swap(value):
    return lax.ppermute(value, ("xl", "core"), [(0, 0), (1, 2), (2, 1), (3, 3)])


def halves(flag, first, second, axis):
    return jnp.where(
        flag == 0,
        jnp.concatenate([first, second], axis),
        jnp.concatenate([second, first], axis),
    )


def dot(a, b, da, db):
    return lax.dot_general(a, b, (((da,), (db,)), ((), ())), preferred_element_type=f32)


def split16(value):
    high = value.astype(bf16)
    return high, (value - high.astype(f32)).astype(bf16)


def spread_to(value, axes):
    count = lax.axis_size(axes)
    many = jnp.broadcast_to(value[None], (count,) + value.shape)
    return lax.all_to_all(many, axes, split_axis=0, concat_axis=0, tiled=True)


def after(value, *others):
    return lax.optimization_barrier((value,) + others)[0]


def place_y(value, y):
    rows, width = value.shape
    whole = jnp.zeros((4 * rows, width), bf16)
    moved = [(0, value)] + [(-step, shift(value, "y", step)) for step in (1, -1, 2)]
    for step, block in moved:
        whole = lax.dynamic_update_slice(whole, block, ((y + step) % 4 * rows, 0))
    return whole


def gather_weight(blocks, xl, core, earlier):
    count, rows, half = blocks.shape
    other = [shift_x(blocks[:2], 1), shift_x(blocks[2:], -1)]
    own_half = jnp.zeros((count, 2, rows, half), bf16)
    own_half = lax.dynamic_update_slice(own_half, blocks[:, None], (0, xl, 0, 0))
    for start, block in zip((0, 2), other):
        own_half = lax.dynamic_update_slice(own_half, block[:, None], (start, 1 - xl, 0, 0))
    own_half = after(own_half.reshape(2 * count * rows, half), earlier)
    weight = jnp.zeros((2 * count * rows, 2 * half), bf16)
    weight = lax.dynamic_update_slice(weight, own_half, (0, core * half))
    return lax.dynamic_update_slice(weight, shift(own_half, "core", 1), (0, (1 - core) * half))


def local(
    image_features, final_norm_gain, final_norm_bias, head_weight, text_embed, log_scale, logit_bias
):
    y, xl, xh, core = (lax.axis_index(a) for a in ("y", "xl", "xh", "core"))
    scale = jnp.exp(log_scale[0])
    offset = logit_bias[0]
    own, width = image_features.shape
    half = width // 2
    block = width // 4

    text_rows = swap(text_embed)
    feature_rows = swap(image_features)
    weight_part = lax.dynamic_slice(head_weight, (0, core * half), (head_weight.shape[0], half))
    weight_blocks = spread_to(weight_part, "y")

    text_values = text_rows.astype(f32)
    inv_text = lax.rsqrt(jnp.sum(text_values * text_values, axis=1, keepdims=True) + epsilon)
    text_unit = (text_values * inv_text).astype(bf16)

    values = feature_rows.astype(f32)
    centre = jnp.mean(values, axis=1, keepdims=True)
    centered = values - centre
    spread = jnp.mean(centered * centered, axis=1, keepdims=True)
    inverse_deviation = lax.rsqrt(spread + epsilon)
    xhat = centered * inverse_deviation
    normed_own = (xhat * final_norm_gain + final_norm_bias).astype(bf16)

    weight_blocks, text_unit, normed_own = lax.optimization_barrier(
        (weight_blocks, text_unit, normed_own)
    )
    text_same = place_y(text_unit, y)
    weight = gather_weight(weight_blocks, xl, core, text_same)
    normed = place_y(normed_own, y)
    text_other = shift(text_same, "core", 1)
    rows = normed.shape[0]

    projected = dot(normed, weight, 1, 0)
    inv_proj = lax.rsqrt(jnp.sum(projected * projected, axis=1, keepdims=True) + epsilon)
    image_unit = (projected * inv_proj).astype(bf16)

    def weights_of(text_rows, diagonal):
        logits = scale * dot(image_unit, text_rows, 1, 1) + offset
        return (loss_scale * (jax.nn.sigmoid(logits) - diagonal)).astype(bf16)

    weights_same = weights_of(text_same, jnp.eye(rows, dtype=f32))
    weights_other = weights_of(text_other, 0.0)
    grad_image = scale * (dot(weights_same, text_same, 1, 0) + dot(weights_other, text_other, 1, 0))
    proj_dot = jnp.sum(projected * grad_image, axis=1, keepdims=True)
    grad_proj = (
        inv_proj * grad_image - inv_proj * inv_proj * inv_proj * proj_dot * projected
    ).astype(bf16)

    normed_block = lax.dynamic_slice(normed, (0, y * block), (rows, block))
    theirs = lax.dynamic_slice(grad_proj, (0, (1 - core) * half), (rows, half))
    sent = dot(normed_block, theirs, 0, 0).astype(bf16)
    grad_proj, sent = lax.optimization_barrier((grad_proj, sent))
    mine = lax.dynamic_slice(grad_proj, (0, core * half), (rows, half))
    head = dot(normed_block, mine, 0, 0) + shift(sent, "core", 1).astype(f32)
    part = block // 4
    head = head.astype(bf16).reshape(4, part, half)
    head = lax.all_to_all(head, ("xl", "xh"), split_axis=0, concat_axis=0, tiled=True)
    head = jnp.sum(head.astype(f32), axis=0)

    grad_own = lax.dynamic_slice(grad_proj, (y * own, 0), (own, width))
    grad_normed = dot(grad_own, weight, 1, 1)
    vectors = jnp.stack([jnp.sum(grad_normed * xhat, axis=0), jnp.sum(grad_normed, axis=0)], 0)
    vectors = jnp.sum(spread_to(vectors, ("y", "xl")), axis=0)

    held = after((weights_same, weights_other, image_unit), head)
    text_part, text_theirs = (
        dot(lax.dynamic_slice(w, (0, y * own), (rows, own)), held[2], 0, 0) for w in held[:2]
    )
    grad_unit_text = text_part + shift(text_theirs, "core", 1)

    lanes = 128
    lines = part // 4
    count = 2 * width // 4 // lanes

    def payload(head_rows, vector):
        lead = vector.shape[:-1]
        high, low = (t.reshape(lead + (-1, lanes)) for t in split16(vector))
        rest = jnp.zeros(lead + (lines - 2 * count, lanes), bf16)
        side = jnp.concatenate([high, low, rest], -2)
        return jnp.concatenate([head_rows.astype(bf16), side], -1)

    def unpack(received):
        side = received[..., half:]
        vector = side[..., :count, :] + side[..., count : 2 * count, :]
        return received[..., :half], vector.reshape(vector.shape[:-2] + (-1,))

    sent = payload(head.reshape(4, lines, half), vectors.reshape(4, 2 * width // 4))
    received = lax.all_to_all(sent, "zl", split_axis=0, concat_axis=0, tiled=True).astype(f32)
    sent = payload(*unpack(jnp.sum(received, axis=0)))

    grad_unit_text, grad_normed = after((grad_unit_text, grad_normed), sent)
    grad_unit_text = scale * grad_unit_text
    text_dot = jnp.sum(text_values * grad_unit_text, axis=1, keepdims=True)
    grad_text = inv_text * grad_unit_text - inv_text * inv_text * inv_text * text_dot * text_values
    scaled = grad_normed * final_norm_gain
    first_mean = jnp.mean(scaled, axis=1, keepdims=True)
    second_mean = jnp.mean(scaled * xhat, axis=1, keepdims=True)
    grad_features = inverse_deviation * (scaled - first_mean - xhat * second_mean)
    returned = swap(jnp.stack([grad_features, grad_text], 0).astype(bf16))

    received = spread_to(sent, "zh").astype(f32)
    sent = payload(*unpack(jnp.sum(received, axis=0)))
    received = spread_to(sent, ("zl", "xh")).reshape(4, 2, lines, half + lanes)
    head_all = received[..., :half].transpose(1, 0, 2, 3).reshape(2 * part, half)
    vector_all = jnp.sum(unpack(received.astype(f32))[1], axis=1).reshape(-1, lanes)
    other_head, other_vector = shift(head_all, "core", 1), shift(vector_all, "core", 1)
    head_all = halves(core, head_all, other_head, 1).astype(f32) / 64.0
    vector_all = (vector_all + other_vector).reshape(2, width) / 64.0

    return (
        returned[0].astype(f32),
        returned[1].astype(f32),
        vector_all[0],
        vector_all[1],
        head_all,
    )


def solution(mesh):
    fine = Mesh(mesh.devices.reshape(SIZES), AXES)
    placed = (P(ROWS, None), P(), P(), P(("y", "xl"), None), P(ROWS, None), P(), P())
    return jax.shard_map(
        local,
        mesh=fine,
        in_specs=placed,
        out_specs=(P(ROWS, None), P(ROWS, None), P(), P(), P(("y", "xl"), None)),
        check_vma=False,
    )
```

time: 227 us -> 197 us (0.87)
  blocking collectives: 23.8 us -> 0 us
  starting transfers between devices: 80 us -> 96.5 us
  other arithmetic: 22.6 us -> 8.05 us
  matrix products: 27.3 us -> 19.6 us
  local copies, waits for them, and re-layouts: 12.7 us -> 17.9 us
  waiting for transfers between devices: 55.9 us -> 51.1 us
    ppermute x5 -> x12, starting transfers between devices: 14.9 us -> 40.5 us  [shift(): lax.ppermute(value, axis, [(i, (i + steps) % count) for i in range(count)])]
    all_to_all x1 -> x0, blocking collectives: 23.8 us -> none  [spread_to(): return lax.all_to_all(many, axes, split_axis=0, concat_axis=0, tiled=True)]
    all_to_all x5 -> x4, waiting for transfers between devices: 34.6 us -> 19.9 us  [spread_to(): return lax.all_to_all(many, axes, split_axis=0, concat_axis=0, tiled=True)]
    dynamic_update_slice x0 -> x13, local copies, waits for them, and re-layouts: none -> 10.5 us  [the longest x8 5.26 us: place_y(): whole = lax.dynamic_update_slice(whole, block, ((y + step) % 4 * rows, 0))]
    select_n x2 -> x0, other arithmetic: 9.38 us -> none  [halves(): jnp.where(flag == 0, jnp.concatenate([first, second], axis), jnp.concaten...]
    dot_general x10, matrix products: 27.3 us -> 19.6 us  [dot(): lax.dot_general(a, b, (((da,), (db,)), ((), ())), preferred_element_type=...]
    ppermute x5 -> x12, waiting for transfers between devices: 0.33 us -> 7.08 us  [shift(): lax.ppermute(value, axis, [(i, (i + steps) % count) for i in range(count)])]
    ppermute x4 -> x3, starting transfers between devices: 18.4 us -> 11.8 us  [swap(): return lax.ppermute(value, ('xl', 'core'), [(0, 0), (1, 2), (2, 1), (3, 3)])]
  transfers between devices with their start and end apart: 18 -> 23, of which waited for: 10 -> 10; matrix products, arithmetic and copies ran while one was open for 21% -> 18% of each run, Pallas kernels for 0% -> 0%
where the time goes in v3:
time: 197 us; the launch traced here: 196 us
  starting transfers between devices  96.5 us (49%)
  waiting for transfers between devices  51.1 us (26%)
  matrix products  19.6 us (10%)
  local copies, waits for them, and re-layouts  17.9 us (9%)
  other arithmetic  8.05 us (4%)
  between operations  2.7 us (1%)
    ppermute x12, starting transfers between devices, shift(): lax.ppermute(value, axis, [(i, (i + steps) % count) for i in range(count)])  40.5 us
    all_to_all x4, starting transfers between devices, spread_to(): return lax.all_to_all(many, axes, split_axis=0, concat_axis=0, tiled=True)  27.7 us
    all_to_all x4, waiting for transfers between devices, spread_to(): return lax.all_to_all(many, axes, split_axis=0, concat_axis=0, tiled=True)  19.9 us
    dot_general x10, matrix products, dot(): lax.dot_general(a, b, (((da,), (db,)), ((), ())), preferred_element_type=...  19.6 us
    ppermute x3, starting transfers between devices, swap(): return lax.ppermute(value, ('xl', 'core'), [(0, 0), (1, 2), (2, 1), (3, 3)])  11.8 us
    all_to_all x1, waiting for transfers between devices, local(): lax.all_to_all(head, ('xl', 'xh'), split_axis=0, concat_axis=0, tiled=True)  9.95 us
    ppermute x2, waiting for transfers between devices, shift_x(): lax.ppermute(value, ('xl', 'xh'), [(index(i), index(i + steps)) for i in...  7.41 us
    ppermute x12, waiting for transfers between devices, shift(): lax.ppermute(value, axis, [(i, (i + steps) % count) for i in range(count)])  7.08 us
  transfers between devices with their start and end apart: 23, of which 10 were waited for; matrix products, arithmetic and copies ran while one was open for 18% of the time, Pallas kernels for 0%

profile of v3, /device:TPU:1, one launch (start us, length us, event | category | flops | bytes accessed | tf_op | source)
XLA Modules:
  0.0 195.8 jit_solution(484290662843941975)
XLA Ops:
  0.6 4.6 %collective-permute-start = (bf16[128,1536]{1,0:T(8,128)(2,1)}, bf16[128,1536]{1,0:T(8,128)(2,1)S(1)}, u32[]{:S(2)}, u32[]{:S(2)}) collective-permute-start(bf16[128,1536]{1,0:T(8,128)(2,1)} %param.7), channel_id=1, source_target_pairs={{0,0},{1,64},{64,1},{65,65},{2,2},{3,66},{66,3},{67,67},{4,4},{5,6... | collective-permute-start | bytes 1179656 | tf_op jit(solution)/shard_map/ppermute | solution.py:29
  6.5 4.2 %all-to-all-start = ((bf16[4,192,768]{2,1,0:T(8,128)(2,1)}), bf16[4,192,768]{2,1,0:T(8,128)(2,1)S(1)}, u32[]{:S(2)}, u32[]{:S(2)}) async-start(bf16[4,192,768]{2,1,0:T(8,128)(2,1)} %broadcast_in_dim.20), calls=%async_computation | async-start | bytes 2359296 | tf_op jit(solution)/shard_map/all_to_all | solution.py:52
  13.5 6.7 %collective-permute-done.1 = bf16[128,1536]{1,0:T(8,128)(2,1)S(1)} collective-permute-done((bf16[128,1536]{1,0:T(8,128)(2,1)S(1)}, bf16[128,1536]{1,0:T(8,128)(2,1)S(1)}, u32[]{:S(2)}, u32[]{:S(2)}) %collective-permute-start.1) | collective-permute-done | bytes 393248 | tf_op jit(solution)/shard_map/ppermute | solution.py:29
  25.8 4.3 %collective-permute-start.8 = (bf16[128,1536]{1,0:T(8,128)(2,1)S(1)}, bf16[128,1536]{1,0:T(8,128)(2,1)S(1)}, u32[]{:S(2)}, u32[]{:S(2)}) collective-permute-start(bf16[128,1536]{1,0:T(8,128)(2,1)S(1)} %fusion.32), channel_id=1, source_target_pairs={{0,384},{128,0},{256,128},{384,256},{1,385},{129,1},{257,129},{385... | collective-permute-start | bytes 1179656 | tf_op jit(solution)/shard_map/ppermute | solution.py:17
  32.1 3.4 %collective-permute-start.5 = (bf16[2,192,768]{2,1,0:T(8,128)(2,1)S(1)}, bf16[2,192,768]{2,1,0:T(8,128)(2,1)S(1)}, u32[]{:S(2)}, u32[]{:S(2)}) collective-permute-start(bf16[2,192,768]{2,1,0:T(8,128)(2,1)S(1)} %get-tuple-element.38), channel_id=1, source_target_pairs={{0,64},{64,2},{2,66},{66,0},{1,65},{65,3},{3,67},{67,1},{4,68},{68... | collective-permute-start | bytes 1769480 | tf_op jit(solution)/shard_map/ppermute | solution.py:25
  35.5 3.1 %collective-permute-start.6 = (bf16[2,192,768]{2,1,0:T(8,128)(2,1)S(1)}, bf16[2,192,768]{2,1,0:T(8,128)(2,1)S(1)}, u32[]{:S(2)}, u32[]{:S(2)}) collective-permute-start(bf16[2,192,768]{2,1,0:T(8,128)(2,1)S(1)} %get-tuple-element.37), channel_id=1, source_target_pairs={{0,66},{64,0},{2,64},{66,2},{1,67},{65,1},{3,65},{67,3},{4,70},{68... | collective-permute-start | bytes 1769480 | tf_op jit(solution)/shard_map/ppermute | solution.py:25
  46.6 7.4 %collective-permute-done.6 = bf16[2,192,768]{2,1,0:T(8,128)(2,1)S(1)} collective-permute-done((bf16[2,192,768]{2,1,0:T(8,128)(2,1)S(1)}, bf16[2,192,768]{2,1,0:T(8,128)(2,1)S(1)}, u32[]{:S(2)}, u32[]{:S(2)}) %collective-permute-start.6) | collective-permute-done | bytes 589856 | tf_op jit(solution)/shard_map/ppermute | solution.py:25
  54.9 3.8 %collective-permute-start.10 = (bf16[1536,768]{1,0:T(8,128)(2,1)}, bf16[1536,768]{1,0:T(8,128)(2,1)S(1)}, u32[]{:S(2)}, u32[]{:S(2)}) collective-permute-start(bf16[1536,768]{1,0:T(8,128)(2,1)} %bitcast.6), channel_id=1, source_target_pairs={{0,1},{1,0},{2,3},{3,2},{4,5},{5,4},{6,7},{7,6},{8,9},{9,8},{10,11... | collective-permute-start | bytes 7077896 | tf_op jit(solution)/shard_map/ppermute | solution.py:17
  62.5 4.0 %collective-permute-start.3 = (bf16[128,1536]{1,0:T(8,128)(2,1)}, bf16[128,1536]{1,0:T(8,128)(2,1)S(1)}, u32[]{:S(2)}, u32[]{:S(2)}) collective-permute-start(bf16[128,1536]{1,0:T(8,128)(2,1)} %fusion.24), channel_id=1, source_target_pairs={{0,384},{128,0},{256,128},{384,256},{1,385},{129,1},{257,129},{385... | collective-permute-start | bytes 1179656 | tf_op jit(solution)/shard_map/ppermute | solution.py:17
  66.5 3.7 %collective-permute-start.4 = (bf16[128,1536]{1,0:T(8,128)(2,1)}, bf16[128,1536]{1,0:T(8,128)(2,1)S(1)}, u32[]{:S(2)}, u32[]{:S(2)}) collective-permute-start(bf16[128,1536]{1,0:T(8,128)(2,1)} %fusion.24), channel_id=1, source_target_pairs={{0,256},{128,384},{256,0},{384,128},{1,257},{129,385},{257,1},{385... | collective-permute-start | bytes 1179656 | tf_op jit(solution)/shard_map/ppermute | solution.py:17
  71.3 2.8 %collective-permute-start.11 = (bf16[512,1536]{1,0:T(8,128)(2,1)}, bf16[512,1536]{1,0:T(8,128)(2,1)S(1)}, u32[]{:S(2)}, u32[]{:S(2)}) collective-permute-start(bf16[512,1536]{1,0:T(8,128)(2,1)} %constant_dynamic-update-slice_fusion.2), channel_id=1, source_target_pairs={{0,1},{1,0},{2,3},{3,2},{4,5},{5,4},{6,7},{7,6},{8,9},{9,8},{10,11... | collective-permute-start | bytes 4718600 | tf_op jit(solution)/shard_map/ppermute | solution.py:17
  76.0 5.3 %collective-permute-done.4 = bf16[128,1536]{1,0:T(8,128)(2,1)S(1)} collective-permute-done((bf16[128,1536]{1,0:T(8,128)(2,1)}, bf16[128,1536]{1,0:T(8,128)(2,1)S(1)}, u32[]{:S(2)}, u32[]{:S(2)}) %collective-permute-start.4) | collective-permute-done | bytes 393248 | tf_op jit(solution)/shard_map/ppermute | solution.py:17
  96.3 5.2 %collective-permute-start.12 = (bf16[384,768]{1,0:T(8,128)(2,1)}, bf16[384,768]{1,0:T(8,128)(2,1)}, u32[]{:S(2)}, u32[]{:S(2)}) collective-permute-start(bf16[384,768]{1,0:T(8,128)(2,1)} %convolution_convert_fusion), channel_id=1, source_target_pairs={{0,1},{1,0},{2,3},{3,2},{4,5},{5,4},{6,7},{7,6},{8,9},{9,8},{10,11... | collective-permute-start | bytes 1769480 | tf_op jit(solution)/shard_map/ppermute | solution.py:17
  103.9 5.7 %all-to-all-start.2 = ((f32[8,2,1536]{2,1,0:T(2,128)}), f32[8,2,1536]{2,1,0:T(2,128)S(1)}, u32[]{:S(2)}, u32[]{:S(2)}) async-start(f32[8,2,1536]{2,1,0:T(2,128)} %broadcast_in_dim.26), calls=%async_computation.2 | async-start | bytes 196608 | tf_op jit(solution)/shard_map/all_to_all | solution.py:52
  115.0 4.1 %all-to-all-start.1 = ((bf16[4,96,768]{2,1,0:T(8,128)(2,1)}), bf16[4,96,768]{2,1,0:T(8,128)(2,1)}, u32[]{:S(2)}, u32[]{:S(2)}) async-start(bf16[4,96,768]{2,1,0:T(8,128)(2,1)} %bitcast.56), calls=%async_computation.1 | async-start | bytes 1179648 | tf_op jit(solution)/shard_map/all_to_all | solution.py:141
  119.3 9.9 %all-to-all-done.1 = bf16[4,96,768]{2,1,0:T(8,128)(2,1)} async-done(((bf16[4,96,768]{2,1,0:T(8,128)(2,1)}), bf16[4,96,768]{2,1,0:T(8,128)(2,1)}, u32[]{:S(2)}, u32[]{:S(2)}) %all-to-all-start.1) | async-done | bytes 589856 | tf_op jit(solution)/shard_map/all_to_all | solution.py:141
  131.1 5.8 %all-to-all-start.3 = ((bf16[4,24,896]{2,1,0:T(8,128)(2,1)}), bf16[4,24,896]{2,1,0:T(8,128)(2,1)S(1)}, u32[]{:S(2)}, u32[]{:S(2)}) async-start(bf16[4,24,896]{2,1,0:T(8,128)(2,1)} %maximum_maximum_fusion), calls=%async_computation.3 | async-start | bytes 344064 | tf_op jit(solution)/shard_map/all_to_all | solution.py:172
  139.1 3.0 %collective-permute-start.13 = (f32[128,1536]{1,0:T(8,128)}, f32[128,1536]{1,0:T(8,128)}, u32[]{:S(2)}, u32[]{:S(2)}) collective-permute-start(f32[128,1536]{1,0:T(8,128)} %fusion.46), channel_id=1, source_target_pairs={{0,1},{1,0},{2,3},{3,2},{4,5},{5,4},{6,7},{7,6},{8,9},{9,8},{10,11... | collective-permute-start | bytes 2359304 | tf_op jit(solution)/shard_map/ppermute | solution.py:17
  142.9 12.3 %all-to-all-start.4 = ((bf16[4,24,896]{2,1,0:T(8,128)(2,1)}), bf16[4,24,896]{2,1,0:T(8,128)(2,1)S(1)}, u32[]{:S(2)}, u32[]{:S(2)}) async-start(bf16[4,24,896]{2,1,0:T(8,128)(2,1)} %broadcast_in_dim.28), calls=%async_computation.4 | async-start | bytes 344064 | tf_op jit(solution)/shard_map/all_to_all | solution.py:52
  157.9 4.9 %collective-permute-start.14 = (bf16[2,128,1536]{2,1,0:T(8,128)(2,1)S(1)}, bf16[2,128,1536]{2,1,0:T(8,128)(2,1)S(1)}, u32[]{:S(2)}, u32[]{:S(2)}) collective-permute-start(bf16[2,128,1536]{2,1,0:T(8,128)(2,1)S(1)} %pad_maximum_fusion), channel_id=1, source_target_pairs={{0,0},{1,64},{64,1},{65,65},{2,2},{3,66},{66,3},{67,67},{4,4},{5,6... | collective-permute-start | bytes 2359304 | tf_op jit(solution)/shard_map/ppermute | solution.py:29
  162.7 7.3 %all-to-all-done.4 = bf16[4,24,896]{2,1,0:T(8,128)(2,1)S(1)} async-done(((bf16[4,24,896]{2,1,0:T(8,128)(2,1)}), bf16[4,24,896]{2,1,0:T(8,128)(2,1)S(1)}, u32[]{:S(2)}, u32[]{:S(2)}) %all-to-all-start.4) | async-done | bytes 172064 | tf_op jit(solution)/shard_map/all_to_all | solution.py:52
  170.8 5.6 %all-to-all-start.5 = ((bf16[8,24,896]{2,1,0:T(8,128)(2,1)}), bf16[8,24,896]{2,1,0:T(8,128)(2,1)S(1)}, u32[]{:S(2)}, u32[]{:S(2)}) async-start(bf16[8,24,896]{2,1,0:T(8,128)(2,1)} %broadcast_in_dim.29), calls=%async_computation.5 | async-start | bytes 688128 | tf_op jit(solution)/shard_map/all_to_all | solution.py:52
  177.7 8.0 %all-to-all-done.5 = bf16[8,24,896]{2,1,0:T(8,128)(2,1)S(1)} async-done(((bf16[8,24,896]{2,1,0:T(8,128)(2,1)}), bf16[8,24,896]{2,1,0:T(8,128)(2,1)S(1)}, u32[]{:S(2)}, u32[]{:S(2)}) %all-to-all-start.5) | async-done | bytes 344096 | tf_op jit(solution)/shard_map/all_to_all | solution.py:52
  185.8 5.3 %collective-permute-start.15 = (f32[24,128]{1,0:T(8,128)S(1)}, f32[24,128]{1,0:T(8,128)S(1)}, u32[]{:S(2)}, u32[]{:S(2)}) collective-permute-start(f32[24,128]{1,0:T(8,128)S(1)} %reshape.117), channel_id=1, source_target_pairs={{0,1},{1,0},{2,3},{3,2},{4,5},{5,4},{6,7},{7,6},{8,9},{9,8},{10,11... | collective-permute-start | bytes 36872 | tf_op jit(solution)/shard_map/ppermute | solution.py:17
  (121 shorter events, 62.8 us)
Async XLA Ops:
  0.6 12.4 %collective-permute-start = (bf16[128,1536]{1,0:T(8,128)(2,1)}, bf16[128,1536]{1,0:T(8,128)(2,1)S(1)}, u32[]{:S(2)}, u32[]{:S(2)}) collective-permute-start(bf16[128,1536]{1,0:T(8,128)(2,1)} %param.7), channel_id=1, source_target_pairs={{0,0},{1,64},{64,1},{65,65},{2,2},{3,66},{66,3},{67,67},{4,4},{5,6... | collective-permute-start | bytes 1179656 | tf_op jit(solution)/shard_map/ppermute | solution.py:29
  6.5 17.1 %all-to-all-start = ((bf16[4,192,768]{2,1,0:T(8,128)(2,1)}), bf16[4,192,768]{2,1,0:T(8,128)(2,1)S(1)}, u32[]{:S(2)}, u32[]{:S(2)}) async-start(bf16[4,192,768]{2,1,0:T(8,128)(2,1)} %broadcast_in_dim.20), calls=%async_computation | async-start | bytes 2359296 | tf_op jit(solution)/shard_map/all_to_all | solution.py:52
  10.6 9.5 %collective-permute-start.1 = (bf16[128,1536]{1,0:T(8,128)(2,1)S(1)}, bf16[128,1536]{1,0:T(8,128)(2,1)S(1)}, u32[]{:S(2)}, u32[]{:S(2)}) collective-permute-start(bf16[128,1536]{1,0:T(8,128)(2,1)S(1)} %copy-done.9), channel_id=1, source_target_pairs={{0,0},{1,64},{64,1},{65,65},{2,2},{3,66},{66,3},{67,67},{4,4},{5,6... | collective-permute-start | bytes 1179656 | tf_op jit(solution)/shard_map/ppermute | solution.py:29
  23.6 19.7 %collective-permute-start.7 = (bf16[128,1536]{1,0:T(8,128)(2,1)S(1)}, bf16[128,1536]{1,0:T(8,128)(2,1)S(1)}, u32[]{:S(2)}, u32[]{:S(2)}) collective-permute-start(bf16[128,1536]{1,0:T(8,128)(2,1)S(1)} %fusion.32), channel_id=1, source_target_pairs={{0,128},{128,256},{256,384},{384,0},{1,129},{129,257},{257,385},{3... | collective-permute-start | bytes 1179656 | tf_op jit(solution)/shard_map/ppermute | solution.py:17
  25.8 18.3 %collective-permute-start.8 = (bf16[128,1536]{1,0:T(8,128)(2,1)S(1)}, bf16[128,1536]{1,0:T(8,128)(2,1)S(1)}, u32[]{:S(2)}, u32[]{:S(2)}) collective-permute-start(bf16[128,1536]{1,0:T(8,128)(2,1)S(1)} %fusion.32), channel_id=1, source_target_pairs={{0,384},{128,0},{256,128},{384,256},{1,385},{129,1},{257,129},{385... | collective-permute-start | bytes 1179656 | tf_op jit(solution)/shard_map/ppermute | solution.py:17
  30.1 14.8 %collective-permute-start.9 = (bf16[128,1536]{1,0:T(8,128)(2,1)S(1)}, bf16[128,1536]{1,0:T(8,128)(2,1)S(1)}, u32[]{:S(2)}, u32[]{:S(2)}) collective-permute-start(bf16[128,1536]{1,0:T(8,128)(2,1)S(1)} %fusion.32), channel_id=1, source_target_pairs={{0,256},{128,384},{256,0},{384,128},{1,257},{129,385},{257,1},{385... | collective-permute-start | bytes 1179656 | tf_op jit(solution)/shard_map/ppermute | solution.py:17
  32.1 13.6 %collective-permute-start.5 = (bf16[2,192,768]{2,1,0:T(8,128)(2,1)S(1)}, bf16[2,192,768]{2,1,0:T(8,128)(2,1)S(1)}, u32[]{:S(2)}, u32[]{:S(2)}) collective-permute-start(bf16[2,192,768]{2,1,0:T(8,128)(2,1)S(1)} %get-tuple-element.38), channel_id=1, source_target_pairs={{0,64},{64,2},{2,66},{66,0},{1,65},{65,3},{3,67},{67,1},{4,68},{68... | collective-permute-start | bytes 1769480 | tf_op jit(solution)/shard_map/ppermute | solution.py:25
  35.5 18.5 %collective-permute-start.6 = (bf16[2,192,768]{2,1,0:T(8,128)(2,1)S(1)}, bf16[2,192,768]{2,1,0:T(8,128)(2,1)S(1)}, u32[]{:S(2)}, u32[]{:S(2)}) collective-permute-start(bf16[2,192,768]{2,1,0:T(8,128)(2,1)S(1)} %get-tuple-element.37), channel_id=1, source_target_pairs={{0,66},{64,0},{2,64},{66,2},{1,67},{65,1},{3,65},{67,3},{4,70},{68... | collective-permute-start | bytes 1769480 | tf_op jit(solution)/shard_map/ppermute | solution.py:25
  54.9 28.9 %collective-permute-start.10 = (bf16[1536,768]{1,0:T(8,128)(2,1)}, bf16[1536,768]{1,0:T(8,128)(2,1)S(1)}, u32[]{:S(2)}, u32[]{:S(2)}) collective-permute-start(bf16[1536,768]{1,0:T(8,128)(2,1)} %bitcast.6), channel_id=1, source_target_pairs={{0,1},{1,0},{2,3},{3,2},{4,5},{5,4},{6,7},{7,6},{8,9},{9,8},{10,11... | collective-permute-start | bytes 7077896 | tf_op jit(solution)/shard_map/ppermute | solution.py:17
  58.6 15.4 %collective-permute-start.2 = (bf16[128,1536]{1,0:T(8,128)(2,1)}, bf16[128,1536]{1,0:T(8,128)(2,1)}, u32[]{:S(2)}, u32[]{:S(2)}) collective-permute-start(bf16[128,1536]{1,0:T(8,128)(2,1)} %fusion.24), channel_id=1, source_target_pairs={{0,128},{128,256},{256,384},{384,0},{1,129},{129,257},{257,385},{3... | collective-permute-start | bytes 1179656 | tf_op jit(solution)/shard_map/ppermute | solution.py:17
  62.5 13.4 %collective-permute-start.3 = (bf16[128,1536]{1,0:T(8,128)(2,1)}, bf16[128,1536]{1,0:T(8,128)(2,1)S(1)}, u32[]{:S(2)}, u32[]{:S(2)}) collective-permute-start(bf16[128,1536]{1,0:T(8,128)(2,1)} %fusion.24), channel_id=1, source_target_pairs={{0,384},{128,0},{256,128},{384,256},{1,385},{129,1},{257,129},{385... | collective-permute-start | bytes 1179656 | tf_op jit(solution)/shard_map/ppermute | solution.py:17
  66.5 14.8 %collective-permute-start.4 = (bf16[128,1536]{1,0:T(8,128)(2,1)}, bf16[128,1536]{1,0:T(8,128)(2,1)S(1)}, u32[]{:S(2)}, u32[]{:S(2)}) collective-permute-start(bf16[128,1536]{1,0:T(8,128)(2,1)} %fusion.24), channel_id=1, source_target_pairs={{0,256},{128,384},{256,0},{384,128},{1,257},{129,385},{257,1},{385... | collective-permute-start | bytes 1179656 | tf_op jit(solution)/shard_map/ppermute | solution.py:17
  71.3 18.3 %collective-permute-start.11 = (bf16[512,1536]{1,0:T(8,128)(2,1)}, bf16[512,1536]{1,0:T(8,128)(2,1)S(1)}, u32[]{:S(2)}, u32[]{:S(2)}) collective-permute-start(bf16[512,1536]{1,0:T(8,128)(2,1)} %constant_dynamic-update-slice_fusion.2), channel_id=1, source_target_pairs={{0,1},{1,0},{2,3},{3,2},{4,5},{5,4},{6,7},{7,6},{8,9},{9,8},{10,11... | collective-permute-start | bytes 4718600 | tf_op jit(solution)/shard_map/ppermute | solution.py:17
  81.3 13.6 %copy-start.4 = (bf16[512,1536]{1,0:T(8,128)(2,1)}, bf16[512,1536]{1,0:T(8,128)(2,1)S(1)}, u32[]{:S(2)}) copy-start(bf16[512,1536]{1,0:T(8,128)(2,1)S(1)} %constant_dynamic-update-slice_fusion.6) | copy-start | bytes 4718596
  96.3 13.3 %collective-permute-start.12 = (bf16[384,768]{1,0:T(8,128)(2,1)}, bf16[384,768]{1,0:T(8,128)(2,1)}, u32[]{:S(2)}, u32[]{:S(2)}) collective-permute-start(bf16[384,768]{1,0:T(8,128)(2,1)} %convolution_convert_fusion), channel_id=1, source_target_pairs={{0,1},{1,0},{2,3},{3,2},{4,5},{5,4},{6,7},{7,6},{8,9},{9,8},{10,11... | collective-permute-start | bytes 1769480 | tf_op jit(solution)/shard_map/ppermute | solution.py:17
  103.9 11.1 %all-to-all-start.2 = ((f32[8,2,1536]{2,1,0:T(2,128)}), f32[8,2,1536]{2,1,0:T(2,128)S(1)}, u32[]{:S(2)}, u32[]{:S(2)}) async-start(f32[8,2,1536]{2,1,0:T(2,128)} %broadcast_in_dim.26), calls=%async_computation.2 | async-start | bytes 196608 | tf_op jit(solution)/shard_map/all_to_all | solution.py:52
  115.0 14.2 %all-to-all-start.1 = ((bf16[4,96,768]{2,1,0:T(8,128)(2,1)}), bf16[4,96,768]{2,1,0:T(8,128)(2,1)}, u32[]{:S(2)}, u32[]{:S(2)}) async-start(bf16[4,96,768]{2,1,0:T(8,128)(2,1)} %bitcast.56), calls=%async_computation.1 | async-start | bytes 1179648 | tf_op jit(solution)/shard_map/all_to_all | solution.py:141
  131.1 11.0 %all-to-all-start.3 = ((bf16[4,24,896]{2,1,0:T(8,128)(2,1)}), bf16[4,24,896]{2,1,0:T(8,128)(2,1)S(1)}, u32[]{:S(2)}, u32[]{:S(2)}) async-start(bf16[4,24,896]{2,1,0:T(8,128)(2,1)} %maximum_maximum_fusion), calls=%async_computation.3 | async-start | bytes 344064 | tf_op jit(solution)/shard_map/all_to_all | solution.py:172
  139.1 16.1 %collective-permute-start.13 = (f32[128,1536]{1,0:T(8,128)}, f32[128,1536]{1,0:T(8,128)}, u32[]{:S(2)}, u32[]{:S(2)}) collective-permute-start(f32[128,1536]{1,0:T(8,128)} %fusion.46), channel_id=1, source_target_pairs={{0,1},{1,0},{2,3},{3,2},{4,5},{5,4},{6,7},{7,6},{8,9},{9,8},{10,11... | collective-permute-start | bytes 2359304 | tf_op jit(solution)/shard_map/ppermute | solution.py:17
  142.9 27.1 %all-to-all-start.4 = ((bf16[4,24,896]{2,1,0:T(8,128)(2,1)}), bf16[4,24,896]{2,1,0:T(8,128)(2,1)S(1)}, u32[]{:S(2)}, u32[]{:S(2)}) async-start(bf16[4,24,896]{2,1,0:T(8,128)(2,1)} %broadcast_in_dim.28), calls=%async_computation.4 | async-start | bytes 344064 | tf_op jit(solution)/shard_map/all_to_all | solution.py:52
  157.9 18.5 %collective-permute-start.14 = (bf16[2,128,1536]{2,1,0:T(8,128)(2,1)S(1)}, bf16[2,128,1536]{2,1,0:T(8,128)(2,1)S(1)}, u32[]{:S(2)}, u32[]{:S(2)}) collective-permute-start(bf16[2,128,1536]{2,1,0:T(8,128)(2,1)S(1)} %pad_maximum_fusion), channel_id=1, source_target_pairs={{0,0},{1,64},{64,1},{65,65},{2,2},{3,66},{66,3},{67,67},{4,4},{5,6... | collective-permute-start | bytes 2359304 | tf_op jit(solution)/shard_map/ppermute | solution.py:29
  170.8 14.9 %all-to-all-start.5 = ((bf16[8,24,896]{2,1,0:T(8,128)(2,1)}), bf16[8,24,896]{2,1,0:T(8,128)(2,1)S(1)}, u32[]{:S(2)}, u32[]{:S(2)}) async-start(bf16[8,24,896]{2,1,0:T(8,128)(2,1)} %broadcast_in_dim.29), calls=%async_computation.5 | async-start | bytes 688128 | tf_op jit(solution)/shard_map/all_to_all | solution.py:52
  185.8 7.2 %collective-permute-start.15 = (f32[24,128]{1,0:T(8,128)S(1)}, f32[24,128]{1,0:T(8,128)S(1)}, u32[]{:S(2)}, u32[]{:S(2)}) collective-permute-start(f32[24,128]{1,0:T(8,128)S(1)} %reshape.117), channel_id=1, source_target_pairs={{0,1},{1,0},{2,3},{3,2},{4,5},{5,4},{6,7},{7,6},{8,9},{9,8},{10,11... | collective-permute-start | bytes 36872 | tf_op jit(solution)/shard_map/ppermute | solution.py:17
  191.1 3.5 %collective-permute-start.16 = (bf16[192,768]{1,0:T(8,128)(2,1)S(1)}, bf16[192,768]{1,0:T(8,128)(2,1)S(1)}, u32[]{:S(2)}, u32[]{:S(2)}) collective-permute-start(bf16[192,768]{1,0:T(8,128)(2,1)S(1)} %bitcast.54), channel_id=1, source_target_pairs={{0,1},{1,0},{2,3},{3,2},{4,5},{5,4},{6,7},{7,6},{8,9},{9,8},{10,11... | collective-permute-start | bytes 884744 | tf_op jit(solution)/shard_map/ppermute | solution.py:17
  (9 other events, 54.7 us)

commit v4 on v3

--- a/solution.py
+++ b/solution.py
@@ -58,11 +58,13 @@
 
 def place_y(value, y):
     rows, width = value.shape
+    half = rows // 2
+    below, above = shift(value, "y", 1), shift(value, "y", -1)
+    far = [shift(above[:half], "y", -1), shift(below[half:], "y", 1)]
     whole = jnp.zeros((4 * rows, width), bf16)
-    moved = [(0, value)] + [(-step, shift(value, "y", step)) for step in (1, -1, 2)]
-    for step, block in moved:
-        whole = lax.dynamic_update_slice(whole, block, ((y + step) % 4 * rows, 0))
-    return whole
+    for step, start, block in ((0, 0, value), (3, 0, below), (1, 0, above), (2, 0, far[0]), (2, half, far[1])):
+        whole = lax.dynamic_update_slice(whole, block, ((y + step) % 4 * rows + start, 0))
+    return whole, below, above
 
 
 def gather_weight(blocks, xl, core, earlier):
@@ -72,7 +74,7 @@
     own_half = lax.dynamic_update_slice(own_half, blocks[:, None], (0, xl, 0, 0))
     for start, block in zip((0, 2), other):
         own_half = lax.dynamic_update_slice(own_half, block[:, None], (start, 1 - xl, 0, 0))
-    own_half = after(own_half.reshape(2 * count * rows, half), earlier)
+    own_half = after(own_half.reshape(2 * count * rows, half), *earlier)
     weight = jnp.zeros((2 * count * rows, 2 * half), bf16)
     weight = lax.dynamic_update_slice(weight, own_half, (0, core * half))
     return lax.dynamic_update_slice(weight, shift(own_half, "core", 1), (0, (1 - core) * half))
@@ -105,12 +107,10 @@
     xhat = centered * inverse_deviation
     normed_own = (xhat * final_norm_gain + final_norm_bias).astype(bf16)
 
-    weight_blocks, text_unit, normed_own = lax.optimization_barrier(
-        (weight_blocks, text_unit, normed_own)
-    )
-    text_same = place_y(text_unit, y)
-    weight = gather_weight(weight_blocks, xl, core, text_same)
-    normed = place_y(normed_own, y)
+    text_same = place_y(text_unit, y)[0]
+    normed, *neighbours = place_y(normed_own, y)
+    weight_blocks = after(weight_blocks, text_unit, normed_own)
+    weight = gather_weight(weight_blocks, xl, core, [text_same] + neighbours)
     text_other = shift(text_same, "core", 1)
     rows = normed.shape[0]
 
@@ -138,13 +138,14 @@
     head = dot(normed_block, mine, 0, 0) + shift(sent, "core", 1).astype(f32)
     part = block // 4
     head = head.astype(bf16).reshape(4, part, half)
+    head_sent = head
     head = lax.all_to_all(head, ("xl", "xh"), split_axis=0, concat_axis=0, tiled=True)
     head = jnp.sum(head.astype(f32), axis=0)
 
     grad_own = lax.dynamic_slice(grad_proj, (y * own, 0), (own, width))
     grad_normed = dot(grad_own, weight, 1, 1)
     vectors = jnp.stack([jnp.sum(grad_normed * xhat, axis=0), jnp.sum(grad_normed, axis=0)], 0)
-    vectors = jnp.sum(spread_to(vectors, ("y", "xl")), axis=0)
+    vectors = jnp.sum(spread_to(after(vectors, head_sent), ("y", "xl", "core")), axis=0)
 
     held = after((weights_same, weights_other, image_unit), head)
     text_part, text_theirs = (
@@ -186,10 +187,8 @@
     sent = payload(*unpack(jnp.sum(received, axis=0)))
     received = spread_to(sent, ("zl", "xh")).reshape(4, 2, lines, half + lanes)
     head_all = received[..., :half].transpose(1, 0, 2, 3).reshape(2 * part, half)
-    vector_all = jnp.sum(unpack(received.astype(f32))[1], axis=1).reshape(-1, lanes)
-    other_head, other_vector = shift(head_all, "core", 1), shift(vector_all, "core", 1)
-    head_all = halves(core, head_all, other_head, 1).astype(f32) / 64.0
-    vector_all = (vector_all + other_vector).reshape(2, width) / 64.0
+    vector_all = jnp.sum(unpack(received.astype(f32))[1], axis=1).reshape(2, width) / 64.0
+    head_all = halves(core, head_all, shift(head_all, "core", 1), 1).astype(f32) / 64.0
 
     return (
         returned[0].astype(f32),

time: 197 us -> 203 us (1.030)
  waiting for transfers between devices: 51.1 us -> 36.7 us
  local copies, waits for them, and re-layouts: 17.9 us -> 28.4 us
  blocking collectives: 0 us -> 9.74 us
  matrix products: 19.6 us -> 17.4 us
    all_to_all x0 -> x1, blocking collectives: none -> 9.74 us  [spread_to(): return lax.all_to_all(many, axes, split_axis=0, concat_axis=0, tiled=True)]
    ppermute x12 -> x13, starting transfers between devices: 40.5 us -> 47.4 us  [shift(): lax.ppermute(value, axis, [(i, (i + steps) % count) for i in range(count)])]
    ppermute x3, waiting for transfers between devices: 6.69 us -> 0.01 us  [swap(): return lax.ppermute(value, ('xl', 'core'), [(0, 0), (1, 2), (2, 1), (3, 3)])]
    all_to_all x4 -> x3, starting transfers between devices: 27.7 us -> 22.2 us  [spread_to(): return lax.all_to_all(many, axes, split_axis=0, concat_axis=0, tiled=True)]
    all_to_all x4 -> x3, waiting for transfers between devices: 19.9 us -> 14.9 us  [spread_to(): return lax.all_to_all(many, axes, split_axis=0, concat_axis=0, tiled=True)]
    unnamed x20 -> x36, local copies, waits for them, and re-layouts: 0.05 us -> 3.7 us
    slice x0 -> x5, local copies, waits for them, and re-layouts: none -> 3.33 us  [the longest x4 3.33 us: place_y(): far = [shift(above[:half], 'y', -1), shift(below[half:], 'y', 1)]]
    dynamic_update_slice x8, local copies, waits for them, and re-layouts: 5.26 us -> 7.85 us  [place_y(): lax.dynamic_update_slice(whole, block, ((y + step) % 4 * rows + start, 0))]
  transfers between devices with their start and end apart: 23 -> 23, of which waited for: 10 -> 7; matrix products, arithmetic and copies ran while one was open for 18% -> 20% of each run, Pallas kernels for 0% -> 0%
where the time goes in v4:
time: 203 us; the launch traced here: 202 us
  starting transfers between devices  97.3 us (48%)
  waiting for transfers between devices  36.7 us (18%)
  local copies, waits for them, and re-layouts  28.4 us (14%)
  matrix products  17.4 us (9%)
  blocking collectives  9.74 us (5%)
  other arithmetic  9.44 us (5%)
  between operations  2.67 us (1%)
    ppermute x13, starting transfers between devices, shift(): lax.ppermute(value, axis, [(i, (i + steps) % count) for i in range(count)])  47.4 us
    all_to_all x3, starting transfers between devices, spread_to(): return lax.all_to_all(many, axes, split_axis=0, concat_axis=0, tiled=True)  22.2 us
    dot_general x10, matrix products, dot(): lax.dot_general(a, b, (((da,), (db,)), ((), ())), preferred_element_type=...  17.4 us
    all_to_all x3, waiting for transfers between devices, spread_to(): return lax.all_to_all(many, axes, split_axis=0, concat_axis=0, tiled=True)  14.9 us
    ppermute x3, starting transfers between devices, swap(): return lax.ppermute(value, ('xl', 'core'), [(0, 0), (1, 2), (2, 1), (3, 3)])  11.4 us
    all_to_all x1, blocking collectives, spread_to(): return lax.all_to_all(many, axes, split_axis=0, concat_axis=0, tiled=True)  9.74 us
    all_to_all x1, waiting for transfers between devices, local(): lax.all_to_all(head, ('xl', 'xh'), split_axis=0, concat_axis=0, tiled=True)  8.05 us
    dynamic_update_slice x8, local copies, waits for them, and re-layouts, place_y(): lax.dynamic_update_slice(whole, block, ((y + step) % 4 * rows + start, 0))  7.85 us
  transfers between devices with their start and end apart: 23, of which 7 were waited for; matrix products, arithmetic and copies ran while one was open for 20% of the time, Pallas kernels for 0%

profile of v4, /device:TPU:1, one launch (start us, length us, event | category | flops | bytes accessed | tf_op | source)
XLA Modules:
  0.0 201.7 jit_solution(16253537339735605817)
XLA Ops:
  0.6 4.6 %collective-permute-start.5 = (bf16[128,1536]{1,0:T(8,128)(2,1)}, bf16[128,1536]{1,0:T(8,128)(2,1)S(1)}, u32[]{:S(2)}, u32[]{:S(2)}) collective-permute-start(bf16[128,1536]{1,0:T(8,128)(2,1)} %param.11), channel_id=1, source_target_pairs={{0,0},{1,64},{64,1},{65,65},{2,2},{3,66},{66,3},{67,67},{4,4},{5,6... | collective-permute-start | bytes 1179656 | tf_op jit(solution)/shard_map/ppermute | solution.py:29
  8.4 4.2 %all-to-all-start = ((bf16[4,192,768]{2,1,0:T(8,128)(2,1)}), bf16[4,192,768]{2,1,0:T(8,128)(2,1)S(1)}, u32[]{:S(2)}, u32[]{:S(2)}) async-start(bf16[4,192,768]{2,1,0:T(8,128)(2,1)} %broadcast_in_dim.22), calls=%async_computation | async-start | bytes 2359296 | tf_op jit(solution)/shard_map/all_to_all | solution.py:52
  14.9 3.4 %collective-permute-start.8 = (bf16[128,1536]{1,0:T(8,128)(2,1)S(1)}, bf16[128,1536]{1,0:T(8,128)(2,1)S(1)}, u32[]{:S(2)}, u32[]{:S(2)}) collective-permute-start(bf16[128,1536]{1,0:T(8,128)(2,1)S(1)} %get-tuple-element.36), channel_id=1, source_target_pairs={{0,128},{128,256},{256,384},{384,0},{1,129},{129,257},{257,385},{3... | collective-permute-start | bytes 1179656 | tf_op jit(solution)/shard_map/ppermute | solution.py:17
  18.3 3.1 %collective-permute-start.9 = (bf16[128,1536]{1,0:T(8,128)(2,1)S(1)}, bf16[128,1536]{1,0:T(8,128)(2,1)S(1)}, u32[]{:S(2)}, u32[]{:S(2)}) collective-permute-start(bf16[128,1536]{1,0:T(8,128)(2,1)S(1)} %get-tuple-element.36), channel_id=1, source_target_pairs={{0,384},{128,0},{256,128},{384,256},{1,385},{129,1},{257,129},{385... | collective-permute-start | bytes 1179656 | tf_op jit(solution)/shard_map/ppermute | solution.py:17
  24.5 4.4 %collective-permute-start.2 = (bf16[128,1536]{1,0:T(8,128)(2,1)S(1)}, bf16[128,1536]{1,0:T(8,128)(2,1)S(1)}, u32[]{:S(2)}, u32[]{:S(2)}) collective-permute-start(bf16[128,1536]{1,0:T(8,128)(2,1)S(1)} %get-tuple-element.38), channel_id=1, source_target_pairs={{0,384},{128,0},{256,128},{384,256},{1,385},{129,1},{257,129},{385... | collective-permute-start | bytes 1179656 | tf_op jit(solution)/shard_map/ppermute | solution.py:17
  28.8 4.2 %collective-permute-done.9 = bf16[128,1536]{1,0:T(8,128)(2,1)S(1)} collective-permute-done((bf16[128,1536]{1,0:T(8,128)(2,1)S(1)}, bf16[128,1536]{1,0:T(8,128)(2,1)S(1)}, u32[]{:S(2)}, u32[]{:S(2)}) %collective-permute-start.9) | collective-permute-done | bytes 393248 | tf_op jit(solution)/shard_map/ppermute | solution.py:17
  33.7 4.4 %collective-permute-start.10 = (bf16[64,1536]{1,0:T(8,128)(2,1)}, bf16[64,1536]{1,0:T(8,128)(2,1)S(1)}, u32[]{:S(2)}, u32[]{:S(2)}) collective-permute-start(bf16[64,1536]{1,0:T(8,128)(2,1)} %slice.91), channel_id=1, source_target_pairs={{0,384},{128,0},{256,128},{384,256},{1,385},{129,1},{257,129},{385... | collective-permute-start | bytes 589832 | tf_op jit(solution)/shard_map/ppermute | solution.py:17
  38.8 3.2 %collective-permute-start.11 = (bf16[64,1536]{1,0:T(8,128)(2,1)}, bf16[64,1536]{1,0:T(8,128)(2,1)}, u32[]{:S(2)}, u32[]{:S(2)}) collective-permute-start(bf16[64,1536]{1,0:T(8,128)(2,1)} %slice.92), channel_id=1, source_target_pairs={{0,128},{128,256},{256,384},{384,0},{1,129},{129,257},{257,385},{3... | collective-permute-start | bytes 589832 | tf_op jit(solution)/shard_map/ppermute | solution.py:17
  48.3 4.6 %collective-permute-start.7 = (bf16[2,192,768]{2,1,0:T(8,128)(2,1)S(1)}, bf16[2,192,768]{2,1,0:T(8,128)(2,1)S(1)}, u32[]{:S(2)}, u32[]{:S(2)}) collective-permute-start(bf16[2,192,768]{2,1,0:T(8,128)(2,1)S(1)} %get-tuple-element.39), channel_id=1, source_target_pairs={{0,66},{64,0},{2,64},{66,2},{1,67},{65,1},{3,65},{67,3},{4,70},{68... | collective-permute-start | bytes 1769480 | tf_op jit(solution)/shard_map/ppermute | solution.py:25
  56.9 6.8 %collective-permute-done.7 = bf16[2,192,768]{2,1,0:T(8,128)(2,1)S(1)} collective-permute-done((bf16[2,192,768]{2,1,0:T(8,128)(2,1)S(1)}, bf16[2,192,768]{2,1,0:T(8,128)(2,1)S(1)}, u32[]{:S(2)}, u32[]{:S(2)}) %collective-permute-start.7) | collective-permute-done | bytes 589856 | tf_op jit(solution)/shard_map/ppermute | solution.py:25
  66.0 6.3 %collective-permute-start.12 = (bf16[1536,768]{1,0:T(8,128)(2,1)}, bf16[1536,768]{1,0:T(8,128)(2,1)S(1)}, u32[]{:S(2)}, u32[]{:S(2)}) collective-permute-start(bf16[1536,768]{1,0:T(8,128)(2,1)} %bitcast.6), channel_id=1, source_target_pairs={{0,1},{1,0},{2,3},{3,2},{4,5},{5,4},{6,7},{7,6},{8,9},{9,8},{10,11... | collective-permute-start | bytes 7077896 | tf_op jit(solution)/shard_map/ppermute | solution.py:17
  74.7 4.6 %collective-permute-start.3 = (bf16[64,1536]{1,0:T(8,128)(2,1)S(1)}, bf16[64,1536]{1,0:T(8,128)(2,1)S(1)}, u32[]{:S(2)}, u32[]{:S(2)}) collective-permute-start(bf16[64,1536]{1,0:T(8,128)(2,1)S(1)} %slice.89), channel_id=1, source_target_pairs={{0,384},{128,0},{256,128},{384,256},{1,385},{129,1},{257,129},{385... | collective-permute-start | bytes 589832 | tf_op jit(solution)/shard_map/ppermute | solution.py:17
  106.0 3.0 %collective-permute-start.14 = (bf16[384,768]{1,0:T(8,128)(2,1)S(1)}, bf16[384,768]{1,0:T(8,128)(2,1)S(1)}, u32[]{:S(2)}, u32[]{:S(2)}) collective-permute-start(bf16[384,768]{1,0:T(8,128)(2,1)S(1)} %convolution_convert_fusion), channel_id=1, source_target_pairs={{0,1},{1,0},{2,3},{3,2},{4,5},{5,4},{6,7},{7,6},{8,9},{9,8},{10,11... | collective-permute-start | bytes 1769480 | tf_op jit(solution)/shard_map/ppermute | solution.py:17
  112.2 9.7 %all_to_all.30 = f32[16,2,1536]{2,1,0:T(2,128)S(1)} all-to-all(f32[16,2,1536]{2,1,0:T(2,128)S(1)} %broadcast_in_dim.26), channel_id=1, replica_groups=mesh['y'=4,'xl'=2,'zh'=4,'zl'=4,'xh'=2,'core'=2] {'y','xl','core'}, dimensions={0} | all-to-all | bytes 393216 | tf_op jit(solution)/shard_map/all_to_all | solution.py:52
  121.9 4.3 %all-to-all-start.1 = ((bf16[4,96,768]{2,1,0:T(8,128)(2,1)}), bf16[4,96,768]{2,1,0:T(8,128)(2,1)}, u32[]{:S(2)}, u32[]{:S(2)}) async-start(bf16[4,96,768]{2,1,0:T(8,128)(2,1)} %bitcast.52), calls=%async_computation.1 | async-start | bytes 1179648 | tf_op jit(solution)/shard_map/all_to_all | solution.py:142
  128.3 8.0 %all-to-all-done.1 = bf16[4,96,768]{2,1,0:T(8,128)(2,1)} async-done(((bf16[4,96,768]{2,1,0:T(8,128)(2,1)}), bf16[4,96,768]{2,1,0:T(8,128)(2,1)}, u32[]{:S(2)}, u32[]{:S(2)}) %all-to-all-start.1) | async-done | bytes 589856 | tf_op jit(solution)/shard_map/all_to_all | solution.py:142
  139.0 5.6 %all-to-all-start.3 = ((bf16[4,24,896]{2,1,0:T(8,128)(2,1)}), bf16[4,24,896]{2,1,0:T(8,128)(2,1)S(1)}, u32[]{:S(2)}, u32[]{:S(2)}) async-start(bf16[4,24,896]{2,1,0:T(8,128)(2,1)} %maximum_maximum_fusion), calls=%async_computation.3 | async-start | bytes 344064 | tf_op jit(solution)/shard_map/all_to_all | solution.py:173
  146.8 3.0 %collective-permute-start.15 = (f32[128,1536]{1,0:T(8,128)}, f32[128,1536]{1,0:T(8,128)}, u32[]{:S(2)}, u32[]{:S(2)}) collective-permute-start(f32[128,1536]{1,0:T(8,128)} %fusion.46), channel_id=1, source_target_pairs={{0,1},{1,0},{2,3},{3,2},{4,5},{5,4},{6,7},{7,6},{8,9},{9,8},{10,11... | collective-permute-start | bytes 2359304 | tf_op jit(solution)/shard_map/ppermute | solution.py:17
  150.6 12.3 %all-to-all-start.4 = ((bf16[4,24,896]{2,1,0:T(8,128)(2,1)}), bf16[4,24,896]{2,1,0:T(8,128)(2,1)S(1)}, u32[]{:S(2)}, u32[]{:S(2)}) async-start(bf16[4,24,896]{2,1,0:T(8,128)(2,1)} %broadcast_in_dim.28), calls=%async_computation.4 | async-start | bytes 344064 | tf_op jit(solution)/shard_map/all_to_all | solution.py:52
  165.8 4.8 %collective-permute-start.16 = (bf16[2,128,1536]{2,1,0:T(8,128)(2,1)S(1)}, bf16[2,128,1536]{2,1,0:T(8,128)(2,1)S(1)}, u32[]{:S(2)}, u32[]{:S(2)}) collective-permute-start(bf16[2,128,1536]{2,1,0:T(8,128)(2,1)S(1)} %pad_maximum_fusion), channel_id=1, source_target_pairs={{0,0},{1,64},{64,1},{65,65},{2,2},{3,66},{66,3},{67,67},{4,4},{5,6... | collective-permute-start | bytes 2359304 | tf_op jit(solution)/shard_map/ppermute | solution.py:29
  170.7 7.0 %all-to-all-done.4 = bf16[4,24,896]{2,1,0:T(8,128)(2,1)S(1)} async-done(((bf16[4,24,896]{2,1,0:T(8,128)(2,1)}), bf16[4,24,896]{2,1,0:T(8,128)(2,1)S(1)}, u32[]{:S(2)}, u32[]{:S(2)}) %all-to-all-start.4) | async-done | bytes 172064 | tf_op jit(solution)/shard_map/all_to_all | solution.py:52
  178.5 5.7 %all-to-all-start.5 = ((bf16[8,24,896]{2,1,0:T(8,128)(2,1)}), bf16[8,24,896]{2,1,0:T(8,128)(2,1)S(1)}, u32[]{:S(2)}, u32[]{:S(2)}) async-start(bf16[8,24,896]{2,1,0:T(8,128)(2,1)} %broadcast_in_dim.29), calls=%async_computation.5 | async-start | bytes 688128 | tf_op jit(solution)/shard_map/all_to_all | solution.py:52
  185.5 7.9 %all-to-all-done.5 = bf16[8,24,896]{2,1,0:T(8,128)(2,1)S(1)} async-done(((bf16[8,24,896]{2,1,0:T(8,128)(2,1)}), bf16[8,24,896]{2,1,0:T(8,128)(2,1)S(1)}, u32[]{:S(2)}, u32[]{:S(2)}) %all-to-all-start.5) | async-done | bytes 344096 | tf_op jit(solution)/shard_map/all_to_all | solution.py:52
  193.5 5.7 %collective-permute-start.17 = (bf16[192,768]{1,0:T(8,128)(2,1)S(1)}, bf16[192,768]{1,0:T(8,128)(2,1)S(1)}, u32[]{:S(2)}, u32[]{:S(2)}) collective-permute-start(bf16[192,768]{1,0:T(8,128)(2,1)S(1)} %bitcast.50), channel_id=1, source_target_pairs={{0,1},{1,0},{2,3},{3,2},{4,5},{5,4},{6,7},{7,6},{8,9},{9,8},{10,11... | collective-permute-start | bytes 884744 | tf_op jit(solution)/shard_map/ppermute | solution.py:17
  (143 shorter events, 68.0 us)
Async XLA Ops:
  0.6 11.9 %collective-permute-start.5 = (bf16[128,1536]{1,0:T(8,128)(2,1)}, bf16[128,1536]{1,0:T(8,128)(2,1)S(1)}, u32[]{:S(2)}, u32[]{:S(2)}) collective-permute-start(bf16[128,1536]{1,0:T(8,128)(2,1)} %param.11), channel_id=1, source_target_pairs={{0,0},{1,64},{64,1},{65,65},{2,2},{3,66},{66,3},{67,67},{4,4},{5,6... | collective-permute-start | bytes 1179656 | tf_op jit(solution)/shard_map/ppermute | solution.py:29
  5.3 16.1 %collective-permute-start = (bf16[128,1536]{1,0:T(8,128)(2,1)}, bf16[128,1536]{1,0:T(8,128)(2,1)S(1)}, u32[]{:S(2)}, u32[]{:S(2)}) collective-permute-start(bf16[128,1536]{1,0:T(8,128)(2,1)} %param.7), channel_id=1, source_target_pairs={{0,0},{1,64},{64,1},{65,65},{2,2},{3,66},{66,3},{67,67},{4,4},{5,6... | collective-permute-start | bytes 1179656 | tf_op jit(solution)/shard_map/ppermute | solution.py:29
  8.4 35.3 %all-to-all-start = ((bf16[4,192,768]{2,1,0:T(8,128)(2,1)}), bf16[4,192,768]{2,1,0:T(8,128)(2,1)S(1)}, u32[]{:S(2)}, u32[]{:S(2)}) async-start(bf16[4,192,768]{2,1,0:T(8,128)(2,1)} %broadcast_in_dim.22), calls=%async_computation | async-start | bytes 2359296 | tf_op jit(solution)/shard_map/all_to_all | solution.py:52
  14.9 23.2 %collective-permute-start.8 = (bf16[128,1536]{1,0:T(8,128)(2,1)S(1)}, bf16[128,1536]{1,0:T(8,128)(2,1)S(1)}, u32[]{:S(2)}, u32[]{:S(2)}) collective-permute-start(bf16[128,1536]{1,0:T(8,128)(2,1)S(1)} %get-tuple-element.36), channel_id=1, source_target_pairs={{0,128},{128,256},{256,384},{384,0},{1,129},{129,257},{257,385},{3... | collective-permute-start | bytes 1179656 | tf_op jit(solution)/shard_map/ppermute | solution.py:17
  18.3 14.7 %collective-permute-start.9 = (bf16[128,1536]{1,0:T(8,128)(2,1)S(1)}, bf16[128,1536]{1,0:T(8,128)(2,1)S(1)}, u32[]{:S(2)}, u32[]{:S(2)}) collective-permute-start(bf16[128,1536]{1,0:T(8,128)(2,1)S(1)} %get-tuple-element.36), channel_id=1, source_target_pairs={{0,384},{128,0},{256,128},{384,256},{1,385},{129,1},{257,129},{385... | collective-permute-start | bytes 1179656 | tf_op jit(solution)/shard_map/ppermute | solution.py:17
  21.8 87.2 %copy-start.11 = (f32[128]{0:T(128)}, f32[128]{0:T(128)S(1)}, u32[]{:S(2)}) copy-start(f32[128]{0:T(128)S(1)} %add_rsqrt_fusion.2) | copy-start | bytes 1540
  22.3 42.2 %collective-permute-start.1 = (bf16[128,1536]{1,0:T(8,128)(2,1)S(1)}, bf16[128,1536]{1,0:T(8,128)(2,1)S(1)}, u32[]{:S(2)}, u32[]{:S(2)}) collective-permute-start(bf16[128,1536]{1,0:T(8,128)(2,1)S(1)} %get-tuple-element.38), channel_id=1, source_target_pairs={{0,128},{128,256},{256,384},{384,0},{1,129},{129,257},{257,385},{3... | collective-permute-start | bytes 1179656 | tf_op jit(solution)/shard_map/ppermute | solution.py:17
  24.5 40.1 %collective-permute-start.2 = (bf16[128,1536]{1,0:T(8,128)(2,1)S(1)}, bf16[128,1536]{1,0:T(8,128)(2,1)S(1)}, u32[]{:S(2)}, u32[]{:S(2)}) collective-permute-start(bf16[128,1536]{1,0:T(8,128)(2,1)S(1)} %get-tuple-element.38), channel_id=1, source_target_pairs={{0,384},{128,0},{256,128},{384,256},{1,385},{129,1},{257,129},{385... | collective-permute-start | bytes 1179656 | tf_op jit(solution)/shard_map/ppermute | solution.py:17
  33.7 14.6 %collective-permute-start.10 = (bf16[64,1536]{1,0:T(8,128)(2,1)}, bf16[64,1536]{1,0:T(8,128)(2,1)S(1)}, u32[]{:S(2)}, u32[]{:S(2)}) collective-permute-start(bf16[64,1536]{1,0:T(8,128)(2,1)} %slice.91), channel_id=1, source_target_pairs={{0,384},{128,0},{256,128},{384,256},{1,385},{129,1},{257,129},{385... | collective-permute-start | bytes 589832 | tf_op jit(solution)/shard_map/ppermute | solution.py:17
  38.8 14.8 %collective-permute-start.11 = (bf16[64,1536]{1,0:T(8,128)(2,1)}, bf16[64,1536]{1,0:T(8,128)(2,1)}, u32[]{:S(2)}, u32[]{:S(2)}) collective-permute-start(bf16[64,1536]{1,0:T(8,128)(2,1)} %slice.92), channel_id=1, source_target_pairs={{0,128},{128,256},{256,384},{384,0},{1,129},{129,257},{257,385},{3... | collective-permute-start | bytes 589832 | tf_op jit(solution)/shard_map/ppermute | solution.py:17
  43.7 12.3 %collective-permute-start.6 = (bf16[2,192,768]{2,1,0:T(8,128)(2,1)S(1)}, bf16[2,192,768]{2,1,0:T(8,128)(2,1)S(1)}, u32[]{:S(2)}, u32[]{:S(2)}) collective-permute-start(bf16[2,192,768]{2,1,0:T(8,128)(2,1)S(1)} %get-tuple-element.40), channel_id=1, source_target_pairs={{0,64},{64,2},{2,66},{66,0},{1,65},{65,3},{3,67},{67,1},{4,68},{68... | collective-permute-start | bytes 1769480 | tf_op jit(solution)/shard_map/ppermute | solution.py:25
  48.3 15.4 %collective-permute-start.7 = (bf16[2,192,768]{2,1,0:T(8,128)(2,1)S(1)}, bf16[2,192,768]{2,1,0:T(8,128)(2,1)S(1)}, u32[]{:S(2)}, u32[]{:S(2)}) collective-permute-start(bf16[2,192,768]{2,1,0:T(8,128)(2,1)S(1)} %get-tuple-element.39), channel_id=1, source_target_pairs={{0,66},{64,0},{2,64},{66,2},{1,67},{65,1},{3,65},{67,3},{4,70},{68... | collective-permute-start | bytes 1769480 | tf_op jit(solution)/shard_map/ppermute | solution.py:25
  66.0 26.4 %collective-permute-start.12 = (bf16[1536,768]{1,0:T(8,128)(2,1)}, bf16[1536,768]{1,0:T(8,128)(2,1)S(1)}, u32[]{:S(2)}, u32[]{:S(2)}) collective-permute-start(bf16[1536,768]{1,0:T(8,128)(2,1)} %bitcast.6), channel_id=1, source_target_pairs={{0,1},{1,0},{2,3},{3,2},{4,5},{5,4},{6,7},{7,6},{8,9},{9,8},{10,11... | collective-permute-start | bytes 7077896 | tf_op jit(solution)/shard_map/ppermute | solution.py:17
  74.7 12.2 %collective-permute-start.3 = (bf16[64,1536]{1,0:T(8,128)(2,1)S(1)}, bf16[64,1536]{1,0:T(8,128)(2,1)S(1)}, u32[]{:S(2)}, u32[]{:S(2)}) collective-permute-start(bf16[64,1536]{1,0:T(8,128)(2,1)S(1)} %slice.89), channel_id=1, source_target_pairs={{0,384},{128,0},{256,128},{384,256},{1,385},{129,1},{257,129},{385... | collective-permute-start | bytes 589832 | tf_op jit(solution)/shard_map/ppermute | solution.py:17
  80.2 9.3 %collective-permute-start.4 = (bf16[64,1536]{1,0:T(8,128)(2,1)S(1)}, bf16[64,1536]{1,0:T(8,128)(2,1)S(1)}, u32[]{:S(2)}, u32[]{:S(2)}) collective-permute-start(bf16[64,1536]{1,0:T(8,128)(2,1)S(1)} %slice.90), channel_id=1, source_target_pairs={{0,128},{128,256},{256,384},{384,0},{1,129},{129,257},{257,385},{3... | collective-permute-start | bytes 589832 | tf_op jit(solution)/shard_map/ppermute | solution.py:17
  84.8 14.7 %collective-permute-start.13 = (bf16[512,1536]{1,0:T(8,128)(2,1)}, bf16[512,1536]{1,0:T(8,128)(2,1)S(1)}, u32[]{:S(2)}, u32[]{:S(2)}) collective-permute-start(bf16[512,1536]{1,0:T(8,128)(2,1)} %constant_dynamic-update-slice_fusion.2), channel_id=1, source_target_pairs={{0,1},{1,0},{2,3},{3,2},{4,5},{5,4},{6,7},{7,6},{8,9},{9,8},{10,11... | collective-permute-start | bytes 4718600 | tf_op jit(solution)/shard_map/ppermute | solution.py:17
  106.0 4.8 %collective-permute-start.14 = (bf16[384,768]{1,0:T(8,128)(2,1)S(1)}, bf16[384,768]{1,0:T(8,128)(2,1)S(1)}, u32[]{:S(2)}, u32[]{:S(2)}) collective-permute-start(bf16[384,768]{1,0:T(8,128)(2,1)S(1)} %convolution_convert_fusion), channel_id=1, source_target_pairs={{0,1},{1,0},{2,3},{3,2},{4,5},{5,4},{6,7},{7,6},{8,9},{9,8},{10,11... | collective-permute-start | bytes 1769480 | tf_op jit(solution)/shard_map/ppermute | solution.py:17
  121.9 14.4 %all-to-all-start.1 = ((bf16[4,96,768]{2,1,0:T(8,128)(2,1)}), bf16[4,96,768]{2,1,0:T(8,128)(2,1)}, u32[]{:S(2)}, u32[]{:S(2)}) async-start(bf16[4,96,768]{2,1,0:T(8,128)(2,1)} %bitcast.52), calls=%async_computation.1 | async-start | bytes 1179648 | tf_op jit(solution)/shard_map/all_to_all | solution.py:142
  139.0 10.8 %all-to-all-start.3 = ((bf16[4,24,896]{2,1,0:T(8,128)(2,1)}), bf16[4,24,896]{2,1,0:T(8,128)(2,1)S(1)}, u32[]{:S(2)}, u32[]{:S(2)}) async-start(bf16[4,24,896]{2,1,0:T(8,128)(2,1)} %maximum_maximum_fusion), calls=%async_computation.3 | async-start | bytes 344064 | tf_op jit(solution)/shard_map/all_to_all | solution.py:173
  146.8 16.1 %collective-permute-start.15 = (f32[128,1536]{1,0:T(8,128)}, f32[128,1536]{1,0:T(8,128)}, u32[]{:S(2)}, u32[]{:S(2)}) collective-permute-start(f32[128,1536]{1,0:T(8,128)} %fusion.46), channel_id=1, source_target_pairs={{0,1},{1,0},{2,3},{3,2},{4,5},{5,4},{6,7},{7,6},{8,9},{9,8},{10,11... | collective-permute-start | bytes 2359304 | tf_op jit(solution)/shard_map/ppermute | solution.py:17
  150.6 27.1 %all-to-all-start.4 = ((bf16[4,24,896]{2,1,0:T(8,128)(2,1)}), bf16[4,24,896]{2,1,0:T(8,128)(2,1)S(1)}, u32[]{:S(2)}, u32[]{:S(2)}) async-start(bf16[4,24,896]{2,1,0:T(8,128)(2,1)} %broadcast_in_dim.28), calls=%async_computation.4 | async-start | bytes 344064 | tf_op jit(solution)/shard_map/all_to_all | solution.py:52
  165.8 18.4 %collective-permute-start.16 = (bf16[2,128,1536]{2,1,0:T(8,128)(2,1)S(1)}, bf16[2,128,1536]{2,1,0:T(8,128)(2,1)S(1)}, u32[]{:S(2)}, u32[]{:S(2)}) collective-permute-start(bf16[2,128,1536]{2,1,0:T(8,128)(2,1)S(1)} %pad_maximum_fusion), channel_id=1, source_target_pairs={{0,0},{1,64},{64,1},{65,65},{2,2},{3,66},{66,3},{67,67},{4,4},{5,6... | collective-permute-start | bytes 2359304 | tf_op jit(solution)/shard_map/ppermute | solution.py:29
  178.5 14.9 %all-to-all-start.5 = ((bf16[8,24,896]{2,1,0:T(8,128)(2,1)}), bf16[8,24,896]{2,1,0:T(8,128)(2,1)S(1)}, u32[]{:S(2)}, u32[]{:S(2)}) async-start(bf16[8,24,896]{2,1,0:T(8,128)(2,1)} %broadcast_in_dim.29), calls=%async_computation.5 | async-start | bytes 688128 | tf_op jit(solution)/shard_map/all_to_all | solution.py:52
  193.5 7.0 %collective-permute-start.17 = (bf16[192,768]{1,0:T(8,128)(2,1)S(1)}, bf16[192,768]{1,0:T(8,128)(2,1)S(1)}, u32[]{:S(2)}, u32[]{:S(2)}) collective-permute-start(bf16[192,768]{1,0:T(8,128)(2,1)S(1)} %bitcast.50), channel_id=1, source_target_pairs={{0,1},{1,0},{2,3},{3,2},{4,5},{5,4},{6,7},{7,6},{8,9},{9,8},{10,11... | collective-permute-start | bytes 884744 | tf_op jit(solution)/shard_map/ppermute | solution.py:17
  (17 other events, 85.0 us)

commit v5 on v4

--- a/solution.py
+++ b/solution.py
@@ -56,28 +56,33 @@
     return lax.optimization_barrier((value,) + others)[0]
 
 
-def place_y(value, y):
-    rows, width = value.shape
-    half = rows // 2
-    below, above = shift(value, "y", 1), shift(value, "y", -1)
-    far = [shift(above[:half], "y", -1), shift(below[half:], "y", 1)]
-    whole = jnp.zeros((4 * rows, width), bf16)
-    for step, start, block in ((0, 0, value), (3, 0, below), (1, 0, above), (2, 0, far[0]), (2, half, far[1])):
-        whole = lax.dynamic_update_slice(whole, block, ((y + step) % 4 * rows + start, 0))
-    return whole, below, above
-
-
-def gather_weight(blocks, xl, core, earlier):
+def gather_weight(blocks, xl, core):
     count, rows, half = blocks.shape
     other = [shift_x(blocks[:2], 1), shift_x(blocks[2:], -1)]
     own_half = jnp.zeros((count, 2, rows, half), bf16)
     own_half = lax.dynamic_update_slice(own_half, blocks[:, None], (0, xl, 0, 0))
     for start, block in zip((0, 2), other):
         own_half = lax.dynamic_update_slice(own_half, block[:, None], (start, 1 - xl, 0, 0))
-    own_half = after(own_half.reshape(2 * count * rows, half), *earlier)
+    own_half = own_half.reshape(2 * count * rows, half)
     weight = jnp.zeros((2 * count * rows, 2 * half), bf16)
     weight = lax.dynamic_update_slice(weight, own_half, (0, core * half))
-    return lax.dynamic_update_slice(weight, shift(own_half, "core", 1), (0, (1 - core) * half))
+    weight = lax.dynamic_update_slice(weight, shift(own_half, "core", 1), (0, (1 - core) * half))
+    return weight, own_half
+
+
+def place_y(value, y, early, late):
+    arrays, rows, width = value.shape
+    moved = [(3, shift(value, "y", 1)), (1, shift(value, "y", -1)), (2, shift(value, "y", 2))]
+    moved[0] = (3, after(moved[0][1], early))
+    moved[1] = (1, after(moved[1][1], early))
+    moved[2] = (2, after(moved[2][1], late))
+    results = []
+    for index in range(arrays):
+        whole = jnp.zeros((4 * rows, width), bf16)
+        for step, blocks in [(0, value)] + moved:
+            whole = lax.dynamic_update_slice(whole, blocks[index], ((y + step) % 4 * rows, 0))
+        results.append(whole)
+    return results
 
 
 def local(
@@ -90,8 +95,7 @@
     half = width // 2
     block = width // 4
 
-    text_rows = swap(text_embed)
-    feature_rows = swap(image_features)
+    text_rows, feature_rows = swap(jnp.stack([text_embed, image_features], 0))
     weight_part = lax.dynamic_slice(head_weight, (0, core * half), (head_weight.shape[0], half))
     weight_blocks = spread_to(weight_part, "y")
 
@@ -107,10 +111,8 @@
     xhat = centered * inverse_deviation
     normed_own = (xhat * final_norm_gain + final_norm_bias).astype(bf16)
 
-    text_same = place_y(text_unit, y)[0]
-    normed, *neighbours = place_y(normed_own, y)
-    weight_blocks = after(weight_blocks, text_unit, normed_own)
-    weight = gather_weight(weight_blocks, xl, core, [text_same] + neighbours)
+    weight, own_half = gather_weight(after(weight_blocks, text_unit, normed_own), xl, core)
+    text_same, normed = place_y(jnp.stack([text_unit, normed_own], 0), y, own_half, weight)
     text_other = shift(text_same, "core", 1)
     rows = normed.shape[0]
 
@@ -137,15 +139,28 @@
     mine = lax.dynamic_slice(grad_proj, (0, core * half), (rows, half))
     head = dot(normed_block, mine, 0, 0) + shift(sent, "core", 1).astype(f32)
     part = block // 4
-    head = head.astype(bf16).reshape(4, part, half)
-    head_sent = head
-    head = lax.all_to_all(head, ("xl", "xh"), split_axis=0, concat_axis=0, tiled=True)
-    head = jnp.sum(head.astype(f32), axis=0)
+    lanes = 128
 
     grad_own = lax.dynamic_slice(grad_proj, (y * own, 0), (own, width))
     grad_normed = dot(grad_own, weight, 1, 1)
     vectors = jnp.stack([jnp.sum(grad_normed * xhat, axis=0), jnp.sum(grad_normed, axis=0)], 0)
-    vectors = jnp.sum(spread_to(after(vectors, head_sent), ("y", "xl", "core")), axis=0)
+
+    def payload(head_rows, vector):
+        lead, lines = head_rows.shape[:-2], head_rows.shape[-2]
+        high, low = (t.reshape(lead + (-1, lanes)) for t in split16(vector))
+        rest = jnp.zeros(lead + (lines - 2 * high.shape[-2], lanes), bf16)
+        side = jnp.concatenate([high, low, rest], -2)
+        return jnp.concatenate([head_rows.astype(bf16), side], -1)
+
+    def unpack(received, count):
+        side = received[..., half:]
+        vector = side[..., :count, :] + side[..., count : 2 * count, :]
+        return received[..., :half], vector
+
+    halved = jnp.broadcast_to(vectors.reshape(1, 2, width), (2, 2, width)).reshape(4, width)
+    sent = payload(head.reshape(4, part, half), halved)
+    received = lax.all_to_all(sent, ("xl", "xh"), split_axis=0, concat_axis=0, tiled=True)
+    head, vector = unpack(jnp.sum(received.astype(f32), axis=0), width // lanes)
 
     held = after((weights_same, weights_other, image_unit), head)
     text_part, text_theirs = (
@@ -153,25 +168,11 @@
     )
     grad_unit_text = text_part + shift(text_theirs, "core", 1)
 
-    lanes = 128
     lines = part // 4
-    count = 2 * width // 4 // lanes
-
-    def payload(head_rows, vector):
-        lead = vector.shape[:-1]
-        high, low = (t.reshape(lead + (-1, lanes)) for t in split16(vector))
-        rest = jnp.zeros(lead + (lines - 2 * count, lanes), bf16)
-        side = jnp.concatenate([high, low, rest], -2)
-        return jnp.concatenate([head_rows.astype(bf16), side], -1)
-
-    def unpack(received):
-        side = received[..., half:]
-        vector = side[..., :count, :] + side[..., count : 2 * count, :]
-        return received[..., :half], vector.reshape(vector.shape[:-2] + (-1,))
-
-    sent = payload(head.reshape(4, lines, half), vectors.reshape(4, 2 * width // 4))
+    count = width // 4 // lanes
+    sent = payload(head.reshape(4, lines, half), vector.reshape(4, width // 4))
     received = lax.all_to_all(sent, "zl", split_axis=0, concat_axis=0, tiled=True).astype(f32)
-    sent = payload(*unpack(jnp.sum(received, axis=0)))
+    sent = payload(*unpack(jnp.sum(received, axis=0), count))
 
     grad_unit_text, grad_normed = after((grad_unit_text, grad_normed), sent)
     grad_unit_text = scale * grad_unit_text
@@ -184,17 +185,18 @@
     returned = swap(jnp.stack([grad_features, grad_text], 0).astype(bf16))
 
     received = spread_to(sent, "zh").astype(f32)
-    sent = payload(*unpack(jnp.sum(received, axis=0)))
+    sent = payload(*unpack(jnp.sum(received, axis=0), count))
     received = spread_to(sent, ("zl", "xh")).reshape(4, 2, lines, half + lanes)
     head_all = received[..., :half].transpose(1, 0, 2, 3).reshape(2 * part, half)
-    vector_all = jnp.sum(unpack(received.astype(f32))[1], axis=1).reshape(2, width) / 64.0
+    vectors = unpack(received.astype(f32), count)[1].transpose(1, 0, 2, 3).reshape(2, width)
+    vectors = jnp.sum(spread_to(vectors, ("y", "core")), axis=0) / 64.0
     head_all = halves(core, head_all, shift(head_all, "core", 1), 1).astype(f32) / 64.0
 
     return (
         returned[0].astype(f32),
         returned[1].astype(f32),
-        vector_all[0],
-        vector_all[1],
+        vectors[0],
+        vectors[1],
         head_all,
     )
 

time: 203 us -> 214 us (1.054)
  waiting for transfers between devices: 36.7 us -> 76.3 us
  starting transfers between devices: 97.3 us -> 78.1 us
  blocking collectives: 9.74 us -> 0 us
  local copies, waits for them, and re-layouts: 28.4 us -> 21.6 us
  other arithmetic: 9.44 us -> 13.9 us
  matrix products: 17.4 us -> 20.4 us
    ppermute x13 -> x8, starting transfers between devices: 47.4 us -> 21.9 us  [shift(): lax.ppermute(value, axis, [(i, (i + steps) % count) for i in range(count)])]
    ppermute x13 -> x8, waiting for transfers between devices: 6.07 us -> 27.6 us  [shift(): lax.ppermute(value, axis, [(i, (i + steps) % count) for i in range(count)])]
    all_to_all x3 -> x4, waiting for transfers between devices: 14.9 us -> 26.5 us  [spread_to(): return lax.all_to_all(many, axes, split_axis=0, concat_axis=0, tiled=True)]
    all_to_all x1 -> x0, blocking collectives: 9.74 us -> none  [spread_to(): return lax.all_to_all(many, axes, split_axis=0, concat_axis=0, tiled=True)]
    all_to_all x3 -> x4, starting transfers between devices: 22.2 us -> 30.5 us  [spread_to(): return lax.all_to_all(many, axes, split_axis=0, concat_axis=0, tiled=True)]
    ppermute x3 -> x2, waiting for transfers between devices: 0.01 us -> 4.34 us  [swap(): return lax.ppermute(value, ('xl', 'core'), [(0, 0), (1, 2), (2, 1), (3, 3)])]
    dynamic_update_slice x8 -> x3, local copies, waits for them, and re-layouts: 7.85 us -> 3.54 us  [place_y(): lax.dynamic_update_slice(whole, blocks[index], ((y + step) % 4 * rows, 0))]
    unnamed x36 -> x32, local copies, waits for them, and re-layouts: 3.7 us -> 0.35 us
  transfers between devices with their start and end apart: 23 -> 18, of which waited for: 7 -> 12; matrix products, arithmetic and copies ran while one was open for 20% -> 16% of each run, Pallas kernels for 0% -> 0%
where the time goes in v5:
time: 214 us; the launch traced here: 213 us
  starting transfers between devices  78.1 us (36%)
  waiting for transfers between devices  76.3 us (36%)
  local copies, waits for them, and re-layouts  21.6 us (10%)
  matrix products  20.4 us (10%)
  other arithmetic  13.9 us (6%)
  between operations  2.66 us (1%)
    all_to_all x4, starting transfers between devices, spread_to(): return lax.all_to_all(many, axes, split_axis=0, concat_axis=0, tiled=True)  30.5 us
    ppermute x8, waiting for transfers between devices, shift(): lax.ppermute(value, axis, [(i, (i + steps) % count) for i in range(count)])  27.6 us
    all_to_all x4, waiting for transfers between devices, spread_to(): return lax.all_to_all(many, axes, split_axis=0, concat_axis=0, tiled=True)  26.5 us
    ppermute x8, starting transfers between devices, shift(): lax.ppermute(value, axis, [(i, (i + steps) % count) for i in range(count)])  21.9 us
    dot_general x10, matrix products, dot(): lax.dot_general(a, b, (((da,), (db,)), ((), ())), preferred_element_type=...  20.4 us
    ppermute x2, starting transfers between devices, swap(): return lax.ppermute(value, ('xl', 'core'), [(0, 0), (1, 2), (2, 1), (3, 3)])  9.23 us
    ppermute x2, waiting for transfers between devices, shift_x(): lax.ppermute(value, ('xl', 'xh'), [(index(i), index(i + steps)) for i in...  8.45 us
    all_to_all x1, waiting for transfers between devices, local(): lax.all_to_all(sent, ('xl', 'xh'), split_axis=0, concat_axis=0, tiled=True)  6.78 us
  transfers between devices with their start and end apart: 18, of which 12 were waited for; matrix products, arithmetic and copies ran while one was open for 16% of the time, Pallas kernels for 0%

profile of v5, /device:TPU:1, one launch (start us, length us, event | category | flops | bytes accessed | tf_op | source)
XLA Modules:
  0.0 213.0 jit_solution(4399378128783958229)
XLA Ops:
  1.9 4.5 %collective-permute-start = (bf16[2,128,1536]{2,1,0:T(8,128)(2,1)S(1)}, bf16[2,128,1536]{2,1,0:T(8,128)(2,1)S(1)}, u32[]{:S(2)}, u32[]{:S(2)}) collective-permute-start(bf16[2,128,1536]{2,1,0:T(8,128)(2,1)S(1)} %pad_maximum_fusion), channel_id=1, source_target_pairs={{0,0},{1,64},{64,1},{65,65},{2,2},{3,66},{66,3},{67,67},{4,4},{5,6... | collective-permute-start | bytes 2359304 | tf_op jit(solution)/shard_map/ppermute | solution.py:29
  7.6 4.2 %all-to-all-start = ((bf16[4,192,768]{2,1,0:T(8,128)(2,1)}), bf16[4,192,768]{2,1,0:T(8,128)(2,1)S(1)}, u32[]{:S(2)}, u32[]{:S(2)}) async-start(bf16[4,192,768]{2,1,0:T(8,128)(2,1)} %broadcast_in_dim.27), calls=%async_computation | async-start | bytes 2359296 | tf_op jit(solution)/shard_map/all_to_all | solution.py:52
  11.7 4.3 %collective-permute-done = bf16[2,128,1536]{2,1,0:T(8,128)(2,1)S(1)} collective-permute-done((bf16[2,128,1536]{2,1,0:T(8,128)(2,1)S(1)}, bf16[2,128,1536]{2,1,0:T(8,128)(2,1)S(1)}, u32[]{:S(2)}, u32[]{:S(2)}) %collective-permute-start) | collective-permute-done | bytes 786464 | tf_op jit(solution)/shard_map/ppermute | solution.py:29
  19.5 6.3 %all-to-all-done = bf16[4,192,768]{2,1,0:T(8,128)(2,1)S(1)} async-done(((bf16[4,192,768]{2,1,0:T(8,128)(2,1)}), bf16[4,192,768]{2,1,0:T(8,128)(2,1)S(1)}, u32[]{:S(2)}, u32[]{:S(2)}) %all-to-all-start) | async-done | bytes 1179680 | tf_op jit(solution)/shard_map/all_to_all | solution.py:52
  28.9 4.6 %collective-permute-start.3 = (bf16[2,192,768]{2,1,0:T(8,128)(2,1)}, bf16[2,192,768]{2,1,0:T(8,128)(2,1)S(1)}, u32[]{:S(2)}, u32[]{:S(2)}) collective-permute-start(bf16[2,192,768]{2,1,0:T(8,128)(2,1)} %get-tuple-element.48), channel_id=1, source_target_pairs={{0,66},{64,0},{2,64},{66,2},{1,67},{65,1},{3,65},{67,3},{4,70},{68... | collective-permute-start | bytes 1769480 | tf_op jit(solution)/shard_map/ppermute | solution.py:25
  36.2 5.7 %collective-permute-done.2 = bf16[2,192,768]{2,1,0:T(8,128)(2,1)} collective-permute-done((bf16[2,192,768]{2,1,0:T(8,128)(2,1)}, bf16[2,192,768]{2,1,0:T(8,128)(2,1)}, u32[]{:S(2)}, u32[]{:S(2)}) %collective-permute-start.2) | collective-permute-done | bytes 589856 | tf_op jit(solution)/shard_map/ppermute | solution.py:25
  43.8 2.7 %collective-permute-done.3 = bf16[2,192,768]{2,1,0:T(8,128)(2,1)S(1)} collective-permute-done((bf16[2,192,768]{2,1,0:T(8,128)(2,1)}, bf16[2,192,768]{2,1,0:T(8,128)(2,1)S(1)}, u32[]{:S(2)}, u32[]{:S(2)}) %collective-permute-start.3) | collective-permute-done | bytes 589856 | tf_op jit(solution)/shard_map/ppermute | solution.py:25
  47.4 4.1 %collective-permute-start.6 = (bf16[1536,768]{1,0:T(8,128)(2,1)}, bf16[1536,768]{1,0:T(8,128)(2,1)}, u32[]{:S(2)}, u32[]{:S(2)}) collective-permute-start(bf16[1536,768]{1,0:T(8,128)(2,1)} %bitcast.10), channel_id=1, source_target_pairs={{0,1},{1,0},{2,3},{3,2},{4,5},{5,4},{6,7},{7,6},{8,9},{9,8},{10,11... | collective-permute-start | bytes 7077896 | tf_op jit(solution)/shard_map/ppermute | solution.py:17
  54.2 4.3 %collective-permute-start.4 = (bf16[2,128,1536]{2,1,0:T(8,128)(2,1)S(1)}, bf16[2,128,1536]{2,1,0:T(8,128)(2,1)S(1)}, u32[]{:S(2)}, u32[]{:S(2)}) collective-permute-start(bf16[2,128,1536]{2,1,0:T(8,128)(2,1)S(1)} %pad_maximum_fusion.1), channel_id=1, source_target_pairs={{0,384},{128,0},{256,128},{384,256},{1,385},{129,1},{257,129},{385... | collective-permute-start | bytes 2359304 | tf_op jit(solution)/shard_map/ppermute | solution.py:17
  64.9 26.3 %collective-permute-done.1 = bf16[2,128,1536]{2,1,0:T(8,128)(2,1)} collective-permute-done((bf16[2,128,1536]{2,1,0:T(8,128)(2,1)S(1)}, bf16[2,128,1536]{2,1,0:T(8,128)(2,1)}, u32[]{:S(2)}, u32[]{:S(2)}) %collective-permute-start.1) | collective-permute-done | bytes 786464 | tf_op jit(solution)/shard_map/ppermute | solution.py:17
  97.3 4.1 %multiply_reduce_fusion.1 = (f32[512]{0:T(512)S(1)}, f32[512,1536]{1,0:T(8,128)S(1)}) fusion(bf16[512,1536]{1,0:T(8,128)(2,1)} %get-tuple-element.55, bf16[1536,1536]{1,0:T(8,128)(2,1)S(1)} %constant_dynamic-update-slice_fusion.1), kind=kOutput, calls=%fused_computation.5 | convolution fusion | flops 2417491456 | bytes 9439232 | tf_op jit(solution)/shard_map/dot_general | solution.py:41
  101.4 3.2 %collective-permute-start.7 = (bf16[512,1536]{1,0:T(8,128)(2,1)S(1)}, bf16[512,1536]{1,0:T(8,128)(2,1)S(1)}, u32[]{:S(2)}, u32[]{:S(2)}) collective-permute-start(bf16[512,1536]{1,0:T(8,128)(2,1)S(1)} %get-tuple-element.54), channel_id=1, source_target_pairs={{0,1},{1,0},{2,3},{3,2},{4,5},{5,4},{6,7},{7,6},{8,9},{9,8},{10,11... | collective-permute-start | bytes 4718600 | tf_op jit(solution)/shard_map/ppermute | solution.py:17
  110.6 2.6 %convolution_convert_fusion = bf16[384,768]{1,0:T(8,128)(2,1)} fusion(bf16[512,1536]{1,0:T(8,128)(2,1)S(1)} %subtract_convert_fusion, s32[]{:T(128)S(6)} %select_n.84, bf16[512,1536]{1,0:T(8,128)(2,1)} %get-tuple-element.55, s32[]{:T(128)S(6)} %select_n.87), kind=kOutput, calls=%fused_computation.10 | convolution fusion | flops 302284800 | bytes 1769480 | tf_op jit(solution)/shard_map/dot_general | solution.py:41
  121.1 4.4 %all-to-all-start.1 = ((bf16[4,96,896]{2,1,0:T(8,128)(2,1)}), bf16[4,96,896]{2,1,0:T(8,128)(2,1)}, u32[]{:S(2)}, u32[]{:S(2)}) async-start(bf16[4,96,896]{2,1,0:T(8,128)(2,1)} %maximum_maximum_fusion), calls=%async_computation.1 | async-start | bytes 1376256 | tf_op jit(solution)/shard_map/all_to_all | solution.py:162
  129.8 6.8 %all-to-all-done.1 = bf16[4,96,896]{2,1,0:T(8,128)(2,1)} async-done(((bf16[4,96,896]{2,1,0:T(8,128)(2,1)}), bf16[4,96,896]{2,1,0:T(8,128)(2,1)}, u32[]{:S(2)}, u32[]{:S(2)}) %all-to-all-start.1) | async-done | bytes 688160 | tf_op jit(solution)/shard_map/all_to_all | solution.py:162
  140.1 5.6 %all-to-all-start.2 = ((bf16[4,24,896]{2,1,0:T(8,128)(2,1)}), bf16[4,24,896]{2,1,0:T(8,128)(2,1)}, u32[]{:S(2)}, u32[]{:S(2)}) async-start(bf16[4,24,896]{2,1,0:T(8,128)(2,1)} %maximum_maximum_fusion.1), calls=%async_computation.2 | async-start | bytes 344064 | tf_op jit(solution)/shard_map/all_to_all | solution.py:174
  148.2 2.7 %all-to-all-done.2 = bf16[4,24,896]{2,1,0:T(8,128)(2,1)} async-done(((bf16[4,24,896]{2,1,0:T(8,128)(2,1)}), bf16[4,24,896]{2,1,0:T(8,128)(2,1)}, u32[]{:S(2)}, u32[]{:S(2)}) %all-to-all-start.2) | async-done | bytes 172064 | tf_op jit(solution)/shard_map/all_to_all | solution.py:174
  154.4 13.1 %all-to-all-start.3 = ((bf16[4,24,896]{2,1,0:T(8,128)(2,1)}), bf16[4,24,896]{2,1,0:T(8,128)(2,1)S(1)}, u32[]{:S(2)}, u32[]{:S(2)}) async-start(bf16[4,24,896]{2,1,0:T(8,128)(2,1)} %broadcast_in_dim.35), calls=%async_computation.3 | async-start | bytes 344064 | tf_op jit(solution)/shard_map/all_to_all | solution.py:52
  168.1 4.7 %collective-permute-start.10 = (bf16[2,128,1536]{2,1,0:T(8,128)(2,1)S(1)}, bf16[2,128,1536]{2,1,0:T(8,128)(2,1)S(1)}, u32[]{:S(2)}, u32[]{:S(2)}) collective-permute-start(bf16[2,128,1536]{2,1,0:T(8,128)(2,1)S(1)} %pad_maximum_fusion.2), channel_id=1, source_target_pairs={{0,0},{1,64},{64,1},{65,65},{2,2},{3,66},{66,3},{67,67},{4,4},{5,6... | collective-permute-start | bytes 2359304 | tf_op jit(solution)/shard_map/ppermute | solution.py:29
  172.9 9.4 %all-to-all-done.3 = bf16[4,24,896]{2,1,0:T(8,128)(2,1)S(1)} async-done(((bf16[4,24,896]{2,1,0:T(8,128)(2,1)}), bf16[4,24,896]{2,1,0:T(8,128)(2,1)S(1)}, u32[]{:S(2)}, u32[]{:S(2)}) %all-to-all-start.3) | async-done | bytes 172064 | tf_op jit(solution)/shard_map/all_to_all | solution.py:52
  183.1 3.4 %all-to-all-start.4 = ((bf16[8,24,896]{2,1,0:T(8,128)(2,1)}), bf16[8,24,896]{2,1,0:T(8,128)(2,1)S(1)}, u32[]{:S(2)}, u32[]{:S(2)}) async-start(bf16[8,24,896]{2,1,0:T(8,128)(2,1)} %broadcast_in_dim.72), calls=%async_computation.4 | async-start | bytes 688128 | tf_op jit(solution)/shard_map/all_to_all | solution.py:52
  187.8 7.8 %all-to-all-done.4 = bf16[8,24,896]{2,1,0:T(8,128)(2,1)S(1)} async-done(((bf16[8,24,896]{2,1,0:T(8,128)(2,1)}), bf16[8,24,896]{2,1,0:T(8,128)(2,1)S(1)}, u32[]{:S(2)}, u32[]{:S(2)}) %all-to-all-start.4) | async-done | bytes 344096 | tf_op jit(solution)/shard_map/all_to_all | solution.py:52
  196.4 9.7 %all-to-all-start.5 = ((f32[8,2,1536]{2,1,0:T(2,128)}), f32[8,2,1536]{2,1,0:T(2,128)S(1)}, u32[]{:S(2)}, u32[]{:S(2)}) async-start(f32[8,2,1536]{2,1,0:T(2,128)} %broadcast_in_dim.74), calls=%async_computation.5 | async-start | bytes 196608 | tf_op jit(solution)/shard_map/all_to_all | solution.py:52
  208.2 3.0 %all-to-all-done.5 = f32[8,2,1536]{2,1,0:T(2,128)S(1)} async-done(((f32[8,2,1536]{2,1,0:T(2,128)}), f32[8,2,1536]{2,1,0:T(2,128)S(1)}, u32[]{:S(2)}, u32[]{:S(2)}) %all-to-all-start.5) | async-done | bytes 98336 | tf_op jit(solution)/shard_map/all_to_all | solution.py:52
  (127 shorter events, 62.6 us)
Async XLA Ops:
  1.9 14.2 %collective-permute-start = (bf16[2,128,1536]{2,1,0:T(8,128)(2,1)S(1)}, bf16[2,128,1536]{2,1,0:T(8,128)(2,1)S(1)}, u32[]{:S(2)}, u32[]{:S(2)}) collective-permute-start(bf16[2,128,1536]{2,1,0:T(8,128)(2,1)S(1)} %pad_maximum_fusion), channel_id=1, source_target_pairs={{0,0},{1,64},{64,1},{65,65},{2,2},{3,66},{66,3},{67,67},{4,4},{5,6... | collective-permute-start | bytes 2359304 | tf_op jit(solution)/shard_map/ppermute | solution.py:29
  7.6 18.3 %all-to-all-start = ((bf16[4,192,768]{2,1,0:T(8,128)(2,1)}), bf16[4,192,768]{2,1,0:T(8,128)(2,1)S(1)}, u32[]{:S(2)}, u32[]{:S(2)}) async-start(bf16[4,192,768]{2,1,0:T(8,128)(2,1)} %broadcast_in_dim.27), calls=%async_computation | async-start | bytes 2359296 | tf_op jit(solution)/shard_map/all_to_all | solution.py:52
  16.2 99.2 %copy-start.10 = (f32[128]{0:T(128)}, f32[128]{0:T(128)S(1)}, u32[]{:S(2)}) copy-start(f32[128]{0:T(128)S(1)} %broadcast_multiply_fusion.3) | copy-start | bytes 1540
  16.5 35.0 %copy-start.12 = (f32[128]{0:T(128)}, f32[128]{0:T(128)S(1)}, u32[]{:S(2)}) copy-start(f32[128]{0:T(128)S(1)} %get-tuple-element.67) | copy-start | bytes 1540
  27.0 14.9 %collective-permute-start.2 = (bf16[2,192,768]{2,1,0:T(8,128)(2,1)}, bf16[2,192,768]{2,1,0:T(8,128)(2,1)}, u32[]{:S(2)}, u32[]{:S(2)}) collective-permute-start(bf16[2,192,768]{2,1,0:T(8,128)(2,1)} %get-tuple-element.49), channel_id=1, source_target_pairs={{0,64},{64,2},{2,66},{66,0},{1,65},{65,3},{3,67},{67,1},{4,68},{68... | collective-permute-start | bytes 1769480 | tf_op jit(solution)/shard_map/ppermute | solution.py:25
  28.9 17.7 %collective-permute-start.3 = (bf16[2,192,768]{2,1,0:T(8,128)(2,1)}, bf16[2,192,768]{2,1,0:T(8,128)(2,1)S(1)}, u32[]{:S(2)}, u32[]{:S(2)}) collective-permute-start(bf16[2,192,768]{2,1,0:T(8,128)(2,1)} %get-tuple-element.48), channel_id=1, source_target_pairs={{0,66},{64,0},{2,64},{66,2},{1,67},{65,1},{3,65},{67,3},{4,70},{68... | collective-permute-start | bytes 1769480 | tf_op jit(solution)/shard_map/ppermute | solution.py:25
  47.4 47.2 %collective-permute-start.6 = (bf16[1536,768]{1,0:T(8,128)(2,1)}, bf16[1536,768]{1,0:T(8,128)(2,1)}, u32[]{:S(2)}, u32[]{:S(2)}) collective-permute-start(bf16[1536,768]{1,0:T(8,128)(2,1)} %bitcast.10), channel_id=1, source_target_pairs={{0,1},{1,0},{2,3},{3,2},{4,5},{5,4},{6,7},{7,6},{8,9},{9,8},{10,11... | collective-permute-start | bytes 7077896 | tf_op jit(solution)/shard_map/ppermute | solution.py:17
  52.0 39.2 %collective-permute-start.1 = (bf16[2,128,1536]{2,1,0:T(8,128)(2,1)S(1)}, bf16[2,128,1536]{2,1,0:T(8,128)(2,1)}, u32[]{:S(2)}, u32[]{:S(2)}) collective-permute-start(bf16[2,128,1536]{2,1,0:T(8,128)(2,1)S(1)} %pad_maximum_fusion.1), channel_id=1, source_target_pairs={{0,128},{128,256},{256,384},{384,0},{1,129},{129,257},{257,385},{3... | collective-permute-start | bytes 2359304 | tf_op jit(solution)/shard_map/ppermute | solution.py:17
  54.2 37.6 %collective-permute-start.4 = (bf16[2,128,1536]{2,1,0:T(8,128)(2,1)S(1)}, bf16[2,128,1536]{2,1,0:T(8,128)(2,1)S(1)}, u32[]{:S(2)}, u32[]{:S(2)}) collective-permute-start(bf16[2,128,1536]{2,1,0:T(8,128)(2,1)S(1)} %pad_maximum_fusion.1), channel_id=1, source_target_pairs={{0,384},{128,0},{256,128},{384,256},{1,385},{129,1},{257,129},{385... | collective-permute-start | bytes 2359304 | tf_op jit(solution)/shard_map/ppermute | solution.py:17
  60.6 35.9 %collective-permute-start.5 = (bf16[2,128,1536]{2,1,0:T(8,128)(2,1)S(1)}, bf16[2,128,1536]{2,1,0:T(8,128)(2,1)S(1)}, u32[]{:S(2)}, u32[]{:S(2)}) collective-permute-start(bf16[2,128,1536]{2,1,0:T(8,128)(2,1)S(1)} %pad_maximum_fusion.1), channel_id=1, source_target_pairs={{0,256},{128,384},{256,0},{384,128},{1,257},{129,385},{257,1},{385... | collective-permute-start | bytes 2359304 | tf_op jit(solution)/shard_map/ppermute | solution.py:17
  62.8 29.0 %copy-start.4 = (bf16[512,1536]{1,0:T(8,128)(2,1)S(1)}, bf16[512,1536]{1,0:T(8,128)(2,1)}, u32[]{:S(2)}) copy-start(bf16[512,1536]{1,0:T(8,128)(2,1)} %copy-done.3) | copy-start | bytes 4718596
  101.4 6.2 %collective-permute-start.7 = (bf16[512,1536]{1,0:T(8,128)(2,1)S(1)}, bf16[512,1536]{1,0:T(8,128)(2,1)S(1)}, u32[]{:S(2)}, u32[]{:S(2)}) collective-permute-start(bf16[512,1536]{1,0:T(8,128)(2,1)S(1)} %get-tuple-element.54), channel_id=1, source_target_pairs={{0,1},{1,0},{2,3},{3,2},{4,5},{5,4},{6,7},{7,6},{8,9},{9,8},{10,11... | collective-permute-start | bytes 4718600 | tf_op jit(solution)/shard_map/ppermute | solution.py:17
  113.2 5.0 %collective-permute-start.8 = (bf16[384,768]{1,0:T(8,128)(2,1)}, bf16[384,768]{1,0:T(8,128)(2,1)}, u32[]{:S(2)}, u32[]{:S(2)}) collective-permute-start(bf16[384,768]{1,0:T(8,128)(2,1)} %convolution_convert_fusion), channel_id=1, source_target_pairs={{0,1},{1,0},{2,3},{3,2},{4,5},{5,4},{6,7},{7,6},{8,9},{9,8},{10,11... | collective-permute-start | bytes 1769480 | tf_op jit(solution)/shard_map/ppermute | solution.py:17
  121.1 15.4 %all-to-all-start.1 = ((bf16[4,96,896]{2,1,0:T(8,128)(2,1)}), bf16[4,96,896]{2,1,0:T(8,128)(2,1)}, u32[]{:S(2)}, u32[]{:S(2)}) async-start(bf16[4,96,896]{2,1,0:T(8,128)(2,1)} %maximum_maximum_fusion), calls=%async_computation.1 | async-start | bytes 1376256 | tf_op jit(solution)/shard_map/all_to_all | solution.py:162
  127.7 18.0 %collective-permute-start.9 = (f32[128,1536]{1,0:T(8,128)}, f32[128,1536]{1,0:T(8,128)}, u32[]{:S(2)}, u32[]{:S(2)}) collective-permute-start(f32[128,1536]{1,0:T(8,128)} %fusion.58), channel_id=1, source_target_pairs={{0,1},{1,0},{2,3},{3,2},{4,5},{5,4},{6,7},{7,6},{8,9},{9,8},{10,11... | collective-permute-start | bytes 2359304 | tf_op jit(solution)/shard_map/ppermute | solution.py:17
  140.1 10.7 %all-to-all-start.2 = ((bf16[4,24,896]{2,1,0:T(8,128)(2,1)}), bf16[4,24,896]{2,1,0:T(8,128)(2,1)}, u32[]{:S(2)}, u32[]{:S(2)}) async-start(bf16[4,24,896]{2,1,0:T(8,128)(2,1)} %maximum_maximum_fusion.1), calls=%async_computation.2 | async-start | bytes 344064 | tf_op jit(solution)/shard_map/all_to_all | solution.py:174
  151.8 15.8 %copy-start.1 = (f32[128,1536]{1,0:T(8,128)S(1)}, f32[128,1536]{1,0:T(8,128)}, u32[]{:S(2)}) copy-start(f32[128,1536]{1,0:T(8,128)} %convolution_add_fusion.1) | copy-start | bytes 2359300
  151.8 15.8 %copy-start.2 = (f32[128,1536]{1,0:T(8,128)S(1)}, f32[128,1536]{1,0:T(8,128)}, u32[]{:S(2)}) copy-start(f32[128,1536]{1,0:T(8,128)} %get-tuple-element.25) | copy-start | bytes 2359300
  151.8 15.8 %copy-start.13 = (f32[128]{0:T(128)S(1)}, f32[128]{0:T(128)}, u32[]{:S(2)}) copy-start(f32[128]{0:T(128)} %copy-done.12) | copy-start | bytes 1540
  154.4 27.8 %all-to-all-start.3 = ((bf16[4,24,896]{2,1,0:T(8,128)(2,1)}), bf16[4,24,896]{2,1,0:T(8,128)(2,1)S(1)}, u32[]{:S(2)}, u32[]{:S(2)}) async-start(bf16[4,24,896]{2,1,0:T(8,128)(2,1)} %broadcast_in_dim.35), calls=%async_computation.3 | async-start | bytes 344064 | tf_op jit(solution)/shard_map/all_to_all | solution.py:52
  168.1 18.4 %collective-permute-start.10 = (bf16[2,128,1536]{2,1,0:T(8,128)(2,1)S(1)}, bf16[2,128,1536]{2,1,0:T(8,128)(2,1)S(1)}, u32[]{:S(2)}, u32[]{:S(2)}) collective-permute-start(bf16[2,128,1536]{2,1,0:T(8,128)(2,1)S(1)} %pad_maximum_fusion.2), channel_id=1, source_target_pairs={{0,0},{1,64},{64,1},{65,65},{2,2},{3,66},{66,3},{67,67},{4,4},{5,6... | collective-permute-start | bytes 2359304 | tf_op jit(solution)/shard_map/ppermute | solution.py:29
  183.1 12.6 %all-to-all-start.4 = ((bf16[8,24,896]{2,1,0:T(8,128)(2,1)}), bf16[8,24,896]{2,1,0:T(8,128)(2,1)S(1)}, u32[]{:S(2)}, u32[]{:S(2)}) async-start(bf16[8,24,896]{2,1,0:T(8,128)(2,1)} %broadcast_in_dim.72), calls=%async_computation.4 | async-start | bytes 688128 | tf_op jit(solution)/shard_map/all_to_all | solution.py:52
  196.4 14.7 %all-to-all-start.5 = ((f32[8,2,1536]{2,1,0:T(2,128)}), f32[8,2,1536]{2,1,0:T(2,128)S(1)}, u32[]{:S(2)}, u32[]{:S(2)}) async-start(f32[8,2,1536]{2,1,0:T(2,128)} %broadcast_in_dim.74), calls=%async_computation.5 | async-start | bytes 196608 | tf_op jit(solution)/shard_map/all_to_all | solution.py:52
  206.2 5.6 %collective-permute-start.11 = (bf16[192,768]{1,0:T(8,128)(2,1)S(1)}, bf16[192,768]{1,0:T(8,128)(2,1)S(1)}, u32[]{:S(2)}, u32[]{:S(2)}) collective-permute-start(bf16[192,768]{1,0:T(8,128)(2,1)S(1)} %bitcast.124), channel_id=1, source_target_pairs={{0,1},{1,0},{2,3},{3,2},{4,5},{5,4},{6,7},{7,6},{8,9},{9,8},{10,11... | collective-permute-start | bytes 884744 | tf_op jit(solution)/shard_map/ppermute | solution.py:17
  (10 other events, 35.3 us)

commit v6 on v5

--- a/solution.py
+++ b/solution.py
@@ -56,33 +56,34 @@
     return lax.optimization_barrier((value,) + others)[0]
 
 
-def gather_weight(blocks, xl, core):
+def gather_weight(blocks, xl, core, earlier):
     count, rows, half = blocks.shape
     other = [shift_x(blocks[:2], 1), shift_x(blocks[2:], -1)]
     own_half = jnp.zeros((count, 2, rows, half), bf16)
     own_half = lax.dynamic_update_slice(own_half, blocks[:, None], (0, xl, 0, 0))
     for start, block in zip((0, 2), other):
         own_half = lax.dynamic_update_slice(own_half, block[:, None], (start, 1 - xl, 0, 0))
-    own_half = own_half.reshape(2 * count * rows, half)
+    own_half = after(own_half.reshape(2 * count * rows, half), *earlier)
     weight = jnp.zeros((2 * count * rows, 2 * half), bf16)
     weight = lax.dynamic_update_slice(weight, own_half, (0, core * half))
     weight = lax.dynamic_update_slice(weight, shift(own_half, "core", 1), (0, (1 - core) * half))
-    return weight, own_half
-
-
-def place_y(value, y, early, late):
-    arrays, rows, width = value.shape
-    moved = [(3, shift(value, "y", 1)), (1, shift(value, "y", -1)), (2, shift(value, "y", 2))]
-    moved[0] = (3, after(moved[0][1], early))
-    moved[1] = (1, after(moved[1][1], early))
-    moved[2] = (2, after(moved[2][1], late))
-    results = []
-    for index in range(arrays):
-        whole = jnp.zeros((4 * rows, width), bf16)
-        for step, blocks in [(0, value)] + moved:
-            whole = lax.dynamic_update_slice(whole, blocks[index], ((y + step) % 4 * rows, 0))
-        results.append(whole)
-    return results
+    return weight
+
+
+def placed(blocks):
+    rows, width = blocks[0].shape
+    whole = lax.optimization_barrier(jnp.zeros((len(blocks) * rows, width), blocks[0].dtype))
+    for index, block in enumerate(blocks):
+        whole = lax.dynamic_update_slice(whole, block, (index * rows, 0))
+    return whole
+
+
+def standardize(block):
+    values = block.astype(f32)
+    centre = jnp.mean(values, axis=1, keepdims=True)
+    centered = values - centre
+    spread = jnp.mean(centered * centered, axis=1, keepdims=True)
+    return centre, lax.rsqrt(spread + epsilon)
 
 
 def local(
@@ -103,16 +104,19 @@
     inv_text = lax.rsqrt(jnp.sum(text_values * text_values, axis=1, keepdims=True) + epsilon)
     text_unit = (text_values * inv_text).astype(bf16)
 
-    values = feature_rows.astype(f32)
-    centre = jnp.mean(values, axis=1, keepdims=True)
-    centered = values - centre
-    spread = jnp.mean(centered * centered, axis=1, keepdims=True)
-    inverse_deviation = lax.rsqrt(spread + epsilon)
-    xhat = centered * inverse_deviation
-    normed_own = (xhat * final_norm_gain + final_norm_bias).astype(bf16)
-
-    weight, own_half = gather_weight(after(weight_blocks, text_unit, normed_own), xl, core)
-    text_same, normed = place_y(jnp.stack([text_unit, normed_own], 0), y, own_half, weight)
+    pair = jnp.stack([text_unit, feature_rows], 0)
+    below, above = shift(pair, "y", 1), shift(pair, "y", -1)
+    weight = gather_weight(weight_blocks, xl, core, [below, above])
+    text_far, feature_far = shift(above[0], "y", -1), shift(below[1], "y", 1)
+    text_same = placed([text_unit, below[0], above[0], text_far])
+    raw = [feature_rows, below[1], above[1], feature_far]
+    stats = [standardize(block) for block in raw]
+    normed = placed(
+        [
+            ((block.astype(f32) - centre) * inverse * final_norm_gain + final_norm_bias).astype(bf16)
+            for block, (centre, inverse) in zip(raw, stats)
+        ]
+    )
     text_other = shift(text_same, "core", 1)
     rows = normed.shape[0]
 
@@ -141,9 +145,12 @@
     part = block // 4
     lanes = 128
 
-    grad_own = lax.dynamic_slice(grad_proj, (y * own, 0), (own, width))
-    grad_normed = dot(grad_own, weight, 1, 1)
+    grad_normed = dot(grad_proj, weight, 1, 1)
+    centre = jnp.concatenate([part[0] for part in stats], 0)
+    inverse_deviation = jnp.concatenate([part[1] for part in stats], 0)
+    xhat = (placed(raw).astype(f32) - centre) * inverse_deviation
     vectors = jnp.stack([jnp.sum(grad_normed * xhat, axis=0), jnp.sum(grad_normed, axis=0)], 0)
+    xhat, grad_normed, inverse_deviation = xhat[:own], grad_normed[:own], inverse_deviation[:own]
 
     def payload(head_rows, vector):
         lead, lines = head_rows.shape[:-2], head_rows.shape[-2]
@@ -164,7 +171,7 @@
 
     held = after((weights_same, weights_other, image_unit), head)
     text_part, text_theirs = (
-        dot(lax.dynamic_slice(w, (0, y * own), (rows, own)), held[2], 0, 0) for w in held[:2]
+        dot(w[:, :own], held[2], 0, 0) for w in held[:2]
     )
     grad_unit_text = text_part + shift(text_theirs, "core", 1)
 
@@ -189,8 +196,11 @@
     received = spread_to(sent, ("zl", "xh")).reshape(4, 2, lines, half + lanes)
     head_all = received[..., :half].transpose(1, 0, 2, 3).reshape(2 * part, half)
     vectors = unpack(received.astype(f32), count)[1].transpose(1, 0, 2, 3).reshape(2, width)
-    vectors = jnp.sum(spread_to(vectors, ("y", "core")), axis=0) / 64.0
-    head_all = halves(core, head_all, shift(head_all, "core", 1), 1).astype(f32) / 64.0
+    sent = jnp.concatenate([head_all, *(t.reshape(-1, half) for t in split16(vectors))], 0)
+    received = shift(sent, "core", 1)
+    head_all = halves(core, head_all, received[: 2 * part], 1).astype(f32) / 64.0
+    high, low = jnp.split(received[2 * part :].astype(f32), 2, 0)
+    vectors = (vectors + (high + low).reshape(2, width)) / 64.0
 
     return (
         returned[0].astype(f32),

time: 214 us -> 196 us (0.916)
  waiting for transfers between devices: 76.3 us -> 33.1 us
  other arithmetic: 13.9 us -> 31.8 us
  starting transfers between devices: 78.1 us -> 85 us
  local copies, waits for them, and re-layouts: 21.6 us -> 17.3 us
  matrix products: 20.4 us -> 23.8 us
    ppermute x8 -> x9, waiting for transfers between devices: 27.6 us -> 3.33 us  [shift(): lax.ppermute(value, axis, [(i, (i + steps) % count) for i in range(count)])]
    all_to_all x4 -> x3, waiting for transfers between devices: 26.5 us -> 11.5 us  [spread_to(): return lax.all_to_all(many, axes, split_axis=0, concat_axis=0, tiled=True)]
    ppermute x8 -> x9, starting transfers between devices: 21.9 us -> 34.5 us  [shift(): lax.ppermute(value, axis, [(i, (i + steps) % count) for i in range(count)])]
    all_to_all x4 -> x3, starting transfers between devices: 30.5 us -> 22.6 us  [spread_to(): return lax.all_to_all(many, axes, split_axis=0, concat_axis=0, tiled=True)]
    reduce_sum x2 -> x8, other arithmetic: 0.18 us -> 7.77 us  [the longest x4 3.01 us: standardize(): spread = jnp.mean(centered * centered, axis=1, keepdims=True)]
    dynamic_update_slice x2 -> x5, other arithmetic: 1.21 us -> 7.67 us  [placed(): whole = lax.dynamic_update_slice(whole, block, (index * rows, 0))]
    unnamed x32 -> x30, local copies, waits for them, and re-layouts: 0.35 us -> 3.77 us
    dot_general x10, matrix products: 20.4 us -> 23.8 us  [dot(): lax.dot_general(a, b, (((da,), (db,)), ((), ())), preferred_element_type=...]
  transfers between devices with their start and end apart: 18 -> 18, of which waited for: 12 -> 8; matrix products, arithmetic and copies ran while one was open for 16% -> 24% of each run, Pallas kernels for 0% -> 0%
where the time goes in v6:
time: 196 us; the launch traced here: 194 us
  starting transfers between devices  85 us (43%)
  waiting for transfers between devices  33.1 us (17%)
  other arithmetic  31.8 us (16%)
  matrix products  23.8 us (12%)
  local copies, waits for them, and re-layouts  17.3 us (9%)
  between operations  2.72 us (1%)
    ppermute x9, starting transfers between devices, shift(): lax.ppermute(value, axis, [(i, (i + steps) % count) for i in range(count)])  34.5 us
    dot_general x10, matrix products, dot(): lax.dot_general(a, b, (((da,), (db,)), ((), ())), preferred_element_type=...  23.8 us
    all_to_all x3, starting transfers between devices, spread_to(): return lax.all_to_all(many, axes, split_axis=0, concat_axis=0, tiled=True)  22.6 us
    all_to_all x3, waiting for transfers between devices, spread_to(): return lax.all_to_all(many, axes, split_axis=0, concat_axis=0, tiled=True)  11.5 us
    ppermute x2, starting transfers between devices, swap(): return lax.ppermute(value, ('xl', 'core'), [(0, 0), (1, 2), (2, 1), (3, 3)])  11 us
    ppermute x2, waiting for transfers between devices, shift_x(): lax.ppermute(value, ('xl', 'xh'), [(index(i), index(i + steps)) for i in...  9.56 us
    dynamic_update_slice x5, other arithmetic, placed(): whole = lax.dynamic_update_slice(whole, block, (index * rows, 0))  7.67 us
    all_to_all x1, waiting for transfers between devices, local(): lax.all_to_all(sent, ('xl', 'xh'), split_axis=0, concat_axis=0, tiled=True)  6.55 us
  transfers between devices with their start and end apart: 18, of which 8 were waited for; matrix products, arithmetic and copies ran while one was open for 24% of the time, Pallas kernels for 0%

profile of v6, /device:TPU:1, one launch (start us, length us, event | category | flops | bytes accessed | tf_op | source)
XLA Modules:
  0.0 193.7 jit_solution(3864692498504101832)
XLA Ops:
  2.8 4.5 %collective-permute-start = (bf16[2,128,1536]{2,1,0:T(8,128)(2,1)}, bf16[2,128,1536]{2,1,0:T(8,128)(2,1)S(1)}, u32[]{:S(2)}, u32[]{:S(2)}) collective-permute-start(bf16[2,128,1536]{2,1,0:T(8,128)(2,1)} %pad_maximum_fusion), channel_id=1, source_target_pairs={{0,0},{1,64},{64,1},{65,65},{2,2},{3,66},{66,3},{67,67},{4,4},{5,6... | collective-permute-start | bytes 2359304 | tf_op jit(solution)/shard_map/ppermute | solution.py:29
  8.4 4.3 %all-to-all-start = ((bf16[4,192,768]{2,1,0:T(8,128)(2,1)}), bf16[4,192,768]{2,1,0:T(8,128)(2,1)}, u32[]{:S(2)}, u32[]{:S(2)}) async-start(bf16[4,192,768]{2,1,0:T(8,128)(2,1)} %broadcast_in_dim.24), calls=%async_computation | async-start | bytes 2359296 | tf_op jit(solution)/shard_map/all_to_all | solution.py:52
  19.1 3.3 %collective-permute-start.1 = (bf16[2,128,1536]{2,1,0:T(8,128)(2,1)}, bf16[2,128,1536]{2,1,0:T(8,128)(2,1)}, u32[]{:S(2)}, u32[]{:S(2)}) collective-permute-start(bf16[2,128,1536]{2,1,0:T(8,128)(2,1)} %pad_maximum_fusion.1), channel_id=1, source_target_pairs={{0,128},{128,256},{256,384},{384,0},{1,129},{129,257},{257,385},{3... | collective-permute-start | bytes 2359304 | tf_op jit(solution)/shard_map/ppermute | solution.py:17
  22.4 3.2 %collective-permute-start.2 = (bf16[2,128,1536]{2,1,0:T(8,128)(2,1)}, bf16[2,128,1536]{2,1,0:T(8,128)(2,1)}, u32[]{:S(2)}, u32[]{:S(2)}) collective-permute-start(bf16[2,128,1536]{2,1,0:T(8,128)(2,1)} %pad_maximum_fusion.1), channel_id=1, source_target_pairs={{0,384},{128,0},{256,128},{384,256},{1,385},{129,1},{257,129},{385... | collective-permute-start | bytes 2359304 | tf_op jit(solution)/shard_map/ppermute | solution.py:17
  31.2 4.6 %collective-permute-start.5 = (bf16[2,192,768]{2,1,0:T(8,128)(2,1)S(1)}, bf16[2,192,768]{2,1,0:T(8,128)(2,1)S(1)}, u32[]{:S(2)}, u32[]{:S(2)}) collective-permute-start(bf16[2,192,768]{2,1,0:T(8,128)(2,1)S(1)} %get-tuple-element.40), channel_id=1, source_target_pairs={{0,66},{64,0},{2,64},{66,2},{1,67},{65,1},{3,65},{67,3},{4,70},{68... | collective-permute-start | bytes 1769480 | tf_op jit(solution)/shard_map/ppermute | solution.py:25
  37.3 4.4 %collective-permute-done.4 = bf16[2,192,768]{2,1,0:T(8,128)(2,1)S(1)} collective-permute-done((bf16[2,192,768]{2,1,0:T(8,128)(2,1)S(1)}, bf16[2,192,768]{2,1,0:T(8,128)(2,1)S(1)}, u32[]{:S(2)}, u32[]{:S(2)}) %collective-permute-start.4) | collective-permute-done | bytes 589856 | tf_op jit(solution)/shard_map/ppermute | solution.py:25
  41.8 5.2 %collective-permute-done.5 = bf16[2,192,768]{2,1,0:T(8,128)(2,1)S(1)} collective-permute-done((bf16[2,192,768]{2,1,0:T(8,128)(2,1)S(1)}, bf16[2,192,768]{2,1,0:T(8,128)(2,1)S(1)}, u32[]{:S(2)}, u32[]{:S(2)}) %collective-permute-start.5) | collective-permute-done | bytes 589856 | tf_op jit(solution)/shard_map/ppermute | solution.py:25
  52.8 3.0 %collective-permute-start.3 = (bf16[128,1536]{1,0:T(8,128)(2,1)S(1)}, bf16[128,1536]{1,0:T(8,128)(2,1)S(1)}, u32[]{:S(2)}, u32[]{:S(2)}) collective-permute-start(bf16[128,1536]{1,0:T(8,128)(2,1)S(1)} %slice_bitcast_fusion.5), channel_id=1, source_target_pairs={{0,128},{128,256},{256,384},{384,0},{1,129},{129,257},{257,385},{3... | collective-permute-start | bytes 1179656 | tf_op jit(solution)/shard_map/ppermute | solution.py:17
  55.9 5.6 %collective-permute-start.6 = (bf16[1536,768]{1,0:T(8,128)(2,1)S(1)}, bf16[1536,768]{1,0:T(8,128)(2,1)S(1)}, u32[]{:S(2)}, u32[]{:S(2)}) collective-permute-start(bf16[1536,768]{1,0:T(8,128)(2,1)S(1)} %bitcast.128), channel_id=1, source_target_pairs={{0,1},{1,0},{2,3},{3,2},{4,5},{5,4},{6,7},{7,6},{8,9},{9,8},{10,11... | collective-permute-start | bytes 7077896 | tf_op jit(solution)/shard_map/ppermute | solution.py:17
  62.5 4.2 %collective-permute-start.7 = (bf16[128,1536]{1,0:T(8,128)(2,1)S(1)}, bf16[128,1536]{1,0:T(8,128)(2,1)S(1)}, u32[]{:S(2)}, u32[]{:S(2)}) collective-permute-start(bf16[128,1536]{1,0:T(8,128)(2,1)S(1)} %slice_bitcast_fusion.2), channel_id=1, source_target_pairs={{0,384},{128,0},{256,128},{384,256},{1,385},{129,1},{257,129},{385... | collective-permute-start | bytes 1179656 | tf_op jit(solution)/shard_map/ppermute | solution.py:17
  71.9 3.3 %collective-permute-done.7 = bf16[128,1536]{1,0:T(8,128)(2,1)S(1)} collective-permute-done((bf16[128,1536]{1,0:T(8,128)(2,1)S(1)}, bf16[128,1536]{1,0:T(8,128)(2,1)S(1)}, u32[]{:S(2)}, u32[]{:S(2)}) %collective-permute-start.7) | collective-permute-done | bytes 393248 | tf_op jit(solution)/shard_map/ppermute | solution.py:17
  76.1 2.9 %collective-permute-start.8 = (bf16[512,1536]{1,0:T(8,128)(2,1)}, bf16[512,1536]{1,0:T(8,128)(2,1)S(1)}, u32[]{:S(2)}, u32[]{:S(2)}) collective-permute-start(bf16[512,1536]{1,0:T(8,128)(2,1)} %constant_dynamic-update-slice_fusion.2), channel_id=1, source_target_pairs={{0,1},{1,0},{2,3},{3,2},{4,5},{5,4},{6,7},{7,6},{8,9},{9,8},{10,11... | collective-permute-start | bytes 4718600 | tf_op jit(solution)/shard_map/ppermute | solution.py:17
  80.8 4.1 %multiply_reduce_fusion.2 = (f32[512]{0:T(512)S(1)}, f32[512,1536]{1,0:T(8,128)S(1)}) fusion(bf16[512,1536]{1,0:T(8,128)(2,1)} %get-tuple-element.51, bf16[1536,1536]{1,0:T(8,128)(2,1)S(1)} %constant_dynamic-update-slice_fusion.4), kind=kOutput, calls=%fused_computation.7 | convolution fusion | flops 2417491456 | bytes 9439232 | tf_op jit(solution)/shard_map/dot_general | solution.py:41
  85.1 3.1 %fusion.14 = bf16[512,512]{1,0:T(8,128)(2,1)S(1)} fusion(bf16[512,1536]{1,0:T(8,128)(2,1)S(1)} %multiply_convert_fusion, bf16[512,1536]{1,0:T(8,128)(2,1)} %constant_dynamic-update-slice_fusion.2, f32[]{:T(128)} %bitcast.126, f32[]{:T(128)} %bitcast.3), kind=kOutput, calls=%fused_computation.26 | convolution fusion | flops 807927808 | bytes 3670024 | tf_op jit(solution)/shard_map/dot_general | solution.py:41
  91.3 2.6 %multiply_reduce_fusion.1 = (f32[512]{0:T(512)S(1)}, f32[512,1536]{1,0:T(8,128)S(1)}) fusion(f32[512,1536]{1,0:T(8,128)S(1)} %get-tuple-element.69, f32[512,1536]{1,0:T(8,128)S(1)} %fusion.89, bf16[512,512]{1,0:T(8,128)(2,1)S(1)} %fusion.14, bf16[512,1536]{1,0:T(8,128)(2,1)} %constant_dynamic-update-slice_fusion.2, f32[]{:T(128)} %bitcast.3), kind=kOutput, calls=%fused_computation.5 | convolution fusion | flops 808451584 | bytes 11536388 | tf_op jit(solution)/shard_map/dot_general | solution.py:41
  94.4 2.6 %convolution_convert_fusion = bf16[384,768]{1,0:T(8,128)(2,1)} fusion(bf16[512,1536]{1,0:T(8,128)(2,1)S(1)} %subtract_convert_fusion, s32[]{:T(128)S(6)} %select_n.30, bf16[512,1536]{1,0:T(8,128)(2,1)} %get-tuple-element.51, s32[]{:T(128)S(6)} %select_n.31), kind=kOutput, calls=%fused_computation.12 | convolution fusion | flops 302284800 | bytes 1769480 | tf_op jit(solution)/shard_map/dot_general | solution.py:41
  108.0 4.2 %all-to-all-start.1 = ((bf16[4,96,896]{2,1,0:T(8,128)(2,1)}), bf16[4,96,896]{2,1,0:T(8,128)(2,1)}, u32[]{:S(2)}, u32[]{:S(2)}) async-start(bf16[4,96,896]{2,1,0:T(8,128)(2,1)} %maximum_maximum_fusion), calls=%async_computation.1 | async-start | bytes 1376256 | tf_op jit(solution)/shard_map/all_to_all | solution.py:169
  116.8 6.5 %all-to-all-done.1 = bf16[4,96,896]{2,1,0:T(8,128)(2,1)} async-done(((bf16[4,96,896]{2,1,0:T(8,128)(2,1)}), bf16[4,96,896]{2,1,0:T(8,128)(2,1)}, u32[]{:S(2)}, u32[]{:S(2)}) %all-to-all-start.1) | async-done | bytes 688160 | tf_op jit(solution)/shard_map/all_to_all | solution.py:169
  126.9 6.3 %all-to-all-start.2 = ((bf16[4,24,896]{2,1,0:T(8,128)(2,1)}), bf16[4,24,896]{2,1,0:T(8,128)(2,1)}, u32[]{:S(2)}, u32[]{:S(2)}) async-start(bf16[4,24,896]{2,1,0:T(8,128)(2,1)} %maximum_maximum_fusion.1), calls=%async_computation.2 | async-start | bytes 344064 | tf_op jit(solution)/shard_map/all_to_all | solution.py:181
  140.0 13.3 %all-to-all-start.3 = ((bf16[4,24,896]{2,1,0:T(8,128)(2,1)}), bf16[4,24,896]{2,1,0:T(8,128)(2,1)S(1)}, u32[]{:S(2)}, u32[]{:S(2)}) async-start(bf16[4,24,896]{2,1,0:T(8,128)(2,1)} %broadcast_in_dim.31), calls=%async_computation.3 | async-start | bytes 344064 | tf_op jit(solution)/shard_map/all_to_all | solution.py:52
  155.3 10.5 %all-to-all-done.3 = bf16[4,24,896]{2,1,0:T(8,128)(2,1)S(1)} async-done(((bf16[4,24,896]{2,1,0:T(8,128)(2,1)}), bf16[4,24,896]{2,1,0:T(8,128)(2,1)S(1)}, u32[]{:S(2)}, u32[]{:S(2)}) %all-to-all-start.3) | async-done | bytes 172064 | tf_op jit(solution)/shard_map/all_to_all | solution.py:52
  166.7 5.1 %all-to-all-start.4 = ((bf16[8,24,896]{2,1,0:T(8,128)(2,1)}), bf16[8,24,896]{2,1,0:T(8,128)(2,1)S(1)}, u32[]{:S(2)}, u32[]{:S(2)}) async-start(bf16[8,24,896]{2,1,0:T(8,128)(2,1)} %broadcast_in_dim.32), calls=%async_computation.4 | async-start | bytes 688128 | tf_op jit(solution)/shard_map/all_to_all | solution.py:52
  173.4 6.5 %collective-permute-start.11 = (bf16[2,128,1536]{2,1,0:T(8,128)(2,1)S(1)}, bf16[2,128,1536]{2,1,0:T(8,128)(2,1)S(1)}, u32[]{:S(2)}, u32[]{:S(2)}) collective-permute-start(bf16[2,128,1536]{2,1,0:T(8,128)(2,1)S(1)} %pad_maximum_fusion.2), channel_id=1, source_target_pairs={{0,0},{1,64},{64,1},{65,65},{2,2},{3,66},{66,3},{67,67},{4,4},{5,6... | collective-permute-start | bytes 2359304 | tf_op jit(solution)/shard_map/ppermute | solution.py:29
  181.1 7.9 %collective-permute-start.12 = (bf16[200,768]{1,0:T(8,128)(2,1)S(1)}, bf16[200,768]{1,0:T(8,128)(2,1)S(1)}, u32[]{:S(2)}, u32[]{:S(2)}) collective-permute-start(bf16[200,768]{1,0:T(8,128)(2,1)S(1)} %pad_maximum_fusion.3), channel_id=1, source_target_pairs={{0,1},{1,0},{2,3},{3,2},{4,5},{5,4},{6,7},{7,6},{8,9},{9,8},{10,11... | collective-permute-start | bytes 921608 | tf_op jit(solution)/shard_map/ppermute | solution.py:17
  (152 shorter events, 69.7 us)
Async XLA Ops:
  2.8 14.4 %collective-permute-start = (bf16[2,128,1536]{2,1,0:T(8,128)(2,1)}, bf16[2,128,1536]{2,1,0:T(8,128)(2,1)S(1)}, u32[]{:S(2)}, u32[]{:S(2)}) collective-permute-start(bf16[2,128,1536]{2,1,0:T(8,128)(2,1)} %pad_maximum_fusion), channel_id=1, source_target_pairs={{0,0},{1,64},{64,1},{65,65},{2,2},{3,66},{66,3},{67,67},{4,4},{5,6... | collective-permute-start | bytes 2359304 | tf_op jit(solution)/shard_map/ppermute | solution.py:29
  8.4 19.5 %all-to-all-start = ((bf16[4,192,768]{2,1,0:T(8,128)(2,1)}), bf16[4,192,768]{2,1,0:T(8,128)(2,1)}, u32[]{:S(2)}, u32[]{:S(2)}) async-start(bf16[4,192,768]{2,1,0:T(8,128)(2,1)} %broadcast_in_dim.24), calls=%async_computation | async-start | bytes 2359296 | tf_op jit(solution)/shard_map/all_to_all | solution.py:52
  18.2 8.7 %copy-start.8 = (f32[1536]{0:T(1024)S(1)}, f32[1536]{0:T(1024)}, u32[]{:S(2)}) copy-start(f32[1536]{0:T(1024)} %param.8) | copy-start | bytes 18436
  18.2 8.7 %copy-start.9 = (f32[1536]{0:T(1024)S(1)}, f32[1536]{0:T(1024)}, u32[]{:S(2)}) copy-start(f32[1536]{0:T(1024)} %param.9) | copy-start | bytes 18436
  19.1 27.9 %collective-permute-start.1 = (bf16[2,128,1536]{2,1,0:T(8,128)(2,1)}, bf16[2,128,1536]{2,1,0:T(8,128)(2,1)}, u32[]{:S(2)}, u32[]{:S(2)}) collective-permute-start(bf16[2,128,1536]{2,1,0:T(8,128)(2,1)} %pad_maximum_fusion.1), channel_id=1, source_target_pairs={{0,128},{128,256},{256,384},{384,0},{1,129},{129,257},{257,385},{3... | collective-permute-start | bytes 2359304 | tf_op jit(solution)/shard_map/ppermute | solution.py:17
  22.4 27.0 %collective-permute-start.2 = (bf16[2,128,1536]{2,1,0:T(8,128)(2,1)}, bf16[2,128,1536]{2,1,0:T(8,128)(2,1)}, u32[]{:S(2)}, u32[]{:S(2)}) collective-permute-start(bf16[2,128,1536]{2,1,0:T(8,128)(2,1)} %pad_maximum_fusion.1), channel_id=1, source_target_pairs={{0,384},{128,0},{256,128},{384,256},{1,385},{129,1},{257,129},{385... | collective-permute-start | bytes 2359304 | tf_op jit(solution)/shard_map/ppermute | solution.py:17
  29.2 12.5 %collective-permute-start.4 = (bf16[2,192,768]{2,1,0:T(8,128)(2,1)S(1)}, bf16[2,192,768]{2,1,0:T(8,128)(2,1)S(1)}, u32[]{:S(2)}, u32[]{:S(2)}) collective-permute-start(bf16[2,192,768]{2,1,0:T(8,128)(2,1)S(1)} %get-tuple-element.41), channel_id=1, source_target_pairs={{0,64},{64,2},{2,66},{66,0},{1,65},{65,3},{3,67},{67,1},{4,68},{68... | collective-permute-start | bytes 1769480 | tf_op jit(solution)/shard_map/ppermute | solution.py:25
  31.2 15.8 %collective-permute-start.5 = (bf16[2,192,768]{2,1,0:T(8,128)(2,1)S(1)}, bf16[2,192,768]{2,1,0:T(8,128)(2,1)S(1)}, u32[]{:S(2)}, u32[]{:S(2)}) collective-permute-start(bf16[2,192,768]{2,1,0:T(8,128)(2,1)S(1)} %get-tuple-element.40), channel_id=1, source_target_pairs={{0,66},{64,0},{2,64},{66,2},{1,67},{65,1},{3,65},{67,3},{4,70},{68... | collective-permute-start | bytes 1769480 | tf_op jit(solution)/shard_map/ppermute | solution.py:25
  52.8 26.1 %collective-permute-start.3 = (bf16[128,1536]{1,0:T(8,128)(2,1)S(1)}, bf16[128,1536]{1,0:T(8,128)(2,1)S(1)}, u32[]{:S(2)}, u32[]{:S(2)}) collective-permute-start(bf16[128,1536]{1,0:T(8,128)(2,1)S(1)} %slice_bitcast_fusion.5), channel_id=1, source_target_pairs={{0,128},{128,256},{256,384},{384,0},{1,129},{129,257},{257,385},{3... | collective-permute-start | bytes 1179656 | tf_op jit(solution)/shard_map/ppermute | solution.py:17
  55.9 24.6 %collective-permute-start.6 = (bf16[1536,768]{1,0:T(8,128)(2,1)S(1)}, bf16[1536,768]{1,0:T(8,128)(2,1)S(1)}, u32[]{:S(2)}, u32[]{:S(2)}) collective-permute-start(bf16[1536,768]{1,0:T(8,128)(2,1)S(1)} %bitcast.128), channel_id=1, source_target_pairs={{0,1},{1,0},{2,3},{3,2},{4,5},{5,4},{6,7},{7,6},{8,9},{9,8},{10,11... | collective-permute-start | bytes 7077896 | tf_op jit(solution)/shard_map/ppermute | solution.py:17
  62.5 12.8 %collective-permute-start.7 = (bf16[128,1536]{1,0:T(8,128)(2,1)S(1)}, bf16[128,1536]{1,0:T(8,128)(2,1)S(1)}, u32[]{:S(2)}, u32[]{:S(2)}) collective-permute-start(bf16[128,1536]{1,0:T(8,128)(2,1)S(1)} %slice_bitcast_fusion.2), channel_id=1, source_target_pairs={{0,384},{128,0},{256,128},{384,256},{1,385},{129,1},{257,129},{385... | collective-permute-start | bytes 1179656 | tf_op jit(solution)/shard_map/ppermute | solution.py:17
  76.1 12.2 %collective-permute-start.8 = (bf16[512,1536]{1,0:T(8,128)(2,1)}, bf16[512,1536]{1,0:T(8,128)(2,1)S(1)}, u32[]{:S(2)}, u32[]{:S(2)}) collective-permute-start(bf16[512,1536]{1,0:T(8,128)(2,1)} %constant_dynamic-update-slice_fusion.2), channel_id=1, source_target_pairs={{0,1},{1,0},{2,3},{3,2},{4,5},{5,4},{6,7},{7,6},{8,9},{9,8},{10,11... | collective-permute-start | bytes 4718600 | tf_op jit(solution)/shard_map/ppermute | solution.py:17
  99.6 4.4 %collective-permute-start.9 = (bf16[384,768]{1,0:T(8,128)(2,1)}, bf16[384,768]{1,0:T(8,128)(2,1)}, u32[]{:S(2)}, u32[]{:S(2)}) collective-permute-start(bf16[384,768]{1,0:T(8,128)(2,1)} %convolution_convert_fusion), channel_id=1, source_target_pairs={{0,1},{1,0},{2,3},{3,2},{4,5},{5,4},{6,7},{7,6},{8,9},{9,8},{10,11... | collective-permute-start | bytes 1769480 | tf_op jit(solution)/shard_map/ppermute | solution.py:17
  108.0 15.4 %all-to-all-start.1 = ((bf16[4,96,896]{2,1,0:T(8,128)(2,1)}), bf16[4,96,896]{2,1,0:T(8,128)(2,1)}, u32[]{:S(2)}, u32[]{:S(2)}) async-start(bf16[4,96,896]{2,1,0:T(8,128)(2,1)} %maximum_maximum_fusion), calls=%async_computation.1 | async-start | bytes 1376256 | tf_op jit(solution)/shard_map/all_to_all | solution.py:169
  114.4 20.9 %collective-permute-start.10 = (f32[128,1536]{1,0:T(8,128)}, f32[128,1536]{1,0:T(8,128)}, u32[]{:S(2)}, u32[]{:S(2)}) collective-permute-start(f32[128,1536]{1,0:T(8,128)} %fusion.68), channel_id=1, source_target_pairs={{0,1},{1,0},{2,3},{3,2},{4,5},{5,4},{6,7},{7,6},{8,9},{9,8},{10,11... | collective-permute-start | bytes 2359304 | tf_op jit(solution)/shard_map/ppermute | solution.py:17
  126.9 11.4 %all-to-all-start.2 = ((bf16[4,24,896]{2,1,0:T(8,128)(2,1)}), bf16[4,24,896]{2,1,0:T(8,128)(2,1)}, u32[]{:S(2)}, u32[]{:S(2)}) async-start(bf16[4,24,896]{2,1,0:T(8,128)(2,1)} %maximum_maximum_fusion.1), calls=%async_computation.2 | async-start | bytes 344064 | tf_op jit(solution)/shard_map/all_to_all | solution.py:181
  140.0 15.3 %copy-start.13 = (f32[128]{0:T(128)S(1)}, f32[128]{0:T(128)}, u32[]{:S(2)}) copy-start(f32[128]{0:T(128)} %copy-done.12) | copy-start | bytes 1540
  140.0 25.8 %all-to-all-start.3 = ((bf16[4,24,896]{2,1,0:T(8,128)(2,1)}), bf16[4,24,896]{2,1,0:T(8,128)(2,1)S(1)}, u32[]{:S(2)}, u32[]{:S(2)}) async-start(bf16[4,24,896]{2,1,0:T(8,128)(2,1)} %broadcast_in_dim.31), calls=%async_computation.3 | async-start | bytes 344064 | tf_op jit(solution)/shard_map/all_to_all | solution.py:52
  153.3 18.5 %copy-start.4 = (f32[128,1536]{1,0:T(8,128)S(1)}, f32[128,1536]{1,0:T(8,128)}, u32[]{:S(2)}) copy-start(f32[128,1536]{1,0:T(8,128)} %convolution_add_fusion.1) | copy-start | bytes 2359300
  155.3 16.7 %copy-start.3 = (f32[128,1536]{1,0:T(8,128)S(1)}, f32[128,1536]{1,0:T(8,128)}, u32[]{:S(2)}) copy-start(f32[128,1536]{1,0:T(8,128)} %slice.135) | copy-start | bytes 2359300
  155.3 16.7 %copy-start.11 = (f32[128]{0:T(128)S(1)}, f32[128]{0:T(128)}, u32[]{:S(2)}) copy-start(f32[128]{0:T(128)} %copy-done.10) | copy-start | bytes 1540
  166.7 14.2 %all-to-all-start.4 = ((bf16[8,24,896]{2,1,0:T(8,128)(2,1)}), bf16[8,24,896]{2,1,0:T(8,128)(2,1)S(1)}, u32[]{:S(2)}, u32[]{:S(2)}) async-start(bf16[8,24,896]{2,1,0:T(8,128)(2,1)} %broadcast_in_dim.32), calls=%async_computation.4 | async-start | bytes 688128 | tf_op jit(solution)/shard_map/all_to_all | solution.py:52
  173.4 17.0 %collective-permute-start.11 = (bf16[2,128,1536]{2,1,0:T(8,128)(2,1)S(1)}, bf16[2,128,1536]{2,1,0:T(8,128)(2,1)S(1)}, u32[]{:S(2)}, u32[]{:S(2)}) collective-permute-start(bf16[2,128,1536]{2,1,0:T(8,128)(2,1)S(1)} %pad_maximum_fusion.2), channel_id=1, source_target_pairs={{0,0},{1,64},{64,1},{65,65},{2,2},{3,66},{66,3},{67,67},{4,4},{5,6... | collective-permute-start | bytes 2359304 | tf_op jit(solution)/shard_map/ppermute | solution.py:29
  181.1 10.7 %collective-permute-start.12 = (bf16[200,768]{1,0:T(8,128)(2,1)S(1)}, bf16[200,768]{1,0:T(8,128)(2,1)S(1)}, u32[]{:S(2)}, u32[]{:S(2)}) collective-permute-start(bf16[200,768]{1,0:T(8,128)(2,1)S(1)} %pad_maximum_fusion.3), channel_id=1, source_target_pairs={{0,1},{1,0},{2,3},{3,2},{4,5},{5,4},{6,7},{7,6},{8,9},{9,8},{10,11... | collective-permute-start | bytes 921608 | tf_op jit(solution)/shard_map/ppermute | solution.py:17
  (8 other events, 30.3 us)

commit v7 on v6

--- a/solution.py
+++ b/solution.py
@@ -39,11 +39,6 @@
 
 def dot(a, b, da, db):
     return lax.dot_general(a, b, (((da,), (db,)), ((), ())), preferred_element_type=f32)
-
-
-def split16(value):
-    high = value.astype(bf16)
-    return high, (value - high.astype(f32)).astype(bf16)
 
 
 def spread_to(value, axes):
@@ -105,11 +100,10 @@
     text_unit = (text_values * inv_text).astype(bf16)
 
     pair = jnp.stack([text_unit, feature_rows], 0)
-    below, above = shift(pair, "y", 1), shift(pair, "y", -1)
-    weight = gather_weight(weight_blocks, xl, core, [below, above])
-    text_far, feature_far = shift(above[0], "y", -1), shift(below[1], "y", 1)
-    text_same = placed([text_unit, below[0], above[0], text_far])
-    raw = [feature_rows, below[1], above[1], feature_far]
+    below, above, far = shift(pair, "y", 1), shift(pair, "y", -1), shift(pair, "y", 2)
+    weight = gather_weight(weight_blocks, xl, core, [below, above, far])
+    text_same = placed([text_unit, below[0], above[0], far[0]])
+    raw = [feature_rows, below[1], above[1], far[1]]
     stats = [standardize(block) for block in raw]
     normed = placed(
         [
@@ -152,22 +146,14 @@
     vectors = jnp.stack([jnp.sum(grad_normed * xhat, axis=0), jnp.sum(grad_normed, axis=0)], 0)
     xhat, grad_normed, inverse_deviation = xhat[:own], grad_normed[:own], inverse_deviation[:own]
 
-    def payload(head_rows, vector):
-        lead, lines = head_rows.shape[:-2], head_rows.shape[-2]
-        high, low = (t.reshape(lead + (-1, lanes)) for t in split16(vector))
-        rest = jnp.zeros(lead + (lines - 2 * high.shape[-2], lanes), bf16)
-        side = jnp.concatenate([high, low, rest], -2)
-        return jnp.concatenate([head_rows.astype(bf16), side], -1)
-
-    def unpack(received, count):
-        side = received[..., half:]
-        vector = side[..., :count, :] + side[..., count : 2 * count, :]
-        return received[..., :half], vector
-
-    halved = jnp.broadcast_to(vectors.reshape(1, 2, width), (2, 2, width)).reshape(4, width)
-    sent = payload(head.reshape(4, part, half), halved)
+    lines = part // 4
+    count = width // 4 // lanes
+    side = vectors.astype(bf16).reshape(1, 2, 4, count, lanes)
+    side = jnp.pad(side, ((0, 0), (0, 0), (0, 0), (0, lines - count), (0, 0)))
+    side = jnp.broadcast_to(side, (2,) + side.shape[1:]).reshape(4, part, lanes)
+    sent = jnp.concatenate([head.astype(bf16).reshape(4, part, half), side], -1)
     received = lax.all_to_all(sent, ("xl", "xh"), split_axis=0, concat_axis=0, tiled=True)
-    head, vector = unpack(jnp.sum(received.astype(f32), axis=0), width // lanes)
+    head = jnp.sum(received.astype(f32), axis=0).astype(bf16)
 
     held = after((weights_same, weights_other, image_unit), head)
     text_part, text_theirs = (
@@ -175,11 +161,9 @@
     )
     grad_unit_text = text_part + shift(text_theirs, "core", 1)
 
-    lines = part // 4
-    count = width // 4 // lanes
-    sent = payload(head.reshape(4, lines, half), vector.reshape(4, width // 4))
-    received = lax.all_to_all(sent, "zl", split_axis=0, concat_axis=0, tiled=True).astype(f32)
-    sent = payload(*unpack(jnp.sum(received, axis=0), count))
+    sent = head.reshape(4, lines, half + lanes)
+    received = lax.all_to_all(sent, "zl", split_axis=0, concat_axis=0, tiled=True)
+    sent = jnp.sum(received.astype(f32), axis=0).astype(bf16)
 
     grad_unit_text, grad_normed = after((grad_unit_text, grad_normed), sent)
     grad_unit_text = scale * grad_unit_text
@@ -191,16 +175,19 @@
     grad_features = inverse_deviation * (scaled - first_mean - xhat * second_mean)
     returned = swap(jnp.stack([grad_features, grad_text], 0).astype(bf16))
 
-    received = spread_to(sent, "zh").astype(f32)
-    sent = payload(*unpack(jnp.sum(received, axis=0), count))
-    received = spread_to(sent, ("zl", "xh")).reshape(4, 2, lines, half + lanes)
-    head_all = received[..., :half].transpose(1, 0, 2, 3).reshape(2 * part, half)
-    vectors = unpack(received.astype(f32), count)[1].transpose(1, 0, 2, 3).reshape(2, width)
-    sent = jnp.concatenate([head_all, *(t.reshape(-1, half) for t in split16(vectors))], 0)
-    received = shift(sent, "core", 1)
-    head_all = halves(core, head_all, received[: 2 * part], 1).astype(f32) / 64.0
-    high, low = jnp.split(received[2 * part :].astype(f32), 2, 0)
-    vectors = (vectors + (high + low).reshape(2, width)) / 64.0
+    received = spread_to(sent, "zh")
+    sent = after(jnp.sum(received.astype(f32), axis=0).astype(bf16), returned)
+    mine = spread_to(sent, ("zl", "xh"))
+    theirs = shift(mine, "core", 1)
+
+    def unpack(received):
+        received = received.reshape(4, 2, lines, half + lanes).transpose(1, 0, 2, 3)
+        vectors = received[..., :count, half:].astype(f32).reshape(2, width)
+        return received[..., :half].reshape(2 * part, half), vectors
+
+    (head_mine, vectors_mine), (head_theirs, vectors_theirs) = unpack(mine), unpack(theirs)
+    head_all = halves(core, head_mine, head_theirs, 1).astype(f32) / 64.0
+    vectors = (vectors_mine + vectors_theirs) / 64.0
 
     return (
         returned[0].astype(f32),

time: 196 us -> 202 us (1.031)
  blocking collectives: 0 us -> 41.9 us
  starting transfers between devices: 85 us -> 56.9 us
  local copies, waits for them, and re-layouts: 17.3 us -> 12.9 us
    all_to_all x0 -> x2, blocking collectives: none -> 41.9 us  [the longest x1 28.1 us: spread_to(): return lax.all_to_all(many, axes, split_axis=0, concat_axis=0, tiled=True)]
    all_to_all x3 -> x2, starting transfers between devices: 22.6 us -> 9.26 us  [spread_to(): return lax.all_to_all(many, axes, split_axis=0, concat_axis=0, tiled=True)]
    ppermute x9 -> x8, starting transfers between devices: 34.5 us -> 26.2 us  [shift(): lax.ppermute(value, axis, [(i, (i + steps) % count) for i in range(count)])]
    ppermute x9 -> x8, waiting for transfers between devices: 3.33 us -> 10.9 us  [shift(): lax.ppermute(value, axis, [(i, (i + steps) % count) for i in range(count)])]
    all_to_all x1 -> x0, waiting for transfers between devices: 6.55 us -> none  [local(): lax.all_to_all(sent, ('xl', 'xh'), split_axis=0, concat_axis=0, tiled=True)]
    all_to_all x1 -> x0, starting transfers between devices: 4.18 us -> none  [local(): lax.all_to_all(sent, ('xl', 'xh'), split_axis=0, concat_axis=0, tiled=True)]
    concatenate x5 -> x1, other arithmetic: 3.68 us -> 0.06 us  [local(): sent = jnp.concatenate([head.astype(bf16).reshape(4, part, half), side], -1)]
    all_to_all x1, waiting for transfers between devices: 0.63 us -> 3.14 us  [local(): lax.all_to_all(sent, 'zl', split_axis=0, concat_axis=0, tiled=True)]
  transfers between devices with their start and end apart: 18 -> 15, of which waited for: 8 -> 7; matrix products, arithmetic and copies ran while one was open for 24% -> 21% of each run, Pallas kernels for 0% -> 0%
where the time goes in v7:
time: 202 us; the launch traced here: 200 us
  starting transfers between devices  56.9 us (28%)
  blocking collectives  41.9 us (21%)
  waiting for transfers between devices  32.6 us (16%)
  other arithmetic  30.5 us (15%)
  matrix products  23 us (11%)
  local copies, waits for them, and re-layouts  12.9 us (6%)
  between operations  2.55 us (1%)
    all_to_all x1, blocking collectives, spread_to(): return lax.all_to_all(many, axes, split_axis=0, concat_axis=0, tiled=True)  28.1 us
    ppermute x8, starting transfers between devices, shift(): lax.ppermute(value, axis, [(i, (i + steps) % count) for i in range(count)])  26.2 us
    dot_general x10, matrix products, dot(): lax.dot_general(a, b, (((da,), (db,)), ((), ())), preferred_element_type=...  23 us
    all_to_all x1, blocking collectives, local(): lax.all_to_all(sent, ('xl', 'xh'), split_axis=0, concat_axis=0, tiled=True)  13.7 us
    ppermute x8, waiting for transfers between devices, shift(): lax.ppermute(value, axis, [(i, (i + steps) % count) for i in range(count)])  10.9 us
    ppermute x2, starting transfers between devices, swap(): return lax.ppermute(value, ('xl', 'core'), [(0, 0), (1, 2), (2, 1), (3, 3)])  9.37 us
    all_to_all x2, waiting for transfers between devices, spread_to(): return lax.all_to_all(many, axes, split_axis=0, concat_axis=0, tiled=True)  9.32 us
    all_to_all x2, starting transfers between devices, spread_to(): return lax.all_to_all(many, axes, split_axis=0, concat_axis=0, tiled=True)  9.26 us
  transfers between devices with their start and end apart: 15, of which 7 were waited for; matrix products, arithmetic and copies ran while one was open for 21% of the time, Pallas kernels for 0%

profile of v7, /device:TPU:1, one launch (start us, length us, event | category | flops | bytes accessed | tf_op | source)
XLA Modules:
  0.0 200.4 jit_solution(12104009959180715124)
XLA Ops:
  2.8 4.5 %collective-permute-start = (bf16[2,128,1536]{2,1,0:T(8,128)(2,1)}, bf16[2,128,1536]{2,1,0:T(8,128)(2,1)S(1)}, u32[]{:S(2)}, u32[]{:S(2)}) collective-permute-start(bf16[2,128,1536]{2,1,0:T(8,128)(2,1)} %pad_maximum_fusion), channel_id=1, source_target_pairs={{0,0},{1,64},{64,1},{65,65},{2,2},{3,66},{66,3},{67,67},{4,4},{5,6... | collective-permute-start | bytes 2359304 | tf_op jit(solution)/shard_map/ppermute | solution.py:29
  8.4 4.3 %all-to-all-start = ((bf16[4,192,768]{2,1,0:T(8,128)(2,1)}), bf16[4,192,768]{2,1,0:T(8,128)(2,1)}, u32[]{:S(2)}, u32[]{:S(2)}) async-start(bf16[4,192,768]{2,1,0:T(8,128)(2,1)} %broadcast_in_dim.22), calls=%async_computation | async-start | bytes 2359296 | tf_op jit(solution)/shard_map/all_to_all | solution.py:47
  18.5 3.2 %collective-permute-start.1 = (bf16[2,128,1536]{2,1,0:T(8,128)(2,1)}, bf16[2,128,1536]{2,1,0:T(8,128)(2,1)}, u32[]{:S(2)}, u32[]{:S(2)}) collective-permute-start(bf16[2,128,1536]{2,1,0:T(8,128)(2,1)} %pad_maximum_fusion.1), channel_id=1, source_target_pairs={{0,128},{128,256},{256,384},{384,0},{1,129},{129,257},{257,385},{3... | collective-permute-start | bytes 2359304 | tf_op jit(solution)/shard_map/ppermute | solution.py:17
  21.7 3.4 %collective-permute-start.2 = (bf16[2,128,1536]{2,1,0:T(8,128)(2,1)}, bf16[2,128,1536]{2,1,0:T(8,128)(2,1)}, u32[]{:S(2)}, u32[]{:S(2)}) collective-permute-start(bf16[2,128,1536]{2,1,0:T(8,128)(2,1)} %pad_maximum_fusion.1), channel_id=1, source_target_pairs={{0,384},{128,0},{256,128},{384,256},{1,385},{129,1},{257,129},{385... | collective-permute-start | bytes 2359304 | tf_op jit(solution)/shard_map/ppermute | solution.py:17
  25.1 3.5 %collective-permute-start.3 = (bf16[2,128,1536]{2,1,0:T(8,128)(2,1)}, bf16[2,128,1536]{2,1,0:T(8,128)(2,1)}, u32[]{:S(2)}, u32[]{:S(2)}) collective-permute-start(bf16[2,128,1536]{2,1,0:T(8,128)(2,1)} %pad_maximum_fusion.1), channel_id=1, source_target_pairs={{0,256},{128,384},{256,0},{384,128},{1,257},{129,385},{257,1},{385... | collective-permute-start | bytes 2359304 | tf_op jit(solution)/shard_map/ppermute | solution.py:17
  34.1 4.6 %collective-permute-start.5 = (bf16[2,192,768]{2,1,0:T(8,128)(2,1)S(1)}, bf16[2,192,768]{2,1,0:T(8,128)(2,1)S(1)}, u32[]{:S(2)}, u32[]{:S(2)}) collective-permute-start(bf16[2,192,768]{2,1,0:T(8,128)(2,1)S(1)} %get-tuple-element.30), channel_id=1, source_target_pairs={{0,66},{64,0},{2,64},{66,2},{1,67},{65,1},{3,65},{67,3},{4,70},{68... | collective-permute-start | bytes 1769480 | tf_op jit(solution)/shard_map/ppermute | solution.py:25
  40.3 5.3 %collective-permute-done.4 = bf16[2,192,768]{2,1,0:T(8,128)(2,1)S(1)} collective-permute-done((bf16[2,192,768]{2,1,0:T(8,128)(2,1)S(1)}, bf16[2,192,768]{2,1,0:T(8,128)(2,1)S(1)}, u32[]{:S(2)}, u32[]{:S(2)}) %collective-permute-start.4) | collective-permute-done | bytes 589856 | tf_op jit(solution)/shard_map/ppermute | solution.py:25
  45.6 3.3 %collective-permute-done.5 = bf16[2,192,768]{2,1,0:T(8,128)(2,1)S(1)} collective-permute-done((bf16[2,192,768]{2,1,0:T(8,128)(2,1)S(1)}, bf16[2,192,768]{2,1,0:T(8,128)(2,1)S(1)}, u32[]{:S(2)}, u32[]{:S(2)}) %collective-permute-start.5) | collective-permute-done | bytes 589856 | tf_op jit(solution)/shard_map/ppermute | solution.py:25
  49.0 10.7 %collective-permute-done.3 = bf16[2,128,1536]{2,1,0:T(8,128)(2,1)} collective-permute-done((bf16[2,128,1536]{2,1,0:T(8,128)(2,1)}, bf16[2,128,1536]{2,1,0:T(8,128)(2,1)}, u32[]{:S(2)}, u32[]{:S(2)}) %collective-permute-start.3) | collective-permute-done | bytes 786464 | tf_op jit(solution)/shard_map/ppermute | solution.py:17
  59.6 6.2 %collective-permute-start.6 = (bf16[1536,768]{1,0:T(8,128)(2,1)S(1)}, bf16[1536,768]{1,0:T(8,128)(2,1)S(1)}, u32[]{:S(2)}, u32[]{:S(2)}) collective-permute-start(bf16[1536,768]{1,0:T(8,128)(2,1)S(1)} %bitcast.151), channel_id=1, source_target_pairs={{0,1},{1,0},{2,3},{3,2},{4,5},{5,4},{6,7},{7,6},{8,9},{9,8},{10,11... | collective-permute-start | bytes 7077896 | tf_op jit(solution)/shard_map/ppermute | solution.py:17
  82.8 4.1 %multiply_reduce_fusion.2 = (f32[512]{0:T(512)S(1)}, f32[512,1536]{1,0:T(8,128)S(1)}) fusion(bf16[512,1536]{1,0:T(8,128)(2,1)} %get-tuple-element.35, bf16[1536,1536]{1,0:T(8,128)(2,1)S(1)} %constant_dynamic-update-slice_fusion), kind=kOutput, calls=%fused_computation.7 | convolution fusion | flops 2417491456 | bytes 9439232 | tf_op jit(solution)/shard_map/dot_general | solution.py:41
  87.1 3.2 %fusion.14 = bf16[512,512]{1,0:T(8,128)(2,1)S(1)} fusion(bf16[512,1536]{1,0:T(8,128)(2,1)S(1)} %multiply_convert_fusion, bf16[512,1536]{1,0:T(8,128)(2,1)} %get-tuple-element.36, f32[]{:T(128)} %bitcast.149, f32[]{:T(128)} %bitcast.3), kind=kOutput, calls=%fused_computation.25 | convolution fusion | flops 807927808 | bytes 3670024 | tf_op jit(solution)/shard_map/dot_general | solution.py:41
  93.3 2.6 %multiply_reduce_fusion.1 = (f32[512]{0:T(512)S(1)}, f32[512,1536]{1,0:T(8,128)S(1)}) fusion(f32[512,1536]{1,0:T(8,128)S(1)} %get-tuple-element.62, f32[512,1536]{1,0:T(8,128)S(1)} %fusion.93, bf16[512,512]{1,0:T(8,128)(2,1)S(1)} %fusion.14, bf16[512,1536]{1,0:T(8,128)(2,1)} %get-tuple-element.36, f32[]{:T(128)} %bitcast.3), kind=kOutput, calls=%fused_computation.5 | convolution fusion | flops 808451584 | bytes 11536388 | tf_op jit(solution)/shard_map/dot_general | solution.py:41
  96.3 2.6 %convolution_convert_fusion = bf16[384,768]{1,0:T(8,128)(2,1)} fusion(bf16[512,1536]{1,0:T(8,128)(2,1)S(1)} %subtract_convert_fusion, s32[]{:T(128)S(6)} %select_n.30, bf16[512,1536]{1,0:T(8,128)(2,1)} %get-tuple-element.35, s32[]{:T(128)S(6)} %select_n.31), kind=kOutput, calls=%fused_computation.11 | convolution fusion | flops 302284800 | bytes 1769480 | tf_op jit(solution)/shard_map/dot_general | solution.py:41
  101.5 2.6 %fusion.94 = f32[512,1536]{1,0:T(8,128)S(1)} fusion(bf16[512,1536]{1,0:T(8,128)(2,1)S(1)} %subtract_convert_fusion, bf16[1536,1536]{1,0:T(8,128)(2,1)S(1)} %constant_dynamic-update-slice_fusion), kind=kOutput, calls=%fused_computation.157 | convolution fusion | flops 2415919104 | bytes 9437184 | tf_op jit(solution)/shard_map/dot_general | solution.py:41
  104.2 2.6 %multiply_reduce_fusion = (bf16[1536]{0:T(1024)(128)(2,1)S(1)}, bf16[1536]{0:T(1024)(128)(2,1)S(1)}, f32[512,1536]{1,0:T(8,128)}) fusion(f32[512,1536]{1,0:T(8,128)S(1)} %fusion.94, f32[512]{0:T(512)S(1)} %bitcast.164, f32[512]{0:T(512)S(1)} %bitcast.165, bf16[512,1536]{1,0:T(8,128)(2,1)S(1)} %get-tuple-element.34), kind=kLoop, calls=%fused_computation.2 | loop fusion | flops 4715520 | bytes 7874560 | tf_op jit(solution)/shard_map/reduce_sum | solution.py:146
  108.9 13.7 %all_to_all.25 = bf16[4,96,896]{2,1,0:T(8,128)(2,1)} all-to-all(bf16[4,96,896]{2,1,0:T(8,128)(2,1)S(1)} %pad_maximum_fusion.3), channel_id=1, replica_groups=mesh['y'=4,'xl'=2,'zh'=4,'zl'=4,'xh'=2,'core'=2] {'xl','xh'}, dimensions={0} | all-to-all | bytes 1376256 | tf_op jit(solution)/shard_map/all_to_all | solution.py:155
  126.7 3.5 %collective-permute-start.9 = (f32[128,1536]{1,0:T(8,128)}, f32[128,1536]{1,0:T(8,128)}, u32[]{:S(2)}, u32[]{:S(2)}) collective-permute-start(f32[128,1536]{1,0:T(8,128)} %fusion.72), channel_id=1, source_target_pairs={{0,1},{1,0},{2,3},{3,2},{4,5},{5,4},{6,7},{7,6},{8,9},{9,8},{10,11... | collective-permute-start | bytes 2359304 | tf_op jit(solution)/shard_map/ppermute | solution.py:17
  130.3 5.6 %all-to-all-start.2 = ((bf16[4,24,896]{2,1,0:T(8,128)(2,1)}), bf16[4,24,896]{2,1,0:T(8,128)(2,1)}, u32[]{:S(2)}, u32[]{:S(2)}) async-start(bf16[4,24,896]{2,1,0:T(8,128)(2,1)} %bitcast.157), calls=%async_computation.2 | async-start | bytes 344064 | tf_op jit(solution)/shard_map/all_to_all | solution.py:165
  138.0 3.1 %all-to-all-done.2 = bf16[4,24,896]{2,1,0:T(8,128)(2,1)} async-done(((bf16[4,24,896]{2,1,0:T(8,128)(2,1)}), bf16[4,24,896]{2,1,0:T(8,128)(2,1)}, u32[]{:S(2)}, u32[]{:S(2)}) %all-to-all-start.2) | async-done | bytes 172064 | tf_op jit(solution)/shard_map/all_to_all | solution.py:165
  146.2 4.9 %collective-permute-start.10 = (bf16[2,128,1536]{2,1,0:T(8,128)(2,1)S(1)}, bf16[2,128,1536]{2,1,0:T(8,128)(2,1)S(1)}, u32[]{:S(2)}, u32[]{:S(2)}) collective-permute-start(bf16[2,128,1536]{2,1,0:T(8,128)(2,1)S(1)} %pad_maximum_fusion.2), channel_id=1, source_target_pairs={{0,0},{1,64},{64,1},{65,65},{2,2},{3,66},{66,3},{67,67},{4,4},{5,6... | collective-permute-start | bytes 2359304 | tf_op jit(solution)/shard_map/ppermute | solution.py:29
  151.1 28.1 %all_to_all.26 = bf16[4,24,896]{2,1,0:T(8,128)(2,1)S(1)} all-to-all(bf16[4,24,896]{2,1,0:T(8,128)(2,1)S(1)} %broadcast_in_dim.28), channel_id=1, replica_groups=mesh['y'=4,'xl'=2,'zh'=4,'zl'=4,'xh'=2,'core'=2] {'zh'}, dimensions={0} | all-to-all | bytes 344064 | tf_op jit(solution)/shard_map/all_to_all | solution.py:47
  180.0 5.0 %all-to-all-start.4 = ((bf16[8,24,896]{2,1,0:T(8,128)(2,1)}), bf16[8,24,896]{2,1,0:T(8,128)(2,1)S(1)}, u32[]{:S(2)}, u32[]{:S(2)}) async-start(bf16[8,24,896]{2,1,0:T(8,128)(2,1)} %broadcast_in_dim.29), calls=%async_computation.4 | async-start | bytes 688128 | tf_op jit(solution)/shard_map/all_to_all | solution.py:47
  185.0 9.3 %all-to-all-done.4 = bf16[8,24,896]{2,1,0:T(8,128)(2,1)S(1)} async-done(((bf16[8,24,896]{2,1,0:T(8,128)(2,1)}), bf16[8,24,896]{2,1,0:T(8,128)(2,1)S(1)}, u32[]{:S(2)}, u32[]{:S(2)}) %all-to-all-start.4) | async-done | bytes 344096 | tf_op jit(solution)/shard_map/all_to_all | solution.py:47
  (113 shorter events, 57.9 us)
Async XLA Ops:
  0.6 6.7 %copy-start = (bf16[192,1536]{1,0:T(8,128)(2,1)S(1)}, bf16[192,1536]{1,0:T(8,128)(2,1)}, u32[]{:S(2)}) copy-start(bf16[192,1536]{1,0:T(8,128)(2,1)} %param.10) | copy-start | bytes 1769476
  2.8 14.4 %collective-permute-start = (bf16[2,128,1536]{2,1,0:T(8,128)(2,1)}, bf16[2,128,1536]{2,1,0:T(8,128)(2,1)S(1)}, u32[]{:S(2)}, u32[]{:S(2)}) collective-permute-start(bf16[2,128,1536]{2,1,0:T(8,128)(2,1)} %pad_maximum_fusion), channel_id=1, source_target_pairs={{0,0},{1,64},{64,1},{65,65},{2,2},{3,66},{66,3},{67,67},{4,4},{5,6... | collective-permute-start | bytes 2359304 | tf_op jit(solution)/shard_map/ppermute | solution.py:29
  8.4 22.4 %all-to-all-start = ((bf16[4,192,768]{2,1,0:T(8,128)(2,1)}), bf16[4,192,768]{2,1,0:T(8,128)(2,1)}, u32[]{:S(2)}, u32[]{:S(2)}) async-start(bf16[4,192,768]{2,1,0:T(8,128)(2,1)} %broadcast_in_dim.22), calls=%async_computation | async-start | bytes 2359296 | tf_op jit(solution)/shard_map/all_to_all | solution.py:47
  17.5 12.3 %copy-start.8 = (f32[1536]{0:T(1024)S(1)}, f32[1536]{0:T(1024)}, u32[]{:S(2)}) copy-start(f32[1536]{0:T(1024)} %param.8) | copy-start | bytes 18436
  17.6 12.2 %copy-start.9 = (f32[1536]{0:T(1024)S(1)}, f32[1536]{0:T(1024)}, u32[]{:S(2)}) copy-start(f32[1536]{0:T(1024)} %param.9) | copy-start | bytes 18436
  18.5 30.4 %collective-permute-start.1 = (bf16[2,128,1536]{2,1,0:T(8,128)(2,1)}, bf16[2,128,1536]{2,1,0:T(8,128)(2,1)}, u32[]{:S(2)}, u32[]{:S(2)}) collective-permute-start(bf16[2,128,1536]{2,1,0:T(8,128)(2,1)} %pad_maximum_fusion.1), channel_id=1, source_target_pairs={{0,128},{128,256},{256,384},{384,0},{1,129},{129,257},{257,385},{3... | collective-permute-start | bytes 2359304 | tf_op jit(solution)/shard_map/ppermute | solution.py:17
  21.7 27.3 %collective-permute-start.2 = (bf16[2,128,1536]{2,1,0:T(8,128)(2,1)}, bf16[2,128,1536]{2,1,0:T(8,128)(2,1)}, u32[]{:S(2)}, u32[]{:S(2)}) collective-permute-start(bf16[2,128,1536]{2,1,0:T(8,128)(2,1)} %pad_maximum_fusion.1), channel_id=1, source_target_pairs={{0,384},{128,0},{256,128},{384,256},{1,385},{129,1},{257,129},{385... | collective-permute-start | bytes 2359304 | tf_op jit(solution)/shard_map/ppermute | solution.py:17
  25.1 34.6 %collective-permute-start.3 = (bf16[2,128,1536]{2,1,0:T(8,128)(2,1)}, bf16[2,128,1536]{2,1,0:T(8,128)(2,1)}, u32[]{:S(2)}, u32[]{:S(2)}) collective-permute-start(bf16[2,128,1536]{2,1,0:T(8,128)(2,1)} %pad_maximum_fusion.1), channel_id=1, source_target_pairs={{0,256},{128,384},{256,0},{384,128},{1,257},{129,385},{257,1},{385... | collective-permute-start | bytes 2359304 | tf_op jit(solution)/shard_map/ppermute | solution.py:17
  32.2 13.4 %collective-permute-start.4 = (bf16[2,192,768]{2,1,0:T(8,128)(2,1)S(1)}, bf16[2,192,768]{2,1,0:T(8,128)(2,1)S(1)}, u32[]{:S(2)}, u32[]{:S(2)}) collective-permute-start(bf16[2,192,768]{2,1,0:T(8,128)(2,1)S(1)} %get-tuple-element.31), channel_id=1, source_target_pairs={{0,64},{64,2},{2,66},{66,0},{1,65},{65,3},{3,67},{67,1},{4,68},{68... | collective-permute-start | bytes 1769480 | tf_op jit(solution)/shard_map/ppermute | solution.py:25
  34.1 14.8 %collective-permute-start.5 = (bf16[2,192,768]{2,1,0:T(8,128)(2,1)S(1)}, bf16[2,192,768]{2,1,0:T(8,128)(2,1)S(1)}, u32[]{:S(2)}, u32[]{:S(2)}) collective-permute-start(bf16[2,192,768]{2,1,0:T(8,128)(2,1)S(1)} %get-tuple-element.30), channel_id=1, source_target_pairs={{0,66},{64,0},{2,64},{66,2},{1,67},{65,1},{3,65},{67,3},{4,70},{68... | collective-permute-start | bytes 1769480 | tf_op jit(solution)/shard_map/ppermute | solution.py:25
  59.6 22.9 %collective-permute-start.6 = (bf16[1536,768]{1,0:T(8,128)(2,1)S(1)}, bf16[1536,768]{1,0:T(8,128)(2,1)S(1)}, u32[]{:S(2)}, u32[]{:S(2)}) collective-permute-start(bf16[1536,768]{1,0:T(8,128)(2,1)S(1)} %bitcast.151), channel_id=1, source_target_pairs={{0,1},{1,0},{2,3},{3,2},{4,5},{5,4},{6,7},{7,6},{8,9},{9,8},{10,11... | collective-permute-start | bytes 7077896 | tf_op jit(solution)/shard_map/ppermute | solution.py:17
  80.0 10.3 %collective-permute-start.7 = (bf16[512,1536]{1,0:T(8,128)(2,1)}, bf16[512,1536]{1,0:T(8,128)(2,1)S(1)}, u32[]{:S(2)}, u32[]{:S(2)}) collective-permute-start(bf16[512,1536]{1,0:T(8,128)(2,1)} %get-tuple-element.36), channel_id=1, source_target_pairs={{0,1},{1,0},{2,3},{3,2},{4,5},{5,4},{6,7},{7,6},{8,9},{9,8},{10,11... | collective-permute-start | bytes 4718600 | tf_op jit(solution)/shard_map/ppermute | solution.py:17
  87.1 3.2 %copy-start.1 = (bf16[512,1536]{1,0:T(8,128)(2,1)}, bf16[512,1536]{1,0:T(8,128)(2,1)S(1)}, u32[]{:S(2)}) copy-start(bf16[512,1536]{1,0:T(8,128)(2,1)S(1)} %multiply_convert_fusion) | copy-start | bytes 4718596
  96.3 7.9 %copy-start.6 = (bf16[512,1536]{1,0:T(8,128)(2,1)}, bf16[512,1536]{1,0:T(8,128)(2,1)S(1)}, u32[]{:S(2)}) copy-start(bf16[512,1536]{1,0:T(8,128)(2,1)S(1)} %subtract_convert_fusion) | copy-start | bytes 4718596
  98.9 7.9 %collective-permute-start.8 = (bf16[384,768]{1,0:T(8,128)(2,1)}, bf16[384,768]{1,0:T(8,128)(2,1)}, u32[]{:S(2)}, u32[]{:S(2)}) collective-permute-start(bf16[384,768]{1,0:T(8,128)(2,1)} %convolution_convert_fusion), channel_id=1, source_target_pairs={{0,1},{1,0},{2,3},{3,2},{4,5},{5,4},{6,7},{7,6},{8,9},{9,8},{10,11... | collective-permute-start | bytes 1769480 | tf_op jit(solution)/shard_map/ppermute | solution.py:17
  104.2 2.6 %copy-start.5 = (f32[512,1536]{1,0:T(8,128)}, f32[512,1536]{1,0:T(8,128)S(1)}, u32[]{:S(2)}) copy-start(f32[512,1536]{1,0:T(8,128)S(1)} %fusion.94) | copy-start | bytes 9437188
  108.8 15.7 %copy-start.2 = (bf16[512,1536]{1,0:T(8,128)(2,1)S(1)}, bf16[512,1536]{1,0:T(8,128)(2,1)}, u32[]{:S(2)}) copy-start(bf16[512,1536]{1,0:T(8,128)(2,1)} %copy-done.1) | copy-start | bytes 4718596
  126.7 15.3 %collective-permute-start.9 = (f32[128,1536]{1,0:T(8,128)}, f32[128,1536]{1,0:T(8,128)}, u32[]{:S(2)}, u32[]{:S(2)}) collective-permute-start(f32[128,1536]{1,0:T(8,128)} %fusion.72), channel_id=1, source_target_pairs={{0,1},{1,0},{2,3},{3,2},{4,5},{5,4},{6,7},{7,6},{8,9},{9,8},{10,11... | collective-permute-start | bytes 2359304 | tf_op jit(solution)/shard_map/ppermute | solution.py:17
  130.3 10.8 %all-to-all-start.2 = ((bf16[4,24,896]{2,1,0:T(8,128)(2,1)}), bf16[4,24,896]{2,1,0:T(8,128)(2,1)}, u32[]{:S(2)}, u32[]{:S(2)}) async-start(bf16[4,24,896]{2,1,0:T(8,128)(2,1)} %bitcast.157), calls=%async_computation.2 | async-start | bytes 344064 | tf_op jit(solution)/shard_map/all_to_all | solution.py:165
  142.1 2.1 %copy-start.3 = (f32[512,1536]{1,0:T(8,128)S(1)}, f32[512,1536]{1,0:T(8,128)}, u32[]{:S(2)}) copy-start(f32[512,1536]{1,0:T(8,128)} %get-tuple-element.29) | copy-start | bytes 9437188
  143.8 1.9 copy-start.4
  146.2 33.1 %collective-permute-start.10 = (bf16[2,128,1536]{2,1,0:T(8,128)(2,1)S(1)}, bf16[2,128,1536]{2,1,0:T(8,128)(2,1)S(1)}, u32[]{:S(2)}, u32[]{:S(2)}) collective-permute-start(bf16[2,128,1536]{2,1,0:T(8,128)(2,1)S(1)} %pad_maximum_fusion.2), channel_id=1, source_target_pairs={{0,0},{1,64},{64,1},{65,65},{2,2},{3,66},{66,3},{67,67},{4,4},{5,6... | collective-permute-start | bytes 2359304 | tf_op jit(solution)/shard_map/ppermute | solution.py:29
  180.0 14.3 %all-to-all-start.4 = ((bf16[8,24,896]{2,1,0:T(8,128)(2,1)}), bf16[8,24,896]{2,1,0:T(8,128)(2,1)S(1)}, u32[]{:S(2)}, u32[]{:S(2)}) async-start(bf16[8,24,896]{2,1,0:T(8,128)(2,1)} %broadcast_in_dim.29), calls=%async_computation.4 | async-start | bytes 688128 | tf_op jit(solution)/shard_map/all_to_all | solution.py:47
  194.3 3.5 %collective-permute-start.11 = (bf16[8,24,896]{2,1,0:T(8,128)(2,1)S(1)}, bf16[8,24,896]{2,1,0:T(8,128)(2,1)S(1)}, u32[]{:S(2)}, u32[]{:S(2)}) collective-permute-start(bf16[8,24,896]{2,1,0:T(8,128)(2,1)S(1)} %all-to-all-done.4), channel_id=1, source_target_pairs={{0,1},{1,0},{2,3},{3,2},{4,5},{5,4},{6,7},{7,6},{8,9},{9,8},{10,11... | collective-permute-start | bytes 1032200 | tf_op jit(solution)/shard_map/ppermute | solution.py:17
  (1 other events, 0.8 us)

commit v8 on v7

--- a/solution.py
+++ b/solution.py
@@ -1,6 +1,8 @@
 import jax
 import jax.numpy as jnp
 from jax import lax
+from jax.experimental import pallas as pl
+from jax.experimental.pallas import tpu as pltpu
 from jax.sharding import Mesh, PartitionSpec as P
 
 epsilon = 1e-06
@@ -65,20 +67,36 @@
     return weight
 
 
-def placed(blocks):
-    rows, width = blocks[0].shape
-    whole = lax.optimization_barrier(jnp.zeros((len(blocks) * rows, width), blocks[0].dtype))
-    for index, block in enumerate(blocks):
-        whole = lax.dynamic_update_slice(whole, block, (index * rows, 0))
-    return whole
-
-
-def standardize(block):
-    values = block.astype(f32)
-    centre = jnp.mean(values, axis=1, keepdims=True)
-    centered = values - centre
-    spread = jnp.mean(centered * centered, axis=1, keepdims=True)
-    return centre, lax.rsqrt(spread + epsilon)
+def place_kernel(own, below, above, far, gain, bias, text, normed, xhat):
+    rows = own.shape[1]
+    lines = 32
+    for index, block in enumerate((own, below, above, far)):
+
+        def body(step, carry, index=index, block=block):
+            start = pl.multiple_of(step * lines, lines)
+            source, target = pl.ds(start, lines), pl.ds(index * rows + start, lines)
+            text[target, :] = block[0, source, :]
+            values = block[1, source, :].astype(f32)
+            centered = values - jnp.mean(values, axis=1, keepdims=True)
+            spread = jnp.mean(centered * centered, axis=1, keepdims=True)
+            standard = centered * lax.rsqrt(spread + epsilon)
+            xhat[target, :] = standard
+            normed[target, :] = (standard * gain[...] + bias[...]).astype(bf16)
+            return carry
+
+        lax.fori_loop(0, rows // lines, body, 0)
+
+
+def place(blocks, gain, bias):
+    rows, width = blocks[0].shape[1:]
+    shape = (len(blocks) * rows, width)
+    return pl.pallas_call(
+        place_kernel,
+        out_shape=[jax.ShapeDtypeStruct(shape, t) for t in (bf16, bf16, f32)],
+        in_specs=[pl.BlockSpec(memory_space=pltpu.VMEM)] * 6,
+        out_specs=[pl.BlockSpec(memory_space=pltpu.VMEM)] * 3,
+        compiler_params=pltpu.CompilerParams(vmem_limit_bytes=40 * 2**20),
+    )(*blocks, gain.reshape(1, width), bias.reshape(1, width))
 
 
 def local(
@@ -91,9 +109,12 @@
     half = width // 2
     block = width // 4
 
+    weight_part = lax.dynamic_slice(head_weight, (0, core * half), (head_weight.shape[0], half))
+    weight_part, text_embed, image_features = lax.optimization_barrier(
+        (jnp.broadcast_to(weight_part[None], (4,) + weight_part.shape), text_embed, image_features)
+    )
+    weight_blocks = lax.all_to_all(weight_part, "y", split_axis=0, concat_axis=0, tiled=True)
     text_rows, feature_rows = swap(jnp.stack([text_embed, image_features], 0))
-    weight_part = lax.dynamic_slice(head_weight, (0, core * half), (head_weight.shape[0], half))
-    weight_blocks = spread_to(weight_part, "y")
 
     text_values = text_rows.astype(f32)
     inv_text = lax.rsqrt(jnp.sum(text_values * text_values, axis=1, keepdims=True) + epsilon)
@@ -102,15 +123,7 @@
     pair = jnp.stack([text_unit, feature_rows], 0)
     below, above, far = shift(pair, "y", 1), shift(pair, "y", -1), shift(pair, "y", 2)
     weight = gather_weight(weight_blocks, xl, core, [below, above, far])
-    text_same = placed([text_unit, below[0], above[0], far[0]])
-    raw = [feature_rows, below[1], above[1], far[1]]
-    stats = [standardize(block) for block in raw]
-    normed = placed(
-        [
-            ((block.astype(f32) - centre) * inverse * final_norm_gain + final_norm_bias).astype(bf16)
-            for block, (centre, inverse) in zip(raw, stats)
-        ]
-    )
+    text_same, normed, xhat = place([pair, below, above, far], final_norm_gain, final_norm_bias)
     text_other = shift(text_same, "core", 1)
     rows = normed.shape[0]
 
@@ -140,22 +153,23 @@
     lanes = 128
 
     grad_normed = dot(grad_proj, weight, 1, 1)
-    centre = jnp.concatenate([part[0] for part in stats], 0)
-    inverse_deviation = jnp.concatenate([part[1] for part in stats], 0)
-    xhat = (placed(raw).astype(f32) - centre) * inverse_deviation
     vectors = jnp.stack([jnp.sum(grad_normed * xhat, axis=0), jnp.sum(grad_normed, axis=0)], 0)
-    xhat, grad_normed, inverse_deviation = xhat[:own], grad_normed[:own], inverse_deviation[:own]
+    xhat, grad_normed = xhat[:own], grad_normed[:own]
+    values = feature_rows.astype(f32)
+    centered = values - jnp.mean(values, axis=1, keepdims=True)
+    inverse_deviation = lax.rsqrt(jnp.mean(centered * centered, axis=1, keepdims=True) + epsilon)
 
     lines = part // 4
     count = width // 4 // lanes
     side = vectors.astype(bf16).reshape(1, 2, 4, count, lanes)
     side = jnp.pad(side, ((0, 0), (0, 0), (0, 0), (0, lines - count), (0, 0)))
     side = jnp.broadcast_to(side, (2,) + side.shape[1:]).reshape(4, part, lanes)
-    sent = jnp.concatenate([head.astype(bf16).reshape(4, part, half), side], -1)
+    head = head.astype(bf16)
+    held = after((weights_same, weights_other, image_unit), head)
+    sent = jnp.concatenate([head.reshape(4, part, half), side], -1)
     received = lax.all_to_all(sent, ("xl", "xh"), split_axis=0, concat_axis=0, tiled=True)
     head = jnp.sum(received.astype(f32), axis=0).astype(bf16)
 
-    held = after((weights_same, weights_other, image_unit), head)
     text_part, text_theirs = (
         dot(w[:, :own], held[2], 0, 0) for w in held[:2]
     )
@@ -176,7 +190,7 @@
     returned = swap(jnp.stack([grad_features, grad_text], 0).astype(bf16))
 
     received = spread_to(sent, "zh")
-    sent = after(jnp.sum(received.astype(f32), axis=0).astype(bf16), returned)
+    sent = jnp.sum(received.astype(f32), axis=0).astype(bf16)
     mine = spread_to(sent, ("zl", "xh"))
     theirs = shift(mine, "core", 1)
 

time: 202 us -> 194 us (0.960)
  blocking collectives: 41.9 us -> 14 us
  other arithmetic: 30.5 us -> 9.39 us
  starting transfers between devices: 56.9 us -> 77.2 us
  waiting for transfers between devices: 32.6 us -> 49.2 us
  local copies, waits for them, and re-layouts: 12.9 us -> 17.8 us
  matrix products: 23 us -> 18.6 us
  Pallas kernels: 0 us -> 3.46 us
    all_to_all x1 -> x0, blocking collectives: 28.1 us -> none  [spread_to(): return lax.all_to_all(many, axes, split_axis=0, concat_axis=0, tiled=True)]
    ppermute x8, waiting for transfers between devices: 10.9 us -> 21 us  [shift(): lax.ppermute(value, axis, [(i, (i + steps) % count) for i in range(count)])]
    reduce_sum x10 -> x2, other arithmetic: 10.2 us -> 0.4 us  [the longest x1 0.27 us: local(): jnp.mean(centered * centered, axis=1, keepdims=True) + epsilon]
    dynamic_update_slice x5 -> x0, other arithmetic: 8.89 us -> none  [placed(): whole = lax.dynamic_update_slice(whole, block, (index * rows, 0))]
    all_to_all x0 -> x1, waiting for transfers between devices: none -> 8.25 us  [local(): lax.all_to_all(weight_part, 'y', split_axis=0, concat_axis=0, tiled=True)]
    ppermute x2, waiting for transfers between devices: 8.59 us -> 0.66 us  [shift_x(): lax.ppermute(value, ('xl', 'xh'), [(index(i), index(i + steps)) for i in...]
    all_to_all x2, starting transfers between devices: 9.26 us -> 16.7 us  [spread_to(): return lax.all_to_all(many, axes, split_axis=0, concat_axis=0, tiled=True)]
    ppermute x8, starting transfers between devices: 26.2 us -> 32 us  [shift(): lax.ppermute(value, axis, [(i, (i + steps) % count) for i in range(count)])]
  transfers between devices with their start and end apart: 15 -> 16, of which waited for: 7 -> 10; matrix products, arithmetic and copies ran while one was open for 21% -> 15% of each run, Pallas kernels for 0% -> 2%
where the time goes in v8:
time: 194 us; the launch traced here: 192 us
  starting transfers between devices  77.2 us (40%)
  waiting for transfers between devices  49.2 us (25%)
  matrix products  18.6 us (10%)
  local copies, waits for them, and re-layouts  17.8 us (9%)
  blocking collectives  14 us (7%)
  other arithmetic  9.39 us (5%)
  Pallas kernels  3.46 us (2%)
  between operations  2.5 us (1%)
    ppermute x8, starting transfers between devices, shift(): lax.ppermute(value, axis, [(i, (i + steps) % count) for i in range(count)])  32 us
    ppermute x8, waiting for transfers between devices, shift(): lax.ppermute(value, axis, [(i, (i + steps) % count) for i in range(count)])  21 us
    dot_general x10, matrix products, dot(): lax.dot_general(a, b, (((da,), (db,)), ((), ())), preferred_element_type=...  18.6 us
    all_to_all x2, starting transfers between devices, spread_to(): return lax.all_to_all(many, axes, split_axis=0, concat_axis=0, tiled=True)  16.7 us
    all_to_all x1, blocking collectives, local(): lax.all_to_all(sent, ('xl', 'xh'), split_axis=0, concat_axis=0, tiled=True)  14 us
    all_to_all x2, waiting for transfers between devices, spread_to(): return lax.all_to_all(many, axes, split_axis=0, concat_axis=0, tiled=True)  12.6 us
    ppermute x2, starting transfers between devices, swap(): return lax.ppermute(value, ('xl', 'core'), [(0, 0), (1, 2), (2, 1), (3, 3)])  12.1 us
    all_to_all x1, waiting for transfers between devices, local(): lax.all_to_all(weight_part, 'y', split_axis=0, concat_axis=0, tiled=True)  8.25 us
  transfers between devices with their start and end apart: 16, of which 10 were waited for; matrix products, arithmetic and copies ran while one was open for 15% of the time, Pallas kernels for 2%

profile of v8, /device:TPU:1, one launch (start us, length us, event | category | flops | bytes accessed | tf_op | source)
XLA Modules:
  0.0 192.1 jit_solution(10894953742940660187)
XLA Ops:
  2.9 4.5 %collective-permute-start = (bf16[2,128,1536]{2,1,0:T(8,128)(2,1)S(1)}, bf16[2,128,1536]{2,1,0:T(8,128)(2,1)S(1)}, u32[]{:S(2)}, u32[]{:S(2)}) collective-permute-start(bf16[2,128,1536]{2,1,0:T(8,128)(2,1)S(1)} %pad_maximum_fusion), channel_id=1, source_target_pairs={{0,0},{1,64},{64,1},{65,65},{2,2},{3,66},{66,3},{67,67},{4,4},{5,6... | collective-permute-start | bytes 2359304 | tf_op jit(solution)/shard_map/ppermute | solution.py:31
  7.4 4.2 %all-to-all-start = ((bf16[4,192,768]{2,1,0:T(8,128)(2,1)}), bf16[4,192,768]{2,1,0:T(8,128)(2,1)S(1)}, u32[]{:S(2)}, u32[]{:S(2)}) async-start(bf16[4,192,768]{2,1,0:T(8,128)(2,1)} %broadcast_in_dim.20), calls=%async_computation | async-start | bytes 2359296 | tf_op jit(solution)/shard_map/all_to_all | solution.py:116
  11.6 5.5 %collective-permute-done = bf16[2,128,1536]{2,1,0:T(8,128)(2,1)S(1)} collective-permute-done((bf16[2,128,1536]{2,1,0:T(8,128)(2,1)S(1)}, bf16[2,128,1536]{2,1,0:T(8,128)(2,1)S(1)}, u32[]{:S(2)}, u32[]{:S(2)}) %collective-permute-start) | collective-permute-done | bytes 786464 | tf_op jit(solution)/shard_map/ppermute | solution.py:31
  17.5 8.3 %all-to-all-done = bf16[4,192,768]{2,1,0:T(8,128)(2,1)S(1)} async-done(((bf16[4,192,768]{2,1,0:T(8,128)(2,1)}), bf16[4,192,768]{2,1,0:T(8,128)(2,1)S(1)}, u32[]{:S(2)}, u32[]{:S(2)}) %all-to-all-start) | async-done | bytes 1179680 | tf_op jit(solution)/shard_map/all_to_all | solution.py:116
  28.0 4.6 %collective-permute-start.5 = (bf16[2,192,768]{2,1,0:T(8,128)(2,1)S(1)}, bf16[2,192,768]{2,1,0:T(8,128)(2,1)S(1)}, u32[]{:S(2)}, u32[]{:S(2)}) collective-permute-start(bf16[2,192,768]{2,1,0:T(8,128)(2,1)S(1)} %get-tuple-element.39), channel_id=1, source_target_pairs={{0,66},{64,0},{2,64},{66,2},{1,67},{65,1},{3,65},{67,3},{4,70},{68... | collective-permute-start | bytes 1769480 | tf_op jit(solution)/shard_map/ppermute | solution.py:27
  32.6 2.3 %collective-permute-start.1 = (bf16[2,128,1536]{2,1,0:T(8,128)(2,1)S(1)}, bf16[2,128,1536]{2,1,0:T(8,128)(2,1)S(1)}, u32[]{:S(2)}, u32[]{:S(2)}) collective-permute-start(bf16[2,128,1536]{2,1,0:T(8,128)(2,1)S(1)} %pad_maximum_fusion.1.own), channel_id=1, source_target_pairs={{0,128},{128,256},{256,384},{384,0},{1,129},{129,257},{257,385},{3... | collective-permute-start | bytes 2359304 | tf_op jit(solution)/shard_map/ppermute | solution.py:19
  35.0 4.3 %collective-permute-start.2 = (bf16[2,128,1536]{2,1,0:T(8,128)(2,1)S(1)}, bf16[2,128,1536]{2,1,0:T(8,128)(2,1)S(1)}, u32[]{:S(2)}, u32[]{:S(2)}) collective-permute-start(bf16[2,128,1536]{2,1,0:T(8,128)(2,1)S(1)} %pad_maximum_fusion.1.own), channel_id=1, source_target_pairs={{0,384},{128,0},{256,128},{384,256},{1,385},{129,1},{257,129},{385... | collective-permute-start | bytes 2359304 | tf_op jit(solution)/shard_map/ppermute | solution.py:19
  46.3 5.3 %collective-permute-done.1.below = bf16[2,128,1536]{2,1,0:T(8,128)(2,1)S(1)} collective-permute-done((bf16[2,128,1536]{2,1,0:T(8,128)(2,1)S(1)}, bf16[2,128,1536]{2,1,0:T(8,128)(2,1)S(1)}, u32[]{:S(2)}, u32[]{:S(2)}) %collective-permute-start.1) | collective-permute-done | bytes 786464 | tf_op jit(solution)/shard_map/ppermute | solution.py:19
  52.6 14.7 %collective-permute-done.3.far = bf16[2,128,1536]{2,1,0:T(8,128)(2,1)S(1)} collective-permute-done((bf16[2,128,1536]{2,1,0:T(8,128)(2,1)S(1)}, bf16[2,128,1536]{2,1,0:T(8,128)(2,1)S(1)}, u32[]{:S(2)}, u32[]{:S(2)}) %collective-permute-start.3) | collective-permute-done | bytes 786464 | tf_op jit(solution)/shard_map/ppermute | solution.py:19
  68.2 8.5 %collective-permute-start.6 = (bf16[1536,768]{1,0:T(8,128)(2,1)}, bf16[1536,768]{1,0:T(8,128)(2,1)}, u32[]{:S(2)}, u32[]{:S(2)}) collective-permute-start(bf16[1536,768]{1,0:T(8,128)(2,1)} %bitcast.10), channel_id=1, source_target_pairs={{0,1},{1,0},{2,3},{3,2},{4,5},{5,4},{6,7},{7,6},{8,9},{9,8},{10,11... | collective-permute-start | bytes 7077896 | tf_op jit(solution)/shard_map/ppermute | solution.py:19
  79.2 3.5 %shard_map.110 = (bf16[512,1536]{1,0:T(8,128)(2,1)S(1)}, bf16[512,1536]{1,0:T(8,128)(2,1)S(1)}, f32[512,1536]{1,0:T(8,128)S(1)}) custom-call(bf16[2,128,1536]{2,1,0:T(8,128)(2,1)S(1)} %pad_maximum_fusion.1.own, bf16[2,128,1536]{2,1,0:T(8,128)(2,1)S(1)} %collective-permute-done.1.below, bf16[2,128,1536]{2,1,0:T(8,128)(2,1)S(1)} %collective-permute-done.2.above, ...), custom_call_target="tpu_custom_call" | custom-call | tf_op jit(solution)/shard_map/pallas_call | solution.py:93
  88.8 2.7 %multiply_reduce_fusion.2 = (f32[512]{0:T(512)S(1)}, f32[512,1536]{1,0:T(8,128)S(1)}) fusion(bf16[512,1536]{1,0:T(8,128)(2,1)S(1)} %get-tuple-element.21, bf16[1536,1536]{1,0:T(8,128)(2,1)S(1)} %constant_dynamic-update-slice_fusion), kind=kOutput, calls=%fused_computation.6 | convolution fusion | flops 2417491456 | bytes 9439232 | tf_op jit(solution)/shard_map/dot_general | solution.py:43
  98.2 2.6 %collective-permute-start.8 = (bf16[384,768]{1,0:T(8,128)(2,1)}, bf16[384,768]{1,0:T(8,128)(2,1)}, u32[]{:S(2)}, u32[]{:S(2)}) collective-permute-start(bf16[384,768]{1,0:T(8,128)(2,1)} %convolution_convert_fusion), channel_id=1, source_target_pairs={{0,1},{1,0},{2,3},{3,2},{4,5},{5,4},{6,7},{7,6},{8,9},{9,8},{10,11... | collective-permute-start | bytes 1769480 | tf_op jit(solution)/shard_map/ppermute | solution.py:19
  100.8 4.3 %multiply_reduce_fusion = (bf16[1536]{0:T(1024)(128)(2,1)S(1)}, bf16[1536]{0:T(1024)(128)(2,1)S(1)}, f32[512,1536]{1,0:T(8,128)}) fusion(f32[512,1536]{1,0:T(8,128)S(1)} %get-tuple-element.30, bf16[512,1536]{1,0:T(8,128)(2,1)S(1)} %subtract_convert_fusion, bf16[1536,1536]{1,0:T(8,128)(2,1)S(1)} %constant_dynamic-update-slice_fusion), kind=kOutput, calls=%fused_computation.2 | convolution fusion | flops 2418275328 | bytes 12589056 | tf_op jit(solution)/shard_map/dot_general | solution.py:43
  105.2 1.9 %fusion.1 = bf16[384,768]{1,0:T(8,128)(2,1)S(1)} fusion(bf16[384,768]{1,0:T(8,128)(2,1)} %collective-permute-done.8, bf16[512,1536]{1,0:T(8,128)(2,1)} %copy-done.11, s32[]{:T(128)S(6)} %select_n.27, bf16[512,1536]{1,0:T(8,128)(2,1)} %copy-done.4, s32[]{:T(128)S(6)} %select_n.31), kind=kOutput, calls=%fused_computation.11 | convolution fusion | flops 302874624 | bytes 2359304 | tf_op jit(solution)/shard_map/dot_general | solution.py:43
  110.4 14.0 %all_to_all.25 = bf16[4,96,896]{2,1,0:T(8,128)(2,1)S(1)} all-to-all(bf16[4,96,896]{2,1,0:T(8,128)(2,1)S(1)} %pad_maximum_fusion.3), channel_id=1, replica_groups=mesh['y'=4,'xl'=2,'zh'=4,'zl'=4,'xh'=2,'core'=2] {'xl','xh'}, dimensions={0} | all-to-all | bytes 1376256 | tf_op jit(solution)/shard_map/all_to_all | solution.py:170
  125.2 5.6 %all-to-all-start.2 = ((bf16[4,24,896]{2,1,0:T(8,128)(2,1)}), bf16[4,24,896]{2,1,0:T(8,128)(2,1)}, u32[]{:S(2)}, u32[]{:S(2)}) async-start(bf16[4,24,896]{2,1,0:T(8,128)(2,1)} %bitcast.92), calls=%async_computation.2 | async-start | bytes 344064 | tf_op jit(solution)/shard_map/all_to_all | solution.py:179
  130.8 2.1 %slice.60 = f32[128,1536]{1,0:T(8,128)} slice(f32[512,1536]{1,0:T(8,128)} %get-tuple-element.49), slice={[0:128], [0:1536]} | slice | bytes 1572864 | tf_op jit(solution)/shard_map/slice | solution.py:157
  132.9 2.5 %convolution_add_fusion.1 = f32[128,1536]{1,0:T(8,128)} fusion(f32[128,1536]{1,0:T(8,128)} %collective-permute-done.9, bf16[512,1536]{1,0:T(8,128)(2,1)S(1)} %multiply_convert_fusion, bf16[512,512]{1,0:T(8,128)(2,1)S(1)} %fusion.15), kind=kOutput, calls=%fused_computation.7 | convolution fusion | flops 201523200 | bytes 3276800 | tf_op jit(solution)/shard_map/dot_general | solution.py:43
  137.5 13.3 %all-to-all-start.3 = ((bf16[4,24,896]{2,1,0:T(8,128)(2,1)}), bf16[4,24,896]{2,1,0:T(8,128)(2,1)S(1)}, u32[]{:S(2)}, u32[]{:S(2)}) async-start(bf16[4,24,896]{2,1,0:T(8,128)(2,1)} %broadcast_in_dim.28), calls=%async_computation.3 | async-start | bytes 344064 | tf_op jit(solution)/shard_map/all_to_all | solution.py:49
  154.1 11.4 %all-to-all-done.3 = bf16[4,24,896]{2,1,0:T(8,128)(2,1)S(1)} async-done(((bf16[4,24,896]{2,1,0:T(8,128)(2,1)}), bf16[4,24,896]{2,1,0:T(8,128)(2,1)S(1)}, u32[]{:S(2)}, u32[]{:S(2)}) %all-to-all-start.3) | async-done | bytes 172064 | tf_op jit(solution)/shard_map/all_to_all | solution.py:49
  166.3 3.4 %all-to-all-start.4 = ((bf16[8,24,896]{2,1,0:T(8,128)(2,1)}), bf16[8,24,896]{2,1,0:T(8,128)(2,1)S(1)}, u32[]{:S(2)}, u32[]{:S(2)}) async-start(bf16[8,24,896]{2,1,0:T(8,128)(2,1)} %broadcast_in_dim.58), calls=%async_computation.4 | async-start | bytes 688128 | tf_op jit(solution)/shard_map/all_to_all | solution.py:49
  170.1 7.6 %collective-permute-start.10 = (bf16[2,128,1536]{2,1,0:T(8,128)(2,1)S(1)}, bf16[2,128,1536]{2,1,0:T(8,128)(2,1)S(1)}, u32[]{:S(2)}, u32[]{:S(2)}) collective-permute-start(bf16[2,128,1536]{2,1,0:T(8,128)(2,1)S(1)} %pad_maximum_fusion.2), channel_id=1, source_target_pairs={{0,0},{1,64},{64,1},{65,65},{2,2},{3,66},{66,3},{67,67},{4,4},{5,6... | collective-permute-start | bytes 2359304 | tf_op jit(solution)/shard_map/ppermute | solution.py:31
  178.9 8.6 %collective-permute-start.11 = (bf16[8,24,896]{2,1,0:T(8,128)(2,1)S(1)}, bf16[8,24,896]{2,1,0:T(8,128)(2,1)S(1)}, u32[]{:S(2)}, u32[]{:S(2)}) collective-permute-start(bf16[8,24,896]{2,1,0:T(8,128)(2,1)S(1)} %all-to-all-done.4), channel_id=1, source_target_pairs={{0,1},{1,0},{2,3},{3,2},{4,5},{5,4},{6,7},{7,6},{8,9},{9,8},{10,11... | collective-permute-start | bytes 1032200 | tf_op jit(solution)/shard_map/ppermute | solution.py:19
  (105 shorter events, 44.0 us)
Async XLA Ops:
  2.9 14.2 %collective-permute-start = (bf16[2,128,1536]{2,1,0:T(8,128)(2,1)S(1)}, bf16[2,128,1536]{2,1,0:T(8,128)(2,1)S(1)}, u32[]{:S(2)}, u32[]{:S(2)}) collective-permute-start(bf16[2,128,1536]{2,1,0:T(8,128)(2,1)S(1)} %pad_maximum_fusion), channel_id=1, source_target_pairs={{0,0},{1,64},{64,1},{65,65},{2,2},{3,66},{66,3},{67,67},{4,4},{5,6... | collective-permute-start | bytes 2359304 | tf_op jit(solution)/shard_map/ppermute | solution.py:31
  7.4 18.3 %all-to-all-start = ((bf16[4,192,768]{2,1,0:T(8,128)(2,1)}), bf16[4,192,768]{2,1,0:T(8,128)(2,1)S(1)}, u32[]{:S(2)}, u32[]{:S(2)}) async-start(bf16[4,192,768]{2,1,0:T(8,128)(2,1)} %broadcast_in_dim.20), calls=%async_computation | async-start | bytes 2359296 | tf_op jit(solution)/shard_map/all_to_all | solution.py:116
  17.1 10.8 %copy-start.7 = (bf16[2,128,1536]{2,1,0:T(8,128)(2,1)}, bf16[2,128,1536]{2,1,0:T(8,128)(2,1)S(1)}, u32[]{:S(2)}) copy-start(bf16[2,128,1536]{2,1,0:T(8,128)(2,1)S(1)} %collective-permute-done) | copy-start | bytes 2359300
  25.8 18.1 %collective-permute-start.4 = (bf16[2,192,768]{2,1,0:T(8,128)(2,1)S(1)}, bf16[2,192,768]{2,1,0:T(8,128)(2,1)S(1)}, u32[]{:S(2)}, u32[]{:S(2)}) collective-permute-start(bf16[2,192,768]{2,1,0:T(8,128)(2,1)S(1)} %get-tuple-element.40), channel_id=1, source_target_pairs={{0,64},{64,2},{2,66},{66,0},{1,65},{65,3},{3,67},{67,1},{4,68},{68... | collective-permute-start | bytes 1769480 | tf_op jit(solution)/shard_map/ppermute | solution.py:27
  28.0 17.5 %collective-permute-start.5 = (bf16[2,192,768]{2,1,0:T(8,128)(2,1)S(1)}, bf16[2,192,768]{2,1,0:T(8,128)(2,1)S(1)}, u32[]{:S(2)}, u32[]{:S(2)}) collective-permute-start(bf16[2,192,768]{2,1,0:T(8,128)(2,1)S(1)} %get-tuple-element.39), channel_id=1, source_target_pairs={{0,66},{64,0},{2,64},{66,2},{1,67},{65,1},{3,65},{67,3},{4,70},{68... | collective-permute-start | bytes 1769480 | tf_op jit(solution)/shard_map/ppermute | solution.py:27
  32.6 19.0 %collective-permute-start.1 = (bf16[2,128,1536]{2,1,0:T(8,128)(2,1)S(1)}, bf16[2,128,1536]{2,1,0:T(8,128)(2,1)S(1)}, u32[]{:S(2)}, u32[]{:S(2)}) collective-permute-start(bf16[2,128,1536]{2,1,0:T(8,128)(2,1)S(1)} %pad_maximum_fusion.1.own), channel_id=1, source_target_pairs={{0,128},{128,256},{256,384},{384,0},{1,129},{129,257},{257,385},{3... | collective-permute-start | bytes 2359304 | tf_op jit(solution)/shard_map/ppermute | solution.py:19
  35.0 17.7 %collective-permute-start.2 = (bf16[2,128,1536]{2,1,0:T(8,128)(2,1)S(1)}, bf16[2,128,1536]{2,1,0:T(8,128)(2,1)S(1)}, u32[]{:S(2)}, u32[]{:S(2)}) collective-permute-start(bf16[2,128,1536]{2,1,0:T(8,128)(2,1)S(1)} %pad_maximum_fusion.1.own), channel_id=1, source_target_pairs={{0,384},{128,0},{256,128},{384,256},{1,385},{129,1},{257,129},{385... | collective-permute-start | bytes 2359304 | tf_op jit(solution)/shard_map/ppermute | solution.py:19
  39.3 28.0 %collective-permute-start.3 = (bf16[2,128,1536]{2,1,0:T(8,128)(2,1)S(1)}, bf16[2,128,1536]{2,1,0:T(8,128)(2,1)S(1)}, u32[]{:S(2)}, u32[]{:S(2)}) collective-permute-start(bf16[2,128,1536]{2,1,0:T(8,128)(2,1)S(1)} %pad_maximum_fusion.1.own), channel_id=1, source_target_pairs={{0,256},{128,384},{256,0},{384,128},{1,257},{129,385},{257,1},{385... | collective-permute-start | bytes 2359304 | tf_op jit(solution)/shard_map/ppermute | solution.py:19
  43.9 32.8 %copy-start.14 = (f32[1536]{0:T(1024)S(1)}, f32[1536]{0:T(1024)}, u32[]{:S(2)}) copy-start(f32[1536]{0:T(1024)} %param.8) | copy-start | bytes 18436
  43.9 32.8 %copy-start.15 = (f32[1536]{0:T(1024)S(1)}, f32[1536]{0:T(1024)}, u32[]{:S(2)}) copy-start(f32[1536]{0:T(1024)} %param.9) | copy-start | bytes 18436
  68.2 18.7 %collective-permute-start.6 = (bf16[1536,768]{1,0:T(8,128)(2,1)}, bf16[1536,768]{1,0:T(8,128)(2,1)}, u32[]{:S(2)}, u32[]{:S(2)}) collective-permute-start(bf16[1536,768]{1,0:T(8,128)(2,1)} %bitcast.10), channel_id=1, source_target_pairs={{0,1},{1,0},{2,3},{3,2},{4,5},{5,4},{6,7},{7,6},{8,9},{9,8},{10,11... | collective-permute-start | bytes 7077896 | tf_op jit(solution)/shard_map/ppermute | solution.py:19
  82.7 14.1 %copy-start.4 = (bf16[512,1536]{1,0:T(8,128)(2,1)}, bf16[512,1536]{1,0:T(8,128)(2,1)S(1)}, u32[]{:S(2)}) copy-start(bf16[512,1536]{1,0:T(8,128)(2,1)S(1)} %get-tuple-element.21) | copy-start | bytes 4718596
  82.7 18.1 %copy-start.1 = (f32[512,1536]{1,0:T(8,128)}, f32[512,1536]{1,0:T(8,128)S(1)}, u32[]{:S(2)}) copy-start(f32[512,1536]{1,0:T(8,128)S(1)} %get-tuple-element.30) | copy-start | bytes 9437188
  82.7 10.2 %collective-permute-start.7 = (bf16[512,1536]{1,0:T(8,128)(2,1)S(1)}, bf16[512,1536]{1,0:T(8,128)(2,1)S(1)}, u32[]{:S(2)}, u32[]{:S(2)}) collective-permute-start(bf16[512,1536]{1,0:T(8,128)(2,1)S(1)} %get-tuple-element.24), channel_id=1, source_target_pairs={{0,1},{1,0},{2,3},{3,2},{4,5},{5,4},{6,7},{7,6},{8,9},{9,8},{10,11... | collective-permute-start | bytes 4718600 | tf_op jit(solution)/shard_map/ppermute | solution.py:19
  98.2 7.0 %collective-permute-start.8 = (bf16[384,768]{1,0:T(8,128)(2,1)}, bf16[384,768]{1,0:T(8,128)(2,1)}, u32[]{:S(2)}, u32[]{:S(2)}) collective-permute-start(bf16[384,768]{1,0:T(8,128)(2,1)} %convolution_convert_fusion), channel_id=1, source_target_pairs={{0,1},{1,0},{2,3},{3,2},{4,5},{5,4},{6,7},{7,6},{8,9},{9,8},{10,11... | collective-permute-start | bytes 1769480 | tf_op jit(solution)/shard_map/ppermute | solution.py:19
  108.4 24.5 %collective-permute-start.9 = (f32[128,1536]{1,0:T(8,128)}, f32[128,1536]{1,0:T(8,128)}, u32[]{:S(2)}, u32[]{:S(2)}) collective-permute-start(f32[128,1536]{1,0:T(8,128)} %fusion.36), channel_id=1, source_target_pairs={{0,1},{1,0},{2,3},{3,2},{4,5},{5,4},{6,7},{7,6},{8,9},{9,8},{10,11... | collective-permute-start | bytes 2359304 | tf_op jit(solution)/shard_map/ppermute | solution.py:19
  125.2 10.6 %all-to-all-start.2 = ((bf16[4,24,896]{2,1,0:T(8,128)(2,1)}), bf16[4,24,896]{2,1,0:T(8,128)(2,1)}, u32[]{:S(2)}, u32[]{:S(2)}) async-start(bf16[4,24,896]{2,1,0:T(8,128)(2,1)} %bitcast.92), calls=%async_computation.2 | async-start | bytes 344064 | tf_op jit(solution)/shard_map/all_to_all | solution.py:179
  132.9 17.8 %copy-start.8 = (bf16[2,128,1536]{2,1,0:T(8,128)(2,1)S(1)}, bf16[2,128,1536]{2,1,0:T(8,128)(2,1)}, u32[]{:S(2)}) copy-start(bf16[2,128,1536]{2,1,0:T(8,128)(2,1)} %copy-done.7) | copy-start | bytes 2359300
  137.5 15.2 %copy-start.10 = (f32[128,1536]{1,0:T(8,128)S(1)}, f32[128,1536]{1,0:T(8,128)}, u32[]{:S(2)}) copy-start(f32[128,1536]{1,0:T(8,128)} %slice.60) | copy-start | bytes 2359300
  137.5 28.1 %all-to-all-start.3 = ((bf16[4,24,896]{2,1,0:T(8,128)(2,1)}), bf16[4,24,896]{2,1,0:T(8,128)(2,1)S(1)}, u32[]{:S(2)}, u32[]{:S(2)}) async-start(bf16[4,24,896]{2,1,0:T(8,128)(2,1)} %broadcast_in_dim.28), calls=%async_computation.3 | async-start | bytes 344064 | tf_op jit(solution)/shard_map/all_to_all | solution.py:49
  152.7 17.1 %copy-start.9 = (f32[128,1536]{1,0:T(8,128)S(1)}, f32[128,1536]{1,0:T(8,128)}, u32[]{:S(2)}) copy-start(f32[128,1536]{1,0:T(8,128)} %convolution_add_fusion.1) | copy-start | bytes 2359300
  166.3 12.5 %all-to-all-start.4 = ((bf16[8,24,896]{2,1,0:T(8,128)(2,1)}), bf16[8,24,896]{2,1,0:T(8,128)(2,1)S(1)}, u32[]{:S(2)}, u32[]{:S(2)}) async-start(bf16[8,24,896]{2,1,0:T(8,128)(2,1)} %broadcast_in_dim.58), calls=%async_computation.4 | async-start | bytes 688128 | tf_op jit(solution)/shard_map/all_to_all | solution.py:49
  170.1 18.2 %collective-permute-start.10 = (bf16[2,128,1536]{2,1,0:T(8,128)(2,1)S(1)}, bf16[2,128,1536]{2,1,0:T(8,128)(2,1)S(1)}, u32[]{:S(2)}, u32[]{:S(2)}) collective-permute-start(bf16[2,128,1536]{2,1,0:T(8,128)(2,1)S(1)} %pad_maximum_fusion.2), channel_id=1, source_target_pairs={{0,0},{1,64},{64,1},{65,65},{2,2},{3,66},{66,3},{67,67},{4,4},{5,6... | collective-permute-start | bytes 2359304 | tf_op jit(solution)/shard_map/ppermute | solution.py:31
  178.9 10.8 %collective-permute-start.11 = (bf16[8,24,896]{2,1,0:T(8,128)(2,1)S(1)}, bf16[8,24,896]{2,1,0:T(8,128)(2,1)S(1)}, u32[]{:S(2)}, u32[]{:S(2)}) collective-permute-start(bf16[8,24,896]{2,1,0:T(8,128)(2,1)S(1)} %all-to-all-done.4), channel_id=1, source_target_pairs={{0,1},{1,0},{2,3},{3,2},{4,5},{5,4},{6,7},{7,6},{8,9},{9,8},{10,11... | collective-permute-start | bytes 1032200 | tf_op jit(solution)/shard_map/ppermute | solution.py:19
  (8 other events, 28.0 us)

commit v9 on v8

--- a/solution.py
+++ b/solution.py
@@ -109,12 +109,9 @@
     half = width // 2
     block = width // 4
 
+    text_rows, feature_rows = swap(jnp.stack([text_embed, image_features], 0))
     weight_part = lax.dynamic_slice(head_weight, (0, core * half), (head_weight.shape[0], half))
-    weight_part, text_embed, image_features = lax.optimization_barrier(
-        (jnp.broadcast_to(weight_part[None], (4,) + weight_part.shape), text_embed, image_features)
-    )
-    weight_blocks = lax.all_to_all(weight_part, "y", split_axis=0, concat_axis=0, tiled=True)
-    text_rows, feature_rows = swap(jnp.stack([text_embed, image_features], 0))
+    weight_blocks = spread_to(weight_part, "y")
 
     text_values = text_rows.astype(f32)
     inv_text = lax.rsqrt(jnp.sum(text_values * text_values, axis=1, keepdims=True) + epsilon)
@@ -154,7 +151,6 @@
 
     grad_normed = dot(grad_proj, weight, 1, 1)
     vectors = jnp.stack([jnp.sum(grad_normed * xhat, axis=0), jnp.sum(grad_normed, axis=0)], 0)
-    xhat, grad_normed = xhat[:own], grad_normed[:own]
     values = feature_rows.astype(f32)
     centered = values - jnp.mean(values, axis=1, keepdims=True)
     inverse_deviation = lax.rsqrt(jnp.mean(centered * centered, axis=1, keepdims=True) + epsilon)
@@ -165,21 +161,18 @@
     side = jnp.pad(side, ((0, 0), (0, 0), (0, 0), (0, lines - count), (0, 0)))
     side = jnp.broadcast_to(side, (2,) + side.shape[1:]).reshape(4, part, lanes)
     head = head.astype(bf16)
-    held = after((weights_same, weights_other, image_unit), head)
     sent = jnp.concatenate([head.reshape(4, part, half), side], -1)
     received = lax.all_to_all(sent, ("xl", "xh"), split_axis=0, concat_axis=0, tiled=True)
     head = jnp.sum(received.astype(f32), axis=0).astype(bf16)
 
-    text_part, text_theirs = (
-        dot(w[:, :own], held[2], 0, 0) for w in held[:2]
-    )
-    grad_unit_text = text_part + shift(text_theirs, "core", 1)
-
     sent = head.reshape(4, lines, half + lanes)
     received = lax.all_to_all(sent, "zl", split_axis=0, concat_axis=0, tiled=True)
     sent = jnp.sum(received.astype(f32), axis=0).astype(bf16)
 
-    grad_unit_text, grad_normed = after((grad_unit_text, grad_normed), sent)
+    held = after((weights_same, weights_other, image_unit, grad_normed, xhat), sent)
+    text_part, text_theirs = (dot(w[:, :own], held[2], 0, 0) for w in held[:2])
+    grad_normed, xhat = held[3][:own], held[4][:own]
+    grad_unit_text = text_part + shift(text_theirs, "core", 1)
     grad_unit_text = scale * grad_unit_text
     text_dot = jnp.sum(text_values * grad_unit_text, axis=1, keepdims=True)
     grad_text = inv_text * grad_unit_text - inv_text * inv_text * inv_text * text_dot * text_values

time: 194 us -> 193 us (level)
  waiting for transfers between devices: 49.2 us -> 44.2 us
  starting transfers between devices: 77.2 us -> 80.2 us
  other arithmetic: 9.39 us -> 11.4 us
    all_to_all x1 -> x0, waiting for transfers between devices: 8.25 us -> none  [local(): lax.all_to_all(weight_part, 'y', split_axis=0, concat_axis=0, tiled=True)]
    all_to_all x1 -> x0, starting transfers between devices: 4.2 us -> none  [local(): lax.all_to_all(weight_part, 'y', split_axis=0, concat_axis=0, tiled=True)]
    all_to_all x2 -> x3, starting transfers between devices: 16.7 us -> 20.9 us  [spread_to(): return lax.all_to_all(many, axes, split_axis=0, concat_axis=0, tiled=True)]
    all_to_all x1, waiting for transfers between devices: 0.44 us -> 4.42 us  [local(): lax.all_to_all(sent, 'zl', split_axis=0, concat_axis=0, tiled=True)]
    ppermute x8, starting transfers between devices: 32 us -> 34.6 us  [shift(): lax.ppermute(value, axis, [(i, (i + steps) % count) for i in range(count)])]
    slice x1 -> x0, local copies, waits for them, and re-layouts: 2.07 us -> none  [local(): xhat, grad_normed = (xhat[:own], grad_normed[:own])]
    all_to_all x2 -> x3, waiting for transfers between devices: 12.6 us -> 11.6 us  [spread_to(): return lax.all_to_all(many, axes, split_axis=0, concat_axis=0, tiled=True)]
  transfers between devices with their start and end apart: 16 -> 16, of which waited for: 10 -> 9; matrix products, arithmetic and copies ran while one was open for 15% -> 16% of each run, Pallas kernels for 2% -> 2%
where the time goes in v9:
time: 193 us; the launch traced here: 190 us
  starting transfers between devices  80.2 us (42%)
  waiting for transfers between devices  44.2 us (23%)
  local copies, waits for them, and re-layouts  17 us (9%)
  matrix products  17 us (9%)
  blocking collectives  14.6 us (8%)
  other arithmetic  11.4 us (6%)
  Pallas kernels  3.46 us (2%)
  between operations  2.55 us (1%)
    ppermute x8, starting transfers between devices, shift(): lax.ppermute(value, axis, [(i, (i + steps) % count) for i in range(count)])  34.6 us
    ppermute x8, waiting for transfers between devices, shift(): lax.ppermute(value, axis, [(i, (i + steps) % count) for i in range(count)])  21 us
    all_to_all x3, starting transfers between devices, spread_to(): return lax.all_to_all(many, axes, split_axis=0, concat_axis=0, tiled=True)  20.9 us
    dot_general x10, matrix products, dot(): lax.dot_general(a, b, (((da,), (db,)), ((), ())), preferred_element_type=...  17 us
    all_to_all x1, blocking collectives, local(): lax.all_to_all(sent, ('xl', 'xh'), split_axis=0, concat_axis=0, tiled=True)  14.6 us
    ppermute x2, starting transfers between devices, swap(): return lax.ppermute(value, ('xl', 'core'), [(0, 0), (1, 2), (2, 1), (3, 3)])  12.6 us
    all_to_all x3, waiting for transfers between devices, spread_to(): return lax.all_to_all(many, axes, split_axis=0, concat_axis=0, tiled=True)  11.6 us
    ppermute x2, waiting for transfers between devices, swap(): return lax.ppermute(value, ('xl', 'core'), [(0, 0), (1, 2), (2, 1), (3, 3)])  6.53 us
  transfers between devices with their start and end apart: 16, of which 9 were waited for; matrix products, arithmetic and copies ran while one was open for 16% of the time, Pallas kernels for 2%

profile of v9, /device:TPU:1, one launch (start us, length us, event | category | flops | bytes accessed | tf_op | source)
XLA Modules:
  0.0 190.3 jit_solution(7090890722143926649)
XLA Ops:
  1.9 4.5 %collective-permute-start = (bf16[2,128,1536]{2,1,0:T(8,128)(2,1)S(1)}, bf16[2,128,1536]{2,1,0:T(8,128)(2,1)S(1)}, u32[]{:S(2)}, u32[]{:S(2)}) collective-permute-start(bf16[2,128,1536]{2,1,0:T(8,128)(2,1)S(1)} %pad_maximum_fusion), channel_id=1, source_target_pairs={{0,0},{1,64},{64,1},{65,65},{2,2},{3,66},{66,3},{67,67},{4,4},{5,6... | collective-permute-start | bytes 2359304 | tf_op jit(solution)/shard_map/ppermute | solution.py:31
  7.6 4.2 %all-to-all-start = ((bf16[4,192,768]{2,1,0:T(8,128)(2,1)}), bf16[4,192,768]{2,1,0:T(8,128)(2,1)S(1)}, u32[]{:S(2)}, u32[]{:S(2)}) async-start(bf16[4,192,768]{2,1,0:T(8,128)(2,1)} %broadcast_in_dim.22), calls=%async_computation | async-start | bytes 2359296 | tf_op jit(solution)/shard_map/all_to_all | solution.py:49
  11.7 4.3 %collective-permute-done = bf16[2,128,1536]{2,1,0:T(8,128)(2,1)S(1)} collective-permute-done((bf16[2,128,1536]{2,1,0:T(8,128)(2,1)S(1)}, bf16[2,128,1536]{2,1,0:T(8,128)(2,1)S(1)}, u32[]{:S(2)}, u32[]{:S(2)}) %collective-permute-start) | collective-permute-done | bytes 786464 | tf_op jit(solution)/shard_map/ppermute | solution.py:31
  17.1 8.8 %all-to-all-done = bf16[4,192,768]{2,1,0:T(8,128)(2,1)S(1)} async-done(((bf16[4,192,768]{2,1,0:T(8,128)(2,1)}), bf16[4,192,768]{2,1,0:T(8,128)(2,1)S(1)}, u32[]{:S(2)}, u32[]{:S(2)}) %all-to-all-start) | async-done | bytes 1179680 | tf_op jit(solution)/shard_map/all_to_all | solution.py:49
  28.1 4.6 %collective-permute-start.5 = (bf16[2,192,768]{2,1,0:T(8,128)(2,1)S(1)}, bf16[2,192,768]{2,1,0:T(8,128)(2,1)S(1)}, u32[]{:S(2)}, u32[]{:S(2)}) collective-permute-start(bf16[2,192,768]{2,1,0:T(8,128)(2,1)S(1)} %get-tuple-element.33), channel_id=1, source_target_pairs={{0,66},{64,0},{2,64},{66,2},{1,67},{65,1},{3,65},{67,3},{4,70},{68... | collective-permute-start | bytes 1769480 | tf_op jit(solution)/shard_map/ppermute | solution.py:27
  32.8 2.3 %collective-permute-start.1 = (bf16[2,128,1536]{2,1,0:T(8,128)(2,1)S(1)}, bf16[2,128,1536]{2,1,0:T(8,128)(2,1)S(1)}, u32[]{:S(2)}, u32[]{:S(2)}) collective-permute-start(bf16[2,128,1536]{2,1,0:T(8,128)(2,1)S(1)} %pad_maximum_fusion.1.own), channel_id=1, source_target_pairs={{0,128},{128,256},{256,384},{384,0},{1,129},{129,257},{257,385},{3... | collective-permute-start | bytes 2359304 | tf_op jit(solution)/shard_map/ppermute | solution.py:19
  35.1 4.3 %collective-permute-start.2 = (bf16[2,128,1536]{2,1,0:T(8,128)(2,1)S(1)}, bf16[2,128,1536]{2,1,0:T(8,128)(2,1)S(1)}, u32[]{:S(2)}, u32[]{:S(2)}) collective-permute-start(bf16[2,128,1536]{2,1,0:T(8,128)(2,1)S(1)} %pad_maximum_fusion.1.own), channel_id=1, source_target_pairs={{0,384},{128,0},{256,128},{384,256},{1,385},{129,1},{257,129},{385... | collective-permute-start | bytes 2359304 | tf_op jit(solution)/shard_map/ppermute | solution.py:19
  46.4 5.3 %collective-permute-done.1.below = bf16[2,128,1536]{2,1,0:T(8,128)(2,1)S(1)} collective-permute-done((bf16[2,128,1536]{2,1,0:T(8,128)(2,1)S(1)}, bf16[2,128,1536]{2,1,0:T(8,128)(2,1)S(1)}, u32[]{:S(2)}, u32[]{:S(2)}) %collective-permute-start.1) | collective-permute-done | bytes 786464 | tf_op jit(solution)/shard_map/ppermute | solution.py:19
  52.8 14.7 %collective-permute-done.3.far = bf16[2,128,1536]{2,1,0:T(8,128)(2,1)S(1)} collective-permute-done((bf16[2,128,1536]{2,1,0:T(8,128)(2,1)S(1)}, bf16[2,128,1536]{2,1,0:T(8,128)(2,1)S(1)}, u32[]{:S(2)}, u32[]{:S(2)}) %collective-permute-start.3) | collective-permute-done | bytes 786464 | tf_op jit(solution)/shard_map/ppermute | solution.py:19
  68.3 8.5 %collective-permute-start.6 = (bf16[1536,768]{1,0:T(8,128)(2,1)}, bf16[1536,768]{1,0:T(8,128)(2,1)}, u32[]{:S(2)}, u32[]{:S(2)}) collective-permute-start(bf16[1536,768]{1,0:T(8,128)(2,1)} %bitcast.10), channel_id=1, source_target_pairs={{0,1},{1,0},{2,3},{3,2},{4,5},{5,4},{6,7},{7,6},{8,9},{9,8},{10,11... | collective-permute-start | bytes 7077896 | tf_op jit(solution)/shard_map/ppermute | solution.py:19
  79.3 3.5 %shard_map.110 = (bf16[512,1536]{1,0:T(8,128)(2,1)S(1)}, bf16[512,1536]{1,0:T(8,128)(2,1)S(1)}, f32[512,1536]{1,0:T(8,128)S(1)}) custom-call(bf16[2,128,1536]{2,1,0:T(8,128)(2,1)S(1)} %pad_maximum_fusion.1.own, bf16[2,128,1536]{2,1,0:T(8,128)(2,1)S(1)} %collective-permute-done.1.below, bf16[2,128,1536]{2,1,0:T(8,128)(2,1)S(1)} %collective-permute-done.2.above, ...), custom_call_target="tpu_custom_call" | custom-call | tf_op jit(solution)/shard_map/pallas_call | solution.py:93
  88.9 2.7 %multiply_reduce_fusion.2 = (f32[512]{0:T(512)S(1)}, f32[512,1536]{1,0:T(8,128)S(1)}) fusion(bf16[512,1536]{1,0:T(8,128)(2,1)S(1)} %get-tuple-element.16, bf16[1536,1536]{1,0:T(8,128)(2,1)S(1)} %constant_dynamic-update-slice_fusion), kind=kOutput, calls=%fused_computation.6 | convolution fusion | flops 2417491456 | bytes 9439232 | tf_op jit(solution)/shard_map/dot_general | solution.py:43
  97.5 2.4 %collective-permute-start.8 = (bf16[384,768]{1,0:T(8,128)(2,1)S(1)}, bf16[384,768]{1,0:T(8,128)(2,1)}, u32[]{:S(2)}, u32[]{:S(2)}) collective-permute-start(bf16[384,768]{1,0:T(8,128)(2,1)S(1)} %convolution_convert_fusion), channel_id=1, source_target_pairs={{0,1},{1,0},{2,3},{3,2},{4,5},{5,4},{6,7},{7,6},{8,9},{9,8},{10,11... | collective-permute-start | bytes 1769480 | tf_op jit(solution)/shard_map/ppermute | solution.py:19
  99.9 4.3 %multiply_reduce_fusion = (bf16[1536]{0:T(1024)(128)(2,1)S(1)}, bf16[1536]{0:T(1024)(128)(2,1)S(1)}, f32[512,1536]{1,0:T(8,128)}) fusion(f32[512,1536]{1,0:T(8,128)S(1)} %get-tuple-element.23, bf16[512,1536]{1,0:T(8,128)(2,1)S(1)} %subtract_convert_fusion, bf16[1536,1536]{1,0:T(8,128)(2,1)S(1)} %constant_dynamic-update-slice_fusion), kind=kOutput, calls=%fused_computation.2 | convolution fusion | flops 2418275328 | bytes 12589056 | tf_op jit(solution)/shard_map/dot_general | solution.py:43
  106.3 14.6 %all_to_all.25 = bf16[4,96,896]{2,1,0:T(8,128)(2,1)S(1)} all-to-all(bf16[4,96,896]{2,1,0:T(8,128)(2,1)S(1)} %pad_maximum_fusion.3), channel_id=1, replica_groups=mesh['y'=4,'xl'=2,'zh'=4,'zl'=4,'xh'=2,'core'=2] {'xl','xh'}, dimensions={0} | all-to-all | bytes 1376256 | tf_op jit(solution)/shard_map/all_to_all | solution.py:165
  121.7 5.6 %all-to-all-start.2 = ((bf16[4,24,896]{2,1,0:T(8,128)(2,1)}), bf16[4,24,896]{2,1,0:T(8,128)(2,1)S(1)}, u32[]{:S(2)}, u32[]{:S(2)}) async-start(bf16[4,24,896]{2,1,0:T(8,128)(2,1)} %bitcast.15), calls=%async_computation.2 | async-start | bytes 344064 | tf_op jit(solution)/shard_map/all_to_all | solution.py:169
  127.8 4.4 %all-to-all-done.2 = bf16[4,24,896]{2,1,0:T(8,128)(2,1)S(1)} async-done(((bf16[4,24,896]{2,1,0:T(8,128)(2,1)}), bf16[4,24,896]{2,1,0:T(8,128)(2,1)S(1)}, u32[]{:S(2)}, u32[]{:S(2)}) %all-to-all-start.2) | async-done | bytes 172064 | tf_op jit(solution)/shard_map/all_to_all | solution.py:169
  133.0 12.5 %all-to-all-start.3 = ((bf16[4,24,896]{2,1,0:T(8,128)(2,1)}), bf16[4,24,896]{2,1,0:T(8,128)(2,1)S(1)}, u32[]{:S(2)}, u32[]{:S(2)}) async-start(bf16[4,24,896]{2,1,0:T(8,128)(2,1)} %broadcast_in_dim.28), calls=%async_computation.3 | async-start | bytes 344064 | tf_op jit(solution)/shard_map/all_to_all | solution.py:49
  146.8 5.4 %collective-permute-start.9 = (f32[128,1536]{1,0:T(8,128)}, f32[128,1536]{1,0:T(8,128)}, u32[]{:S(2)}, u32[]{:S(2)}) collective-permute-start(f32[128,1536]{1,0:T(8,128)} %fusion.38), channel_id=1, source_target_pairs={{0,1},{1,0},{2,3},{3,2},{4,5},{5,4},{6,7},{7,6},{8,9},{9,8},{10,11... | collective-permute-start | bytes 2359304 | tf_op jit(solution)/shard_map/ppermute | solution.py:19
  155.4 2.8 %all-to-all-done.3 = bf16[4,24,896]{2,1,0:T(8,128)(2,1)S(1)} async-done(((bf16[4,24,896]{2,1,0:T(8,128)(2,1)}), bf16[4,24,896]{2,1,0:T(8,128)(2,1)S(1)}, u32[]{:S(2)}, u32[]{:S(2)}) %all-to-all-start.3) | async-done | bytes 172064 | tf_op jit(solution)/shard_map/all_to_all | solution.py:49
  160.4 4.1 %all-to-all-start.4 = ((bf16[8,24,896]{2,1,0:T(8,128)(2,1)}), bf16[8,24,896]{2,1,0:T(8,128)(2,1)}, u32[]{:S(2)}, u32[]{:S(2)}) async-start(bf16[8,24,896]{2,1,0:T(8,128)(2,1)} %broadcast_in_dim.58), calls=%async_computation.4 | async-start | bytes 688128 | tf_op jit(solution)/shard_map/all_to_all | solution.py:49
  166.6 8.1 %collective-permute-start.10 = (bf16[2,128,1536]{2,1,0:T(8,128)(2,1)S(1)}, bf16[2,128,1536]{2,1,0:T(8,128)(2,1)S(1)}, u32[]{:S(2)}, u32[]{:S(2)}) collective-permute-start(bf16[2,128,1536]{2,1,0:T(8,128)(2,1)S(1)} %pad_maximum_fusion.2), channel_id=1, source_target_pairs={{0,0},{1,64},{64,1},{65,65},{2,2},{3,66},{66,3},{67,67},{4,4},{5,6... | collective-permute-start | bytes 2359304 | tf_op jit(solution)/shard_map/ppermute | solution.py:31
  174.7 7.9 %collective-permute-start.11 = (bf16[8,24,896]{2,1,0:T(8,128)(2,1)}, bf16[8,24,896]{2,1,0:T(8,128)(2,1)S(1)}, u32[]{:S(2)}, u32[]{:S(2)}) collective-permute-start(bf16[8,24,896]{2,1,0:T(8,128)(2,1)} %all-to-all-done.4), channel_id=1, source_target_pairs={{0,1},{1,0},{2,3},{3,2},{4,5},{5,4},{6,7},{7,6},{8,9},{9,8},{10,11... | collective-permute-start | bytes 1032200 | tf_op jit(solution)/shard_map/ppermute | solution.py:19
  182.6 2.2 %collective-permute-done.10 = bf16[2,128,1536]{2,1,0:T(8,128)(2,1)S(1)} collective-permute-done((bf16[2,128,1536]{2,1,0:T(8,128)(2,1)S(1)}, bf16[2,128,1536]{2,1,0:T(8,128)(2,1)S(1)}, u32[]{:S(2)}, u32[]{:S(2)}) %collective-permute-start.10) | collective-permute-done | bytes 786464 | tf_op jit(solution)/shard_map/ppermute | solution.py:31
  (107 shorter events, 45.8 us)
Async XLA Ops:
  1.9 14.2 %collective-permute-start = (bf16[2,128,1536]{2,1,0:T(8,128)(2,1)S(1)}, bf16[2,128,1536]{2,1,0:T(8,128)(2,1)S(1)}, u32[]{:S(2)}, u32[]{:S(2)}) collective-permute-start(bf16[2,128,1536]{2,1,0:T(8,128)(2,1)S(1)} %pad_maximum_fusion), channel_id=1, source_target_pairs={{0,0},{1,64},{64,1},{65,65},{2,2},{3,66},{66,3},{67,67},{4,4},{5,6... | collective-permute-start | bytes 2359304 | tf_op jit(solution)/shard_map/ppermute | solution.py:31
  7.6 18.3 %all-to-all-start = ((bf16[4,192,768]{2,1,0:T(8,128)(2,1)}), bf16[4,192,768]{2,1,0:T(8,128)(2,1)S(1)}, u32[]{:S(2)}, u32[]{:S(2)}) async-start(bf16[4,192,768]{2,1,0:T(8,128)(2,1)} %broadcast_in_dim.22), calls=%async_computation | async-start | bytes 2359296 | tf_op jit(solution)/shard_map/all_to_all | solution.py:49
  16.1 12.0 %copy-start.7 = (bf16[2,128,1536]{2,1,0:T(8,128)(2,1)}, bf16[2,128,1536]{2,1,0:T(8,128)(2,1)S(1)}, u32[]{:S(2)}) copy-start(bf16[2,128,1536]{2,1,0:T(8,128)(2,1)S(1)} %collective-permute-done) | copy-start | bytes 2359300
  17.1 11.0 %copy-start.13 = (f32[128]{0:T(128)}, f32[128]{0:T(128)S(1)}, u32[]{:S(2)}) copy-start(f32[128]{0:T(128)S(1)} %add_rsqrt_fusion.1) | copy-start | bytes 1540
  26.0 18.1 %collective-permute-start.4 = (bf16[2,192,768]{2,1,0:T(8,128)(2,1)S(1)}, bf16[2,192,768]{2,1,0:T(8,128)(2,1)S(1)}, u32[]{:S(2)}, u32[]{:S(2)}) collective-permute-start(bf16[2,192,768]{2,1,0:T(8,128)(2,1)S(1)} %get-tuple-element.34), channel_id=1, source_target_pairs={{0,64},{64,2},{2,66},{66,0},{1,65},{65,3},{3,67},{67,1},{4,68},{68... | collective-permute-start | bytes 1769480 | tf_op jit(solution)/shard_map/ppermute | solution.py:27
  28.1 17.5 %collective-permute-start.5 = (bf16[2,192,768]{2,1,0:T(8,128)(2,1)S(1)}, bf16[2,192,768]{2,1,0:T(8,128)(2,1)S(1)}, u32[]{:S(2)}, u32[]{:S(2)}) collective-permute-start(bf16[2,192,768]{2,1,0:T(8,128)(2,1)S(1)} %get-tuple-element.33), channel_id=1, source_target_pairs={{0,66},{64,0},{2,64},{66,2},{1,67},{65,1},{3,65},{67,3},{4,70},{68... | collective-permute-start | bytes 1769480 | tf_op jit(solution)/shard_map/ppermute | solution.py:27
  32.8 10.2 %copy-start.6 = (bf16[4,192,768]{2,1,0:T(8,128)(2,1)S(1)}, bf16[4,192,768]{2,1,0:T(8,128)(2,1)}, u32[]{:S(2)}) copy-start(bf16[4,192,768]{2,1,0:T(8,128)(2,1)} %copy-done.5) | copy-start | bytes 3538948
  32.8 19.0 %collective-permute-start.1 = (bf16[2,128,1536]{2,1,0:T(8,128)(2,1)S(1)}, bf16[2,128,1536]{2,1,0:T(8,128)(2,1)S(1)}, u32[]{:S(2)}, u32[]{:S(2)}) collective-permute-start(bf16[2,128,1536]{2,1,0:T(8,128)(2,1)S(1)} %pad_maximum_fusion.1.own), channel_id=1, source_target_pairs={{0,128},{128,256},{256,384},{384,0},{1,129},{129,257},{257,385},{3... | collective-permute-start | bytes 2359304 | tf_op jit(solution)/shard_map/ppermute | solution.py:19
  35.1 17.7 %collective-permute-start.2 = (bf16[2,128,1536]{2,1,0:T(8,128)(2,1)S(1)}, bf16[2,128,1536]{2,1,0:T(8,128)(2,1)S(1)}, u32[]{:S(2)}, u32[]{:S(2)}) collective-permute-start(bf16[2,128,1536]{2,1,0:T(8,128)(2,1)S(1)} %pad_maximum_fusion.1.own), channel_id=1, source_target_pairs={{0,384},{128,0},{256,128},{384,256},{1,385},{129,1},{257,129},{385... | collective-permute-start | bytes 2359304 | tf_op jit(solution)/shard_map/ppermute | solution.py:19
  39.4 28.0 %collective-permute-start.3 = (bf16[2,128,1536]{2,1,0:T(8,128)(2,1)S(1)}, bf16[2,128,1536]{2,1,0:T(8,128)(2,1)S(1)}, u32[]{:S(2)}, u32[]{:S(2)}) collective-permute-start(bf16[2,128,1536]{2,1,0:T(8,128)(2,1)S(1)} %pad_maximum_fusion.1.own), channel_id=1, source_target_pairs={{0,256},{128,384},{256,0},{384,128},{1,257},{129,385},{257,1},{385... | collective-permute-start | bytes 2359304 | tf_op jit(solution)/shard_map/ppermute | solution.py:19
  44.0 32.8 %copy-start.11 = (f32[1536]{0:T(1024)S(1)}, f32[1536]{0:T(1024)}, u32[]{:S(2)}) copy-start(f32[1536]{0:T(1024)} %param.8) | copy-start | bytes 18436
  44.0 32.8 %copy-start.12 = (f32[1536]{0:T(1024)S(1)}, f32[1536]{0:T(1024)}, u32[]{:S(2)}) copy-start(f32[1536]{0:T(1024)} %param.9) | copy-start | bytes 18436
  68.3 18.7 %collective-permute-start.6 = (bf16[1536,768]{1,0:T(8,128)(2,1)}, bf16[1536,768]{1,0:T(8,128)(2,1)}, u32[]{:S(2)}, u32[]{:S(2)}) collective-permute-start(bf16[1536,768]{1,0:T(8,128)(2,1)} %bitcast.10), channel_id=1, source_target_pairs={{0,1},{1,0},{2,3},{3,2},{4,5},{5,4},{6,7},{7,6},{8,9},{9,8},{10,11... | collective-permute-start | bytes 7077896 | tf_op jit(solution)/shard_map/ppermute | solution.py:19
  82.8 14.2 %copy-start.4 = (bf16[512,1536]{1,0:T(8,128)(2,1)}, bf16[512,1536]{1,0:T(8,128)(2,1)S(1)}, u32[]{:S(2)}) copy-start(bf16[512,1536]{1,0:T(8,128)(2,1)S(1)} %get-tuple-element.16) | copy-start | bytes 4718596
  82.8 17.1 %copy-start.1 = (f32[512,1536]{1,0:T(8,128)}, f32[512,1536]{1,0:T(8,128)S(1)}, u32[]{:S(2)}) copy-start(f32[512,1536]{1,0:T(8,128)S(1)} %get-tuple-element.23) | copy-start | bytes 9437188
  82.8 10.2 %collective-permute-start.7 = (bf16[512,1536]{1,0:T(8,128)(2,1)S(1)}, bf16[512,1536]{1,0:T(8,128)(2,1)S(1)}, u32[]{:S(2)}, u32[]{:S(2)}) collective-permute-start(bf16[512,1536]{1,0:T(8,128)(2,1)S(1)} %get-tuple-element.18), channel_id=1, source_target_pairs={{0,1},{1,0},{2,3},{3,2},{4,5},{5,4},{6,7},{7,6},{8,9},{9,8},{10,11... | collective-permute-start | bytes 4718600 | tf_op jit(solution)/shard_map/ppermute | solution.py:19
  97.5 6.8 %collective-permute-start.8 = (bf16[384,768]{1,0:T(8,128)(2,1)S(1)}, bf16[384,768]{1,0:T(8,128)(2,1)}, u32[]{:S(2)}, u32[]{:S(2)}) collective-permute-start(bf16[384,768]{1,0:T(8,128)(2,1)S(1)} %convolution_convert_fusion), channel_id=1, source_target_pairs={{0,1},{1,0},{2,3},{3,2},{4,5},{5,4},{6,7},{7,6},{8,9},{9,8},{10,11... | collective-permute-start | bytes 1769480 | tf_op jit(solution)/shard_map/ppermute | solution.py:19
  121.7 10.6 %all-to-all-start.2 = ((bf16[4,24,896]{2,1,0:T(8,128)(2,1)}), bf16[4,24,896]{2,1,0:T(8,128)(2,1)S(1)}, u32[]{:S(2)}, u32[]{:S(2)}) async-start(bf16[4,24,896]{2,1,0:T(8,128)(2,1)} %bitcast.15), calls=%async_computation.2 | async-start | bytes 344064 | tf_op jit(solution)/shard_map/all_to_all | solution.py:169
  133.0 25.2 %all-to-all-start.3 = ((bf16[4,24,896]{2,1,0:T(8,128)(2,1)}), bf16[4,24,896]{2,1,0:T(8,128)(2,1)S(1)}, u32[]{:S(2)}, u32[]{:S(2)}) async-start(bf16[4,24,896]{2,1,0:T(8,128)(2,1)} %broadcast_in_dim.28), calls=%async_computation.3 | async-start | bytes 344064 | tf_op jit(solution)/shard_map/all_to_all | solution.py:49
  146.8 17.7 %collective-permute-start.9 = (f32[128,1536]{1,0:T(8,128)}, f32[128,1536]{1,0:T(8,128)}, u32[]{:S(2)}, u32[]{:S(2)}) collective-permute-start(f32[128,1536]{1,0:T(8,128)} %fusion.38), channel_id=1, source_target_pairs={{0,1},{1,0},{2,3},{3,2},{4,5},{5,4},{6,7},{7,6},{8,9},{9,8},{10,11... | collective-permute-start | bytes 2359304 | tf_op jit(solution)/shard_map/ppermute | solution.py:19
  153.8 10.8 %copy-start.8 = (bf16[2,128,1536]{2,1,0:T(8,128)(2,1)S(1)}, bf16[2,128,1536]{2,1,0:T(8,128)(2,1)}, u32[]{:S(2)}) copy-start(bf16[2,128,1536]{2,1,0:T(8,128)(2,1)} %copy-done.7) | copy-start | bytes 2359300
  160.4 14.3 %all-to-all-start.4 = ((bf16[8,24,896]{2,1,0:T(8,128)(2,1)}), bf16[8,24,896]{2,1,0:T(8,128)(2,1)}, u32[]{:S(2)}, u32[]{:S(2)}) async-start(bf16[8,24,896]{2,1,0:T(8,128)(2,1)} %broadcast_in_dim.58), calls=%async_computation.4 | async-start | bytes 688128 | tf_op jit(solution)/shard_map/all_to_all | solution.py:49
  166.6 18.2 %collective-permute-start.10 = (bf16[2,128,1536]{2,1,0:T(8,128)(2,1)S(1)}, bf16[2,128,1536]{2,1,0:T(8,128)(2,1)S(1)}, u32[]{:S(2)}, u32[]{:S(2)}) collective-permute-start(bf16[2,128,1536]{2,1,0:T(8,128)(2,1)S(1)} %pad_maximum_fusion.2), channel_id=1, source_target_pairs={{0,0},{1,64},{64,1},{65,65},{2,2},{3,66},{66,3},{67,67},{4,4},{5,6... | collective-permute-start | bytes 2359304 | tf_op jit(solution)/shard_map/ppermute | solution.py:31
  174.7 12.4 %collective-permute-start.11 = (bf16[8,24,896]{2,1,0:T(8,128)(2,1)}, bf16[8,24,896]{2,1,0:T(8,128)(2,1)S(1)}, u32[]{:S(2)}, u32[]{:S(2)}) collective-permute-start(bf16[8,24,896]{2,1,0:T(8,128)(2,1)} %all-to-all-done.4), channel_id=1, source_target_pairs={{0,1},{1,0},{2,3},{3,2},{4,5},{5,4},{6,7},{7,6},{8,9},{9,8},{10,11... | collective-permute-start | bytes 1032200 | tf_op jit(solution)/shard_map/ppermute | solution.py:19
  (10 other events, 31.8 us)

commit v10 on v9

--- a/solution.py
+++ b/solution.py
@@ -60,9 +60,10 @@
     own_half = lax.dynamic_update_slice(own_half, blocks[:, None], (0, xl, 0, 0))
     for start, block in zip((0, 2), other):
         own_half = lax.dynamic_update_slice(own_half, block[:, None], (start, 1 - xl, 0, 0))
-    own_half = after(own_half.reshape(2 * count * rows, half), *earlier)
+    own_half = own_half.reshape(2 * count * rows, half)
     weight = jnp.zeros((2 * count * rows, 2 * half), bf16)
     weight = lax.dynamic_update_slice(weight, own_half, (0, core * half))
+    own_half, weight = lax.optimization_barrier((own_half, weight, *earlier))[:2]
     weight = lax.dynamic_update_slice(weight, shift(own_half, "core", 1), (0, (1 - core) * half))
     return weight
 
@@ -95,6 +96,9 @@
         out_shape=[jax.ShapeDtypeStruct(shape, t) for t in (bf16, bf16, f32)],
         in_specs=[pl.BlockSpec(memory_space=pltpu.VMEM)] * 6,
         out_specs=[pl.BlockSpec(memory_space=pltpu.VMEM)] * 3,
+        cost_estimate=pl.CostEstimate(
+            flops=40 * shape[0] * width, bytes_accessed=48 * shape[0] * width, transcendentals=shape[0]
+        ),
         compiler_params=pltpu.CompilerParams(vmem_limit_bytes=40 * 2**20),
     )(*blocks, gain.reshape(1, width), bias.reshape(1, width))
 
@@ -119,7 +123,7 @@
 
     pair = jnp.stack([text_unit, feature_rows], 0)
     below, above, far = shift(pair, "y", 1), shift(pair, "y", -1), shift(pair, "y", 2)
-    weight = gather_weight(weight_blocks, xl, core, [below, above, far])
+    weight = gather_weight(weight_blocks, xl, core, [below, above])
     text_same, normed, xhat = place([pair, below, above, far], final_norm_gain, final_norm_bias)
     text_other = shift(text_same, "core", 1)
     rows = normed.shape[0]

time: 193 us -> 197 us (1.021)
    unnamed x36 -> x38, local copies, waits for them, and re-layouts: 2.67 us -> 0.61 us
    ppermute x2, waiting for transfers between devices: 0.64 us -> 2.62 us  [shift_x(): lax.ppermute(value, ('xl', 'xh'), [(index(i), index(i + steps)) for i in...]
  transfers between devices with their start and end apart: 16 -> 16, of which waited for: 9 -> 9; matrix products, arithmetic and copies ran while one was open for 16% -> 17% of each run, Pallas kernels for 2% -> 2%
where the time goes in v10:
time: 197 us; the launch traced here: 195 us
  starting transfers between devices  80.7 us (41%)
  waiting for transfers between devices  46 us (23%)
  matrix products  18.9 us (10%)
  local copies, waits for them, and re-layouts  16.3 us (8%)
  blocking collectives  14.1 us (7%)
  other arithmetic  11.4 us (6%)
  Pallas kernels  4.6 us (2%)
  between operations  2.6 us (1%)
    ppermute x8, starting transfers between devices, shift(): lax.ppermute(value, axis, [(i, (i + steps) % count) for i in range(count)])  35.4 us
    all_to_all x3, starting transfers between devices, spread_to(): return lax.all_to_all(many, axes, split_axis=0, concat_axis=0, tiled=True)  20.9 us
    ppermute x8, waiting for transfers between devices, shift(): lax.ppermute(value, axis, [(i, (i + steps) % count) for i in range(count)])  20.8 us
    dot_general x10, matrix products, dot(): lax.dot_general(a, b, (((da,), (db,)), ((), ())), preferred_element_type=...  18.9 us
    all_to_all x1, blocking collectives, local(): lax.all_to_all(sent, ('xl', 'xh'), split_axis=0, concat_axis=0, tiled=True)  14.1 us
    ppermute x2, starting transfers between devices, swap(): return lax.ppermute(value, ('xl', 'core'), [(0, 0), (1, 2), (2, 1), (3, 3)])  12.4 us
    all_to_all x3, waiting for transfers between devices, spread_to(): return lax.all_to_all(many, axes, split_axis=0, concat_axis=0, tiled=True)  11.9 us
    ppermute x2, starting transfers between devices, shift_x(): lax.ppermute(value, ('xl', 'xh'), [(index(i), index(i + steps)) for i in...  6.49 us
  transfers between devices with their start and end apart: 16, of which 9 were waited for; matrix products, arithmetic and copies ran while one was open for 17% of the time, Pallas kernels for 2%

profile of v10, /device:TPU:1, one launch (start us, length us, event | category | flops | bytes accessed | tf_op | source)
XLA Modules:
  0.0 194.5 jit_solution(5340419682443243557)
XLA Ops:
  1.9 4.5 %collective-permute-start = (bf16[2,128,1536]{2,1,0:T(8,128)(2,1)S(1)}, bf16[2,128,1536]{2,1,0:T(8,128)(2,1)S(1)}, u32[]{:S(2)}, u32[]{:S(2)}) collective-permute-start(bf16[2,128,1536]{2,1,0:T(8,128)(2,1)S(1)} %pad_maximum_fusion), channel_id=1, source_target_pairs={{0,0},{1,64},{64,1},{65,65},{2,2},{3,66},{66,3},{67,67},{4,4},{5,6... | collective-permute-start | bytes 2359304 | tf_op jit(solution)/shard_map/ppermute | solution.py:31
  7.6 4.2 %all-to-all-start = ((bf16[4,192,768]{2,1,0:T(8,128)(2,1)}), bf16[4,192,768]{2,1,0:T(8,128)(2,1)S(1)}, u32[]{:S(2)}, u32[]{:S(2)}) async-start(bf16[4,192,768]{2,1,0:T(8,128)(2,1)} %broadcast_in_dim.21), calls=%async_computation | async-start | bytes 2359296 | tf_op jit(solution)/shard_map/all_to_all | solution.py:49
  11.7 4.3 %collective-permute-done = bf16[2,128,1536]{2,1,0:T(8,128)(2,1)S(1)} collective-permute-done((bf16[2,128,1536]{2,1,0:T(8,128)(2,1)S(1)}, bf16[2,128,1536]{2,1,0:T(8,128)(2,1)S(1)}, u32[]{:S(2)}, u32[]{:S(2)}) %collective-permute-start) | collective-permute-done | bytes 786464 | tf_op jit(solution)/shard_map/ppermute | solution.py:31
  17.0 8.9 %all-to-all-done = bf16[4,192,768]{2,1,0:T(8,128)(2,1)S(1)} async-done(((bf16[4,192,768]{2,1,0:T(8,128)(2,1)}), bf16[4,192,768]{2,1,0:T(8,128)(2,1)S(1)}, u32[]{:S(2)}, u32[]{:S(2)}) %all-to-all-start) | async-done | bytes 1179680 | tf_op jit(solution)/shard_map/all_to_all | solution.py:49
  28.1 4.6 %collective-permute-start.5 = (bf16[2,192,768]{2,1,0:T(8,128)(2,1)S(1)}, bf16[2,192,768]{2,1,0:T(8,128)(2,1)S(1)}, u32[]{:S(2)}, u32[]{:S(2)}) collective-permute-start(bf16[2,192,768]{2,1,0:T(8,128)(2,1)S(1)} %get-tuple-element.35), channel_id=1, source_target_pairs={{0,66},{64,0},{2,64},{66,2},{1,67},{65,1},{3,65},{67,3},{4,70},{68... | collective-permute-start | bytes 1769480 | tf_op jit(solution)/shard_map/ppermute | solution.py:27
  35.1 4.3 %collective-permute-start.2 = (bf16[2,128,1536]{2,1,0:T(8,128)(2,1)S(1)}, bf16[2,128,1536]{2,1,0:T(8,128)(2,1)S(1)}, u32[]{:S(2)}, u32[]{:S(2)}) collective-permute-start(bf16[2,128,1536]{2,1,0:T(8,128)(2,1)S(1)} %pad_maximum_fusion.1.own), channel_id=1, source_target_pairs={{0,384},{128,0},{256,128},{384,256},{1,385},{129,1},{257,129},{385... | collective-permute-start | bytes 2359304 | tf_op jit(solution)/shard_map/ppermute | solution.py:19
  42.9 2.6 %collective-permute-done.5 = bf16[2,192,768]{2,1,0:T(8,128)(2,1)S(1)} collective-permute-done((bf16[2,192,768]{2,1,0:T(8,128)(2,1)S(1)}, bf16[2,192,768]{2,1,0:T(8,128)(2,1)S(1)}, u32[]{:S(2)}, u32[]{:S(2)}) %collective-permute-start.5) | collective-permute-done | bytes 589856 | tf_op jit(solution)/shard_map/ppermute | solution.py:27
  52.1 7.0 %collective-permute-start.6 = (bf16[1536,768]{1,0:T(8,128)(2,1)}, bf16[1536,768]{1,0:T(8,128)(2,1)}, u32[]{:S(2)}, u32[]{:S(2)}) collective-permute-start(bf16[1536,768]{1,0:T(8,128)(2,1)} %bitcast.10), channel_id=1, source_target_pairs={{0,1},{1,0},{2,3},{3,2},{4,5},{5,4},{6,7},{7,6},{8,9},{9,8},{10,11... | collective-permute-start | bytes 7077896 | tf_op jit(solution)/shard_map/ppermute | solution.py:19
  59.0 3.8 %collective-permute-start.3 = (bf16[2,128,1536]{2,1,0:T(8,128)(2,1)S(1)}, bf16[2,128,1536]{2,1,0:T(8,128)(2,1)}, u32[]{:S(2)}, u32[]{:S(2)}) collective-permute-start(bf16[2,128,1536]{2,1,0:T(8,128)(2,1)S(1)} %pad_maximum_fusion.1.own), channel_id=1, source_target_pairs={{0,256},{128,384},{256,0},{384,128},{1,257},{129,385},{257,1},{385... | collective-permute-start | bytes 2359304 | tf_op jit(solution)/shard_map/ppermute | solution.py:19
  64.3 17.4 %collective-permute-done.3.far = bf16[2,128,1536]{2,1,0:T(8,128)(2,1)} collective-permute-done((bf16[2,128,1536]{2,1,0:T(8,128)(2,1)S(1)}, bf16[2,128,1536]{2,1,0:T(8,128)(2,1)}, u32[]{:S(2)}, u32[]{:S(2)}) %collective-permute-start.3) | collective-permute-done | bytes 786464 | tf_op jit(solution)/shard_map/ppermute | solution.py:19
  81.7 4.6 %shard_map.110 = (bf16[512,1536]{1,0:T(8,128)(2,1)S(1)}, bf16[512,1536]{1,0:T(8,128)(2,1)S(1)}, f32[512,1536]{1,0:T(8,128)S(1)}) custom-call(bf16[2,128,1536]{2,1,0:T(8,128)(2,1)S(1)} %pad_maximum_fusion.1.own, bf16[2,128,1536]{2,1,0:T(8,128)(2,1)S(1)} %collective-permute-done.1.below, bf16[2,128,1536]{2,1,0:T(8,128)(2,1)S(1)} %collective-permute-done.2.above, ...), custom_call_target="tpu_custom_call" | custom-call | flops 31457280 | bytes 37748736 | tf_op jit(solution)/shard_map/pallas_call | solution.py:94
  86.3 2.7 %collective-permute-start.7 = (bf16[512,1536]{1,0:T(8,128)(2,1)S(1)}, bf16[512,1536]{1,0:T(8,128)(2,1)S(1)}, u32[]{:S(2)}, u32[]{:S(2)}) collective-permute-start(bf16[512,1536]{1,0:T(8,128)(2,1)S(1)} %get-tuple-element.20), channel_id=1, source_target_pairs={{0,1},{1,0},{2,3},{3,2},{4,5},{5,4},{6,7},{7,6},{8,9},{9,8},{10,11... | collective-permute-start | bytes 4718600 | tf_op jit(solution)/shard_map/ppermute | solution.py:19
  89.1 3.3 %constant_dynamic-update-slice_fusion = bf16[1536,1536]{1,0:T(8,128)(2,1)} fusion(bf16[1536,1536]{1,0:T(8,128)(2,1)} %copy-done.7, bf16[1536,768]{1,0:T(8,128)(2,1)} %collective-permute-done.6, s32[]{:T(128)S(6)} %select_n.30), kind=kLoop, calls=%fused_computation.80 | loop fusion | bytes 4718596 | tf_op jit(solution)/shard_map/dynamic_update_slice | solution.py:67
  92.3 4.6 %multiply_reduce_fusion.2 = (f32[512]{0:T(512)S(1)}, f32[512,1536]{1,0:T(8,128)S(1)}) fusion(bf16[512,1536]{1,0:T(8,128)(2,1)S(1)} %get-tuple-element.17, bf16[1536,1536]{1,0:T(8,128)(2,1)} %constant_dynamic-update-slice_fusion), kind=kOutput, calls=%fused_computation.6 | convolution fusion | flops 2417491456 | bytes 9439232 | tf_op jit(solution)/shard_map/dot_general | solution.py:43
  104.9 4.3 %multiply_reduce_fusion = (bf16[1536]{0:T(1024)(128)(2,1)S(1)}, bf16[1536]{0:T(1024)(128)(2,1)S(1)}, f32[512,1536]{1,0:T(8,128)}) fusion(f32[512,1536]{1,0:T(8,128)S(1)} %get-tuple-element.25, bf16[512,1536]{1,0:T(8,128)(2,1)S(1)} %subtract_convert_fusion, bf16[1536,1536]{1,0:T(8,128)(2,1)S(1)} %bitcast.89), kind=kOutput, calls=%fused_computation.2 | convolution fusion | flops 2418275328 | bytes 12589056 | tf_op jit(solution)/shard_map/dot_general | solution.py:43
  111.2 14.1 %all_to_all.25 = bf16[4,96,896]{2,1,0:T(8,128)(2,1)S(1)} all-to-all(bf16[4,96,896]{2,1,0:T(8,128)(2,1)S(1)} %pad_maximum_fusion.3), channel_id=1, replica_groups=mesh['y'=4,'xl'=2,'zh'=4,'zl'=4,'xh'=2,'core'=2] {'xl','xh'}, dimensions={0} | all-to-all | bytes 1376256 | tf_op jit(solution)/shard_map/all_to_all | solution.py:169
  126.1 5.6 %all-to-all-start.2 = ((bf16[4,24,896]{2,1,0:T(8,128)(2,1)}), bf16[4,24,896]{2,1,0:T(8,128)(2,1)S(1)}, u32[]{:S(2)}, u32[]{:S(2)}) async-start(bf16[4,24,896]{2,1,0:T(8,128)(2,1)} %bitcast.15), calls=%async_computation.2 | async-start | bytes 344064 | tf_op jit(solution)/shard_map/all_to_all | solution.py:173
  132.2 4.4 %all-to-all-done.2 = bf16[4,24,896]{2,1,0:T(8,128)(2,1)S(1)} async-done(((bf16[4,24,896]{2,1,0:T(8,128)(2,1)}), bf16[4,24,896]{2,1,0:T(8,128)(2,1)S(1)}, u32[]{:S(2)}, u32[]{:S(2)}) %all-to-all-start.2) | async-done | bytes 172064 | tf_op jit(solution)/shard_map/all_to_all | solution.py:173
  137.3 12.5 %all-to-all-start.3 = ((bf16[4,24,896]{2,1,0:T(8,128)(2,1)}), bf16[4,24,896]{2,1,0:T(8,128)(2,1)S(1)}, u32[]{:S(2)}, u32[]{:S(2)}) async-start(bf16[4,24,896]{2,1,0:T(8,128)(2,1)} %broadcast_in_dim.28), calls=%async_computation.3 | async-start | bytes 344064 | tf_op jit(solution)/shard_map/all_to_all | solution.py:49
  151.1 5.1 %collective-permute-start.9 = (f32[128,1536]{1,0:T(8,128)}, f32[128,1536]{1,0:T(8,128)}, u32[]{:S(2)}, u32[]{:S(2)}) collective-permute-start(f32[128,1536]{1,0:T(8,128)} %fusion.38), channel_id=1, source_target_pairs={{0,1},{1,0},{2,3},{3,2},{4,5},{5,4},{6,7},{7,6},{8,9},{9,8},{10,11... | collective-permute-start | bytes 2359304 | tf_op jit(solution)/shard_map/ppermute | solution.py:19
  159.5 3.0 %all-to-all-done.3 = bf16[4,24,896]{2,1,0:T(8,128)(2,1)S(1)} async-done(((bf16[4,24,896]{2,1,0:T(8,128)(2,1)}), bf16[4,24,896]{2,1,0:T(8,128)(2,1)S(1)}, u32[]{:S(2)}, u32[]{:S(2)}) %all-to-all-start.3) | async-done | bytes 172064 | tf_op jit(solution)/shard_map/all_to_all | solution.py:49
  164.7 4.2 %all-to-all-start.4 = ((bf16[8,24,896]{2,1,0:T(8,128)(2,1)}), bf16[8,24,896]{2,1,0:T(8,128)(2,1)}, u32[]{:S(2)}, u32[]{:S(2)}) async-start(bf16[8,24,896]{2,1,0:T(8,128)(2,1)} %broadcast_in_dim.58), calls=%async_computation.4 | async-start | bytes 688128 | tf_op jit(solution)/shard_map/all_to_all | solution.py:49
  171.0 7.9 %collective-permute-start.10 = (bf16[2,128,1536]{2,1,0:T(8,128)(2,1)S(1)}, bf16[2,128,1536]{2,1,0:T(8,128)(2,1)S(1)}, u32[]{:S(2)}, u32[]{:S(2)}) collective-permute-start(bf16[2,128,1536]{2,1,0:T(8,128)(2,1)S(1)} %pad_maximum_fusion.2), channel_id=1, source_target_pairs={{0,0},{1,64},{64,1},{65,65},{2,2},{3,66},{66,3},{67,67},{4,4},{5,6... | collective-permute-start | bytes 2359304 | tf_op jit(solution)/shard_map/ppermute | solution.py:31
  178.9 8.1 %collective-permute-start.11 = (bf16[8,24,896]{2,1,0:T(8,128)(2,1)}, bf16[8,24,896]{2,1,0:T(8,128)(2,1)S(1)}, u32[]{:S(2)}, u32[]{:S(2)}) collective-permute-start(bf16[8,24,896]{2,1,0:T(8,128)(2,1)} %all-to-all-done.4), channel_id=1, source_target_pairs={{0,1},{1,0},{2,3},{3,2},{4,5},{5,4},{6,7},{7,6},{8,9},{9,8},{10,11... | collective-permute-start | bytes 1032200 | tf_op jit(solution)/shard_map/ppermute | solution.py:19
  (110 shorter events, 45.9 us)
Async XLA Ops:
  1.9 14.2 %collective-permute-start = (bf16[2,128,1536]{2,1,0:T(8,128)(2,1)S(1)}, bf16[2,128,1536]{2,1,0:T(8,128)(2,1)S(1)}, u32[]{:S(2)}, u32[]{:S(2)}) collective-permute-start(bf16[2,128,1536]{2,1,0:T(8,128)(2,1)S(1)} %pad_maximum_fusion), channel_id=1, source_target_pairs={{0,0},{1,64},{64,1},{65,65},{2,2},{3,66},{66,3},{67,67},{4,4},{5,6... | collective-permute-start | bytes 2359304 | tf_op jit(solution)/shard_map/ppermute | solution.py:31
  7.6 18.3 %all-to-all-start = ((bf16[4,192,768]{2,1,0:T(8,128)(2,1)}), bf16[4,192,768]{2,1,0:T(8,128)(2,1)S(1)}, u32[]{:S(2)}, u32[]{:S(2)}) async-start(bf16[4,192,768]{2,1,0:T(8,128)(2,1)} %broadcast_in_dim.21), calls=%async_computation | async-start | bytes 2359296 | tf_op jit(solution)/shard_map/all_to_all | solution.py:49
  16.1 12.0 %copy-start.5 = (bf16[2,128,1536]{2,1,0:T(8,128)(2,1)}, bf16[2,128,1536]{2,1,0:T(8,128)(2,1)S(1)}, u32[]{:S(2)}) copy-start(bf16[2,128,1536]{2,1,0:T(8,128)(2,1)S(1)} %collective-permute-done) | copy-start | bytes 2359300
  17.0 11.0 %copy-start.12 = (f32[128]{0:T(128)}, f32[128]{0:T(128)S(1)}, u32[]{:S(2)}) copy-start(f32[128]{0:T(128)S(1)} %add_rsqrt_fusion.1) | copy-start | bytes 1540
  26.0 16.1 %collective-permute-start.4 = (bf16[2,192,768]{2,1,0:T(8,128)(2,1)S(1)}, bf16[2,192,768]{2,1,0:T(8,128)(2,1)S(1)}, u32[]{:S(2)}, u32[]{:S(2)}) collective-permute-start(bf16[2,192,768]{2,1,0:T(8,128)(2,1)S(1)} %get-tuple-element.36), channel_id=1, source_target_pairs={{0,64},{64,2},{2,66},{66,0},{1,65},{65,3},{3,67},{67,1},{4,68},{68... | collective-permute-start | bytes 1769480 | tf_op jit(solution)/shard_map/ppermute | solution.py:27
  28.1 17.5 %collective-permute-start.5 = (bf16[2,192,768]{2,1,0:T(8,128)(2,1)S(1)}, bf16[2,192,768]{2,1,0:T(8,128)(2,1)S(1)}, u32[]{:S(2)}, u32[]{:S(2)}) collective-permute-start(bf16[2,192,768]{2,1,0:T(8,128)(2,1)S(1)} %get-tuple-element.35), channel_id=1, source_target_pairs={{0,66},{64,0},{2,64},{66,2},{1,67},{65,1},{3,65},{67,3},{4,70},{68... | collective-permute-start | bytes 1769480 | tf_op jit(solution)/shard_map/ppermute | solution.py:27
  32.8 8.2 %copy-start.4 = (bf16[4,192,768]{2,1,0:T(8,128)(2,1)S(1)}, bf16[4,192,768]{2,1,0:T(8,128)(2,1)}, u32[]{:S(2)}) copy-start(bf16[4,192,768]{2,1,0:T(8,128)(2,1)} %copy-done.3) | copy-start | bytes 3538948
  32.8 18.4 %collective-permute-start.1 = (bf16[2,128,1536]{2,1,0:T(8,128)(2,1)S(1)}, bf16[2,128,1536]{2,1,0:T(8,128)(2,1)S(1)}, u32[]{:S(2)}, u32[]{:S(2)}) collective-permute-start(bf16[2,128,1536]{2,1,0:T(8,128)(2,1)S(1)} %pad_maximum_fusion.1.own), channel_id=1, source_target_pairs={{0,128},{128,256},{256,384},{384,0},{1,129},{129,257},{257,385},{3... | collective-permute-start | bytes 2359304 | tf_op jit(solution)/shard_map/ppermute | solution.py:19
  35.1 17.0 %collective-permute-start.2 = (bf16[2,128,1536]{2,1,0:T(8,128)(2,1)S(1)}, bf16[2,128,1536]{2,1,0:T(8,128)(2,1)S(1)}, u32[]{:S(2)}, u32[]{:S(2)}) collective-permute-start(bf16[2,128,1536]{2,1,0:T(8,128)(2,1)S(1)} %pad_maximum_fusion.1.own), channel_id=1, source_target_pairs={{0,384},{128,0},{256,128},{384,256},{1,385},{129,1},{257,129},{385... | collective-permute-start | bytes 2359304 | tf_op jit(solution)/shard_map/ppermute | solution.py:19
  46.7 16.2 %copy-start.10 = (f32[1536]{0:T(1024)S(1)}, f32[1536]{0:T(1024)}, u32[]{:S(2)}) copy-start(f32[1536]{0:T(1024)} %param.8) | copy-start | bytes 18436
  46.7 16.2 %copy-start.11 = (f32[1536]{0:T(1024)S(1)}, f32[1536]{0:T(1024)}, u32[]{:S(2)}) copy-start(f32[1536]{0:T(1024)} %param.9) | copy-start | bytes 18436
  52.1 37.0 %collective-permute-start.6 = (bf16[1536,768]{1,0:T(8,128)(2,1)}, bf16[1536,768]{1,0:T(8,128)(2,1)}, u32[]{:S(2)}, u32[]{:S(2)}) collective-permute-start(bf16[1536,768]{1,0:T(8,128)(2,1)} %bitcast.10), channel_id=1, source_target_pairs={{0,1},{1,0},{2,3},{3,2},{4,5},{5,4},{6,7},{7,6},{8,9},{9,8},{10,11... | collective-permute-start | bytes 7077896 | tf_op jit(solution)/shard_map/ppermute | solution.py:19
  59.0 22.7 %collective-permute-start.3 = (bf16[2,128,1536]{2,1,0:T(8,128)(2,1)S(1)}, bf16[2,128,1536]{2,1,0:T(8,128)(2,1)}, u32[]{:S(2)}, u32[]{:S(2)}) collective-permute-start(bf16[2,128,1536]{2,1,0:T(8,128)(2,1)S(1)} %pad_maximum_fusion.1.own), channel_id=1, source_target_pairs={{0,256},{128,384},{256,0},{384,128},{1,257},{129,385},{257,1},{385... | collective-permute-start | bytes 2359304 | tf_op jit(solution)/shard_map/ppermute | solution.py:19
  86.3 16.0 %copy-start.2 = (bf16[512,1536]{1,0:T(8,128)(2,1)}, bf16[512,1536]{1,0:T(8,128)(2,1)S(1)}, u32[]{:S(2)}) copy-start(bf16[512,1536]{1,0:T(8,128)(2,1)S(1)} %get-tuple-element.17) | copy-start | bytes 4718596
  86.3 18.5 %copy-start.1 = (f32[512,1536]{1,0:T(8,128)}, f32[512,1536]{1,0:T(8,128)S(1)}, u32[]{:S(2)}) copy-start(f32[512,1536]{1,0:T(8,128)S(1)} %get-tuple-element.25) | copy-start | bytes 9437188
  86.3 12.1 %collective-permute-start.7 = (bf16[512,1536]{1,0:T(8,128)(2,1)S(1)}, bf16[512,1536]{1,0:T(8,128)(2,1)S(1)}, u32[]{:S(2)}, u32[]{:S(2)}) collective-permute-start(bf16[512,1536]{1,0:T(8,128)(2,1)S(1)} %get-tuple-element.20), channel_id=1, source_target_pairs={{0,1},{1,0},{2,3},{3,2},{4,5},{5,4},{6,7},{7,6},{8,9},{9,8},{10,11... | collective-permute-start | bytes 4718600 | tf_op jit(solution)/shard_map/ppermute | solution.py:19
  102.9 6.3 %collective-permute-start.8 = (bf16[384,768]{1,0:T(8,128)(2,1)S(1)}, bf16[384,768]{1,0:T(8,128)(2,1)}, u32[]{:S(2)}, u32[]{:S(2)}) collective-permute-start(bf16[384,768]{1,0:T(8,128)(2,1)S(1)} %convolution_convert_fusion), channel_id=1, source_target_pairs={{0,1},{1,0},{2,3},{3,2},{4,5},{5,4},{6,7},{7,6},{8,9},{9,8},{10,11... | collective-permute-start | bytes 1769480 | tf_op jit(solution)/shard_map/ppermute | solution.py:19
  126.1 10.5 %all-to-all-start.2 = ((bf16[4,24,896]{2,1,0:T(8,128)(2,1)}), bf16[4,24,896]{2,1,0:T(8,128)(2,1)S(1)}, u32[]{:S(2)}, u32[]{:S(2)}) async-start(bf16[4,24,896]{2,1,0:T(8,128)(2,1)} %bitcast.15), calls=%async_computation.2 | async-start | bytes 344064 | tf_op jit(solution)/shard_map/all_to_all | solution.py:173
  137.3 25.2 %all-to-all-start.3 = ((bf16[4,24,896]{2,1,0:T(8,128)(2,1)}), bf16[4,24,896]{2,1,0:T(8,128)(2,1)S(1)}, u32[]{:S(2)}, u32[]{:S(2)}) async-start(bf16[4,24,896]{2,1,0:T(8,128)(2,1)} %broadcast_in_dim.28), calls=%async_computation.3 | async-start | bytes 344064 | tf_op jit(solution)/shard_map/all_to_all | solution.py:49
  151.1 17.8 %collective-permute-start.9 = (f32[128,1536]{1,0:T(8,128)}, f32[128,1536]{1,0:T(8,128)}, u32[]{:S(2)}, u32[]{:S(2)}) collective-permute-start(f32[128,1536]{1,0:T(8,128)} %fusion.38), channel_id=1, source_target_pairs={{0,1},{1,0},{2,3},{3,2},{4,5},{5,4},{6,7},{7,6},{8,9},{9,8},{10,11... | collective-permute-start | bytes 2359304 | tf_op jit(solution)/shard_map/ppermute | solution.py:19
  157.9 11.1 %copy-start.6 = (bf16[2,128,1536]{2,1,0:T(8,128)(2,1)S(1)}, bf16[2,128,1536]{2,1,0:T(8,128)(2,1)}, u32[]{:S(2)}) copy-start(bf16[2,128,1536]{2,1,0:T(8,128)(2,1)} %copy-done.5) | copy-start | bytes 2359300
  164.7 14.2 %all-to-all-start.4 = ((bf16[8,24,896]{2,1,0:T(8,128)(2,1)}), bf16[8,24,896]{2,1,0:T(8,128)(2,1)}, u32[]{:S(2)}, u32[]{:S(2)}) async-start(bf16[8,24,896]{2,1,0:T(8,128)(2,1)} %broadcast_in_dim.58), calls=%async_computation.4 | async-start | bytes 688128 | tf_op jit(solution)/shard_map/all_to_all | solution.py:49
  171.0 18.0 %collective-permute-start.10 = (bf16[2,128,1536]{2,1,0:T(8,128)(2,1)S(1)}, bf16[2,128,1536]{2,1,0:T(8,128)(2,1)S(1)}, u32[]{:S(2)}, u32[]{:S(2)}) collective-permute-start(bf16[2,128,1536]{2,1,0:T(8,128)(2,1)S(1)} %pad_maximum_fusion.2), channel_id=1, source_target_pairs={{0,0},{1,64},{64,1},{65,65},{2,2},{3,66},{66,3},{67,67},{4,4},{5,6... | collective-permute-start | bytes 2359304 | tf_op jit(solution)/shard_map/ppermute | solution.py:31
  178.9 12.4 %collective-permute-start.11 = (bf16[8,24,896]{2,1,0:T(8,128)(2,1)}, bf16[8,24,896]{2,1,0:T(8,128)(2,1)S(1)}, u32[]{:S(2)}, u32[]{:S(2)}) collective-permute-start(bf16[8,24,896]{2,1,0:T(8,128)(2,1)} %all-to-all-done.4), channel_id=1, source_target_pairs={{0,1},{1,0},{2,3},{3,2},{4,5},{5,4},{6,7},{7,6},{8,9},{9,8},{10,11... | collective-permute-start | bytes 1032200 | tf_op jit(solution)/shard_map/ppermute | solution.py:19
  (11 other events, 41.9 us)

commit v11 on v9

--- a/solution.py
+++ b/solution.py
@@ -119,7 +119,8 @@
 
     pair = jnp.stack([text_unit, feature_rows], 0)
     below, above, far = shift(pair, "y", 1), shift(pair, "y", -1), shift(pair, "y", 2)
-    weight = gather_weight(weight_blocks, xl, core, [below, above, far])
+    weight_blocks = after(weight_blocks, below, above)
+    weight = gather_weight(weight_blocks, xl, core, [far])
     text_same, normed, xhat = place([pair, below, above, far], final_norm_gain, final_norm_bias)
     text_other = shift(text_same, "core", 1)
     rows = normed.shape[0]

time: 193 us -> 193 us (level)
  local copies, waits for them, and re-layouts: 17 us -> 21.5 us
  starting transfers between devices: 80.2 us -> 76.7 us
    all_to_all x3, waiting for transfers between devices: 11.6 us -> 3.42 us  [spread_to(): return lax.all_to_all(many, axes, split_axis=0, concat_axis=0, tiled=True)]
    ppermute x8, waiting for transfers between devices: 21 us -> 26.8 us  [shift(): lax.ppermute(value, axis, [(i, (i + steps) % count) for i in range(count)])]
    ppermute x2, waiting for transfers between devices: 0.64 us -> 3.21 us  [shift_x(): lax.ppermute(value, ('xl', 'xh'), [(index(i), index(i + steps)) for i in...]
    ppermute x8, starting transfers between devices: 34.6 us -> 32.1 us  [shift(): lax.ppermute(value, axis, [(i, (i + steps) % count) for i in range(count)])]
    slice x1, local copies, waits for them, and re-layouts: 0.08 us -> 2.33 us  [gather_weight(): other = [shift_x(blocks[:2], 1), shift_x(blocks[2:], -1)]]
  transfers between devices with their start and end apart: 16 -> 16, of which waited for: 9 -> 8; matrix products, arithmetic and copies ran while one was open for 16% -> 17% of each run, Pallas kernels for 2% -> 2%
where the time goes in v11:
time: 193 us; the launch traced here: 191 us
  starting transfers between devices  76.7 us (40%)
  waiting for transfers between devices  44.3 us (23%)
  local copies, waits for them, and re-layouts  21.5 us (11%)
  matrix products  17 us (9%)
  blocking collectives  13.5 us (7%)
  other arithmetic  11.9 us (6%)
  Pallas kernels  3.46 us (2%)
  between operations  2.54 us (1%)
    ppermute x8, starting transfers between devices, shift(): lax.ppermute(value, axis, [(i, (i + steps) % count) for i in range(count)])  32.1 us
    ppermute x8, waiting for transfers between devices, shift(): lax.ppermute(value, axis, [(i, (i + steps) % count) for i in range(count)])  26.8 us
    all_to_all x3, starting transfers between devices, spread_to(): return lax.all_to_all(many, axes, split_axis=0, concat_axis=0, tiled=True)  20.9 us
    dot_general x10, matrix products, dot(): lax.dot_general(a, b, (((da,), (db,)), ((), ())), preferred_element_type=...  17 us
    all_to_all x1, blocking collectives, local(): lax.all_to_all(sent, ('xl', 'xh'), split_axis=0, concat_axis=0, tiled=True)  13.5 us
    ppermute x2, starting transfers between devices, swap(): return lax.ppermute(value, ('xl', 'core'), [(0, 0), (1, 2), (2, 1), (3, 3)])  12.6 us
    ppermute x2, starting transfers between devices, shift_x(): lax.ppermute(value, ('xl', 'xh'), [(index(i), index(i + steps)) for i in...  6.48 us
    ppermute x2, waiting for transfers between devices, swap(): return lax.ppermute(value, ('xl', 'core'), [(0, 0), (1, 2), (2, 1), (3, 3)])  6.44 us
  transfers between devices with their start and end apart: 16, of which 8 were waited for; matrix products, arithmetic and copies ran while one was open for 17% of the time, Pallas kernels for 2%

profile of v11, /device:TPU:1, one launch (start us, length us, event | category | flops | bytes accessed | tf_op | source)
XLA Modules:
  0.0 190.9 jit_solution(8008767808816949152)
XLA Ops:
  1.9 4.5 %collective-permute-start = (bf16[2,128,1536]{2,1,0:T(8,128)(2,1)S(1)}, bf16[2,128,1536]{2,1,0:T(8,128)(2,1)S(1)}, u32[]{:S(2)}, u32[]{:S(2)}) collective-permute-start(bf16[2,128,1536]{2,1,0:T(8,128)(2,1)S(1)} %pad_maximum_fusion), channel_id=1, source_target_pairs={{0,0},{1,64},{64,1},{65,65},{2,2},{3,66},{66,3},{67,67},{4,4},{5,6... | collective-permute-start | bytes 2359304 | tf_op jit(solution)/shard_map/ppermute | solution.py:31
  7.6 4.3 %all-to-all-start = ((bf16[4,192,768]{2,1,0:T(8,128)(2,1)}), bf16[4,192,768]{2,1,0:T(8,128)(2,1)}, u32[]{:S(2)}, u32[]{:S(2)}) async-start(bf16[4,192,768]{2,1,0:T(8,128)(2,1)} %broadcast_in_dim.22), calls=%async_computation | async-start | bytes 2359296 | tf_op jit(solution)/shard_map/all_to_all | solution.py:49
  11.8 4.2 %collective-permute-done = bf16[2,128,1536]{2,1,0:T(8,128)(2,1)S(1)} collective-permute-done((bf16[2,128,1536]{2,1,0:T(8,128)(2,1)S(1)}, bf16[2,128,1536]{2,1,0:T(8,128)(2,1)S(1)}, u32[]{:S(2)}, u32[]{:S(2)}) %collective-permute-start) | collective-permute-done | bytes 786464 | tf_op jit(solution)/shard_map/ppermute | solution.py:31
  17.8 3.2 %collective-permute-start.1 = (bf16[2,128,1536]{2,1,0:T(8,128)(2,1)S(1)}, bf16[2,128,1536]{2,1,0:T(8,128)(2,1)S(1)}, u32[]{:S(2)}, u32[]{:S(2)}) collective-permute-start(bf16[2,128,1536]{2,1,0:T(8,128)(2,1)S(1)} %pad_maximum_fusion.1.own), channel_id=1, source_target_pairs={{0,128},{128,256},{256,384},{384,0},{1,129},{129,257},{257,385},{3... | collective-permute-start | bytes 2359304 | tf_op jit(solution)/shard_map/ppermute | solution.py:19
  21.0 3.4 %collective-permute-start.2 = (bf16[2,128,1536]{2,1,0:T(8,128)(2,1)S(1)}, bf16[2,128,1536]{2,1,0:T(8,128)(2,1)S(1)}, u32[]{:S(2)}, u32[]{:S(2)}) collective-permute-start(bf16[2,128,1536]{2,1,0:T(8,128)(2,1)S(1)} %pad_maximum_fusion.1.own), channel_id=1, source_target_pairs={{0,384},{128,0},{256,128},{384,256},{1,385},{129,1},{257,129},{385... | collective-permute-start | bytes 2359304 | tf_op jit(solution)/shard_map/ppermute | solution.py:19
  25.1 19.5 %collective-permute-done.1.below = bf16[2,128,1536]{2,1,0:T(8,128)(2,1)S(1)} collective-permute-done((bf16[2,128,1536]{2,1,0:T(8,128)(2,1)S(1)}, bf16[2,128,1536]{2,1,0:T(8,128)(2,1)S(1)}, u32[]{:S(2)}, u32[]{:S(2)}) %collective-permute-start.1) | collective-permute-done | bytes 786464 | tf_op jit(solution)/shard_map/ppermute | solution.py:19
  48.8 4.6 %collective-permute-start.5 = (bf16[2,192,768]{2,1,0:T(8,128)(2,1)}, bf16[2,192,768]{2,1,0:T(8,128)(2,1)S(1)}, u32[]{:S(2)}, u32[]{:S(2)}) collective-permute-start(bf16[2,192,768]{2,1,0:T(8,128)(2,1)} %get-tuple-element.35), channel_id=1, source_target_pairs={{0,66},{64,0},{2,64},{66,2},{1,67},{65,1},{3,65},{67,3},{4,70},{68... | collective-permute-start | bytes 1769480 | tf_op jit(solution)/shard_map/ppermute | solution.py:27
  53.4 3.0 %collective-permute-start.3 = (bf16[2,128,1536]{2,1,0:T(8,128)(2,1)S(1)}, bf16[2,128,1536]{2,1,0:T(8,128)(2,1)S(1)}, u32[]{:S(2)}, u32[]{:S(2)}) collective-permute-start(bf16[2,128,1536]{2,1,0:T(8,128)(2,1)S(1)} %pad_maximum_fusion.1.own), channel_id=1, source_target_pairs={{0,256},{128,384},{256,0},{384,128},{1,257},{129,385},{257,1},{385... | collective-permute-start | bytes 2359304 | tf_op jit(solution)/shard_map/ppermute | solution.py:19
  60.4 3.2 %collective-permute-done.4 = bf16[2,192,768]{2,1,0:T(8,128)(2,1)} collective-permute-done((bf16[2,192,768]{2,1,0:T(8,128)(2,1)}, bf16[2,192,768]{2,1,0:T(8,128)(2,1)}, u32[]{:S(2)}, u32[]{:S(2)}) %collective-permute-start.4) | collective-permute-done | bytes 589856 | tf_op jit(solution)/shard_map/ppermute | solution.py:27
  66.4 7.3 %collective-permute-done.3.far = bf16[2,128,1536]{2,1,0:T(8,128)(2,1)S(1)} collective-permute-done((bf16[2,128,1536]{2,1,0:T(8,128)(2,1)S(1)}, bf16[2,128,1536]{2,1,0:T(8,128)(2,1)S(1)}, u32[]{:S(2)}, u32[]{:S(2)}) %collective-permute-start.3) | collective-permute-done | bytes 786464 | tf_op jit(solution)/shard_map/ppermute | solution.py:19
  74.6 4.9 %collective-permute-start.6 = (bf16[1536,768]{1,0:T(8,128)(2,1)}, bf16[1536,768]{1,0:T(8,128)(2,1)}, u32[]{:S(2)}, u32[]{:S(2)}) collective-permute-start(bf16[1536,768]{1,0:T(8,128)(2,1)} %bitcast.10), channel_id=1, source_target_pairs={{0,1},{1,0},{2,3},{3,2},{4,5},{5,4},{6,7},{7,6},{8,9},{9,8},{10,11... | collective-permute-start | bytes 7077896 | tf_op jit(solution)/shard_map/ppermute | solution.py:19
  82.1 3.5 %shard_map.110 = (bf16[512,1536]{1,0:T(8,128)(2,1)S(1)}, bf16[512,1536]{1,0:T(8,128)(2,1)S(1)}, f32[512,1536]{1,0:T(8,128)S(1)}) custom-call(bf16[2,128,1536]{2,1,0:T(8,128)(2,1)S(1)} %pad_maximum_fusion.1.own, bf16[2,128,1536]{2,1,0:T(8,128)(2,1)S(1)} %collective-permute-done.1.below, bf16[2,128,1536]{2,1,0:T(8,128)(2,1)S(1)} %collective-permute-done.2.above, ...), custom_call_target="tpu_custom_call" | custom-call | tf_op jit(solution)/shard_map/pallas_call | solution.py:93
  91.6 2.7 %multiply_reduce_fusion.2 = (f32[512]{0:T(512)S(1)}, f32[512,1536]{1,0:T(8,128)S(1)}) fusion(bf16[512,1536]{1,0:T(8,128)(2,1)S(1)} %get-tuple-element.17, bf16[1536,1536]{1,0:T(8,128)(2,1)S(1)} %constant_dynamic-update-slice_fusion), kind=kOutput, calls=%fused_computation.6 | convolution fusion | flops 2417491456 | bytes 9439232 | tf_op jit(solution)/shard_map/dot_general | solution.py:43
  100.2 2.4 %collective-permute-start.8 = (bf16[384,768]{1,0:T(8,128)(2,1)S(1)}, bf16[384,768]{1,0:T(8,128)(2,1)}, u32[]{:S(2)}, u32[]{:S(2)}) collective-permute-start(bf16[384,768]{1,0:T(8,128)(2,1)S(1)} %convolution_convert_fusion), channel_id=1, source_target_pairs={{0,1},{1,0},{2,3},{3,2},{4,5},{5,4},{6,7},{7,6},{8,9},{9,8},{10,11... | collective-permute-start | bytes 1769480 | tf_op jit(solution)/shard_map/ppermute | solution.py:19
  102.6 4.3 %multiply_reduce_fusion = (bf16[1536]{0:T(1024)(128)(2,1)S(1)}, bf16[1536]{0:T(1024)(128)(2,1)S(1)}, f32[512,1536]{1,0:T(8,128)}) fusion(f32[512,1536]{1,0:T(8,128)S(1)} %get-tuple-element.25, bf16[512,1536]{1,0:T(8,128)(2,1)S(1)} %subtract_convert_fusion, bf16[1536,1536]{1,0:T(8,128)(2,1)S(1)} %constant_dynamic-update-slice_fusion), kind=kOutput, calls=%fused_computation.2 | convolution fusion | flops 2418275328 | bytes 12589056 | tf_op jit(solution)/shard_map/dot_general | solution.py:43
  109.1 13.5 %all_to_all.25 = bf16[4,96,896]{2,1,0:T(8,128)(2,1)S(1)} all-to-all(bf16[4,96,896]{2,1,0:T(8,128)(2,1)S(1)} %pad_maximum_fusion.3), channel_id=1, replica_groups=mesh['y'=4,'xl'=2,'zh'=4,'zl'=4,'xh'=2,'core'=2] {'xl','xh'}, dimensions={0} | all-to-all | bytes 1376256 | tf_op jit(solution)/shard_map/all_to_all | solution.py:166
  123.4 4.6 %all-to-all-start.2 = ((bf16[4,24,896]{2,1,0:T(8,128)(2,1)}), bf16[4,24,896]{2,1,0:T(8,128)(2,1)S(1)}, u32[]{:S(2)}, u32[]{:S(2)}) async-start(bf16[4,24,896]{2,1,0:T(8,128)(2,1)} %bitcast.15), calls=%async_computation.2 | async-start | bytes 344064 | tf_op jit(solution)/shard_map/all_to_all | solution.py:170
  128.5 4.4 %all-to-all-done.2 = bf16[4,24,896]{2,1,0:T(8,128)(2,1)S(1)} async-done(((bf16[4,24,896]{2,1,0:T(8,128)(2,1)}), bf16[4,24,896]{2,1,0:T(8,128)(2,1)S(1)}, u32[]{:S(2)}, u32[]{:S(2)}) %all-to-all-start.2) | async-done | bytes 172064 | tf_op jit(solution)/shard_map/all_to_all | solution.py:170
  133.6 12.5 %all-to-all-start.3 = ((bf16[4,24,896]{2,1,0:T(8,128)(2,1)}), bf16[4,24,896]{2,1,0:T(8,128)(2,1)S(1)}, u32[]{:S(2)}, u32[]{:S(2)}) async-start(bf16[4,24,896]{2,1,0:T(8,128)(2,1)} %broadcast_in_dim.28), calls=%async_computation.3 | async-start | bytes 344064 | tf_op jit(solution)/shard_map/all_to_all | solution.py:49
  147.4 5.4 %collective-permute-start.9 = (f32[128,1536]{1,0:T(8,128)}, f32[128,1536]{1,0:T(8,128)}, u32[]{:S(2)}, u32[]{:S(2)}) collective-permute-start(f32[128,1536]{1,0:T(8,128)} %fusion.38), channel_id=1, source_target_pairs={{0,1},{1,0},{2,3},{3,2},{4,5},{5,4},{6,7},{7,6},{8,9},{9,8},{10,11... | collective-permute-start | bytes 2359304 | tf_op jit(solution)/shard_map/ppermute | solution.py:19
  156.1 2.8 %all-to-all-done.3 = bf16[4,24,896]{2,1,0:T(8,128)(2,1)S(1)} async-done(((bf16[4,24,896]{2,1,0:T(8,128)(2,1)}), bf16[4,24,896]{2,1,0:T(8,128)(2,1)S(1)}, u32[]{:S(2)}, u32[]{:S(2)}) %all-to-all-start.3) | async-done | bytes 172064 | tf_op jit(solution)/shard_map/all_to_all | solution.py:49
  161.0 4.1 %all-to-all-start.4 = ((bf16[8,24,896]{2,1,0:T(8,128)(2,1)}), bf16[8,24,896]{2,1,0:T(8,128)(2,1)}, u32[]{:S(2)}, u32[]{:S(2)}) async-start(bf16[8,24,896]{2,1,0:T(8,128)(2,1)} %broadcast_in_dim.58), calls=%async_computation.4 | async-start | bytes 688128 | tf_op jit(solution)/shard_map/all_to_all | solution.py:49
  167.2 8.1 %collective-permute-start.10 = (bf16[2,128,1536]{2,1,0:T(8,128)(2,1)S(1)}, bf16[2,128,1536]{2,1,0:T(8,128)(2,1)S(1)}, u32[]{:S(2)}, u32[]{:S(2)}) collective-permute-start(bf16[2,128,1536]{2,1,0:T(8,128)(2,1)S(1)} %pad_maximum_fusion.2), channel_id=1, source_target_pairs={{0,0},{1,64},{64,1},{65,65},{2,2},{3,66},{66,3},{67,67},{4,4},{5,6... | collective-permute-start | bytes 2359304 | tf_op jit(solution)/shard_map/ppermute | solution.py:31
  175.3 7.9 %collective-permute-start.11 = (bf16[8,24,896]{2,1,0:T(8,128)(2,1)}, bf16[8,24,896]{2,1,0:T(8,128)(2,1)S(1)}, u32[]{:S(2)}, u32[]{:S(2)}) collective-permute-start(bf16[8,24,896]{2,1,0:T(8,128)(2,1)} %all-to-all-done.4), channel_id=1, source_target_pairs={{0,1},{1,0},{2,3},{3,2},{4,5},{5,4},{6,7},{7,6},{8,9},{9,8},{10,11... | collective-permute-start | bytes 1032200 | tf_op jit(solution)/shard_map/ppermute | solution.py:19
  (105 shorter events, 50.1 us)
Async XLA Ops:
  1.9 14.2 %collective-permute-start = (bf16[2,128,1536]{2,1,0:T(8,128)(2,1)S(1)}, bf16[2,128,1536]{2,1,0:T(8,128)(2,1)S(1)}, u32[]{:S(2)}, u32[]{:S(2)}) collective-permute-start(bf16[2,128,1536]{2,1,0:T(8,128)(2,1)S(1)} %pad_maximum_fusion), channel_id=1, source_target_pairs={{0,0},{1,64},{64,1},{65,65},{2,2},{3,66},{66,3},{67,67},{4,4},{5,6... | collective-permute-start | bytes 2359304 | tf_op jit(solution)/shard_map/ppermute | solution.py:31
  7.6 17.5 %all-to-all-start = ((bf16[4,192,768]{2,1,0:T(8,128)(2,1)}), bf16[4,192,768]{2,1,0:T(8,128)(2,1)}, u32[]{:S(2)}, u32[]{:S(2)}) async-start(bf16[4,192,768]{2,1,0:T(8,128)(2,1)} %broadcast_in_dim.22), calls=%async_computation | async-start | bytes 2359296 | tf_op jit(solution)/shard_map/all_to_all | solution.py:49
  17.8 26.7 %collective-permute-start.1 = (bf16[2,128,1536]{2,1,0:T(8,128)(2,1)S(1)}, bf16[2,128,1536]{2,1,0:T(8,128)(2,1)S(1)}, u32[]{:S(2)}, u32[]{:S(2)}) collective-permute-start(bf16[2,128,1536]{2,1,0:T(8,128)(2,1)S(1)} %pad_maximum_fusion.1.own), channel_id=1, source_target_pairs={{0,128},{128,256},{256,384},{384,0},{1,129},{129,257},{257,385},{3... | collective-permute-start | bytes 2359304 | tf_op jit(solution)/shard_map/ppermute | solution.py:19
  21.0 23.5 %collective-permute-start.2 = (bf16[2,128,1536]{2,1,0:T(8,128)(2,1)S(1)}, bf16[2,128,1536]{2,1,0:T(8,128)(2,1)S(1)}, u32[]{:S(2)}, u32[]{:S(2)}) collective-permute-start(bf16[2,128,1536]{2,1,0:T(8,128)(2,1)S(1)} %pad_maximum_fusion.1.own), channel_id=1, source_target_pairs={{0,384},{128,0},{256,128},{384,256},{1,385},{129,1},{257,129},{385... | collective-permute-start | bytes 2359304 | tf_op jit(solution)/shard_map/ppermute | solution.py:19
  46.9 16.7 %collective-permute-start.4 = (bf16[2,192,768]{2,1,0:T(8,128)(2,1)}, bf16[2,192,768]{2,1,0:T(8,128)(2,1)}, u32[]{:S(2)}, u32[]{:S(2)}) collective-permute-start(bf16[2,192,768]{2,1,0:T(8,128)(2,1)} %get-tuple-element.36), channel_id=1, source_target_pairs={{0,64},{64,2},{2,66},{66,0},{1,65},{65,3},{3,67},{67,1},{4,68},{68... | collective-permute-start | bytes 1769480 | tf_op jit(solution)/shard_map/ppermute | solution.py:27
  48.8 16.7 %collective-permute-start.5 = (bf16[2,192,768]{2,1,0:T(8,128)(2,1)}, bf16[2,192,768]{2,1,0:T(8,128)(2,1)S(1)}, u32[]{:S(2)}, u32[]{:S(2)}) collective-permute-start(bf16[2,192,768]{2,1,0:T(8,128)(2,1)} %get-tuple-element.35), channel_id=1, source_target_pairs={{0,66},{64,0},{2,64},{66,2},{1,67},{65,1},{3,65},{67,3},{4,70},{68... | collective-permute-start | bytes 1769480 | tf_op jit(solution)/shard_map/ppermute | solution.py:27
  53.4 20.3 %collective-permute-start.3 = (bf16[2,128,1536]{2,1,0:T(8,128)(2,1)S(1)}, bf16[2,128,1536]{2,1,0:T(8,128)(2,1)S(1)}, u32[]{:S(2)}, u32[]{:S(2)}) collective-permute-start(bf16[2,128,1536]{2,1,0:T(8,128)(2,1)S(1)} %pad_maximum_fusion.1.own), channel_id=1, source_target_pairs={{0,256},{128,384},{256,0},{384,128},{1,257},{129,385},{257,1},{385... | collective-permute-start | bytes 2359304 | tf_op jit(solution)/shard_map/ppermute | solution.py:19
  60.4 19.2 %copy-start.9 = (f32[1536]{0:T(1024)S(1)}, f32[1536]{0:T(1024)}, u32[]{:S(2)}) copy-start(f32[1536]{0:T(1024)} %param.8) | copy-start | bytes 18436
  60.4 19.2 %copy-start.10 = (f32[1536]{0:T(1024)S(1)}, f32[1536]{0:T(1024)}, u32[]{:S(2)}) copy-start(f32[1536]{0:T(1024)} %param.9) | copy-start | bytes 18436
  74.6 15.1 %collective-permute-start.6 = (bf16[1536,768]{1,0:T(8,128)(2,1)}, bf16[1536,768]{1,0:T(8,128)(2,1)}, u32[]{:S(2)}, u32[]{:S(2)}) collective-permute-start(bf16[1536,768]{1,0:T(8,128)(2,1)} %bitcast.10), channel_id=1, source_target_pairs={{0,1},{1,0},{2,3},{3,2},{4,5},{5,4},{6,7},{7,6},{8,9},{9,8},{10,11... | collective-permute-start | bytes 7077896 | tf_op jit(solution)/shard_map/ppermute | solution.py:19
  85.5 14.2 %copy-start.4 = (bf16[512,1536]{1,0:T(8,128)(2,1)}, bf16[512,1536]{1,0:T(8,128)(2,1)S(1)}, u32[]{:S(2)}) copy-start(bf16[512,1536]{1,0:T(8,128)(2,1)S(1)} %get-tuple-element.17) | copy-start | bytes 4718596
  85.5 17.1 %copy-start.1 = (f32[512,1536]{1,0:T(8,128)}, f32[512,1536]{1,0:T(8,128)S(1)}, u32[]{:S(2)}) copy-start(f32[512,1536]{1,0:T(8,128)S(1)} %get-tuple-element.25) | copy-start | bytes 9437188
  85.5 10.2 %collective-permute-start.7 = (bf16[512,1536]{1,0:T(8,128)(2,1)S(1)}, bf16[512,1536]{1,0:T(8,128)(2,1)S(1)}, u32[]{:S(2)}, u32[]{:S(2)}) collective-permute-start(bf16[512,1536]{1,0:T(8,128)(2,1)S(1)} %get-tuple-element.20), channel_id=1, source_target_pairs={{0,1},{1,0},{2,3},{3,2},{4,5},{5,4},{6,7},{7,6},{8,9},{9,8},{10,11... | collective-permute-start | bytes 4718600 | tf_op jit(solution)/shard_map/ppermute | solution.py:19
  99.7 7.3 %copy-start.7 = (bf16[512,1536]{1,0:T(8,128)(2,1)}, bf16[512,1536]{1,0:T(8,128)(2,1)S(1)}, u32[]{:S(2)}) copy-start(bf16[512,1536]{1,0:T(8,128)(2,1)S(1)} %subtract_convert_fusion) | copy-start | bytes 4718596
  100.2 6.8 %collective-permute-start.8 = (bf16[384,768]{1,0:T(8,128)(2,1)S(1)}, bf16[384,768]{1,0:T(8,128)(2,1)}, u32[]{:S(2)}, u32[]{:S(2)}) collective-permute-start(bf16[384,768]{1,0:T(8,128)(2,1)S(1)} %convolution_convert_fusion), channel_id=1, source_target_pairs={{0,1},{1,0},{2,3},{3,2},{4,5},{5,4},{6,7},{7,6},{8,9},{9,8},{10,11... | collective-permute-start | bytes 1769480 | tf_op jit(solution)/shard_map/ppermute | solution.py:19
  109.1 18.9 %copy-start.15 = (f32[128]{0:T(128)S(1)}, f32[128]{0:T(128)}, u32[]{:S(2)}) copy-start(f32[128]{0:T(128)} %get-tuple-element.33) | copy-start | bytes 1540
  123.4 9.5 %all-to-all-start.2 = ((bf16[4,24,896]{2,1,0:T(8,128)(2,1)}), bf16[4,24,896]{2,1,0:T(8,128)(2,1)S(1)}, u32[]{:S(2)}, u32[]{:S(2)}) async-start(bf16[4,24,896]{2,1,0:T(8,128)(2,1)} %bitcast.15), calls=%async_computation.2 | async-start | bytes 344064 | tf_op jit(solution)/shard_map/all_to_all | solution.py:170
  133.6 25.2 %all-to-all-start.3 = ((bf16[4,24,896]{2,1,0:T(8,128)(2,1)}), bf16[4,24,896]{2,1,0:T(8,128)(2,1)S(1)}, u32[]{:S(2)}, u32[]{:S(2)}) async-start(bf16[4,24,896]{2,1,0:T(8,128)(2,1)} %broadcast_in_dim.28), calls=%async_computation.3 | async-start | bytes 344064 | tf_op jit(solution)/shard_map/all_to_all | solution.py:49
  146.2 8.2 %copy-start.16 = (f32[128]{0:T(128)S(1)}, f32[128]{0:T(128)}, u32[]{:S(2)}) copy-start(f32[128]{0:T(128)} %add_rsqrt_fusion.2) | copy-start | bytes 1540
  147.4 17.7 %collective-permute-start.9 = (f32[128,1536]{1,0:T(8,128)}, f32[128,1536]{1,0:T(8,128)}, u32[]{:S(2)}, u32[]{:S(2)}) collective-permute-start(f32[128,1536]{1,0:T(8,128)} %fusion.38), channel_id=1, source_target_pairs={{0,1},{1,0},{2,3},{3,2},{4,5},{5,4},{6,7},{7,6},{8,9},{9,8},{10,11... | collective-permute-start | bytes 2359304 | tf_op jit(solution)/shard_map/ppermute | solution.py:19
  154.4 10.8 %copy-start.6 = (bf16[2,128,1536]{2,1,0:T(8,128)(2,1)S(1)}, bf16[2,128,1536]{2,1,0:T(8,128)(2,1)}, u32[]{:S(2)}) copy-start(bf16[2,128,1536]{2,1,0:T(8,128)(2,1)} %copy-done.5) | copy-start | bytes 2359300
  161.0 14.3 %all-to-all-start.4 = ((bf16[8,24,896]{2,1,0:T(8,128)(2,1)}), bf16[8,24,896]{2,1,0:T(8,128)(2,1)}, u32[]{:S(2)}, u32[]{:S(2)}) async-start(bf16[8,24,896]{2,1,0:T(8,128)(2,1)} %broadcast_in_dim.58), calls=%async_computation.4 | async-start | bytes 688128 | tf_op jit(solution)/shard_map/all_to_all | solution.py:49
  167.2 18.2 %collective-permute-start.10 = (bf16[2,128,1536]{2,1,0:T(8,128)(2,1)S(1)}, bf16[2,128,1536]{2,1,0:T(8,128)(2,1)S(1)}, u32[]{:S(2)}, u32[]{:S(2)}) collective-permute-start(bf16[2,128,1536]{2,1,0:T(8,128)(2,1)S(1)} %pad_maximum_fusion.2), channel_id=1, source_target_pairs={{0,0},{1,64},{64,1},{65,65},{2,2},{3,66},{66,3},{67,67},{4,4},{5,6... | collective-permute-start | bytes 2359304 | tf_op jit(solution)/shard_map/ppermute | solution.py:31
  175.3 12.4 %collective-permute-start.11 = (bf16[8,24,896]{2,1,0:T(8,128)(2,1)}, bf16[8,24,896]{2,1,0:T(8,128)(2,1)S(1)}, u32[]{:S(2)}, u32[]{:S(2)}) collective-permute-start(bf16[8,24,896]{2,1,0:T(8,128)(2,1)} %all-to-all-done.4), channel_id=1, source_target_pairs={{0,1},{1,0},{2,3},{3,2},{4,5},{5,4},{6,7},{7,6},{8,9},{9,8},{10,11... | collective-permute-start | bytes 1032200 | tf_op jit(solution)/shard_map/ppermute | solution.py:19
  (9 other events, 15.7 us)

commit v12 on v9

--- a/solution.py
+++ b/solution.py
@@ -67,6 +67,16 @@
     return weight
 
 
+def swap_along(value, steps):
+    pairs = [
+        (4 * y + 2 * xl + core, 4 * ((y + steps) % 4) + 2 * core + xl)
+        for y in range(4)
+        for xl in range(2)
+        for core in range(2)
+    ]
+    return lax.ppermute(value, ("y", "xl", "core"), pairs)
+
+
 def place_kernel(own, below, above, far, gain, bias, text, normed, xhat):
     rows = own.shape[1]
     lines = 32
@@ -75,7 +85,9 @@
         def body(step, carry, index=index, block=block):
             start = pl.multiple_of(step * lines, lines)
             source, target = pl.ds(start, lines), pl.ds(index * rows + start, lines)
-            text[target, :] = block[0, source, :]
+            words = block[0, source, :].astype(f32)
+            inverse = lax.rsqrt(jnp.sum(words * words, axis=1, keepdims=True) + epsilon)
+            text[target, :] = (words * inverse).astype(bf16)
             values = block[1, source, :].astype(f32)
             centered = values - jnp.mean(values, axis=1, keepdims=True)
             spread = jnp.mean(centered * centered, axis=1, keepdims=True)
@@ -109,18 +121,17 @@
     half = width // 2
     block = width // 4
 
-    text_rows, feature_rows = swap(jnp.stack([text_embed, image_features], 0))
     weight_part = lax.dynamic_slice(head_weight, (0, core * half), (head_weight.shape[0], half))
     weight_blocks = spread_to(weight_part, "y")
 
+    pair = jnp.stack([text_embed, image_features], 0)
+    mine, below, above, far = (swap_along(pair, step) for step in (0, 1, -1, 2))
+    weight_blocks = after(weight_blocks, mine, below, above)
+    weight = gather_weight(weight_blocks, xl, core, [far])
+    text_rows, feature_rows = mine
     text_values = text_rows.astype(f32)
     inv_text = lax.rsqrt(jnp.sum(text_values * text_values, axis=1, keepdims=True) + epsilon)
-    text_unit = (text_values * inv_text).astype(bf16)
-
-    pair = jnp.stack([text_unit, feature_rows], 0)
-    below, above, far = shift(pair, "y", 1), shift(pair, "y", -1), shift(pair, "y", 2)
-    weight = gather_weight(weight_blocks, xl, core, [below, above, far])
-    text_same, normed, xhat = place([pair, below, above, far], final_norm_gain, final_norm_bias)
+    text_same, normed, xhat = place([mine, below, above, far], final_norm_gain, final_norm_bias)
     text_other = shift(text_same, "core", 1)
     rows = normed.shape[0]
 
@@ -144,8 +155,8 @@
     theirs = lax.dynamic_slice(grad_proj, (0, (1 - core) * half), (rows, half))
     sent = dot(normed_block, theirs, 0, 0).astype(bf16)
     grad_proj, sent = lax.optimization_barrier((grad_proj, sent))
-    mine = lax.dynamic_slice(grad_proj, (0, core * half), (rows, half))
-    head = dot(normed_block, mine, 0, 0) + shift(sent, "core", 1).astype(f32)
+    kept = lax.dynamic_slice(grad_proj, (0, core * half), (rows, half))
+    head = dot(normed_block, kept, 0, 0) + shift(sent, "core", 1).astype(f32)
     part = block // 4
     lanes = 128
 

time: 193 us -> 198 us (1.026)
  starting transfers between devices: 80.2 us -> 69.4 us
  blocking collectives: 14.6 us -> 24.4 us
  waiting for transfers between devices: 44.2 us -> 49 us
    ppermute x0 -> x4, waiting for transfers between devices: none -> 30.6 us  [swap_along(): return lax.ppermute(value, ('y', 'xl', 'core'), pairs)]
    ppermute x8 -> x5, waiting for transfers between devices: 21 us -> 0.01 us  [shift(): lax.ppermute(value, axis, [(i, (i + steps) % count) for i in range(count)])]
    ppermute x0 -> x4, starting transfers between devices: none -> 16.5 us  [swap_along(): return lax.ppermute(value, ('y', 'xl', 'core'), pairs)]
    ppermute x8 -> x5, starting transfers between devices: 34.6 us -> 18.8 us  [shift(): lax.ppermute(value, axis, [(i, (i + steps) % count) for i in range(count)])]
    all_to_all x0 -> x1, blocking collectives: none -> 10.2 us  [local(): lax.all_to_all(sent, 'zl', split_axis=0, concat_axis=0, tiled=True)]
    ppermute x2 -> x1, starting transfers between devices: 12.6 us -> 4.32 us  [swap(): return lax.ppermute(value, ('xl', 'core'), [(0, 0), (1, 2), (2, 1), (3, 3)])]
    all_to_all x1 -> x0, starting transfers between devices: 5.62 us -> none  [local(): lax.all_to_all(sent, 'zl', split_axis=0, concat_axis=0, tiled=True)]
    all_to_all x1 -> x0, waiting for transfers between devices: 4.42 us -> none  [local(): lax.all_to_all(sent, 'zl', split_axis=0, concat_axis=0, tiled=True)]
  transfers between devices with their start and end apart: 16 -> 15, of which waited for: 9 -> 9; matrix products, arithmetic and copies ran while one was open for 16% -> 15% of each run, Pallas kernels for 2% -> 2%
where the time goes in v12:
time: 198 us; the launch traced here: 197 us
  starting transfers between devices  69.4 us (35%)
  waiting for transfers between devices  49 us (25%)
  blocking collectives  24.4 us (12%)
  local copies, waits for them, and re-layouts  18.2 us (9%)
  matrix products  18 us (9%)
  other arithmetic  10.7 us (5%)
  Pallas kernels  4.83 us (2%)
  between operations  2.43 us (1%)
    ppermute x4, waiting for transfers between devices, swap_along(): return lax.ppermute(value, ('y', 'xl', 'core'), pairs)  30.6 us
    all_to_all x3, starting transfers between devices, spread_to(): return lax.all_to_all(many, axes, split_axis=0, concat_axis=0, tiled=True)  23.3 us
    ppermute x5, starting transfers between devices, shift(): lax.ppermute(value, axis, [(i, (i + steps) % count) for i in range(count)])  18.8 us
    dot_general x10, matrix products, dot(): lax.dot_general(a, b, (((da,), (db,)), ((), ())), preferred_element_type=...  18 us
    ppermute x4, starting transfers between devices, swap_along(): return lax.ppermute(value, ('y', 'xl', 'core'), pairs)  16.5 us
    all_to_all x1, blocking collectives, local(): lax.all_to_all(sent, ('xl', 'xh'), split_axis=0, concat_axis=0, tiled=True)  14.2 us
    all_to_all x3, waiting for transfers between devices, spread_to(): return lax.all_to_all(many, axes, split_axis=0, concat_axis=0, tiled=True)  12.6 us
    all_to_all x1, blocking collectives, local(): lax.all_to_all(sent, 'zl', split_axis=0, concat_axis=0, tiled=True)  10.2 us
  transfers between devices with their start and end apart: 15, of which 9 were waited for; matrix products, arithmetic and copies ran while one was open for 15% of the time, Pallas kernels for 2%

profile of v12, /device:TPU:1, one launch (start us, length us, event | category | flops | bytes accessed | tf_op | source)
XLA Modules:
  0.0 197.0 jit_solution(2694819355926642528)
XLA Ops:
  2.8 5.0 %all-to-all-start = ((bf16[4,192,768]{2,1,0:T(8,128)(2,1)}), bf16[4,192,768]{2,1,0:T(8,128)(2,1)}, u32[]{:S(2)}, u32[]{:S(2)}) async-start(bf16[4,192,768]{2,1,0:T(8,128)(2,1)} %broadcast_in_dim.22), calls=%async_computation | async-start | bytes 2359296 | tf_op jit(solution)/shard_map/all_to_all | solution.py:49
  8.8 3.9 %collective-permute-start = (bf16[2,128,1536]{2,1,0:T(8,128)(2,1)}, bf16[2,128,1536]{2,1,0:T(8,128)(2,1)S(1)}, u32[]{:S(2)}, u32[]{:S(2)}) collective-permute-start(bf16[2,128,1536]{2,1,0:T(8,128)(2,1)} %pad_maximum_fusion), channel_id=1, source_target_pairs={{0,0},{1,64},{64,1},{65,65},{128,128},{129,192},{192,129},{193,193... | collective-permute-start | bytes 2359304 | tf_op jit(solution)/shard_map/ppermute | solution.py:77
  12.8 3.4 %collective-permute-start.1 = (bf16[2,128,1536]{2,1,0:T(8,128)(2,1)}, bf16[2,128,1536]{2,1,0:T(8,128)(2,1)S(1)}, u32[]{:S(2)}, u32[]{:S(2)}) collective-permute-start(bf16[2,128,1536]{2,1,0:T(8,128)(2,1)} %pad_maximum_fusion), channel_id=1, source_target_pairs={{0,128},{1,192},{64,129},{65,193},{128,256},{129,320},{192,257},{1... | collective-permute-start | bytes 2359304 | tf_op jit(solution)/shard_map/ppermute | solution.py:77
  16.1 4.3 %collective-permute-start.2 = (bf16[2,128,1536]{2,1,0:T(8,128)(2,1)}, bf16[2,128,1536]{2,1,0:T(8,128)(2,1)S(1)}, u32[]{:S(2)}, u32[]{:S(2)}) collective-permute-start(bf16[2,128,1536]{2,1,0:T(8,128)(2,1)} %pad_maximum_fusion), channel_id=1, source_target_pairs={{0,384},{1,448},{64,385},{65,449},{128,0},{129,64},{192,1},{193,65... | collective-permute-start | bytes 2359304 | tf_op jit(solution)/shard_map/ppermute | solution.py:77
  20.4 2.6 %collective-permute-done.own = bf16[2,128,1536]{2,1,0:T(8,128)(2,1)S(1)} collective-permute-done((bf16[2,128,1536]{2,1,0:T(8,128)(2,1)}, bf16[2,128,1536]{2,1,0:T(8,128)(2,1)S(1)}, u32[]{:S(2)}, u32[]{:S(2)}) %collective-permute-start) | collective-permute-done | bytes 786464 | tf_op jit(solution)/shard_map/ppermute | solution.py:77
  23.0 10.8 %collective-permute-done.1.below = bf16[2,128,1536]{2,1,0:T(8,128)(2,1)S(1)} collective-permute-done((bf16[2,128,1536]{2,1,0:T(8,128)(2,1)}, bf16[2,128,1536]{2,1,0:T(8,128)(2,1)S(1)}, u32[]{:S(2)}, u32[]{:S(2)}) %collective-permute-start.1) | collective-permute-done | bytes 786464 | tf_op jit(solution)/shard_map/ppermute | solution.py:77
  33.8 7.5 %collective-permute-done.2.above = bf16[2,128,1536]{2,1,0:T(8,128)(2,1)S(1)} collective-permute-done((bf16[2,128,1536]{2,1,0:T(8,128)(2,1)}, bf16[2,128,1536]{2,1,0:T(8,128)(2,1)S(1)}, u32[]{:S(2)}, u32[]{:S(2)}) %collective-permute-start.2) | collective-permute-done | bytes 786464 | tf_op jit(solution)/shard_map/ppermute | solution.py:77
  43.7 3.1 %collective-permute-start.4 = (bf16[2,192,768]{2,1,0:T(8,128)(2,1)}, bf16[2,192,768]{2,1,0:T(8,128)(2,1)}, u32[]{:S(2)}, u32[]{:S(2)}) collective-permute-start(bf16[2,192,768]{2,1,0:T(8,128)(2,1)} %get-tuple-element.37), channel_id=1, source_target_pairs={{0,64},{64,2},{2,66},{66,0},{1,65},{65,3},{3,67},{67,1},{4,68},{68... | collective-permute-start | bytes 1769480 | tf_op jit(solution)/shard_map/ppermute | solution.py:27
  46.7 3.4 %collective-permute-start.5 = (bf16[2,192,768]{2,1,0:T(8,128)(2,1)}, bf16[2,192,768]{2,1,0:T(8,128)(2,1)S(1)}, u32[]{:S(2)}, u32[]{:S(2)}) collective-permute-start(bf16[2,192,768]{2,1,0:T(8,128)(2,1)} %get-tuple-element.36), channel_id=1, source_target_pairs={{0,66},{64,0},{2,64},{66,2},{1,67},{65,1},{3,65},{67,3},{4,70},{68... | collective-permute-start | bytes 1769480 | tf_op jit(solution)/shard_map/ppermute | solution.py:27
  50.2 4.9 %collective-permute-start.3 = (bf16[2,128,1536]{2,1,0:T(8,128)(2,1)}, bf16[2,128,1536]{2,1,0:T(8,128)(2,1)}, u32[]{:S(2)}, u32[]{:S(2)}) collective-permute-start(bf16[2,128,1536]{2,1,0:T(8,128)(2,1)} %pad_maximum_fusion), channel_id=1, source_target_pairs={{0,256},{1,320},{64,257},{65,321},{128,384},{129,448},{192,385},{1... | collective-permute-start | bytes 2359304 | tf_op jit(solution)/shard_map/ppermute | solution.py:77
  64.0 9.7 %collective-permute-done.3.far = bf16[2,128,1536]{2,1,0:T(8,128)(2,1)} collective-permute-done((bf16[2,128,1536]{2,1,0:T(8,128)(2,1)}, bf16[2,128,1536]{2,1,0:T(8,128)(2,1)}, u32[]{:S(2)}, u32[]{:S(2)}) %collective-permute-start.3) | collective-permute-done | bytes 786464 | tf_op jit(solution)/shard_map/ppermute | solution.py:77
  73.8 4.8 %collective-permute-start.6 = (bf16[1536,768]{1,0:T(8,128)(2,1)}, bf16[1536,768]{1,0:T(8,128)(2,1)}, u32[]{:S(2)}, u32[]{:S(2)}) collective-permute-start(bf16[1536,768]{1,0:T(8,128)(2,1)} %bitcast.9), channel_id=1, source_target_pairs={{0,1},{1,0},{2,3},{3,2},{4,5},{5,4},{6,7},{7,6},{8,9},{9,8},{10,11... | collective-permute-start | bytes 7077896 | tf_op jit(solution)/shard_map/ppermute | solution.py:19
  79.9 4.8 %shard_map.110 = (bf16[512,1536]{1,0:T(8,128)(2,1)S(1)}, bf16[512,1536]{1,0:T(8,128)(2,1)S(1)}, f32[512,1536]{1,0:T(8,128)S(1)}) custom-call(bf16[2,128,1536]{2,1,0:T(8,128)(2,1)S(1)} %collective-permute-done.own, bf16[2,128,1536]{2,1,0:T(8,128)(2,1)S(1)} %collective-permute-done.1.below, bf16[2,128,1536]{2,1,0:T(8,128)(2,1)S(1)} %collective-permute-done.2.above, ...), custom_call_target="tpu_custom_call" | custom-call | tf_op jit(solution)/shard_map/pallas_call | solution.py:105
  90.9 2.7 %multiply_reduce_fusion.2 = (f32[512]{0:T(512)S(1)}, f32[512,1536]{1,0:T(8,128)S(1)}) fusion(bf16[512,1536]{1,0:T(8,128)(2,1)S(1)} %get-tuple-element.17, bf16[1536,1536]{1,0:T(8,128)(2,1)S(1)} %constant_dynamic-update-slice_fusion), kind=kOutput, calls=%fused_computation.6 | convolution fusion | flops 2417491456 | bytes 9439232 | tf_op jit(solution)/shard_map/dot_general | solution.py:43
  102.7 4.3 %multiply_reduce_fusion = (bf16[1536]{0:T(1024)(128)(2,1)S(1)}, bf16[1536]{0:T(1024)(128)(2,1)S(1)}, f32[512,1536]{1,0:T(8,128)}) fusion(f32[512,1536]{1,0:T(8,128)S(1)} %get-tuple-element.25, bf16[512,1536]{1,0:T(8,128)(2,1)S(1)} %subtract_convert_fusion, bf16[1536,1536]{1,0:T(8,128)(2,1)S(1)} %constant_dynamic-update-slice_fusion), kind=kOutput, calls=%fused_computation.2 | convolution fusion | flops 2418275328 | bytes 12589056 | tf_op jit(solution)/shard_map/dot_general | solution.py:43
  109.2 14.2 %all_to_all.25 = bf16[4,96,896]{2,1,0:T(8,128)(2,1)} all-to-all(bf16[4,96,896]{2,1,0:T(8,128)(2,1)S(1)} %pad_maximum_fusion.2), channel_id=1, replica_groups=mesh['y'=4,'xl'=2,'zh'=4,'zl'=4,'xh'=2,'core'=2] {'xl','xh'}, dimensions={0} | all-to-all | bytes 1376256 | tf_op jit(solution)/shard_map/all_to_all | solution.py:176
  125.3 10.2 %all_to_all.26 = bf16[4,24,896]{2,1,0:T(8,128)(2,1)} all-to-all(bf16[4,24,896]{2,1,0:T(8,128)(2,1)} %bitcast.83), channel_id=1, replica_groups=mesh['y'=4,'xl'=2,'zh'=4,'zl'=4,'xh'=2,'core'=2] {'zl'}, dimensions={0} | all-to-all | bytes 344064 | tf_op jit(solution)/shard_map/all_to_all | solution.py:180
  137.7 4.5 %collective-permute-start.9 = (f32[128,1536]{1,0:T(8,128)}, f32[128,1536]{1,0:T(8,128)}, u32[]{:S(2)}, u32[]{:S(2)}) collective-permute-start(f32[128,1536]{1,0:T(8,128)} %fusion.34), channel_id=1, source_target_pairs={{0,1},{1,0},{2,3},{3,2},{4,5},{5,4},{6,7},{7,6},{8,9},{9,8},{10,11... | collective-permute-start | bytes 2359304 | tf_op jit(solution)/shard_map/ppermute | solution.py:19
  143.1 13.0 %all-to-all-start.3 = ((bf16[4,24,896]{2,1,0:T(8,128)(2,1)}), bf16[4,24,896]{2,1,0:T(8,128)(2,1)S(1)}, u32[]{:S(2)}, u32[]{:S(2)}) async-start(bf16[4,24,896]{2,1,0:T(8,128)(2,1)} %broadcast_in_dim.28), calls=%async_computation.3 | async-start | bytes 344064 | tf_op jit(solution)/shard_map/all_to_all | solution.py:49
  157.6 11.3 %all-to-all-done.3 = bf16[4,24,896]{2,1,0:T(8,128)(2,1)S(1)} async-done(((bf16[4,24,896]{2,1,0:T(8,128)(2,1)}), bf16[4,24,896]{2,1,0:T(8,128)(2,1)S(1)}, u32[]{:S(2)}, u32[]{:S(2)}) %all-to-all-start.3) | async-done | bytes 172064 | tf_op jit(solution)/shard_map/all_to_all | solution.py:49
  169.7 5.3 %all-to-all-start.4 = ((bf16[8,24,896]{2,1,0:T(8,128)(2,1)}), bf16[8,24,896]{2,1,0:T(8,128)(2,1)S(1)}, u32[]{:S(2)}, u32[]{:S(2)}) async-start(bf16[8,24,896]{2,1,0:T(8,128)(2,1)} %broadcast_in_dim.58), calls=%async_computation.4 | async-start | bytes 688128 | tf_op jit(solution)/shard_map/all_to_all | solution.py:49
  178.7 4.3 %collective-permute-start.10 = (bf16[2,128,1536]{2,1,0:T(8,128)(2,1)S(1)}, bf16[2,128,1536]{2,1,0:T(8,128)(2,1)S(1)}, u32[]{:S(2)}, u32[]{:S(2)}) collective-permute-start(bf16[2,128,1536]{2,1,0:T(8,128)(2,1)S(1)} %pad_maximum_fusion.1), channel_id=1, source_target_pairs={{0,0},{1,64},{64,1},{65,65},{2,2},{3,66},{66,3},{67,67},{4,4},{5,6... | collective-permute-start | bytes 2359304 | tf_op jit(solution)/shard_map/ppermute | solution.py:31
  184.3 5.2 %collective-permute-start.11 = (bf16[8,24,896]{2,1,0:T(8,128)(2,1)S(1)}, bf16[8,24,896]{2,1,0:T(8,128)(2,1)S(1)}, u32[]{:S(2)}, u32[]{:S(2)}) collective-permute-start(bf16[8,24,896]{2,1,0:T(8,128)(2,1)S(1)} %all-to-all-done.4), channel_id=1, source_target_pairs={{0,1},{1,0},{2,3},{3,2},{4,5},{5,4},{6,7},{7,6},{8,9},{9,8},{10,11... | collective-permute-start | bytes 1032200 | tf_op jit(solution)/shard_map/ppermute | solution.py:19
  189.6 3.5 %collective-permute-done.10 = bf16[2,128,1536]{2,1,0:T(8,128)(2,1)S(1)} collective-permute-done((bf16[2,128,1536]{2,1,0:T(8,128)(2,1)S(1)}, bf16[2,128,1536]{2,1,0:T(8,128)(2,1)S(1)}, u32[]{:S(2)}, u32[]{:S(2)}) %collective-permute-start.10) | collective-permute-done | bytes 786464 | tf_op jit(solution)/shard_map/ppermute | solution.py:31
  (82 shorter events, 47.7 us)
Async XLA Ops:
  0.6 1.1 copy-start
  1.7 6.1 %copy-start.5 = (bf16[128,1536]{1,0:T(8,128)(2,1)S(1)}, bf16[128,1536]{1,0:T(8,128)(2,1)}, u32[]{:S(2)}) copy-start(bf16[128,1536]{1,0:T(8,128)(2,1)} %param.7) | copy-start | bytes 1179652
  1.7 6.1 %copy-start.6 = (bf16[128,1536]{1,0:T(8,128)(2,1)S(1)}, bf16[128,1536]{1,0:T(8,128)(2,1)}, u32[]{:S(2)}) copy-start(bf16[128,1536]{1,0:T(8,128)(2,1)} %param.11) | copy-start | bytes 1179652
  2.8 38.5 %all-to-all-start = ((bf16[4,192,768]{2,1,0:T(8,128)(2,1)}), bf16[4,192,768]{2,1,0:T(8,128)(2,1)}, u32[]{:S(2)}, u32[]{:S(2)}) async-start(bf16[4,192,768]{2,1,0:T(8,128)(2,1)} %broadcast_in_dim.22), calls=%async_computation | async-start | bytes 2359296 | tf_op jit(solution)/shard_map/all_to_all | solution.py:49
  8.8 14.2 %collective-permute-start = (bf16[2,128,1536]{2,1,0:T(8,128)(2,1)}, bf16[2,128,1536]{2,1,0:T(8,128)(2,1)S(1)}, u32[]{:S(2)}, u32[]{:S(2)}) collective-permute-start(bf16[2,128,1536]{2,1,0:T(8,128)(2,1)} %pad_maximum_fusion), channel_id=1, source_target_pairs={{0,0},{1,64},{64,1},{65,65},{128,128},{129,192},{192,129},{193,193... | collective-permute-start | bytes 2359304 | tf_op jit(solution)/shard_map/ppermute | solution.py:77
  12.8 21.0 %collective-permute-start.1 = (bf16[2,128,1536]{2,1,0:T(8,128)(2,1)}, bf16[2,128,1536]{2,1,0:T(8,128)(2,1)S(1)}, u32[]{:S(2)}, u32[]{:S(2)}) collective-permute-start(bf16[2,128,1536]{2,1,0:T(8,128)(2,1)} %pad_maximum_fusion), channel_id=1, source_target_pairs={{0,128},{1,192},{64,129},{65,193},{128,256},{129,320},{192,257},{1... | collective-permute-start | bytes 2359304 | tf_op jit(solution)/shard_map/ppermute | solution.py:77
  16.1 25.2 %collective-permute-start.2 = (bf16[2,128,1536]{2,1,0:T(8,128)(2,1)}, bf16[2,128,1536]{2,1,0:T(8,128)(2,1)S(1)}, u32[]{:S(2)}, u32[]{:S(2)}) collective-permute-start(bf16[2,128,1536]{2,1,0:T(8,128)(2,1)} %pad_maximum_fusion), channel_id=1, source_target_pairs={{0,384},{1,448},{64,385},{65,449},{128,0},{129,64},{192,1},{193,65... | collective-permute-start | bytes 2359304 | tf_op jit(solution)/shard_map/ppermute | solution.py:77
  43.7 16.4 %collective-permute-start.4 = (bf16[2,192,768]{2,1,0:T(8,128)(2,1)}, bf16[2,192,768]{2,1,0:T(8,128)(2,1)}, u32[]{:S(2)}, u32[]{:S(2)}) collective-permute-start(bf16[2,192,768]{2,1,0:T(8,128)(2,1)} %get-tuple-element.37), channel_id=1, source_target_pairs={{0,64},{64,2},{2,66},{66,0},{1,65},{65,3},{3,67},{67,1},{4,68},{68... | collective-permute-start | bytes 1769480 | tf_op jit(solution)/shard_map/ppermute | solution.py:27
  46.7 16.4 %collective-permute-start.5 = (bf16[2,192,768]{2,1,0:T(8,128)(2,1)}, bf16[2,192,768]{2,1,0:T(8,128)(2,1)S(1)}, u32[]{:S(2)}, u32[]{:S(2)}) collective-permute-start(bf16[2,192,768]{2,1,0:T(8,128)(2,1)} %get-tuple-element.36), channel_id=1, source_target_pairs={{0,66},{64,0},{2,64},{66,2},{1,67},{65,1},{3,65},{67,3},{4,70},{68... | collective-permute-start | bytes 1769480 | tf_op jit(solution)/shard_map/ppermute | solution.py:27
  50.2 23.6 %collective-permute-start.3 = (bf16[2,128,1536]{2,1,0:T(8,128)(2,1)}, bf16[2,128,1536]{2,1,0:T(8,128)(2,1)}, u32[]{:S(2)}, u32[]{:S(2)}) collective-permute-start(bf16[2,128,1536]{2,1,0:T(8,128)(2,1)} %pad_maximum_fusion), channel_id=1, source_target_pairs={{0,256},{1,320},{64,257},{65,321},{128,384},{129,448},{192,385},{1... | collective-permute-start | bytes 2359304 | tf_op jit(solution)/shard_map/ppermute | solution.py:77
  59.0 19.6 %copy-start.7 = (f32[1536]{0:T(1024)S(1)}, f32[1536]{0:T(1024)}, u32[]{:S(2)}) copy-start(f32[1536]{0:T(1024)} %param.8) | copy-start | bytes 18436
  59.0 19.6 %copy-start.8 = (f32[1536]{0:T(1024)S(1)}, f32[1536]{0:T(1024)}, u32[]{:S(2)}) copy-start(f32[1536]{0:T(1024)} %param.9) | copy-start | bytes 18436
  73.8 15.2 %collective-permute-start.6 = (bf16[1536,768]{1,0:T(8,128)(2,1)}, bf16[1536,768]{1,0:T(8,128)(2,1)}, u32[]{:S(2)}, u32[]{:S(2)}) collective-permute-start(bf16[1536,768]{1,0:T(8,128)(2,1)} %bitcast.9), channel_id=1, source_target_pairs={{0,1},{1,0},{2,3},{3,2},{4,5},{5,4},{6,7},{7,6},{8,9},{9,8},{10,11... | collective-permute-start | bytes 7077896 | tf_op jit(solution)/shard_map/ppermute | solution.py:19
  84.8 14.2 %copy-start.2 = (bf16[512,1536]{1,0:T(8,128)(2,1)}, bf16[512,1536]{1,0:T(8,128)(2,1)S(1)}, u32[]{:S(2)}) copy-start(bf16[512,1536]{1,0:T(8,128)(2,1)S(1)} %get-tuple-element.17) | copy-start | bytes 4718596
  84.8 17.9 %copy-start.1 = (f32[512,1536]{1,0:T(8,128)}, f32[512,1536]{1,0:T(8,128)S(1)}, u32[]{:S(2)}) copy-start(f32[512,1536]{1,0:T(8,128)S(1)} %get-tuple-element.25) | copy-start | bytes 9437188
  84.8 10.2 %collective-permute-start.7 = (bf16[512,1536]{1,0:T(8,128)(2,1)S(1)}, bf16[512,1536]{1,0:T(8,128)(2,1)S(1)}, u32[]{:S(2)}, u32[]{:S(2)}) collective-permute-start(bf16[512,1536]{1,0:T(8,128)(2,1)S(1)} %get-tuple-element.20), channel_id=1, source_target_pairs={{0,1},{1,0},{2,3},{3,2},{4,5},{5,4},{6,7},{7,6},{8,9},{9,8},{10,11... | collective-permute-start | bytes 4718600 | tf_op jit(solution)/shard_map/ppermute | solution.py:19
  95.0 2.2 %copy-start.4 = (bf16[512,512]{1,0:T(8,128)(2,1)}, bf16[512,512]{1,0:T(8,128)(2,1)S(1)}, u32[]{:S(2)}) copy-start(bf16[512,512]{1,0:T(8,128)(2,1)S(1)} %fusion.16) | copy-start | bytes 1572868
  99.0 8.1 %copy-start.3 = (bf16[512,1536]{1,0:T(8,128)(2,1)}, bf16[512,1536]{1,0:T(8,128)(2,1)S(1)}, u32[]{:S(2)}) copy-start(bf16[512,1536]{1,0:T(8,128)(2,1)S(1)} %subtract_convert_fusion) | copy-start | bytes 4718596
  100.3 6.8 %collective-permute-start.8 = (bf16[384,768]{1,0:T(8,128)(2,1)}, bf16[384,768]{1,0:T(8,128)(2,1)}, u32[]{:S(2)}, u32[]{:S(2)}) collective-permute-start(bf16[384,768]{1,0:T(8,128)(2,1)} %convolution_convert_fusion), channel_id=1, source_target_pairs={{0,1},{1,0},{2,3},{3,2},{4,5},{5,4},{6,7},{7,6},{8,9},{9,8},{10,11... | collective-permute-start | bytes 1769480 | tf_op jit(solution)/shard_map/ppermute | solution.py:19
  137.7 37.3 %collective-permute-start.9 = (f32[128,1536]{1,0:T(8,128)}, f32[128,1536]{1,0:T(8,128)}, u32[]{:S(2)}, u32[]{:S(2)}) collective-permute-start(f32[128,1536]{1,0:T(8,128)} %fusion.34), channel_id=1, source_target_pairs={{0,1},{1,0},{2,3},{3,2},{4,5},{5,4},{6,7},{7,6},{8,9},{9,8},{10,11... | collective-permute-start | bytes 2359304 | tf_op jit(solution)/shard_map/ppermute | solution.py:19
  143.1 25.9 %all-to-all-start.3 = ((bf16[4,24,896]{2,1,0:T(8,128)(2,1)}), bf16[4,24,896]{2,1,0:T(8,128)(2,1)S(1)}, u32[]{:S(2)}, u32[]{:S(2)}) async-start(bf16[4,24,896]{2,1,0:T(8,128)(2,1)} %broadcast_in_dim.28), calls=%async_computation.3 | async-start | bytes 344064 | tf_op jit(solution)/shard_map/all_to_all | solution.py:49
  169.7 14.6 %all-to-all-start.4 = ((bf16[8,24,896]{2,1,0:T(8,128)(2,1)}), bf16[8,24,896]{2,1,0:T(8,128)(2,1)S(1)}, u32[]{:S(2)}, u32[]{:S(2)}) async-start(bf16[8,24,896]{2,1,0:T(8,128)(2,1)} %broadcast_in_dim.58), calls=%async_computation.4 | async-start | bytes 688128 | tf_op jit(solution)/shard_map/all_to_all | solution.py:49
  178.7 14.4 %collective-permute-start.10 = (bf16[2,128,1536]{2,1,0:T(8,128)(2,1)S(1)}, bf16[2,128,1536]{2,1,0:T(8,128)(2,1)S(1)}, u32[]{:S(2)}, u32[]{:S(2)}) collective-permute-start(bf16[2,128,1536]{2,1,0:T(8,128)(2,1)S(1)} %pad_maximum_fusion.1), channel_id=1, source_target_pairs={{0,0},{1,64},{64,1},{65,65},{2,2},{3,66},{66,3},{67,67},{4,4},{5,6... | collective-permute-start | bytes 2359304 | tf_op jit(solution)/shard_map/ppermute | solution.py:31
  184.3 10.1 %collective-permute-start.11 = (bf16[8,24,896]{2,1,0:T(8,128)(2,1)S(1)}, bf16[8,24,896]{2,1,0:T(8,128)(2,1)S(1)}, u32[]{:S(2)}, u32[]{:S(2)}) collective-permute-start(bf16[8,24,896]{2,1,0:T(8,128)(2,1)S(1)} %all-to-all-done.4), channel_id=1, source_target_pairs={{0,1},{1,0},{2,3},{3,2},{4,5},{5,4},{6,7},{7,6},{8,9},{9,8},{10,11... | collective-permute-start | bytes 1032200 | tf_op jit(solution)/shard_map/ppermute | solution.py:19

commit v13 on v9

--- a/solution.py
+++ b/solution.py
@@ -17,14 +17,6 @@
 def shift(value, axis, steps):
     count = lax.axis_size(axis)
     return lax.ppermute(value, axis, [(i, (i + steps) % count) for i in range(count)])
-
-
-def shift_x(value, steps):
-    def index(place):
-        place = place % 4
-        return (place % 2) * 2 + place // 2
-
-    return lax.ppermute(value, ("xl", "xh"), [(index(i), index(i + steps)) for i in range(4)])
 
 
 def swap(value):
@@ -51,20 +43,6 @@
 
 def after(value, *others):
     return lax.optimization_barrier((value,) + others)[0]
-
-
-def gather_weight(blocks, xl, core, earlier):
-    count, rows, half = blocks.shape
-    other = [shift_x(blocks[:2], 1), shift_x(blocks[2:], -1)]
-    own_half = jnp.zeros((count, 2, rows, half), bf16)
-    own_half = lax.dynamic_update_slice(own_half, blocks[:, None], (0, xl, 0, 0))
-    for start, block in zip((0, 2), other):
-        own_half = lax.dynamic_update_slice(own_half, block[:, None], (start, 1 - xl, 0, 0))
-    own_half = after(own_half.reshape(2 * count * rows, half), *earlier)
-    weight = jnp.zeros((2 * count * rows, 2 * half), bf16)
-    weight = lax.dynamic_update_slice(weight, own_half, (0, core * half))
-    weight = lax.dynamic_update_slice(weight, shift(own_half, "core", 1), (0, (1 - core) * half))
-    return weight
 
 
 def place_kernel(own, below, above, far, gain, bias, text, normed, xhat):
@@ -111,7 +89,7 @@
 
     text_rows, feature_rows = swap(jnp.stack([text_embed, image_features], 0))
     weight_part = lax.dynamic_slice(head_weight, (0, core * half), (head_weight.shape[0], half))
-    weight_blocks = spread_to(weight_part, "y")
+    weight_half = spread_to(weight_part, ("y", "xl")).reshape(width, half)
 
     text_values = text_rows.astype(f32)
     inv_text = lax.rsqrt(jnp.sum(text_values * text_values, axis=1, keepdims=True) + epsilon)
@@ -119,7 +97,10 @@
 
     pair = jnp.stack([text_unit, feature_rows], 0)
     below, above, far = shift(pair, "y", 1), shift(pair, "y", -1), shift(pair, "y", 2)
-    weight = gather_weight(weight_blocks, xl, core, [below, above, far])
+    weight = jnp.zeros((width, width), bf16)
+    weight = lax.dynamic_update_slice(weight, weight_half, (0, core * half))
+    weight_half = shift(after(weight_half, below, above, far), "core", 1)
+    weight = lax.dynamic_update_slice(weight, weight_half, (0, (1 - core) * half))
     text_same, normed, xhat = place([pair, below, above, far], final_norm_gain, final_norm_bias)
     text_other = shift(text_same, "core", 1)
     rows = normed.shape[0]

time: 193 us -> 194 us (level)
  waiting for transfers between devices: 44.2 us -> 57.3 us
  starting transfers between devices: 80.2 us -> 73.5 us
  local copies, waits for them, and re-layouts: 17 us -> 12.8 us
    ppermute x8, waiting for transfers between devices: 21 us -> 43.1 us  [shift(): lax.ppermute(value, axis, [(i, (i + steps) % count) for i in range(count)])]
    all_to_all x3, waiting for transfers between devices: 11.6 us -> 2.77 us  [spread_to(): return lax.all_to_all(many, axes, split_axis=0, concat_axis=0, tiled=True)]
    ppermute x2 -> x0, starting transfers between devices: 6.49 us -> none  [shift_x(): lax.ppermute(value, ('xl', 'xh'), [(index(i), index(i + steps)) for i in...]
    dynamic_update_slice x5 -> x2, local copies, waits for them, and re-layouts: 6.7 us -> 3.84 us  [the longest x1 1.92 us: local(): lax.dynamic_update_slice(weight, weight_half, (0, (1 - core) * half))]
  transfers between devices with their start and end apart: 16 -> 14, of which waited for: 9 -> 6; matrix products, arithmetic and copies ran while one was open for 16% -> 14% of each run, Pallas kernels for 2% -> 2%
where the time goes in v13:
time: 194 us; the launch traced here: 192 us
  starting transfers between devices  73.5 us (38%)
  waiting for transfers between devices  57.3 us (30%)
  matrix products  17 us (9%)
  blocking collectives  14.5 us (7%)
  local copies, waits for them, and re-layouts  12.8 us (7%)
  other arithmetic  11.4 us (6%)
  Pallas kernels  3.46 us (2%)
  between operations  2.54 us (1%)
    ppermute x8, waiting for transfers between devices, shift(): lax.ppermute(value, axis, [(i, (i + steps) % count) for i in range(count)])  43.1 us
    ppermute x8, starting transfers between devices, shift(): lax.ppermute(value, axis, [(i, (i + steps) % count) for i in range(count)])  34.2 us
    all_to_all x3, starting transfers between devices, spread_to(): return lax.all_to_all(many, axes, split_axis=0, concat_axis=0, tiled=True)  21 us
    dot_general x10, matrix products, dot(): lax.dot_general(a, b, (((da,), (db,)), ((), ())), preferred_element_type=...  17 us
    all_to_all x1, blocking collectives, local(): lax.all_to_all(sent, ('xl', 'xh'), split_axis=0, concat_axis=0, tiled=True)  14.5 us
    ppermute x2, starting transfers between devices, swap(): return lax.ppermute(value, ('xl', 'core'), [(0, 0), (1, 2), (2, 1), (3, 3)])  12.6 us
    ppermute x2, waiting for transfers between devices, swap(): return lax.ppermute(value, ('xl', 'core'), [(0, 0), (1, 2), (2, 1), (3, 3)])  6.96 us
    all_to_all x1, starting transfers between devices, local(): lax.all_to_all(sent, 'zl', split_axis=0, concat_axis=0, tiled=True)  5.62 us
  transfers between devices with their start and end apart: 14, of which 6 were waited for; matrix products, arithmetic and copies ran while one was open for 14% of the time, Pallas kernels for 2%

profile of v13, /device:TPU:1, one launch (start us, length us, event | category | flops | bytes accessed | tf_op | source)
XLA Modules:
  0.0 192.3 jit_solution(9133147238094366363)
XLA Ops:
  1.9 4.5 %collective-permute-start = (bf16[2,128,1536]{2,1,0:T(8,128)(2,1)S(1)}, bf16[2,128,1536]{2,1,0:T(8,128)(2,1)S(1)}, u32[]{:S(2)}, u32[]{:S(2)}) collective-permute-start(bf16[2,128,1536]{2,1,0:T(8,128)(2,1)S(1)} %pad_maximum_fusion), channel_id=1, source_target_pairs={{0,0},{1,64},{64,1},{65,65},{2,2},{3,66},{66,3},{67,67},{4,4},{5,6... | collective-permute-start | bytes 2359304 | tf_op jit(solution)/shard_map/ppermute | solution.py:23
  8.0 4.4 %all-to-all-start = ((bf16[8,192,768]{2,1,0:T(8,128)(2,1)}), bf16[8,192,768]{2,1,0:T(8,128)(2,1)}, u32[]{:S(2)}, u32[]{:S(2)}) async-start(bf16[8,192,768]{2,1,0:T(8,128)(2,1)} %broadcast_in_dim.13), calls=%async_computation | async-start | bytes 4718592 | tf_op jit(solution)/shard_map/all_to_all | solution.py:41
  12.4 4.8 %collective-permute-done = bf16[2,128,1536]{2,1,0:T(8,128)(2,1)S(1)} collective-permute-done((bf16[2,128,1536]{2,1,0:T(8,128)(2,1)S(1)}, bf16[2,128,1536]{2,1,0:T(8,128)(2,1)S(1)}, u32[]{:S(2)}, u32[]{:S(2)}) %collective-permute-start) | collective-permute-done | bytes 786464 | tf_op jit(solution)/shard_map/ppermute | solution.py:23
  18.3 3.7 %collective-permute-start.1 = (bf16[2,128,1536]{2,1,0:T(8,128)(2,1)S(1)}, bf16[2,128,1536]{2,1,0:T(8,128)(2,1)S(1)}, u32[]{:S(2)}, u32[]{:S(2)}) collective-permute-start(bf16[2,128,1536]{2,1,0:T(8,128)(2,1)S(1)} %pad_maximum_fusion.1.own), channel_id=1, source_target_pairs={{0,128},{128,256},{256,384},{384,0},{1,129},{129,257},{257,385},{3... | collective-permute-start | bytes 2359304 | tf_op jit(solution)/shard_map/ppermute | solution.py:19
  22.0 3.6 %collective-permute-start.2 = (bf16[2,128,1536]{2,1,0:T(8,128)(2,1)S(1)}, bf16[2,128,1536]{2,1,0:T(8,128)(2,1)S(1)}, u32[]{:S(2)}, u32[]{:S(2)}) collective-permute-start(bf16[2,128,1536]{2,1,0:T(8,128)(2,1)S(1)} %pad_maximum_fusion.1.own), channel_id=1, source_target_pairs={{0,384},{128,0},{256,128},{384,256},{1,385},{129,1},{257,129},{385... | collective-permute-start | bytes 2359304 | tf_op jit(solution)/shard_map/ppermute | solution.py:19
  25.6 3.4 %collective-permute-start.3 = (bf16[2,128,1536]{2,1,0:T(8,128)(2,1)S(1)}, bf16[2,128,1536]{2,1,0:T(8,128)(2,1)S(1)}, u32[]{:S(2)}, u32[]{:S(2)}) collective-permute-start(bf16[2,128,1536]{2,1,0:T(8,128)(2,1)S(1)} %pad_maximum_fusion.1.own), channel_id=1, source_target_pairs={{0,256},{128,384},{256,0},{384,128},{1,257},{129,385},{257,1},{385... | collective-permute-start | bytes 2359304 | tf_op jit(solution)/shard_map/ppermute | solution.py:19
  29.0 30.9 %collective-permute-done.1.below = bf16[2,128,1536]{2,1,0:T(8,128)(2,1)S(1)} collective-permute-done((bf16[2,128,1536]{2,1,0:T(8,128)(2,1)S(1)}, bf16[2,128,1536]{2,1,0:T(8,128)(2,1)S(1)}, u32[]{:S(2)}, u32[]{:S(2)}) %collective-permute-start.1) | collective-permute-done | bytes 786464 | tf_op jit(solution)/shard_map/ppermute | solution.py:19
  59.9 12.2 %collective-permute-done.3.far = bf16[2,128,1536]{2,1,0:T(8,128)(2,1)S(1)} collective-permute-done((bf16[2,128,1536]{2,1,0:T(8,128)(2,1)S(1)}, bf16[2,128,1536]{2,1,0:T(8,128)(2,1)S(1)}, u32[]{:S(2)}, u32[]{:S(2)}) %collective-permute-start.3) | collective-permute-done | bytes 786464 | tf_op jit(solution)/shard_map/ppermute | solution.py:19
  73.0 5.9 %collective-permute-start.4 = (bf16[1536,768]{1,0:T(8,128)(2,1)}, bf16[1536,768]{1,0:T(8,128)(2,1)}, u32[]{:S(2)}, u32[]{:S(2)}) collective-permute-start(bf16[1536,768]{1,0:T(8,128)(2,1)} %bitcast.5), channel_id=1, source_target_pairs={{0,1},{1,0},{2,3},{3,2},{4,5},{5,4},{6,7},{7,6},{8,9},{9,8},{10,11... | collective-permute-start | bytes 7077896 | tf_op jit(solution)/shard_map/ppermute | solution.py:19
  81.4 3.5 %shard_map.110 = (bf16[512,1536]{1,0:T(8,128)(2,1)S(1)}, bf16[512,1536]{1,0:T(8,128)(2,1)S(1)}, f32[512,1536]{1,0:T(8,128)S(1)}) custom-call(bf16[2,128,1536]{2,1,0:T(8,128)(2,1)S(1)} %pad_maximum_fusion.1.own, bf16[2,128,1536]{2,1,0:T(8,128)(2,1)S(1)} %collective-permute-done.1.below, bf16[2,128,1536]{2,1,0:T(8,128)(2,1)S(1)} %collective-permute-done.2.above, ...), custom_call_target="tpu_custom_call" | custom-call | tf_op jit(solution)/shard_map/pallas_call | solution.py:71
  91.0 2.7 %multiply_reduce_fusion.2 = (f32[512]{0:T(512)S(1)}, f32[512,1536]{1,0:T(8,128)S(1)}) fusion(bf16[512,1536]{1,0:T(8,128)(2,1)S(1)} %get-tuple-element.16, bf16[1536,1536]{1,0:T(8,128)(2,1)S(1)} %constant_dynamic-update-slice_fusion), kind=kOutput, calls=%fused_computation.6 | convolution fusion | flops 2417491456 | bytes 9439232 | tf_op jit(solution)/shard_map/dot_general | solution.py:35
  99.6 2.4 %collective-permute-start.6 = (bf16[384,768]{1,0:T(8,128)(2,1)S(1)}, bf16[384,768]{1,0:T(8,128)(2,1)}, u32[]{:S(2)}, u32[]{:S(2)}) collective-permute-start(bf16[384,768]{1,0:T(8,128)(2,1)S(1)} %convolution_convert_fusion), channel_id=1, source_target_pairs={{0,1},{1,0},{2,3},{3,2},{4,5},{5,4},{6,7},{7,6},{8,9},{9,8},{10,11... | collective-permute-start | bytes 1769480 | tf_op jit(solution)/shard_map/ppermute | solution.py:19
  102.0 4.3 %multiply_reduce_fusion = (bf16[1536]{0:T(1024)(128)(2,1)S(1)}, bf16[1536]{0:T(1024)(128)(2,1)S(1)}, f32[512,1536]{1,0:T(8,128)}) fusion(f32[512,1536]{1,0:T(8,128)S(1)} %get-tuple-element.23, bf16[512,1536]{1,0:T(8,128)(2,1)S(1)} %subtract_convert_fusion, bf16[1536,1536]{1,0:T(8,128)(2,1)S(1)} %constant_dynamic-update-slice_fusion), kind=kOutput, calls=%fused_computation.2 | convolution fusion | flops 2418275328 | bytes 12589056 | tf_op jit(solution)/shard_map/dot_general | solution.py:35
  106.4 1.9 %fusion.2 = bf16[384,768]{1,0:T(8,128)(2,1)S(1)} fusion(bf16[384,768]{1,0:T(8,128)(2,1)} %collective-permute-done.6, bf16[512,1536]{1,0:T(8,128)(2,1)} %copy-done.7, s32[]{:T(128)S(6)} %select_n.20, bf16[512,1536]{1,0:T(8,128)(2,1)} %copy-done.4, s32[]{:T(128)S(6)} %select_n.22), kind=kOutput, calls=%fused_computation.12 | convolution fusion | flops 302874624 | bytes 2359304 | tf_op jit(solution)/shard_map/dot_general | solution.py:35
  108.4 14.5 %all_to_all.25 = bf16[4,96,896]{2,1,0:T(8,128)(2,1)S(1)} all-to-all(bf16[4,96,896]{2,1,0:T(8,128)(2,1)S(1)} %pad_maximum_fusion.3), channel_id=1, replica_groups=mesh['y'=4,'xl'=2,'zh'=4,'zl'=4,'xh'=2,'core'=2] {'xl','xh'}, dimensions={0} | all-to-all | bytes 1376256 | tf_op jit(solution)/shard_map/all_to_all | solution.py:146
  123.7 5.6 %all-to-all-start.2 = ((bf16[4,24,896]{2,1,0:T(8,128)(2,1)}), bf16[4,24,896]{2,1,0:T(8,128)(2,1)S(1)}, u32[]{:S(2)}, u32[]{:S(2)}) async-start(bf16[4,24,896]{2,1,0:T(8,128)(2,1)} %bitcast.10), calls=%async_computation.2 | async-start | bytes 344064 | tf_op jit(solution)/shard_map/all_to_all | solution.py:150
  129.8 4.4 %all-to-all-done.2 = bf16[4,24,896]{2,1,0:T(8,128)(2,1)S(1)} async-done(((bf16[4,24,896]{2,1,0:T(8,128)(2,1)}), bf16[4,24,896]{2,1,0:T(8,128)(2,1)S(1)}, u32[]{:S(2)}, u32[]{:S(2)}) %all-to-all-start.2) | async-done | bytes 172064 | tf_op jit(solution)/shard_map/all_to_all | solution.py:150
  135.0 12.5 %all-to-all-start.3 = ((bf16[4,24,896]{2,1,0:T(8,128)(2,1)}), bf16[4,24,896]{2,1,0:T(8,128)(2,1)S(1)}, u32[]{:S(2)}, u32[]{:S(2)}) async-start(bf16[4,24,896]{2,1,0:T(8,128)(2,1)} %broadcast_in_dim.16), calls=%async_computation.3 | async-start | bytes 344064 | tf_op jit(solution)/shard_map/all_to_all | solution.py:41
  148.8 5.4 %collective-permute-start.7 = (f32[128,1536]{1,0:T(8,128)}, f32[128,1536]{1,0:T(8,128)}, u32[]{:S(2)}, u32[]{:S(2)}) collective-permute-start(f32[128,1536]{1,0:T(8,128)} %fusion.38), channel_id=1, source_target_pairs={{0,1},{1,0},{2,3},{3,2},{4,5},{5,4},{6,7},{7,6},{8,9},{9,8},{10,11... | collective-permute-start | bytes 2359304 | tf_op jit(solution)/shard_map/ppermute | solution.py:19
  157.4 2.8 %all-to-all-done.3 = bf16[4,24,896]{2,1,0:T(8,128)(2,1)S(1)} async-done(((bf16[4,24,896]{2,1,0:T(8,128)(2,1)}), bf16[4,24,896]{2,1,0:T(8,128)(2,1)S(1)}, u32[]{:S(2)}, u32[]{:S(2)}) %all-to-all-start.3) | async-done | bytes 172064 | tf_op jit(solution)/shard_map/all_to_all | solution.py:41
  162.4 4.1 %all-to-all-start.4 = ((bf16[8,24,896]{2,1,0:T(8,128)(2,1)}), bf16[8,24,896]{2,1,0:T(8,128)(2,1)}, u32[]{:S(2)}, u32[]{:S(2)}) async-start(bf16[8,24,896]{2,1,0:T(8,128)(2,1)} %broadcast_in_dim.17), calls=%async_computation.4 | async-start | bytes 688128 | tf_op jit(solution)/shard_map/all_to_all | solution.py:41
  168.6 8.1 %collective-permute-start.8 = (bf16[2,128,1536]{2,1,0:T(8,128)(2,1)S(1)}, bf16[2,128,1536]{2,1,0:T(8,128)(2,1)S(1)}, u32[]{:S(2)}, u32[]{:S(2)}) collective-permute-start(bf16[2,128,1536]{2,1,0:T(8,128)(2,1)S(1)} %pad_maximum_fusion.2), channel_id=1, source_target_pairs={{0,0},{1,64},{64,1},{65,65},{2,2},{3,66},{66,3},{67,67},{4,4},{5,6... | collective-permute-start | bytes 2359304 | tf_op jit(solution)/shard_map/ppermute | solution.py:23
  176.7 7.9 %collective-permute-start.9 = (bf16[8,24,896]{2,1,0:T(8,128)(2,1)}, bf16[8,24,896]{2,1,0:T(8,128)(2,1)S(1)}, u32[]{:S(2)}, u32[]{:S(2)}) collective-permute-start(bf16[8,24,896]{2,1,0:T(8,128)(2,1)} %all-to-all-done.4), channel_id=1, source_target_pairs={{0,1},{1,0},{2,3},{3,2},{4,5},{5,4},{6,7},{7,6},{8,9},{9,8},{10,11... | collective-permute-start | bytes 1032200 | tf_op jit(solution)/shard_map/ppermute | solution.py:19
  184.6 2.2 %collective-permute-done.8 = bf16[2,128,1536]{2,1,0:T(8,128)(2,1)S(1)} collective-permute-done((bf16[2,128,1536]{2,1,0:T(8,128)(2,1)S(1)}, bf16[2,128,1536]{2,1,0:T(8,128)(2,1)S(1)}, u32[]{:S(2)}, u32[]{:S(2)}) %collective-permute-start.8) | collective-permute-done | bytes 786464 | tf_op jit(solution)/shard_map/ppermute | solution.py:23
  (94 shorter events, 34.2 us)
Async XLA Ops:
  0.6 5.8 %copy-start = (bf16[192,1536]{1,0:T(8,128)(2,1)S(1)}, bf16[192,1536]{1,0:T(8,128)(2,1)}, u32[]{:S(2)}) copy-start(bf16[192,1536]{1,0:T(8,128)(2,1)} %param.10) | copy-start | bytes 1769476
  1.9 15.3 %collective-permute-start = (bf16[2,128,1536]{2,1,0:T(8,128)(2,1)S(1)}, bf16[2,128,1536]{2,1,0:T(8,128)(2,1)S(1)}, u32[]{:S(2)}, u32[]{:S(2)}) collective-permute-start(bf16[2,128,1536]{2,1,0:T(8,128)(2,1)S(1)} %pad_maximum_fusion), channel_id=1, source_target_pairs={{0,0},{1,64},{64,1},{65,65},{2,2},{3,66},{66,3},{67,67},{4,4},{5,6... | collective-permute-start | bytes 2359304 | tf_op jit(solution)/shard_map/ppermute | solution.py:23
  8.0 65.0 %all-to-all-start = ((bf16[8,192,768]{2,1,0:T(8,128)(2,1)}), bf16[8,192,768]{2,1,0:T(8,128)(2,1)}, u32[]{:S(2)}, u32[]{:S(2)}) async-start(bf16[8,192,768]{2,1,0:T(8,128)(2,1)} %broadcast_in_dim.13), calls=%async_computation | async-start | bytes 4718592 | tf_op jit(solution)/shard_map/all_to_all | solution.py:41
  17.4 61.6 %copy-start.9 = (f32[1536]{0:T(1024)S(1)}, f32[1536]{0:T(1024)}, u32[]{:S(2)}) copy-start(f32[1536]{0:T(1024)} %param.8) | copy-start | bytes 18436
  17.4 61.6 %copy-start.10 = (f32[1536]{0:T(1024)S(1)}, f32[1536]{0:T(1024)}, u32[]{:S(2)}) copy-start(f32[1536]{0:T(1024)} %param.9) | copy-start | bytes 18436
  17.6 67.3 %copy-start.13 = (f32[128]{0:T(128)}, f32[128]{0:T(128)S(1)}, u32[]{:S(2)}) copy-start(f32[128]{0:T(128)S(1)} %get-tuple-element.32) | copy-start | bytes 1540
  18.1 66.9 %copy-start.11 = (f32[128]{0:T(128)}, f32[128]{0:T(128)S(1)}, u32[]{:S(2)}) copy-start(f32[128]{0:T(128)S(1)} %add_rsqrt_fusion.1) | copy-start | bytes 1540
  18.3 41.6 %collective-permute-start.1 = (bf16[2,128,1536]{2,1,0:T(8,128)(2,1)S(1)}, bf16[2,128,1536]{2,1,0:T(8,128)(2,1)S(1)}, u32[]{:S(2)}, u32[]{:S(2)}) collective-permute-start(bf16[2,128,1536]{2,1,0:T(8,128)(2,1)S(1)} %pad_maximum_fusion.1.own), channel_id=1, source_target_pairs={{0,128},{128,256},{256,384},{384,0},{1,129},{129,257},{257,385},{3... | collective-permute-start | bytes 2359304 | tf_op jit(solution)/shard_map/ppermute | solution.py:19
  22.0 37.9 %collective-permute-start.2 = (bf16[2,128,1536]{2,1,0:T(8,128)(2,1)S(1)}, bf16[2,128,1536]{2,1,0:T(8,128)(2,1)S(1)}, u32[]{:S(2)}, u32[]{:S(2)}) collective-permute-start(bf16[2,128,1536]{2,1,0:T(8,128)(2,1)S(1)} %pad_maximum_fusion.1.own), channel_id=1, source_target_pairs={{0,384},{128,0},{256,128},{384,256},{1,385},{129,1},{257,129},{385... | collective-permute-start | bytes 2359304 | tf_op jit(solution)/shard_map/ppermute | solution.py:19
  25.6 46.5 %collective-permute-start.3 = (bf16[2,128,1536]{2,1,0:T(8,128)(2,1)S(1)}, bf16[2,128,1536]{2,1,0:T(8,128)(2,1)S(1)}, u32[]{:S(2)}, u32[]{:S(2)}) collective-permute-start(bf16[2,128,1536]{2,1,0:T(8,128)(2,1)S(1)} %pad_maximum_fusion.1.own), channel_id=1, source_target_pairs={{0,256},{128,384},{256,0},{384,128},{1,257},{129,385},{257,1},{385... | collective-permute-start | bytes 2359304 | tf_op jit(solution)/shard_map/ppermute | solution.py:19
  73.0 16.1 %collective-permute-start.4 = (bf16[1536,768]{1,0:T(8,128)(2,1)}, bf16[1536,768]{1,0:T(8,128)(2,1)}, u32[]{:S(2)}, u32[]{:S(2)}) collective-permute-start(bf16[1536,768]{1,0:T(8,128)(2,1)} %bitcast.5), channel_id=1, source_target_pairs={{0,1},{1,0},{2,3},{3,2},{4,5},{5,4},{6,7},{7,6},{8,9},{9,8},{10,11... | collective-permute-start | bytes 7077896 | tf_op jit(solution)/shard_map/ppermute | solution.py:19
  84.9 14.2 %copy-start.4 = (bf16[512,1536]{1,0:T(8,128)(2,1)}, bf16[512,1536]{1,0:T(8,128)(2,1)S(1)}, u32[]{:S(2)}) copy-start(bf16[512,1536]{1,0:T(8,128)(2,1)S(1)} %get-tuple-element.16) | copy-start | bytes 4718596
  84.9 17.1 %copy-start.1 = (f32[512,1536]{1,0:T(8,128)}, f32[512,1536]{1,0:T(8,128)S(1)}, u32[]{:S(2)}) copy-start(f32[512,1536]{1,0:T(8,128)S(1)} %get-tuple-element.23) | copy-start | bytes 9437188
  84.9 10.2 %collective-permute-start.5 = (bf16[512,1536]{1,0:T(8,128)(2,1)S(1)}, bf16[512,1536]{1,0:T(8,128)(2,1)S(1)}, u32[]{:S(2)}, u32[]{:S(2)}) collective-permute-start(bf16[512,1536]{1,0:T(8,128)(2,1)S(1)} %get-tuple-element.18), channel_id=1, source_target_pairs={{0,1},{1,0},{2,3},{3,2},{4,5},{5,4},{6,7},{7,6},{8,9},{9,8},{10,11... | collective-permute-start | bytes 4718600 | tf_op jit(solution)/shard_map/ppermute | solution.py:19
  99.1 7.3 %copy-start.7 = (bf16[512,1536]{1,0:T(8,128)(2,1)}, bf16[512,1536]{1,0:T(8,128)(2,1)S(1)}, u32[]{:S(2)}) copy-start(bf16[512,1536]{1,0:T(8,128)(2,1)S(1)} %subtract_convert_fusion) | copy-start | bytes 4718596
  99.6 6.8 %collective-permute-start.6 = (bf16[384,768]{1,0:T(8,128)(2,1)S(1)}, bf16[384,768]{1,0:T(8,128)(2,1)}, u32[]{:S(2)}, u32[]{:S(2)}) collective-permute-start(bf16[384,768]{1,0:T(8,128)(2,1)S(1)} %convolution_convert_fusion), channel_id=1, source_target_pairs={{0,1},{1,0},{2,3},{3,2},{4,5},{5,4},{6,7},{7,6},{8,9},{9,8},{10,11... | collective-permute-start | bytes 1769480 | tf_op jit(solution)/shard_map/ppermute | solution.py:19
  123.7 10.6 %all-to-all-start.2 = ((bf16[4,24,896]{2,1,0:T(8,128)(2,1)}), bf16[4,24,896]{2,1,0:T(8,128)(2,1)S(1)}, u32[]{:S(2)}, u32[]{:S(2)}) async-start(bf16[4,24,896]{2,1,0:T(8,128)(2,1)} %bitcast.10), calls=%async_computation.2 | async-start | bytes 344064 | tf_op jit(solution)/shard_map/all_to_all | solution.py:150
  135.0 25.2 %all-to-all-start.3 = ((bf16[4,24,896]{2,1,0:T(8,128)(2,1)}), bf16[4,24,896]{2,1,0:T(8,128)(2,1)S(1)}, u32[]{:S(2)}, u32[]{:S(2)}) async-start(bf16[4,24,896]{2,1,0:T(8,128)(2,1)} %broadcast_in_dim.16), calls=%async_computation.3 | async-start | bytes 344064 | tf_op jit(solution)/shard_map/all_to_all | solution.py:41
  147.5 8.2 %copy-start.15 = (f32[128]{0:T(128)S(1)}, f32[128]{0:T(128)}, u32[]{:S(2)}) copy-start(f32[128]{0:T(128)} %add_rsqrt_fusion.2) | copy-start | bytes 1540
  148.8 17.7 %collective-permute-start.7 = (f32[128,1536]{1,0:T(8,128)}, f32[128,1536]{1,0:T(8,128)}, u32[]{:S(2)}, u32[]{:S(2)}) collective-permute-start(f32[128,1536]{1,0:T(8,128)} %fusion.38), channel_id=1, source_target_pairs={{0,1},{1,0},{2,3},{3,2},{4,5},{5,4},{6,7},{7,6},{8,9},{9,8},{10,11... | collective-permute-start | bytes 2359304 | tf_op jit(solution)/shard_map/ppermute | solution.py:19
  155.8 10.8 %copy-start.6 = (bf16[2,128,1536]{2,1,0:T(8,128)(2,1)S(1)}, bf16[2,128,1536]{2,1,0:T(8,128)(2,1)}, u32[]{:S(2)}) copy-start(bf16[2,128,1536]{2,1,0:T(8,128)(2,1)} %copy-done.5) | copy-start | bytes 2359300
  162.4 14.3 %all-to-all-start.4 = ((bf16[8,24,896]{2,1,0:T(8,128)(2,1)}), bf16[8,24,896]{2,1,0:T(8,128)(2,1)}, u32[]{:S(2)}, u32[]{:S(2)}) async-start(bf16[8,24,896]{2,1,0:T(8,128)(2,1)} %broadcast_in_dim.17), calls=%async_computation.4 | async-start | bytes 688128 | tf_op jit(solution)/shard_map/all_to_all | solution.py:41
  168.6 18.2 %collective-permute-start.8 = (bf16[2,128,1536]{2,1,0:T(8,128)(2,1)S(1)}, bf16[2,128,1536]{2,1,0:T(8,128)(2,1)S(1)}, u32[]{:S(2)}, u32[]{:S(2)}) collective-permute-start(bf16[2,128,1536]{2,1,0:T(8,128)(2,1)S(1)} %pad_maximum_fusion.2), channel_id=1, source_target_pairs={{0,0},{1,64},{64,1},{65,65},{2,2},{3,66},{66,3},{67,67},{4,4},{5,6... | collective-permute-start | bytes 2359304 | tf_op jit(solution)/shard_map/ppermute | solution.py:23
  176.7 12.4 %collective-permute-start.9 = (bf16[8,24,896]{2,1,0:T(8,128)(2,1)}, bf16[8,24,896]{2,1,0:T(8,128)(2,1)S(1)}, u32[]{:S(2)}, u32[]{:S(2)}) collective-permute-start(bf16[8,24,896]{2,1,0:T(8,128)(2,1)} %all-to-all-done.4), channel_id=1, source_target_pairs={{0,1},{1,0},{2,3},{3,2},{4,5},{5,4},{6,7},{7,6},{8,9},{9,8},{10,11... | collective-permute-start | bytes 1032200 | tf_op jit(solution)/shard_map/ppermute | solution.py:19
  (6 other events, 8.6 us)
